TPU v7x, 32 devices: a whole 2x2x4 slice. The times are simulated.
32 devices in a mesh: real: 8 (over y, x, core), site: 4 (over z).
Axes of the slice: x: 2, y: 2, z: 4, core: 2. Of those that a mesh axis runs over, the one named last changes fastest.
Arguments:
- noise: bfloat16 [4096, 6144], P('site', 'real'), may hold values from -6 to 6
- v_factors: bfloat16 [4, 1024, 1024], P('site', 'real'), may hold values from -0.1875 to 0.1875
- u_factors: bfloat16 [4, 1024, 1024], P('site', 'real'), may hold values from -0.1875 to 0.1875
- ranks: int32 [4, 4], replicated, may hold values from 1 to 2, as said below
- skew_g: float32 [4096], P('site'), may hold values from 0.1 to 0.6
- tail_h: float32 [4096], P('site'), may hold values from 0.05 to 0.3
Outputs:
- field: float32 [4096, 6144], P('site', 'real')
Inputs may be any that keep to these rules, and one draw needn't show every extreme that they name: `ranks`: every tile has at least one rank block, and some tile has 2.
All inputs are finite; a program needn't handle non-finite values.
Results may differ from a plain program's by a relative error of at most 0.012.
The roundings to bfloat16 on the way count: a program that leaves them out, or rounds other values in their place, can miss the bound.
Values may be sent and summed in bfloat16 or wider, within the bound.
No kernel may reach another device: no remote copies, remote signals or barrier semaphores. Data moves between devices by JAX's collectives and lax.ppermute only.
A program may use at most 128 MiB of HBM per device.

v0:
```python
import jax
import jax.numpy as jnp
from jax import lax
from jax.sharding import PartitionSpec as P

CAP = 2


def per_device(noise, v_factors, u_factors, ranks, skew_g, tail_h):
    group_count = lax.axis_size("site")
    myself = lax.axis_index("site")
    columns = v_factors.shape[2]
    per_dest = columns // group_count
    real_count = noise.shape[1]
    groups = jnp.arange(group_count, dtype=jnp.int32)
    own_column = jnp.sum(jnp.where(groups[None, :] == myself, ranks, 0), axis=1)
    levels = jnp.arange(CAP, dtype=jnp.int32)
    alive = (levels[None, :] < own_column[:, None]).astype(jnp.float32)
    v_whole = lax.all_gather(v_factors, "real", axis=1, tiled=True)[0]
    projected = lax.dot_general(
        v_whole, noise, (((0,), (0,)), ((), ())), preferred_element_type=jnp.float32
    )
    masked = (
        projected.reshape(group_count, CAP, per_dest // CAP, real_count) * alive[:, :, None, None]
    )
    sending = masked.astype(jnp.bfloat16).reshape(group_count, per_dest, real_count)
    received = lax.all_to_all(sending, "site", split_axis=0, concat_axis=0, tiled=True)
    flattened = received.reshape(columns, real_count)
    gaussian = jnp.dot(
        lax.all_gather(u_factors, "real", axis=1, tiled=True)[0],
        flattened,
        preferred_element_type=jnp.float32,
    )
    skew_col = skew_g[:, None]
    tail_col = tail_h[:, None]
    return jnp.expm1(skew_col * gaussian) / skew_col * jnp.exp(0.5 * tail_col * gaussian * gaussian)


def solution(mesh):
    placed = (
        P("site", "real"),
        P("site", "real", None),
        P("site", "real", None),
        P(),
        P("site"),
        P("site"),
    )
    return jax.shard_map(
        per_device, mesh=mesh, in_specs=placed, out_specs=P("site", "real"), check_vma=False
    )
```

profile of v0, /device:TPU:0, one launch (start us, length us, event | category | flops | bytes accessed | tf_op | source)
XLA Modules:
  0.0 107.1 jit_solution(15902613895336631046)
XLA Ops:
  6.5 0.0 copy-start
  6.5 0.0 all-gather.3.cloned.1.call-start
  6.5 0.7 all-gather.3.cloned.1.call-update
  7.3 0.0 all-gather.5.cloned.1.call-start
  7.3 0.7 all-gather.5.cloned.1.call-update
  8.0 0.8 select_reduce_fusion
  8.8 0.1 fusion.9
  8.9 31.0 %all-gather.3.cloned.1.call-done = bf16[1,1024,1024]{2,1,0:T(8,128)(2,1)} async-done(((bf16[1,128,1024]{2,1,0:T(8,128)(2,1)}), bf16[1,1024,1024]{2,1,0:T(8,128)(2,1)}) %all-gather.3.cloned.1.call-update) | async-done | bytes 2097168 | tf_op jit(solution)/shard_map/all_gather | solution.py:19
  39.9 3.9 %copy.7 = bf16[1024,1024]{1,0:T(8,128)(2,1)} copy(bf16[1024,1024]{0,1:T(8,128)(2,1)} %bitcast.27) | data formatting | bytes 4194304 | tf_op jit(solution)/shard_map/dot_general | solution.py:20
  43.8 0.0 copy-done
  43.8 4.5 %multiply_convert_fusion = bf16[4,2,128,768]{3,2,1,0:T(8,128)(2,1)} fusion(bf16[4,2,128,1024]{3,2,1,0:T(8,128)(2,1)} %bitcast.28, bf16[1024,768]{1,0:T(8,128)(2,1)S(1)} %copy-done, f32[4,2]{1,0:T(4,128)S(1)} %fusion.9), kind=kOutput, calls=%fused_computation.6 | convolution fusion | flops 1612185600 | bytes 5242912 | tf_op jit(solution)/shard_map/dot_general | solution.py:20
  48.3 0.0 copy-start.1
  48.3 0.0 copy-start.2
  48.3 4.7 %all-to-all-start = ((bf16[4,256,768]{2,1,0:T(8,128)(2,1)}), bf16[4,256,768]{2,1,0:T(8,128)(2,1)S(1)}, u32[]{:S(2)}, u32[]{:S(2)}) async-start(bf16[4,256,768]{2,1,0:T(8,128)(2,1)} %bitcast.30), calls=%async_computation | async-start | bytes 3145728 | tf_op jit(solution)/shard_map/all_to_all | solution.py:27
  53.1 0.0 copy-done.1
  53.1 16.6 %all-gather.5.cloned.1.call-done = bf16[1,1024,1024]{2,1,0:T(8,128)(2,1)} async-done(((bf16[1,128,1024]{2,1,0:T(8,128)(2,1)}), bf16[1,1024,1024]{2,1,0:T(8,128)(2,1)}) %all-gather.5.cloned.1.call-update) | async-done | bytes 2097168 | tf_op jit(solution)/shard_map/all_gather | solution.py:30
  69.7 20.8 %all-to-all-done = bf16[4,256,768]{2,1,0:T(8,128)(2,1)S(1)} async-done(((bf16[4,256,768]{2,1,0:T(8,128)(2,1)}), bf16[4,256,768]{2,1,0:T(8,128)(2,1)S(1)}, u32[]{:S(2)}, u32[]{:S(2)}) %all-to-all-start) | async-done | bytes 1572896 | tf_op jit(solution)/shard_map/all_to_all | solution.py:27
  90.5 0.0 copy-done.2
  90.5 6.3 %fusion.1 = f32[1024,768]{0,1:T(8,128)} fusion(f32[1024]{0:T(1024)S(1)} %broadcast_multiply_fusion, f32[1024]{0:T(1024)S(1)} %copy-done.2, bf16[1024,768]{1,0:T(8,128)(2,1)S(1)} %bitcast.29, bf16[1,1024,1024]{2,1,0:T(8,128)(2,1)} %all-gather.5.cloned.1.call-done), kind=kOutput, calls=%fused_computation.2 | convolution fusion | flops 1614544896 | bytes 6823936 | tf_op jit(solution)/shard_map/dot_general | solution.py:29
  96.7 3.5 %copy.8 = f32[1024,768]{1,0:T(8,128)} copy(f32[1024,768]{0,1:T(8,128)} %fusion.1) | data formatting | bytes 6291456 | tf_op jit(solution)/shard_map/mul | solution.py:36
  (2 shorter events, 0.0 us)
Async XLA Ops:
  6.5 37.3 %copy-start = (bf16[1024,768]{1,0:T(8,128)(2,1)S(1)}, bf16[1024,768]{1,0:T(8,128)(2,1)}, u32[]{:S(2)}) copy-start(bf16[1024,768]{1,0:T(8,128)(2,1)} %param.6) | copy-start | bytes 4718596
  6.5 33.3 %all-gather.3.cloned.1.call-start = ((), (), s32[]{:S(2)}) async-start(), calls=%async_computation.1 | async-start | bytes 2359296 | tf_op jit(solution)/shard_map/all_gather | solution.py:19
  7.3 62.4 %all-gather.5.cloned.1.call-start = ((), (), s32[]{:S(2)}) async-start(), calls=%async_computation.2 | async-start | bytes 2359296 | tf_op jit(solution)/shard_map/all_gather | solution.py:30
  48.3 4.7 %copy-start.1 = (f32[1024]{0:T(1024)S(1)}, f32[1024]{0:T(1024)}, u32[]{:S(2)}) copy-start(f32[1024]{0:T(1024)} %param.11) | copy-start | bytes 12292
  48.3 42.1 %copy-start.2 = (f32[1024]{0:T(1024)S(1)}, f32[1024]{0:T(1024)}, u32[]{:S(2)}) copy-start(f32[1024]{0:T(1024)} %param.10) | copy-start | bytes 12292
  48.3 42.1 %all-to-all-start = ((bf16[4,256,768]{2,1,0:T(8,128)(2,1)}), bf16[4,256,768]{2,1,0:T(8,128)(2,1)S(1)}, u32[]{:S(2)}, u32[]{:S(2)}) async-start(bf16[4,256,768]{2,1,0:T(8,128)(2,1)} %bitcast.30), calls=%async_computation | async-start | bytes 3145728 | tf_op jit(solution)/shard_map/all_to_all | solution.py:27
Sparse Core Ops, SparseCore 0:
  9.2 30.5 all-gather.2
  41.8 27.8 all-gather.4
where the time goes:
time: 107 us
  waiting for transfers between devices  69.8 us (65%)
  between operations  13.4 us (13%)
  matrix products  10.8 us (10%)
  local copies, waits for them, and re-layouts  7.48 us (7%)
  starting transfers between devices  4.77 us (4%)
    all_gather x1, waiting for transfers between devices, per_device(): v_whole = lax.all_gather(v_factors, 'real', axis=1, tiled=True)[0]  31 us
    all_to_all x1, waiting for transfers between devices, per_device(): lax.all_to_all(sending, 'site', split_axis=0, concat_axis=0, tiled=True)  20.8 us
    all_gather x1, waiting for transfers between devices, per_device(): lax.all_gather(u_factors, 'real', axis=1, tiled=True)[0]  16.6 us
    dot_general x1, matrix products, per_device(): jnp.dot(lax.all_gather(u_factors, 'real', axis=1, tiled=True)[0], flatten...  6.26 us
    all_to_all x1, starting transfers between devices, per_device(): lax.all_to_all(sending, 'site', split_axis=0, concat_axis=0, tiled=True)  4.73 us
    dot_general x1, matrix products, per_device(): lax.dot_general(v_whole, noise, (((0,), (0,)), ((), ())), preferred_eleme...  4.53 us
    dot_general x1, local copies, waits for them, and re-layouts, per_device(): lax.dot_general(v_whole, noise, (((0,), (0,)), ((), ())), preferred_eleme...  3.93 us
    mul x1, local copies, waits for them, and re-layouts, per_device(): jnp.expm1(skew_col * gaussian) / skew_col  3.54 us
  transfers between devices with their start and end apart: 3, of which 3 were waited for; matrix products, arithmetic and copies ran while one was open for 9% of the time, Pallas kernels for 0%

commit v1 on v0

v1 whole, which is shorter than its diff:
```python
import functools

import jax
import jax.numpy as jnp
from jax import lax
from jax.experimental import pallas as pl
from jax.experimental.pallas import tpu as pltpu
from jax.sharding import PartitionSpec as P

CAP = 2


def project_kernel(shifts, n_pieces, ranks_ref, noise_ref, *refs):
    pieces, outs, whole = refs[:n_pieces], refs[n_pieces:-1], refs[-1]
    site_count = lax.axis_size("site")
    source = lax.axis_index("site")
    me = lax.axis_index("real")
    rows = pieces[0].shape[0]
    for distance, piece in enumerate(pieces):
        start = pl.multiple_of((me ^ distance) * rows, rows)
        whole[pl.ds(start, rows), :] = piece[...]
    for place, (shift, out_ref) in enumerate(zip(shifts, outs)):
        target = lax.rem(source + shift, site_count)
        columns = out_ref.shape[0]
        projected = lax.dot_general(
            whole[:, place * columns : (place + 1) * columns],
            noise_ref[...],
            (((0,), (0,)), ((), ())),
            preferred_element_type=jnp.float32,
        )
        rank = ranks_ref[target, source]
        block = columns // CAP
        for level in range(CAP):
            part = projected[level * block : (level + 1) * block]
            part = part * jnp.where(level < rank, 1.0, 0.0)
            out_ref[level * block : (level + 1) * block, :] = part.astype(out_ref.dtype)


def project(shifts, ranks, noise, pieces):
    sites, reals = noise.shape
    columns = pieces[0].shape[1]
    return pl.pallas_call(
        functools.partial(project_kernel, shifts, len(pieces)),
        out_shape=[jax.ShapeDtypeStruct((columns // len(shifts), reals), jnp.bfloat16)]
        * len(shifts),
        in_specs=[pl.BlockSpec(memory_space=pltpu.SMEM)]
        + [pl.BlockSpec(memory_space=pltpu.VMEM)] * (1 + len(pieces)),
        out_specs=[pl.BlockSpec(memory_space=pltpu.VMEM)] * len(shifts),
        scratch_shapes=[pltpu.VMEM((sites, columns), jnp.bfloat16)],
        compiler_params=pltpu.CompilerParams(vmem_limit_bytes=44 * 2**20),
        cost_estimate=pl.CostEstimate(
            flops=2 * sites * columns * reals,
            bytes_accessed=2 * (sites * columns + sites * reals + columns * reals),
            transcendentals=0,
        ),
        name=f"project_{len(shifts)}",
    )(ranks, noise, *pieces)


def finish_kernel(shifts, u_ref, skew_ref, tail_ref, *refs):
    coefs, out_ref = refs[: len(shifts)], refs[len(shifts)]
    site_count = lax.axis_size("site")
    target = lax.axis_index("site")
    gaussian = jnp.zeros(out_ref.shape, jnp.float32)
    for shift, coef in zip(shifts, coefs):
        columns = coef.shape[0]
        source = lax.rem(target + (site_count - shift), site_count)
        start = pl.multiple_of(source * columns, columns)
        gaussian += jnp.dot(
            u_ref[:, pl.ds(start, columns)], coef[...], preferred_element_type=jnp.float32
        )
    skew, tail = skew_ref[...], tail_ref[...]
    scaled = skew * gaussian
    series = 1.0 + scaled * (0.5 + scaled * (1 / 6 + scaled * (1 / 24 + scaled * (1 / 120))))
    grown = jnp.where(jnp.abs(scaled) < 0.125, scaled * series, jnp.exp(scaled) - 1.0)
    out_ref[...] = grown * (1.0 / skew) * jnp.exp((0.5 * tail) * gaussian * gaussian)


def finish(shifts, u_whole, skew, tail, coefs):
    rows, columns = u_whole.shape
    reals = coefs[0].shape[1]
    block = min(rows, 256)
    by_row = lambda i: (i, 0)
    fixed = lambda i: (0, 0)
    return pl.pallas_call(
        functools.partial(finish_kernel, shifts),
        out_shape=jax.ShapeDtypeStruct((rows, reals), jnp.float32),
        grid=(rows // block,),
        in_specs=[
            pl.BlockSpec((block, columns), by_row),
            pl.BlockSpec((block, 1), by_row),
            pl.BlockSpec((block, 1), by_row),
        ]
        + [pl.BlockSpec(coef.shape, fixed) for coef in coefs],
        out_specs=pl.BlockSpec((block, reals), by_row),
        compiler_params=pltpu.CompilerParams(vmem_limit_bytes=40 * 2**20),
        cost_estimate=pl.CostEstimate(
            flops=2 * rows * columns * reals,
            bytes_accessed=2 * rows * columns + 2 * columns * reals + 4 * rows * reals,
            transcendentals=2 * rows * reals,
        ),
        name="finish",
    )(u_whole, skew, tail, *coefs)


def gather_pieces(own, count):
    pieces = {0: own}
    for distance in range(2, count, 2):
        pieces[distance] = lax.ppermute(own, "real", [(k, k ^ distance) for k in range(count)])
    for distance in range(0, count, 2):
        pieces[distance + 1] = lax.ppermute(
            pieces[distance], "real", [(k, k ^ 1) for k in range(count)]
        )
    return [pieces[distance] for distance in range(count)]


def per_device(noise, v_factors, u_factors, ranks, skew_g, tail_h):
    site_count = lax.axis_size("site")
    real_count = lax.axis_size("real")
    source = lax.axis_index("site")
    rows, columns = v_factors.shape[1:]
    per_dest = columns // site_count
    middle = site_count // 2
    shifts = [middle]
    for step in range(1, site_count):
        for shift in (middle - step, middle + step):
            if 0 < shift < site_count and shift not in shifts:
                shifts.append(shift)
    shifts.append(0)
    coefs = []
    done = v_factors
    for group in (shifts[:1], shifts[1:]):
        v_own = lax.optimization_barrier((v_factors, done))[0][0]
        own = jnp.concatenate(
            [
                lax.dynamic_slice(
                    v_own, (0, lax.rem(source + shift, site_count) * per_dest), (rows, per_dest)
                )
                for shift in group
            ],
            axis=1,
        )
        group_coefs = project(tuple(group), ranks, noise, gather_pieces(own, real_count))
        done = group_coefs[0]
        for shift, coef in zip(group, group_coefs):
            if shift:
                coef = lax.ppermute(
                    coef, "site", [(k, (k + shift) % site_count) for k in range(site_count)]
                )
            coefs.append(coef)
    u_whole = lax.all_gather(u_factors, "real", axis=1, tiled=True)[0]
    return finish(tuple(shifts), u_whole, skew_g[:, None], tail_h[:, None], coefs)


def solution(mesh):
    placed = (
        P("site", "real"),
        P("site", "real", None),
        P("site", "real", None),
        P(),
        P("site"),
        P("site"),
    )
    return jax.shard_map(
        per_device, mesh=mesh, in_specs=placed, out_specs=P("site", "real"), check_vma=False
    )
```

time: 107 us -> 84.1 us (0.79)
  the two profiles are of different devices: /device:TPU:0 before, /device:TPU:17 now
where the time goes in v1:
time: 84.1 us; the launch traced here: 83.8 us
  waiting for transfers between devices  41 us (49%)
  starting transfers between devices  15.3 us (18%)
  between operations  13.5 us (16%)
  Pallas kernels  8.94 us (11%)
  local copies, waits for them, and re-layouts  5.08 us (6%)
    ppermute x3, waiting for transfers between devices, per_device(): lax.ppermute(coef, 'site', [(k, (k + shift) % site_count) for k in range(...  31 us
    ppermute x8, starting transfers between devices, gather_pieces(): lax.ppermute(pieces[distance], 'real', [(k, k ^ 1) for k in range(count)])  8.41 us
    ppermute x6, waiting for transfers between devices, gather_pieces(): lax.ppermute(own, 'real', [(k, k ^ distance) for k in range(count)])  6.77 us
    ppermute x6, starting transfers between devices, gather_pieces(): lax.ppermute(own, 'real', [(k, k ^ distance) for k in range(count)])  5.36 us
    pallas_call x1, Pallas kernels, finish(): pl.pallas_call(functools.partial(finish_kernel, shifts), out_shape=jax.Sh...  5.05 us
    pallas_call x2, Pallas kernels, project(): pl.pallas_call(functools.partial(project_kernel, shifts, len(pieces)), ou...  3.89 us
    unnamed x12, local copies, waits for them, and re-layouts  3.76 us
    ppermute x8, waiting for transfers between devices, gather_pieces(): lax.ppermute(pieces[distance], 'real', [(k, k ^ 1) for k in range(count)])  2.53 us
  transfers between devices with their start and end apart: 18, of which 8 were waited for; matrix products, arithmetic and copies ran while one was open for 2% of the time, Pallas kernels for 5%

profile of v1, /device:TPU:17, one launch (start us, length us, event | category | flops | bytes accessed | tf_op | source)
XLA Modules:
  0.0 83.8 jit_solution(14816037644282356571)
XLA Ops:
  6.5 0.7 all-gather.2.cloned.1.call-update
  7.3 0.8 %dynamic-slice_bitcast_fusion.3.refs_0_ = bf16[128,256]{1,0:T(8,128)(2,1)S(1)} fusion(bf16[1,128,1024]{2,1,0:T(8,128)(2,1)} %param.7, s32[]{:T(128)S(6)} %select_n.12), kind=kLoop, calls=%fused_computation.4 | loop fusion | bytes 131076 | tf_op jit(solution)/shard_map/dynamic_slice | solution.py:136
  8.1 2.2 %collective-permute-start.5 = (bf16[128,256]{1,0:T(8,128)(2,1)S(1)}, bf16[128,256]{1,0:T(8,128)(2,1)S(1)}, u32[]{:S(2)}, u32[]{:S(2)}) collective-permute-start(bf16[128,256]{1,0:T(8,128)(2,1)S(1)} %dynamic-slice_bitcast_fusion.3.refs_0_), channel_id=1, source_target_pairs={{0,24},{4,28},{8,16},{12,20},{16,8},{20,12},{24,0},{28,4},{1,25},{... | collective-permute-start | bytes 196616 | tf_op jit(solution)/shard_map/ppermute | solution.py:109
  10.3 0.2 collective-permute-start.3
  10.5 0.3 collective-permute-start.1
  10.8 1.5 %collective-permute-start = (bf16[128,256]{1,0:T(8,128)(2,1)S(1)}, bf16[128,256]{1,0:T(8,128)(2,1)S(1)}, u32[]{:S(2)}, u32[]{:S(2)}) collective-permute-start(bf16[128,256]{1,0:T(8,128)(2,1)S(1)} %dynamic-slice_bitcast_fusion.3.refs_0_), channel_id=1, source_target_pairs={{0,4},{4,0},{8,12},{12,8},{16,20},{20,16},{24,28},{28,24},{1,5},{5... | collective-permute-start | bytes 196616 | tf_op jit(solution)/shard_map/ppermute | solution.py:111
  12.3 1.7 %collective-permute-start.6 = (bf16[128,256]{1,0:T(8,128)(2,1)S(1)}, bf16[128,256]{1,0:T(8,128)(2,1)S(1)}, u32[]{:S(2)}, u32[]{:S(2)}) collective-permute-start(bf16[128,256]{1,0:T(8,128)(2,1)S(1)} %collective-permute-done.5.refs_6_), channel_id=1, source_target_pairs={{0,4},{4,0},{8,12},{12,8},{16,20},{20,16},{24,28},{28,24},{1,5},{5... | collective-permute-start | bytes 196616 | tf_op jit(solution)/shard_map/ppermute | solution.py:111
  14.0 1.5 %collective-permute-start.4 = (bf16[128,256]{1,0:T(8,128)(2,1)S(1)}, bf16[128,256]{1,0:T(8,128)(2,1)S(1)}, u32[]{:S(2)}, u32[]{:S(2)}) collective-permute-start(bf16[128,256]{1,0:T(8,128)(2,1)S(1)} %collective-permute-done.3.refs_4_), channel_id=1, source_target_pairs={{0,4},{4,0},{8,12},{12,8},{16,20},{20,16},{24,28},{28,24},{1,5},{5... | collective-permute-start | bytes 196616 | tf_op jit(solution)/shard_map/ppermute | solution.py:111
  15.5 0.5 collective-permute-start.2
  16.0 0.4 collective-permute-done.4.refs_5_
  16.4 0.5 collective-permute-done.2.refs_3_
  16.9 1.5 %copy-done.1 = bf16[1024,768]{1,0:T(8,128)(2,1)S(1)} copy-done((bf16[1024,768]{1,0:T(8,128)(2,1)S(1)}, bf16[1024,768]{1,0:T(8,128)(2,1)}, u32[]{:S(2)}) %copy-start.1) | copy-done | bytes 1572888
  18.4 0.7 copy-done.2
  19.1 1.2 %project_1.1 = bf16[256,768]{1,0:T(8,128)(2,1)S(1)} custom-call(s32[4,4]{1,0:T(4,128)S(1)} %copy-done.2, bf16[1024,768]{1,0:T(8,128)(2,1)S(1)} %copy-done.1, bf16[128,256]{1,0:T(8,128)(2,1)S(1)} %dynamic-slice_bitcast_fusion.3.refs_0_, bf16[128,256]{1,0:T(8,128)(2,1)S(1)} %collective-permute-done.refs_1_, ...), custom_call_target="tpu_custom_call" | custom-call | flops 402653184 | bytes 2490368 | tf_op jit(solution)/shard_map/project_1/pallas_call | solution.py:42
  20.4 1.2 %collective-permute-start.13 = (bf16[128,768]{1,0:T(8,128)(2,1)S(1)}, bf16[128,768]{1,0:T(8,128)(2,1)S(1)}, u32[]{:S(2)}, u32[]{:S(2)}) collective-permute-start(bf16[128,768]{1,0:T(8,128)(2,1)S(1)} %pad_maximum_fusion.refs_0_), channel_id=1, source_target_pairs={{0,24},{4,28},{8,16},{12,20},{16,8},{20,12},{24,0},{28,4},{1,25},{... | collective-permute-start | bytes 589832 | tf_op jit(solution)/shard_map/ppermute | solution.py:109
  21.6 0.5 collective-permute-start.11
  22.1 1.0 %collective-permute-start.9 = (bf16[128,768]{1,0:T(8,128)(2,1)S(1)}, bf16[128,768]{1,0:T(8,128)(2,1)S(1)}, u32[]{:S(2)}, u32[]{:S(2)}) collective-permute-start(bf16[128,768]{1,0:T(8,128)(2,1)S(1)} %pad_maximum_fusion.refs_0_), channel_id=1, source_target_pairs={{0,8},{4,12},{8,0},{12,4},{16,24},{20,28},{24,16},{28,20},{1,9},{5... | collective-permute-start | bytes 589832 | tf_op jit(solution)/shard_map/ppermute | solution.py:109
  23.1 1.2 %collective-permute-start.8 = (bf16[128,768]{1,0:T(8,128)(2,1)S(1)}, bf16[128,768]{1,0:T(8,128)(2,1)S(1)}, u32[]{:S(2)}, u32[]{:S(2)}) collective-permute-start(bf16[128,768]{1,0:T(8,128)(2,1)S(1)} %pad_maximum_fusion.refs_0_), channel_id=1, source_target_pairs={{0,4},{4,0},{8,12},{12,8},{16,20},{20,16},{24,28},{28,24},{1,5},{5... | collective-permute-start | bytes 589832 | tf_op jit(solution)/shard_map/ppermute | solution.py:111
  24.3 3.9 %collective-permute-done.13.refs_6_ = bf16[128,768]{1,0:T(8,128)(2,1)S(1)} collective-permute-done((bf16[128,768]{1,0:T(8,128)(2,1)S(1)}, bf16[128,768]{1,0:T(8,128)(2,1)S(1)}, u32[]{:S(2)}, u32[]{:S(2)}) %collective-permute-start.13) | collective-permute-done | bytes 196640 | tf_op jit(solution)/shard_map/ppermute | solution.py:109
  28.2 1.3 %collective-permute-start.14 = (bf16[128,768]{1,0:T(8,128)(2,1)S(1)}, bf16[128,768]{1,0:T(8,128)(2,1)S(1)}, u32[]{:S(2)}, u32[]{:S(2)}) collective-permute-start(bf16[128,768]{1,0:T(8,128)(2,1)S(1)} %collective-permute-done.13.refs_6_), channel_id=1, source_target_pairs={{0,4},{4,0},{8,12},{12,8},{16,20},{20,16},{24,28},{28,24},{1,5},{5... | collective-permute-start | bytes 589832 | tf_op jit(solution)/shard_map/ppermute | solution.py:111
  29.5 2.9 %collective-permute-done.11.refs_4_ = bf16[128,768]{1,0:T(8,128)(2,1)S(1)} collective-permute-done((bf16[128,768]{1,0:T(8,128)(2,1)S(1)}, bf16[128,768]{1,0:T(8,128)(2,1)S(1)}, u32[]{:S(2)}, u32[]{:S(2)}) %collective-permute-start.11) | collective-permute-done | bytes 196640 | tf_op jit(solution)/shard_map/ppermute | solution.py:109
  32.4 0.7 collective-permute-start.12
  33.1 1.0 %collective-permute-done.12.refs_5_ = bf16[128,768]{1,0:T(8,128)(2,1)S(1)} collective-permute-done((bf16[128,768]{1,0:T(8,128)(2,1)S(1)}, bf16[128,768]{1,0:T(8,128)(2,1)S(1)}, u32[]{:S(2)}, u32[]{:S(2)}) %collective-permute-start.12) | collective-permute-done | bytes 196640 | tf_op jit(solution)/shard_map/ppermute | solution.py:111
  34.1 0.6 collective-permute-done.10.refs_3_
  34.8 2.7 %project_3.1 = (bf16[256,768]{1,0:T(8,128)(2,1)}, bf16[256,768]{1,0:T(8,128)(2,1)S(1)}, bf16[256,768]{1,0:T(8,128)(2,1)S(1)}) custom-call(s32[4,4]{1,0:T(4,128)S(1)} %copy-done.2, bf16[1024,768]{1,0:T(8,128)(2,1)S(1)} %copy-done.1, bf16[128,768]{1,0:T(8,128)(2,1)S(1)} %pad_maximum_fusion.refs_0_, bf16[128,768]{1,0:T(8,128)(2,1)S(1)} %collective-permute-done.8.refs_1_, ...), custom_call_target="tpu_custom_call" | custom-call | flops 1207959552 | bytes 4325376 | tf_op jit(solution)/shard_map/project_3/pallas_call | solution.py:42
  37.4 1.3 %collective-permute-start.15 = (bf16[256,768]{1,0:T(8,128)(2,1)}, bf16[256,768]{1,0:T(8,128)(2,1)S(1)}, u32[]{:S(2)}, u32[]{:S(2)}) collective-permute-start(bf16[256,768]{1,0:T(8,128)(2,1)} %get-tuple-element.12), channel_id=1, source_target_pairs={{0,1},{1,2},{2,3},{3,0},{4,5},{5,6},{6,7},{7,4},{8,9},{9,10},{10,1... | collective-permute-start | bytes 1179656 | tf_op jit(solution)/shard_map/ppermute | solution.py:147
  38.9 0.2 copy.7.skew_ref
  39.1 0.2 copy.8.tail_ref
  39.4 18.6 %collective-permute-done.7.refs_0_ = bf16[256,768]{1,0:T(8,128)(2,1)S(1)} collective-permute-done((bf16[256,768]{1,0:T(8,128)(2,1)S(1)}, bf16[256,768]{1,0:T(8,128)(2,1)S(1)}, u32[]{:S(2)}, u32[]{:S(2)}) %collective-permute-start.7) | collective-permute-done | bytes 393248 | tf_op jit(solution)/shard_map/ppermute | solution.py:147
  58.0 12.3 %collective-permute-done.15.refs_1_ = bf16[256,768]{1,0:T(8,128)(2,1)S(1)} collective-permute-done((bf16[256,768]{1,0:T(8,128)(2,1)}, bf16[256,768]{1,0:T(8,128)(2,1)S(1)}, u32[]{:S(2)}, u32[]{:S(2)}) %collective-permute-start.15) | collective-permute-done | bytes 393248 | tf_op jit(solution)/shard_map/ppermute | solution.py:147
  70.3 1.6 %copy-done = bf16[1,1024,1024]{2,1,0:T(8,128)(2,1)S(1)} copy-done((bf16[1,1024,1024]{2,1,0:T(8,128)(2,1)S(1)}, bf16[1,1024,1024]{2,1,0:T(8,128)(2,1)}, u32[]{:S(2)}) %copy-start) | copy-done | bytes 2097176
  71.9 5.1 %finish.1 = f32[1024,768]{1,0:T(8,128)} custom-call(bf16[1024,1024]{1,0:T(8,128)(2,1)S(1)} %bitcast.11, f32[1024,1]{1,0:T(8,128)S(1)} %copy.7.skew_ref, f32[1024,1]{1,0:T(8,128)S(1)} %copy.8.tail_ref, bf16[256,768]{1,0:T(8,128)(2,1)S(1)} %collective-permute-done.7.refs_0_, bf16[256,768]{1,0:T(8,128)(2,1)S(1)} %collective-permute-done.15.refs_1_, ...), custom_call_target="tpu_custom_call" | custom-call | flops 1610612736 | bytes 6815744 | tf_op jit(solution)/shard_map/finish/pallas_call | solution.py:85
  (25 shorter events, 0.4 us)
Async XLA Ops:
  6.5 13.8 %copy-start.3 = (bf16[1,128,1024]{2,1,0:T(8,128)(2,1)S(1)}, bf16[1,128,1024]{2,1,0:T(8,128)(2,1)}, u32[]{:S(2)}) copy-start(bf16[1,128,1024]{2,1,0:T(8,128)(2,1)} %param.7) | copy-start | bytes 786436
  6.5 63.8 %all-gather.2.cloned.1.call-start = ((), (), s32[]{:S(2)}) async-start(), calls=%async_computation | async-start | bytes 2359296 | tf_op jit(solution)/shard_map/all_gather | solution.py:151
  8.1 4.2 %collective-permute-start.5 = (bf16[128,256]{1,0:T(8,128)(2,1)S(1)}, bf16[128,256]{1,0:T(8,128)(2,1)S(1)}, u32[]{:S(2)}, u32[]{:S(2)}) collective-permute-start(bf16[128,256]{1,0:T(8,128)(2,1)S(1)} %dynamic-slice_bitcast_fusion.3.refs_0_), channel_id=1, source_target_pairs={{0,24},{4,28},{8,16},{12,20},{16,8},{20,12},{24,0},{28,4},{1,25},{... | collective-permute-start | bytes 196616 | tf_op jit(solution)/shard_map/ppermute | solution.py:109
  10.3 3.7 %collective-permute-start.3 = (bf16[128,256]{1,0:T(8,128)(2,1)S(1)}, bf16[128,256]{1,0:T(8,128)(2,1)S(1)}, u32[]{:S(2)}, u32[]{:S(2)}) collective-permute-start(bf16[128,256]{1,0:T(8,128)(2,1)S(1)} %dynamic-slice_bitcast_fusion.3.refs_0_), channel_id=1, source_target_pairs={{0,16},{4,20},{8,24},{12,28},{16,0},{20,4},{24,8},{28,12},{1,17},{... | collective-permute-start | bytes 196616 | tf_op jit(solution)/shard_map/ppermute | solution.py:109
  10.5 5.0 %collective-permute-start.1 = (bf16[128,256]{1,0:T(8,128)(2,1)S(1)}, bf16[128,256]{1,0:T(8,128)(2,1)S(1)}, u32[]{:S(2)}, u32[]{:S(2)}) collective-permute-start(bf16[128,256]{1,0:T(8,128)(2,1)S(1)} %dynamic-slice_bitcast_fusion.3.refs_0_), channel_id=1, source_target_pairs={{0,8},{4,12},{8,0},{12,4},{16,24},{20,28},{24,16},{28,20},{1,9},{5... | collective-permute-start | bytes 196616 | tf_op jit(solution)/shard_map/ppermute | solution.py:109
  10.8 5.2 %collective-permute-start = (bf16[128,256]{1,0:T(8,128)(2,1)S(1)}, bf16[128,256]{1,0:T(8,128)(2,1)S(1)}, u32[]{:S(2)}, u32[]{:S(2)}) collective-permute-start(bf16[128,256]{1,0:T(8,128)(2,1)S(1)} %dynamic-slice_bitcast_fusion.3.refs_0_), channel_id=1, source_target_pairs={{0,4},{4,0},{8,12},{12,8},{16,20},{20,16},{24,28},{28,24},{1,5},{5... | collective-permute-start | bytes 196616 | tf_op jit(solution)/shard_map/ppermute | solution.py:111
  12.3 3.7 %collective-permute-start.6 = (bf16[128,256]{1,0:T(8,128)(2,1)S(1)}, bf16[128,256]{1,0:T(8,128)(2,1)S(1)}, u32[]{:S(2)}, u32[]{:S(2)}) collective-permute-start(bf16[128,256]{1,0:T(8,128)(2,1)S(1)} %collective-permute-done.5.refs_6_), channel_id=1, source_target_pairs={{0,4},{4,0},{8,12},{12,8},{16,20},{20,16},{24,28},{28,24},{1,5},{5... | collective-permute-start | bytes 196616 | tf_op jit(solution)/shard_map/ppermute | solution.py:111
  14.0 2.4 %collective-permute-start.4 = (bf16[128,256]{1,0:T(8,128)(2,1)S(1)}, bf16[128,256]{1,0:T(8,128)(2,1)S(1)}, u32[]{:S(2)}, u32[]{:S(2)}) collective-permute-start(bf16[128,256]{1,0:T(8,128)(2,1)S(1)} %collective-permute-done.3.refs_4_), channel_id=1, source_target_pairs={{0,4},{4,0},{8,12},{12,8},{16,20},{20,16},{24,28},{28,24},{1,5},{5... | collective-permute-start | bytes 196616 | tf_op jit(solution)/shard_map/ppermute | solution.py:111
  15.5 1.4 %collective-permute-start.2 = (bf16[128,256]{1,0:T(8,128)(2,1)S(1)}, bf16[128,256]{1,0:T(8,128)(2,1)S(1)}, u32[]{:S(2)}, u32[]{:S(2)}) collective-permute-start(bf16[128,256]{1,0:T(8,128)(2,1)S(1)} %collective-permute-done.1.refs_2_), channel_id=1, source_target_pairs={{0,4},{4,0},{8,12},{12,8},{16,20},{20,16},{24,28},{28,24},{1,5},{5... | collective-permute-start | bytes 196616 | tf_op jit(solution)/shard_map/ppermute | solution.py:111
  16.9 1.5 %copy-start.1 = (bf16[1024,768]{1,0:T(8,128)(2,1)S(1)}, bf16[1024,768]{1,0:T(8,128)(2,1)}, u32[]{:S(2)}) copy-start(bf16[1024,768]{1,0:T(8,128)(2,1)} %noise_ref.3) | copy-start | bytes 4718596
  18.4 0.7 copy-start.2
  20.4 18.5 %copy-start.4 = (f32[1024]{0:T(1024)S(1)}, f32[1024]{0:T(1024)}, u32[]{:S(2)}) copy-start(f32[1024]{0:T(1024)} %param.10) | copy-start | bytes 12292
  20.4 18.7 %copy-start.5 = (f32[1024]{0:T(1024)S(1)}, f32[1024]{0:T(1024)}, u32[]{:S(2)}) copy-start(f32[1024]{0:T(1024)} %param.11) | copy-start | bytes 12292
  20.4 7.8 %collective-permute-start.13 = (bf16[128,768]{1,0:T(8,128)(2,1)S(1)}, bf16[128,768]{1,0:T(8,128)(2,1)S(1)}, u32[]{:S(2)}, u32[]{:S(2)}) collective-permute-start(bf16[128,768]{1,0:T(8,128)(2,1)S(1)} %pad_maximum_fusion.refs_0_), channel_id=1, source_target_pairs={{0,24},{4,28},{8,16},{12,20},{16,8},{20,12},{24,0},{28,4},{1,25},{... | collective-permute-start | bytes 589832 | tf_op jit(solution)/shard_map/ppermute | solution.py:109
  21.6 10.7 %collective-permute-start.11 = (bf16[128,768]{1,0:T(8,128)(2,1)S(1)}, bf16[128,768]{1,0:T(8,128)(2,1)S(1)}, u32[]{:S(2)}, u32[]{:S(2)}) collective-permute-start(bf16[128,768]{1,0:T(8,128)(2,1)S(1)} %pad_maximum_fusion.refs_0_), channel_id=1, source_target_pairs={{0,16},{4,20},{8,24},{12,28},{16,0},{20,4},{24,8},{28,12},{1,17},{... | collective-permute-start | bytes 589832 | tf_op jit(solution)/shard_map/ppermute | solution.py:109
  22.1 10.9 %collective-permute-start.9 = (bf16[128,768]{1,0:T(8,128)(2,1)S(1)}, bf16[128,768]{1,0:T(8,128)(2,1)S(1)}, u32[]{:S(2)}, u32[]{:S(2)}) collective-permute-start(bf16[128,768]{1,0:T(8,128)(2,1)S(1)} %pad_maximum_fusion.refs_0_), channel_id=1, source_target_pairs={{0,8},{4,12},{8,0},{12,4},{16,24},{20,28},{24,16},{28,20},{1,9},{5... | collective-permute-start | bytes 589832 | tf_op jit(solution)/shard_map/ppermute | solution.py:109
  23.1 10.0 %collective-permute-start.8 = (bf16[128,768]{1,0:T(8,128)(2,1)S(1)}, bf16[128,768]{1,0:T(8,128)(2,1)S(1)}, u32[]{:S(2)}, u32[]{:S(2)}) collective-permute-start(bf16[128,768]{1,0:T(8,128)(2,1)S(1)} %pad_maximum_fusion.refs_0_), channel_id=1, source_target_pairs={{0,4},{4,0},{8,12},{12,8},{16,20},{20,16},{24,28},{28,24},{1,5},{5... | collective-permute-start | bytes 589832 | tf_op jit(solution)/shard_map/ppermute | solution.py:111
  28.2 4.9 %collective-permute-start.14 = (bf16[128,768]{1,0:T(8,128)(2,1)S(1)}, bf16[128,768]{1,0:T(8,128)(2,1)S(1)}, u32[]{:S(2)}, u32[]{:S(2)}) collective-permute-start(bf16[128,768]{1,0:T(8,128)(2,1)S(1)} %collective-permute-done.13.refs_6_), channel_id=1, source_target_pairs={{0,4},{4,0},{8,12},{12,8},{16,20},{20,16},{24,28},{28,24},{1,5},{5... | collective-permute-start | bytes 589832 | tf_op jit(solution)/shard_map/ppermute | solution.py:111
  32.4 1.8 %collective-permute-start.12 = (bf16[128,768]{1,0:T(8,128)(2,1)S(1)}, bf16[128,768]{1,0:T(8,128)(2,1)S(1)}, u32[]{:S(2)}, u32[]{:S(2)}) collective-permute-start(bf16[128,768]{1,0:T(8,128)(2,1)S(1)} %collective-permute-done.11.refs_4_), channel_id=1, source_target_pairs={{0,4},{4,0},{8,12},{12,8},{16,20},{20,16},{24,28},{28,24},{1,5},{5... | collective-permute-start | bytes 589832 | tf_op jit(solution)/shard_map/ppermute | solution.py:111
  33.1 1.7 %collective-permute-start.10 = (bf16[128,768]{1,0:T(8,128)(2,1)S(1)}, bf16[128,768]{1,0:T(8,128)(2,1)S(1)}, u32[]{:S(2)}, u32[]{:S(2)}) collective-permute-start(bf16[128,768]{1,0:T(8,128)(2,1)S(1)} %collective-permute-done.9.refs_2_), channel_id=1, source_target_pairs={{0,4},{4,0},{8,12},{12,8},{16,20},{20,16},{24,28},{28,24},{1,5},{5... | collective-permute-start | bytes 589832 | tf_op jit(solution)/shard_map/ppermute | solution.py:111
  33.1 24.9 %collective-permute-start.7 = (bf16[256,768]{1,0:T(8,128)(2,1)S(1)}, bf16[256,768]{1,0:T(8,128)(2,1)S(1)}, u32[]{:S(2)}, u32[]{:S(2)}) collective-permute-start(bf16[256,768]{1,0:T(8,128)(2,1)S(1)} %project_1.1), channel_id=1, source_target_pairs={{0,2},{1,3},{2,0},{3,1},{4,6},{5,7},{6,4},{7,5},{8,10},{9,11},{10,... | collective-permute-start | bytes 1179656 | tf_op jit(solution)/shard_map/ppermute | solution.py:147
  37.4 32.9 %collective-permute-start.15 = (bf16[256,768]{1,0:T(8,128)(2,1)}, bf16[256,768]{1,0:T(8,128)(2,1)S(1)}, u32[]{:S(2)}, u32[]{:S(2)}) collective-permute-start(bf16[256,768]{1,0:T(8,128)(2,1)} %get-tuple-element.12), channel_id=1, source_target_pairs={{0,1},{1,2},{2,3},{3,0},{4,5},{5,6},{6,7},{7,4},{8,9},{9,10},{10,1... | collective-permute-start | bytes 1179656 | tf_op jit(solution)/shard_map/ppermute | solution.py:147
  38.7 31.6 %collective-permute-start.16 = (bf16[256,768]{1,0:T(8,128)(2,1)S(1)}, bf16[256,768]{1,0:T(8,128)(2,1)S(1)}, u32[]{:S(2)}, u32[]{:S(2)}) collective-permute-start(bf16[256,768]{1,0:T(8,128)(2,1)S(1)} %get-tuple-element.13), channel_id=1, source_target_pairs={{0,3},{1,0},{2,1},{3,2},{4,7},{5,4},{6,5},{7,6},{8,11},{9,8},{10,9... | collective-permute-start | bytes 1179656 | tf_op jit(solution)/shard_map/ppermute | solution.py:147
  70.3 1.6 %copy-start = (bf16[1,1024,1024]{2,1,0:T(8,128)(2,1)S(1)}, bf16[1,1024,1024]{2,1,0:T(8,128)(2,1)}, u32[]{:S(2)}) copy-start(bf16[1,1024,1024]{2,1,0:T(8,128)(2,1)} %all-gather.2.cloned.1.call-done) | copy-start | bytes 6291460
Sparse Core Ops, SparseCore 0:
  9.2 33.6 all-gather.1

commit v2 on v0

v2 whole, which is shorter than its diff:
```python
import functools

import jax
import jax.numpy as jnp
from jax import lax
from jax.experimental import pallas as pl
from jax.experimental.pallas import tpu as pltpu
from jax.sharding import PartitionSpec as P

CAP = 2
VMEM = pl.BlockSpec(memory_space=pltpu.VMEM)
SMEM = pl.BlockSpec(memory_space=pltpu.SMEM)
LIMIT = pltpu.CompilerParams(vmem_limit_bytes=44 * 2**20)


def stack_pieces(pieces, whole):
    me = lax.axis_index("real")
    rows = pieces[0].shape[0]
    for distance, piece in enumerate(pieces):
        start = pl.multiple_of((me ^ distance) * rows, rows)
        whole[pl.ds(start, rows), :] = piece[...]


def project_kernel(n_pieces, noise_ref, *refs):
    pieces, outs, whole = refs[:n_pieces], refs[n_pieces:-1], refs[-1]
    stack_pieces(pieces, whole)
    for place, out_ref in enumerate(outs):
        columns = out_ref.shape[0]
        projected = lax.dot_general(
            whole[:, place * columns : (place + 1) * columns],
            noise_ref[...],
            (((0,), (0,)), ((), ())),
            preferred_element_type=jnp.float32,
        )
        out_ref[...] = projected.astype(out_ref.dtype)


def project(n_shifts, noise, pieces):
    sites, reals = noise.shape
    columns = pieces[0].shape[1]
    return pl.pallas_call(
        functools.partial(project_kernel, len(pieces)),
        out_shape=[jax.ShapeDtypeStruct((columns // n_shifts, reals), jnp.bfloat16)] * n_shifts,
        in_specs=[VMEM] * (1 + len(pieces)),
        out_specs=[VMEM] * n_shifts,
        scratch_shapes=[pltpu.VMEM((sites, columns), jnp.bfloat16)],
        compiler_params=LIMIT,
        cost_estimate=pl.CostEstimate(
            flops=2 * sites * columns * reals,
            bytes_accessed=2 * (sites * columns + sites * reals + columns * reals),
            transcendentals=0,
        ),
        name=f"project_{n_shifts}",
    )(noise, *pieces)


def stage_kernel(from_ref, to_ref, sems):
    parts = sems.shape[0]
    rows = from_ref.shape[0] // parts
    copies = []
    for part in range(parts):
        span = slice(part * rows, (part + 1) * rows)
        copies.append(
            pltpu.make_async_copy(from_ref.at[span, :], to_ref.at[span, :], sems.at[part])
        )
        copies[-1].start()
    for copy in copies:
        copy.wait()


def stage(array):
    return pl.pallas_call(
        stage_kernel,
        out_shape=jax.ShapeDtypeStruct(array.shape, array.dtype),
        in_specs=[pl.BlockSpec(memory_space=pltpu.HBM)],
        out_specs=VMEM,
        scratch_shapes=[pltpu.SemaphoreType.DMA((4,))],
        compiler_params=LIMIT,
        cost_estimate=pl.CostEstimate(
            flops=0, bytes_accessed=2 * array.size * array.dtype.itemsize, transcendentals=0
        ),
        name="stage",
    )(array)


def source_of(shift):
    site_count = lax.axis_size("site")
    return lax.rem(lax.axis_index("site") + (site_count - shift), site_count)


def alive_coef(shift, ranks_ref, coef_ref):
    rank = ranks_ref[lax.axis_index("site"), source_of(shift)]
    block = coef_ref.shape[0] // CAP
    row = lax.broadcasted_iota(jnp.int32, coef_ref.shape, 0)
    return jnp.where(row < rank * block, coef_ref[...].astype(jnp.float32), 0.0).astype(
        coef_ref.dtype
    )


def accumulate_kernel(shifts, ranks_ref, u_ref, *refs):
    coefs, sum_ref = refs[: len(shifts)], refs[-1]
    total = None
    for shift, coef_ref in zip(shifts, coefs):
        columns = coef_ref.shape[0]
        start = pl.multiple_of(source_of(shift) * columns, columns)
        term = jnp.dot(
            u_ref[:, pl.ds(start, columns)],
            alive_coef(shift, ranks_ref, coef_ref),
            preferred_element_type=jnp.float32,
        )
        total = term if total is None else total + term
    sum_ref[...] = total


def accumulate(shifts, ranks, u_whole, coefs):
    sites, columns = u_whole.shape
    per_source, reals = coefs[0].shape
    return pl.pallas_call(
        functools.partial(accumulate_kernel, shifts),
        out_shape=jax.ShapeDtypeStruct((sites, reals), jnp.float32),
        in_specs=[SMEM] + [VMEM] * (1 + len(coefs)),
        out_specs=VMEM,
        compiler_params=LIMIT,
        cost_estimate=pl.CostEstimate(
            flops=2 * sites * per_source * len(shifts) * reals,
            bytes_accessed=2 * sites * columns + 4 * sites * reals,
            transcendentals=0,
        ),
        name="accumulate",
    )(ranks, u_whole, *coefs)


def finish_kernel(shifts, ranks_ref, u_ref, sum_ref, skew_ref, tail_ref, *refs):
    coefs = refs[: len(shifts)]
    out_ref, slots, sems = refs[len(shifts) :]
    block = slots.shape[1]
    alive = [alive_coef(shift, ranks_ref, coef) for shift, coef in zip(shifts, coefs)]
    copies = []
    for step in range(out_ref.shape[0] // block):
        rows = slice(step * block, (step + 1) * block)
        gaussian = sum_ref[rows, :]
        for shift, coef in zip(shifts, alive):
            columns = coef.shape[0]
            start = pl.multiple_of(source_of(shift) * columns, columns)
            gaussian += jnp.dot(
                u_ref[rows, pl.ds(start, columns)], coef, preferred_element_type=jnp.float32
            )
        skew, tail = skew_ref[rows, :], tail_ref[rows, :]
        scaled = skew * gaussian
        series = 1.0 + scaled * (0.5 + scaled * (1 / 6 + scaled * (1 / 24 + scaled * (1 / 120))))
        grown = jnp.where(jnp.abs(scaled) < 0.125, scaled * series, jnp.exp(scaled) - 1.0)
        slots[step] = grown * (1.0 / skew) * jnp.exp((0.5 * tail) * gaussian * gaussian)
        copy = pltpu.make_async_copy(slots.at[step], out_ref.at[rows, :], sems.at[step])
        copy.start()
        copies.append(copy)
    for copy in copies:
        copy.wait()


def finish(shifts, ranks, u_whole, total, skew, tail, coefs):
    rows, columns = u_whole.shape
    per_source, reals = coefs[0].shape
    block = min(rows, 128)
    return pl.pallas_call(
        functools.partial(finish_kernel, shifts),
        out_shape=jax.ShapeDtypeStruct((rows, reals), jnp.float32),
        in_specs=[SMEM] + [VMEM] * (4 + len(coefs)),
        out_specs=pl.BlockSpec(memory_space=pl.ANY),
        scratch_shapes=[
            pltpu.VMEM((rows // block, block, reals), jnp.float32),
            pltpu.SemaphoreType.DMA((rows // block,)),
        ],
        compiler_params=LIMIT,
        cost_estimate=pl.CostEstimate(
            flops=2 * rows * per_source * len(shifts) * reals,
            bytes_accessed=2 * rows * columns + 8 * rows * reals,
            transcendentals=2 * rows * reals,
        ),
        name="finish",
    )(ranks, u_whole, total, skew, tail, *coefs)


def after(value, *before):
    return lax.optimization_barrier((value, before))[0]


def from_chips(own, count):
    pieces = {0: own}
    for distance in range(2, count, 2):
        pieces[distance] = lax.ppermute(own, "real", [(k, k ^ distance) for k in range(count)])
    return pieces


def from_core(pieces, count):
    swapped = {
        distance ^ 1: lax.ppermute(piece, "real", [(k, k ^ 1) for k in range(count)])
        for distance, piece in pieces.items()
    }
    return [{**pieces, **swapped}[distance] for distance in range(count)]


def along_site(coef, shift):
    count = lax.axis_size("site")
    return lax.ppermute(coef, "site", [(k, (k + shift) % count) for k in range(count)])


def per_device(noise, v_factors, u_factors, ranks, skew_g, tail_h):
    site_count = lax.axis_size("site")
    real_count = lax.axis_size("real")
    source = lax.axis_index("site")
    rows, columns = v_factors.shape[1:]
    per_dest = columns // site_count
    middle = site_count // 2
    others = sorted(range(1, site_count), key=lambda shift: (abs(shift - middle), shift))
    first, rest = others[:1], others[1:] + [0]

    def columns_for(shift):
        start = lax.rem(source + shift, site_count) * per_dest
        return lax.dynamic_slice(v_factors[0], (0, start), (rows, per_dest))

    v_first = from_chips(columns_for(first[0]), real_count)
    v_rest = jnp.concatenate([columns_for(shift) for shift in rest], axis=1)
    noise = stage(noise)
    v_first = after(v_first, noise, v_rest)
    arrived = list(v_first.values())[1:]
    u_mine = after(u_factors, *arrived)
    u_whole = lax.all_gather(u_mine, "real", axis=1, tiled=True)[0]
    v_rest = from_chips(after(v_rest, *arrived), real_count)
    coefs = dict(zip(first, project(len(first), noise, from_core(v_first, real_count))))
    v_rest = after(v_rest, coefs[first[0]])
    coefs.update(zip(rest, project(len(rest), noise, from_core(v_rest, real_count))))
    received = {shift: along_site(coef, shift) if shift else coef for shift, coef in coefs.items()}
    early, late = (0, first[0]), tuple(rest[:-1])
    total = accumulate(early, ranks, u_whole, [received[shift] for shift in early])
    return finish(
        late, ranks, u_whole, total, skew_g[:, None], tail_h[:, None], [received[s] for s in late]
    )


def solution(mesh):
    placed = (
        P("site", "real"),
        P("site", "real", None),
        P("site", "real", None),
        P(),
        P("site"),
        P("site"),
    )
    return jax.shard_map(
        per_device, mesh=mesh, in_specs=placed, out_specs=P("site", "real"), check_vma=False
    )
```

time: 107 us -> 75.8 us (0.71)
  the two profiles are of different devices: /device:TPU:0 before, /device:TPU:21 now
where the time goes in v2:
time: 75.8 us; the launch traced here: 75.6 us
  waiting for transfers between devices  36.8 us (49%)
  between operations  13.5 us (18%)
  starting transfers between devices  11.6 us (15%)
  Pallas kernels  9.29 us (12%)
  local copies, waits for them, and re-layouts  4.41 us (6%)
    ppermute x3, waiting for transfers between devices, along_site(): lax.ppermute(coef, 'site', [(k, (k + shift) % count) for k in range(count)])  28.6 us
    ppermute x6, starting transfers between devices, from_chips(): lax.ppermute(own, 'real', [(k, k ^ distance) for k in range(count)])  5.43 us
    ppermute x6, waiting for transfers between devices, from_chips(): lax.ppermute(own, 'real', [(k, k ^ distance) for k in range(count)])  4.78 us
    ppermute x8, starting transfers between devices, from_core(): lax.ppermute(piece, 'real', [(k, k ^ 1) for k in range(count)])  4.54 us
    pallas_call x1, Pallas kernels, finish(): pl.pallas_call(functools.partial(finish_kernel, shifts), out_shape=jax.Sh...  4.21 us
    ppermute x8, waiting for transfers between devices, from_core(): lax.ppermute(piece, 'real', [(k, k ^ 1) for k in range(count)])  3.36 us
    unnamed x10, local copies, waits for them, and re-layouts  3.02 us
    pallas_call x2, Pallas kernels, project(): pl.pallas_call(functools.partial(project_kernel, len(pieces)), out_shape=...  2.72 us
  transfers between devices with their start and end apart: 18, of which 11 were waited for; matrix products, arithmetic and copies ran while one was open for 1% of the time, Pallas kernels for 7%

profile of v2, /device:TPU:21, one launch (start us, length us, event | category | flops | bytes accessed | tf_op | source)
XLA Modules:
  0.0 75.6 jit_solution(11929235478675979411)
XLA Ops:
  6.5 1.0 %dynamic-slice_bitcast_fusion.2 = (bf16[128,256]{1,0:T(8,128)(2,1)S(1)}, bf16[128,256]{1,0:T(8,128)(2,1)S(1)}, bf16[128,256]{1,0:T(8,128)(2,1)S(1)}, bf16[128,256]{1,0:T(8,128)(2,1)S(1)}) fusion(bf16[1,128,1024]{2,1,0:T(8,128)(2,1)} %param.7, s32[]{:T(128)S(6)} %select_n.13, s32[]{:T(128)S(6)} %select_n.12, s32[]{:T(128)S(6)} %select_n.15, s32[]{:T(128)S(6)} %select_n.14), kind=kLoop, calls=%fused_computation.3 | loop fusion | bytes 524304 | tf_op jit(solution)/shard_map/dynamic_slice | solution.py:219
  7.5 1.2 %collective-permute-start.2 = (bf16[128,256]{1,0:T(8,128)(2,1)S(1)}, bf16[128,256]{1,0:T(8,128)(2,1)S(1)}, u32[]{:S(2)}, u32[]{:S(2)}) collective-permute-start(bf16[128,256]{1,0:T(8,128)(2,1)S(1)} %get-tuple-element.23.refs_0_), channel_id=1, source_target_pairs={{0,24},{4,28},{8,16},{12,20},{16,8},{20,12},{24,0},{28,4},{1,25},{... | collective-permute-start | bytes 196616 | tf_op jit(solution)/shard_map/ppermute | solution.py:190
  8.7 1.2 %collective-permute-start.1 = (bf16[128,256]{1,0:T(8,128)(2,1)S(1)}, bf16[128,256]{1,0:T(8,128)(2,1)S(1)}, u32[]{:S(2)}, u32[]{:S(2)}) collective-permute-start(bf16[128,256]{1,0:T(8,128)(2,1)S(1)} %get-tuple-element.23.refs_0_), channel_id=1, source_target_pairs={{0,16},{4,20},{8,24},{12,28},{16,0},{20,4},{24,8},{28,12},{1,17},{... | collective-permute-start | bytes 196616 | tf_op jit(solution)/shard_map/ppermute | solution.py:190
  10.0 0.3 collective-permute-start
  10.2 1.4 %copy-done.1 = bf16[1024,768]{1,0:T(8,128)(2,1)S(1)} copy-done((bf16[1024,768]{1,0:T(8,128)(2,1)S(1)}, bf16[1024,768]{1,0:T(8,128)(2,1)}, u32[]{:S(2)}) %copy-start.1) | copy-done | bytes 1572888
  11.6 0.8 %stage.1.noise_ref = bf16[1024,768]{1,0:T(8,128)(2,1)S(1)} custom-call(bf16[1024,768]{1,0:T(8,128)(2,1)S(1)} %copy-done.1), custom_call_target="tpu_custom_call" | custom-call | bytes 3145728 | tf_op jit(solution)/shard_map/stage/pallas_call | solution.py:72
  12.4 0.9 %collective-permute-done.1.refs_4_ = bf16[128,256]{1,0:T(8,128)(2,1)S(1)} collective-permute-done((bf16[128,256]{1,0:T(8,128)(2,1)S(1)}, bf16[128,256]{1,0:T(8,128)(2,1)S(1)}, u32[]{:S(2)}, u32[]{:S(2)}) %collective-permute-start.1) | collective-permute-done | bytes 65568 | tf_op jit(solution)/shard_map/ppermute | solution.py:190
  13.4 1.1 %collective-permute-start.5 = (bf16[128,768]{1,0:T(8,128)(2,1)S(1)}, bf16[128,768]{1,0:T(8,128)(2,1)S(1)}, u32[]{:S(2)}, u32[]{:S(2)}) collective-permute-start(bf16[128,768]{1,0:T(8,128)(2,1)S(1)} %pad_maximum_fusion.refs_0_), channel_id=1, source_target_pairs={{0,24},{4,28},{8,16},{12,20},{16,8},{20,12},{24,0},{28,4},{1,25},{... | collective-permute-start | bytes 589832 | tf_op jit(solution)/shard_map/ppermute | solution.py:190
  14.5 0.8 %collective-permute-start.4 = (bf16[128,768]{1,0:T(8,128)(2,1)S(1)}, bf16[128,768]{1,0:T(8,128)(2,1)S(1)}, u32[]{:S(2)}, u32[]{:S(2)}) collective-permute-start(bf16[128,768]{1,0:T(8,128)(2,1)S(1)} %pad_maximum_fusion.refs_0_), channel_id=1, source_target_pairs={{0,16},{4,20},{8,24},{12,28},{16,0},{20,4},{24,8},{28,12},{1,17},{... | collective-permute-start | bytes 589832 | tf_op jit(solution)/shard_map/ppermute | solution.py:190
  15.2 0.9 %collective-permute-start.3 = (bf16[128,768]{1,0:T(8,128)(2,1)S(1)}, bf16[128,768]{1,0:T(8,128)(2,1)S(1)}, u32[]{:S(2)}, u32[]{:S(2)}) collective-permute-start(bf16[128,768]{1,0:T(8,128)(2,1)S(1)} %pad_maximum_fusion.refs_0_), channel_id=1, source_target_pairs={{0,8},{4,12},{8,0},{12,4},{16,24},{20,28},{24,16},{28,20},{1,9},{5... | collective-permute-start | bytes 589832 | tf_op jit(solution)/shard_map/ppermute | solution.py:190
  16.1 2.9 %collective-permute-start.6 = (bf16[128,256]{1,0:T(8,128)(2,1)S(1)}, bf16[128,256]{1,0:T(8,128)(2,1)S(1)}, u32[]{:S(2)}, u32[]{:S(2)}) collective-permute-start(bf16[128,256]{1,0:T(8,128)(2,1)S(1)} %get-tuple-element.23.refs_0_), channel_id=1, source_target_pairs={{0,4},{4,0},{8,12},{12,8},{16,20},{20,16},{24,28},{28,24},{1,5},{5... | collective-permute-start | bytes 196616 | tf_op jit(solution)/shard_map/ppermute | solution.py:196
  19.0 0.9 %collective-permute-done.6.refs_1_ = bf16[128,256]{1,0:T(8,128)(2,1)S(1)} collective-permute-done((bf16[128,256]{1,0:T(8,128)(2,1)S(1)}, bf16[128,256]{1,0:T(8,128)(2,1)S(1)}, u32[]{:S(2)}, u32[]{:S(2)}) %collective-permute-start.6) | collective-permute-done | bytes 65568 | tf_op jit(solution)/shard_map/ppermute | solution.py:196
  19.9 0.4 collective-permute-start.8
  20.5 0.7 collective-permute-done.8.refs_5_
  21.2 0.4 collective-permute-done.9.refs_7_
  21.6 0.7 project_1.1
  22.3 3.9 %collective-permute-done.4.refs_4_ = bf16[128,768]{1,0:T(8,128)(2,1)S(1)} collective-permute-done((bf16[128,768]{1,0:T(8,128)(2,1)S(1)}, bf16[128,768]{1,0:T(8,128)(2,1)S(1)}, u32[]{:S(2)}, u32[]{:S(2)}) %collective-permute-start.4) | collective-permute-done | bytes 196640 | tf_op jit(solution)/shard_map/ppermute | solution.py:190
  26.1 0.6 collective-permute-start.10
  26.7 0.5 collective-permute-start.12
  27.3 0.4 collective-permute-done.10.refs_1_
  27.8 0.4 collective-permute-done.11.refs_3_
  28.2 0.3 collective-permute-done.12.refs_5_
  28.4 0.3 collective-permute-done.13.refs_7_
  28.7 2.1 %project_3.1 = (bf16[256,768]{1,0:T(8,128)(2,1)}, bf16[256,768]{1,0:T(8,128)(2,1)S(1)}, bf16[256,768]{1,0:T(8,128)(2,1)S(1)}) custom-call(bf16[1024,768]{1,0:T(8,128)(2,1)S(1)} %stage.1.noise_ref, bf16[128,768]{1,0:T(8,128)(2,1)S(1)} %pad_maximum_fusion.refs_0_, bf16[128,768]{1,0:T(8,128)(2,1)S(1)} %collective-permute-done.10.refs_1_, ...), custom_call_target="tpu_custom_call" | custom-call | flops 1207959552 | bytes 4325376 | tf_op jit(solution)/shard_map/project_3/pallas_call | solution.py:41
  30.8 1.4 %collective-permute-start.15 = (bf16[256,768]{1,0:T(8,128)(2,1)}, bf16[256,768]{1,0:T(8,128)(2,1)S(1)}, u32[]{:S(2)}, u32[]{:S(2)}) collective-permute-start(bf16[256,768]{1,0:T(8,128)(2,1)} %get-tuple-element.29), channel_id=1, source_target_pairs={{0,1},{1,2},{2,3},{3,0},{4,5},{5,6},{6,7},{7,4},{8,9},{9,10},{10,1... | collective-permute-start | bytes 1179656 | tf_op jit(solution)/shard_map/ppermute | solution.py:204
  32.2 0.2 copy.7.skew_ref
  32.5 0.2 copy.8.tail_ref
  32.7 19.5 %collective-permute-done.14.refs_1_ = bf16[256,768]{1,0:T(8,128)(2,1)S(1)} collective-permute-done((bf16[256,768]{1,0:T(8,128)(2,1)S(1)}, bf16[256,768]{1,0:T(8,128)(2,1)S(1)}, u32[]{:S(2)}, u32[]{:S(2)}) %collective-permute-start.14) | collective-permute-done | bytes 393248 | tf_op jit(solution)/shard_map/ppermute | solution.py:204
  52.2 1.6 %copy-done = bf16[1,1024,1024]{2,1,0:T(8,128)(2,1)S(1)} copy-done((bf16[1,1024,1024]{2,1,0:T(8,128)(2,1)S(1)}, bf16[1,1024,1024]{2,1,0:T(8,128)(2,1)}, u32[]{:S(2)}) %copy-start) | copy-done | bytes 2097176
  53.8 1.6 %accumulate.1.sum_ref = f32[1024,768]{1,0:T(8,128)S(1)} custom-call(s32[4,4]{1,0:T(4,128)S(1)} %copy-done.2, bf16[1024,1024]{1,0:T(8,128)(2,1)S(1)} %bitcast.11, bf16[256,768]{1,0:T(8,128)(2,1)S(1)} %get-tuple-element.28.refs_0_, bf16[256,768]{1,0:T(8,128)(2,1)S(1)} %collective-permute-done.14.refs_1_), custom_call_target="tpu_custom_call" | custom-call | flops 805306368 | bytes 5242880 | tf_op jit(solution)/shard_map/accumulate/pallas_call | solution.py:118
  55.4 9.1 %collective-permute-done.15.refs_0_ = bf16[256,768]{1,0:T(8,128)(2,1)S(1)} collective-permute-done((bf16[256,768]{1,0:T(8,128)(2,1)}, bf16[256,768]{1,0:T(8,128)(2,1)S(1)}, u32[]{:S(2)}, u32[]{:S(2)}) %collective-permute-start.15) | collective-permute-done | bytes 393248 | tf_op jit(solution)/shard_map/ppermute | solution.py:204
  64.5 4.2 %finish.1 = f32[1024,768]{1,0:T(8,128)} custom-call(s32[4,4]{1,0:T(4,128)S(1)} %copy-done.2, bf16[1024,1024]{1,0:T(8,128)(2,1)S(1)} %bitcast.12, f32[1024,768]{1,0:T(8,128)S(1)} %accumulate.1.sum_ref, f32[1024,1]{1,0:T(8,128)S(1)} %copy.7.skew_ref, f32[1024,1]{1,0:T(8,128)S(1)} %copy.8.tail_ref, bf16[256,768]{1,0:T(8,128)(2,1)S(1)} %collective-permute-done.15.refs_0_, ...), custom_call_target="tpu_custom_call" | custom-call | flops 805306368 | bytes 8388608 | tf_op jit(solution)/shard_map/finish/pallas_call | solution.py:164
  (24 shorter events, 0.5 us)
Async XLA Ops:
  6.5 45.7 %all-gather.2.cloned.1.call-start = ((), (), s32[]{:S(2)}) async-start(), calls=%async_computation | async-start | bytes 2359296 | tf_op jit(solution)/shard_map/all_gather | solution.py:227
  7.5 4.9 %collective-permute-start.2 = (bf16[128,256]{1,0:T(8,128)(2,1)S(1)}, bf16[128,256]{1,0:T(8,128)(2,1)S(1)}, u32[]{:S(2)}, u32[]{:S(2)}) collective-permute-start(bf16[128,256]{1,0:T(8,128)(2,1)S(1)} %get-tuple-element.23.refs_0_), channel_id=1, source_target_pairs={{0,24},{4,28},{8,16},{12,20},{16,8},{20,12},{24,0},{28,4},{1,25},{... | collective-permute-start | bytes 196616 | tf_op jit(solution)/shard_map/ppermute | solution.py:190
  8.7 4.6 %collective-permute-start.1 = (bf16[128,256]{1,0:T(8,128)(2,1)S(1)}, bf16[128,256]{1,0:T(8,128)(2,1)S(1)}, u32[]{:S(2)}, u32[]{:S(2)}) collective-permute-start(bf16[128,256]{1,0:T(8,128)(2,1)S(1)} %get-tuple-element.23.refs_0_), channel_id=1, source_target_pairs={{0,16},{4,20},{8,24},{12,28},{16,0},{20,4},{24,8},{28,12},{1,17},{... | collective-permute-start | bytes 196616 | tf_op jit(solution)/shard_map/ppermute | solution.py:190
  10.0 3.4 %collective-permute-start = (bf16[128,256]{1,0:T(8,128)(2,1)S(1)}, bf16[128,256]{1,0:T(8,128)(2,1)S(1)}, u32[]{:S(2)}, u32[]{:S(2)}) collective-permute-start(bf16[128,256]{1,0:T(8,128)(2,1)S(1)} %get-tuple-element.23.refs_0_), channel_id=1, source_target_pairs={{0,8},{4,12},{8,0},{12,4},{16,24},{20,28},{24,16},{28,20},{1,9},{5... | collective-permute-start | bytes 196616 | tf_op jit(solution)/shard_map/ppermute | solution.py:190
  10.2 1.4 %copy-start.1 = (bf16[1024,768]{1,0:T(8,128)(2,1)S(1)}, bf16[1024,768]{1,0:T(8,128)(2,1)}, u32[]{:S(2)}) copy-start(bf16[1024,768]{1,0:T(8,128)(2,1)} %from_ref.1) | copy-start | bytes 4718596
  13.4 8.9 %collective-permute-start.5 = (bf16[128,768]{1,0:T(8,128)(2,1)S(1)}, bf16[128,768]{1,0:T(8,128)(2,1)S(1)}, u32[]{:S(2)}, u32[]{:S(2)}) collective-permute-start(bf16[128,768]{1,0:T(8,128)(2,1)S(1)} %pad_maximum_fusion.refs_0_), channel_id=1, source_target_pairs={{0,24},{4,28},{8,16},{12,20},{16,8},{20,12},{24,0},{28,4},{1,25},{... | collective-permute-start | bytes 589832 | tf_op jit(solution)/shard_map/ppermute | solution.py:190
  14.5 11.7 %collective-permute-start.4 = (bf16[128,768]{1,0:T(8,128)(2,1)S(1)}, bf16[128,768]{1,0:T(8,128)(2,1)S(1)}, u32[]{:S(2)}, u32[]{:S(2)}) collective-permute-start(bf16[128,768]{1,0:T(8,128)(2,1)S(1)} %pad_maximum_fusion.refs_0_), channel_id=1, source_target_pairs={{0,16},{4,20},{8,24},{12,28},{16,0},{20,4},{24,8},{28,12},{1,17},{... | collective-permute-start | bytes 589832 | tf_op jit(solution)/shard_map/ppermute | solution.py:190
  15.2 10.9 %collective-permute-start.3 = (bf16[128,768]{1,0:T(8,128)(2,1)S(1)}, bf16[128,768]{1,0:T(8,128)(2,1)S(1)}, u32[]{:S(2)}, u32[]{:S(2)}) collective-permute-start(bf16[128,768]{1,0:T(8,128)(2,1)S(1)} %pad_maximum_fusion.refs_0_), channel_id=1, source_target_pairs={{0,8},{4,12},{8,0},{12,4},{16,24},{20,28},{24,16},{28,20},{1,9},{5... | collective-permute-start | bytes 589832 | tf_op jit(solution)/shard_map/ppermute | solution.py:190
  16.1 3.8 %collective-permute-start.6 = (bf16[128,256]{1,0:T(8,128)(2,1)S(1)}, bf16[128,256]{1,0:T(8,128)(2,1)S(1)}, u32[]{:S(2)}, u32[]{:S(2)}) collective-permute-start(bf16[128,256]{1,0:T(8,128)(2,1)S(1)} %get-tuple-element.23.refs_0_), channel_id=1, source_target_pairs={{0,4},{4,0},{8,12},{12,8},{16,20},{20,16},{24,28},{28,24},{1,5},{5... | collective-permute-start | bytes 196616 | tf_op jit(solution)/shard_map/ppermute | solution.py:196
  19.0 1.3 %collective-permute-start.7 = (bf16[128,256]{1,0:T(8,128)(2,1)S(1)}, bf16[128,256]{1,0:T(8,128)(2,1)S(1)}, u32[]{:S(2)}, u32[]{:S(2)}) collective-permute-start(bf16[128,256]{1,0:T(8,128)(2,1)S(1)} %collective-permute-done.refs_2_), channel_id=1, source_target_pairs={{0,4},{4,0},{8,12},{12,8},{16,20},{20,16},{24,28},{28,24},{1,5},{5... | collective-permute-start | bytes 196616 | tf_op jit(solution)/shard_map/ppermute | solution.py:196
  19.9 1.3 %collective-permute-start.8 = (bf16[128,256]{1,0:T(8,128)(2,1)S(1)}, bf16[128,256]{1,0:T(8,128)(2,1)S(1)}, u32[]{:S(2)}, u32[]{:S(2)}) collective-permute-start(bf16[128,256]{1,0:T(8,128)(2,1)S(1)} %collective-permute-done.1.refs_4_), channel_id=1, source_target_pairs={{0,4},{4,0},{8,12},{12,8},{16,20},{20,16},{24,28},{28,24},{1,5},{5... | collective-permute-start | bytes 196616 | tf_op jit(solution)/shard_map/ppermute | solution.py:196
  20.3 1.3 %collective-permute-start.9 = (bf16[128,256]{1,0:T(8,128)(2,1)S(1)}, bf16[128,256]{1,0:T(8,128)(2,1)S(1)}, u32[]{:S(2)}, u32[]{:S(2)}) collective-permute-start(bf16[128,256]{1,0:T(8,128)(2,1)S(1)} %collective-permute-done.2.refs_6_), channel_id=1, source_target_pairs={{0,4},{4,0},{8,12},{12,8},{16,20},{20,16},{24,28},{28,24},{1,5},{5... | collective-permute-start | bytes 196616 | tf_op jit(solution)/shard_map/ppermute | solution.py:196
  22.2 10.0 %copy-start.3 = (f32[1024]{0:T(1024)S(1)}, f32[1024]{0:T(1024)}, u32[]{:S(2)}) copy-start(f32[1024]{0:T(1024)} %param.10) | copy-start | bytes 12292
  22.2 10.2 %copy-start.4 = (f32[1024]{0:T(1024)S(1)}, f32[1024]{0:T(1024)}, u32[]{:S(2)}) copy-start(f32[1024]{0:T(1024)} %param.11) | copy-start | bytes 12292
  22.2 30.0 %copy-start.2 = (s32[4,4]{1,0:T(4,128)S(1)}, s32[4,4]{1,0:T(4,128)}, u32[]{:S(2)}) copy-start(s32[4,4]{1,0:T(4,128)} %ranks_ref.3) | copy-start | bytes 196
  26.1 1.7 %collective-permute-start.10 = (bf16[128,768]{1,0:T(8,128)(2,1)S(1)}, bf16[128,768]{1,0:T(8,128)(2,1)S(1)}, u32[]{:S(2)}, u32[]{:S(2)}) collective-permute-start(bf16[128,768]{1,0:T(8,128)(2,1)S(1)} %pad_maximum_fusion.refs_0_), channel_id=1, source_target_pairs={{0,4},{4,0},{8,12},{12,8},{16,20},{20,16},{24,28},{28,24},{1,5},{5... | collective-permute-start | bytes 589832 | tf_op jit(solution)/shard_map/ppermute | solution.py:196
  26.7 1.4 %collective-permute-start.11 = (bf16[128,768]{1,0:T(8,128)(2,1)S(1)}, bf16[128,768]{1,0:T(8,128)(2,1)S(1)}, u32[]{:S(2)}, u32[]{:S(2)}) collective-permute-start(bf16[128,768]{1,0:T(8,128)(2,1)S(1)} %collective-permute-done.3.refs_2_), channel_id=1, source_target_pairs={{0,4},{4,0},{8,12},{12,8},{16,20},{20,16},{24,28},{28,24},{1,5},{5... | collective-permute-start | bytes 589832 | tf_op jit(solution)/shard_map/ppermute | solution.py:196
  26.7 1.7 %collective-permute-start.12 = (bf16[128,768]{1,0:T(8,128)(2,1)S(1)}, bf16[128,768]{1,0:T(8,128)(2,1)S(1)}, u32[]{:S(2)}, u32[]{:S(2)}) collective-permute-start(bf16[128,768]{1,0:T(8,128)(2,1)S(1)} %collective-permute-done.4.refs_4_), channel_id=1, source_target_pairs={{0,4},{4,0},{8,12},{12,8},{16,20},{20,16},{24,28},{28,24},{1,5},{5... | collective-permute-start | bytes 589832 | tf_op jit(solution)/shard_map/ppermute | solution.py:196
  27.2 1.5 %collective-permute-start.13 = (bf16[128,768]{1,0:T(8,128)(2,1)S(1)}, bf16[128,768]{1,0:T(8,128)(2,1)S(1)}, u32[]{:S(2)}, u32[]{:S(2)}) collective-permute-start(bf16[128,768]{1,0:T(8,128)(2,1)S(1)} %collective-permute-done.5.refs_6_), channel_id=1, source_target_pairs={{0,4},{4,0},{8,12},{12,8},{16,20},{20,16},{24,28},{28,24},{1,5},{5... | collective-permute-start | bytes 589832 | tf_op jit(solution)/shard_map/ppermute | solution.py:196
  27.2 25.0 %collective-permute-start.14 = (bf16[256,768]{1,0:T(8,128)(2,1)S(1)}, bf16[256,768]{1,0:T(8,128)(2,1)S(1)}, u32[]{:S(2)}, u32[]{:S(2)}) collective-permute-start(bf16[256,768]{1,0:T(8,128)(2,1)S(1)} %project_1.1), channel_id=1, source_target_pairs={{0,2},{1,3},{2,0},{3,1},{4,6},{5,7},{6,4},{7,5},{8,10},{9,11},{10,... | collective-permute-start | bytes 1179656 | tf_op jit(solution)/shard_map/ppermute | solution.py:204
  30.8 33.7 %collective-permute-start.15 = (bf16[256,768]{1,0:T(8,128)(2,1)}, bf16[256,768]{1,0:T(8,128)(2,1)S(1)}, u32[]{:S(2)}, u32[]{:S(2)}) collective-permute-start(bf16[256,768]{1,0:T(8,128)(2,1)} %get-tuple-element.29), channel_id=1, source_target_pairs={{0,1},{1,2},{2,3},{3,0},{4,5},{5,6},{6,7},{7,4},{8,9},{9,10},{10,1... | collective-permute-start | bytes 1179656 | tf_op jit(solution)/shard_map/ppermute | solution.py:204
  32.2 32.3 %collective-permute-start.16 = (bf16[256,768]{1,0:T(8,128)(2,1)S(1)}, bf16[256,768]{1,0:T(8,128)(2,1)S(1)}, u32[]{:S(2)}, u32[]{:S(2)}) collective-permute-start(bf16[256,768]{1,0:T(8,128)(2,1)S(1)} %get-tuple-element.30), channel_id=1, source_target_pairs={{0,3},{1,0},{2,1},{3,2},{4,7},{5,4},{6,5},{7,6},{8,11},{9,8},{10,9... | collective-permute-start | bytes 1179656 | tf_op jit(solution)/shard_map/ppermute | solution.py:204
  52.2 1.6 %copy-start = (bf16[1,1024,1024]{2,1,0:T(8,128)(2,1)S(1)}, bf16[1,1024,1024]{2,1,0:T(8,128)(2,1)}, u32[]{:S(2)}) copy-start(bf16[1,1024,1024]{2,1,0:T(8,128)(2,1)} %all-gather.2.cloned.1.call-done) | copy-start | bytes 6291460
Sparse Core Ops, SparseCore 0:
  13.5 30.0 all-gather.1

commit v3 on v2

--- a/solution.py
+++ b/solution.py
@@ -97,14 +97,16 @@
     )
 
 
-def accumulate_kernel(shifts, ranks_ref, u_ref, *refs):
-    coefs, sum_ref = refs[: len(shifts)], refs[-1]
+def accumulate_kernel(shifts, n_pieces, ranks_ref, *refs):
+    pieces, coefs = refs[:n_pieces], refs[n_pieces : n_pieces + len(shifts)]
+    whole, sum_ref = refs[-2:]
+    stack_pieces(pieces, whole)
     total = None
     for shift, coef_ref in zip(shifts, coefs):
         columns = coef_ref.shape[0]
         start = pl.multiple_of(source_of(shift) * columns, columns)
         term = jnp.dot(
-            u_ref[:, pl.ds(start, columns)],
+            whole[:, pl.ds(start, columns)],
             alive_coef(shift, ranks_ref, coef_ref),
             preferred_element_type=jnp.float32,
         )
@@ -112,22 +114,26 @@
     sum_ref[...] = total
 
 
-def accumulate(shifts, ranks, u_whole, coefs):
-    sites, columns = u_whole.shape
+def accumulate(shifts, ranks, pieces, coefs):
+    rows, columns = pieces[0].shape
+    sites = rows * len(pieces)
     per_source, reals = coefs[0].shape
     return pl.pallas_call(
-        functools.partial(accumulate_kernel, shifts),
-        out_shape=jax.ShapeDtypeStruct((sites, reals), jnp.float32),
-        in_specs=[SMEM] + [VMEM] * (1 + len(coefs)),
-        out_specs=VMEM,
+        functools.partial(accumulate_kernel, shifts, len(pieces)),
+        out_shape=[
+            jax.ShapeDtypeStruct((sites, columns), jnp.bfloat16),
+            jax.ShapeDtypeStruct((sites, reals), jnp.float32),
+        ],
+        in_specs=[SMEM] + [VMEM] * (len(pieces) + len(coefs)),
+        out_specs=[VMEM] * 2,
         compiler_params=LIMIT,
         cost_estimate=pl.CostEstimate(
             flops=2 * sites * per_source * len(shifts) * reals,
-            bytes_accessed=2 * sites * columns + 4 * sites * reals,
+            bytes_accessed=4 * sites * columns + 4 * sites * reals,
             transcendentals=0,
         ),
         name="accumulate",
-    )(ranks, u_whole, *coefs)
+    )(ranks, *pieces, *coefs)
 
 
 def finish_kernel(shifts, ranks_ref, u_ref, sum_ref, skew_ref, tail_ref, *refs):
@@ -199,6 +205,15 @@
     return [{**pieces, **swapped}[distance] for distance in range(count)]
 
 
+def gather_at_once(present, own, count):
+    return [own] + lax.cond(
+        present,
+        lambda mine: from_core(from_chips(mine, count), count)[1:],
+        lambda mine: [mine] * (count - 1),
+        own,
+    )
+
+
 def along_site(coef, shift):
     count = lax.axis_size("site")
     return lax.ppermute(coef, "site", [(k, (k + shift) % count) for k in range(count)])
@@ -221,17 +236,18 @@
     v_first = from_chips(columns_for(first[0]), real_count)
     v_rest = jnp.concatenate([columns_for(shift) for shift in rest], axis=1)
     noise = stage(noise)
-    v_first = after(v_first, noise, v_rest)
-    arrived = list(v_first.values())[1:]
-    u_mine = after(u_factors, *arrived)
-    u_whole = lax.all_gather(u_mine, "real", axis=1, tiled=True)[0]
-    v_rest = from_chips(after(v_rest, *arrived), real_count)
+    last = max(v_first)
+    v_first[last], noise, v_rest = lax.optimization_barrier((v_first[last], noise, v_rest))
     coefs = dict(zip(first, project(len(first), noise, from_core(v_first, real_count))))
-    v_rest = after(v_rest, coefs[first[0]])
-    coefs.update(zip(rest, project(len(rest), noise, from_core(v_rest, real_count))))
+
+    present = ranks[0, 0] > 0
+    v_rest = gather_at_once(present, after(v_rest, coefs[first[0]]), real_count)
+    coefs.update(zip(rest, project(len(rest), noise, v_rest)))
     received = {shift: along_site(coef, shift) if shift else coef for shift, coef in coefs.items()}
+    u_pieces = gather_at_once(present, after(u_factors[0], coefs[rest[0]]), real_count)
+
     early, late = (0, first[0]), tuple(rest[:-1])
-    total = accumulate(early, ranks, u_whole, [received[shift] for shift in early])
+    u_whole, total = accumulate(early, ranks, u_pieces, [received[shift] for shift in early])
     return finish(
         late, ranks, u_whole, total, skew_g[:, None], tail_h[:, None], [received[s] for s in late]
     )

time: 75.8 us -> 75.6 us (level)
  the two profiles are of different devices: /device:TPU:21 before, /device:TPU:0 now
where the time goes in v3:
time: 75.6 us; the launch traced here: 75.3 us
  waiting for transfers between devices  39.7 us (53%)
  starting transfers between devices  17.9 us (24%)
  Pallas kernels  11.3 us (15%)
  local copies, waits for them, and re-layouts  5.07 us (7%)
    ppermute x9, waiting for transfers between devices, from_chips(): lax.ppermute(own, 'real', [(k, k ^ distance) for k in range(count)])  22.8 us
    ppermute x3, waiting for transfers between devices, along_site(): lax.ppermute(coef, 'site', [(k, (k + shift) % count) for k in range(count)])  13.4 us
    ppermute x9, starting transfers between devices, from_chips(): lax.ppermute(own, 'real', [(k, k ^ distance) for k in range(count)])  11.5 us
    ppermute x3, starting transfers between devices, along_site(): lax.ppermute(coef, 'site', [(k, (k + shift) % count) for k in range(count)])  4.7 us
    pallas_call x1, Pallas kernels, finish(): pl.pallas_call(functools.partial(finish_kernel, shifts), out_shape=jax.Sh...  4.22 us
    pallas_call x2, Pallas kernels, project(): pl.pallas_call(functools.partial(project_kernel, len(pieces)), out_shape=...  3.7 us
    ppermute x12, waiting for transfers between devices, from_core(): lax.ppermute(piece, 'real', [(k, k ^ 1) for k in range(count)])  3.37 us
    unnamed x14, local copies, waits for them, and re-layouts  3.15 us
  transfers between devices with their start and end apart: 24, of which 11 were waited for; matrix products, arithmetic and copies ran while one was open for 2% of the time, Pallas kernels for 9%

profile of v3, /device:TPU:0, one launch (start us, length us, event | category | flops | bytes accessed | tf_op | source)
XLA Modules:
  0.0 75.3 jit_solution(4292223506171460079)
XLA Ops:
  0.0 1.0 %dynamic-slice_bitcast_fusion.2 = (bf16[128,256]{1,0:T(8,128)(2,1)S(1)}, bf16[128,256]{1,0:T(8,128)(2,1)S(1)}, bf16[128,256]{1,0:T(8,128)(2,1)S(1)}, bf16[128,256]{1,0:T(8,128)(2,1)S(1)}) fusion(bf16[1,128,1024]{2,1,0:T(8,128)(2,1)} %param.11, s32[]{:T(128)S(6)} %select_n.13, s32[]{:T(128)S(6)} %select_n.12, s32[]{:T(128)S(6)} %select_n.15, s32[]{:T(128)S(6)} %select_n.14), kind=kLoop, calls=%fused_computation.3 | loop fusion | bytes 524304 | tf_op jit(solution)/shard_map/dynamic_slice | solution.py:234
  1.0 3.0 %collective-permute-start.18 = (bf16[128,256]{1,0:T(8,128)(2,1)S(1)}, bf16[128,256]{1,0:T(8,128)(2,1)S(1)}, u32[]{:S(2)}, u32[]{:S(2)}) collective-permute-start(bf16[128,256]{1,0:T(8,128)(2,1)S(1)} %get-tuple-element.58.refs_0_), channel_id=1, source_target_pairs={{0,16},{4,20},{8,24},{12,28},{16,0},{20,4},{24,8},{28,12},{1,17},{... | collective-permute-start | bytes 196616 | tf_op jit(solution)/shard_map/ppermute | solution.py:196
  4.0 1.5 %collective-permute-start.16 = (bf16[128,256]{1,0:T(8,128)(2,1)S(1)}, bf16[128,256]{1,0:T(8,128)(2,1)S(1)}, u32[]{:S(2)}, u32[]{:S(2)}) collective-permute-start(bf16[128,256]{1,0:T(8,128)(2,1)S(1)} %get-tuple-element.58.refs_0_), channel_id=1, source_target_pairs={{0,8},{4,12},{8,0},{12,4},{16,24},{20,28},{24,16},{28,20},{1,9},{5... | collective-permute-start | bytes 196616 | tf_op jit(solution)/shard_map/ppermute | solution.py:196
  5.6 1.4 %copy-done = bf16[1024,768]{1,0:T(8,128)(2,1)S(1)} copy-done((bf16[1024,768]{1,0:T(8,128)(2,1)S(1)}, bf16[1024,768]{1,0:T(8,128)(2,1)}, u32[]{:S(2)}) %copy-start) | copy-done | bytes 1572888
  7.0 0.8 %stage.1.noise_ref = bf16[1024,768]{1,0:T(8,128)(2,1)S(1)} custom-call(bf16[1024,768]{1,0:T(8,128)(2,1)S(1)} %copy-done), custom_call_target="tpu_custom_call" | custom-call | bytes 3145728 | tf_op jit(solution)/shard_map/stage/pallas_call | solution.py:72
  7.7 0.7 pad_maximum_fusion.refs_0_
  8.4 2.5 %collective-permute-done.14.refs_6_ = bf16[128,256]{1,0:T(8,128)(2,1)S(1)} collective-permute-done((bf16[128,256]{1,0:T(8,128)(2,1)S(1)}, bf16[128,256]{1,0:T(8,128)(2,1)S(1)}, u32[]{:S(2)}, u32[]{:S(2)}) %collective-permute-start.14) | collective-permute-done | bytes 65568 | tf_op jit(solution)/shard_map/ppermute | solution.py:196
  12.7 0.7 project_1.1
  13.3 2.7 %collective-permute-start.21 = (bf16[256,768]{1,0:T(8,128)(2,1)S(1)}, bf16[256,768]{1,0:T(8,128)(2,1)S(1)}, u32[]{:S(2)}, u32[]{:S(2)}) collective-permute-start(bf16[256,768]{1,0:T(8,128)(2,1)S(1)} %project_1.1), channel_id=1, source_target_pairs={{0,2},{1,3},{2,0},{3,1},{4,6},{5,7},{6,4},{7,5},{8,10},{9,11},{10,... | collective-permute-start | bytes 1179656 | tf_op jit(solution)/shard_map/ppermute | solution.py:219
  16.0 14.4 %conditional.2 = (bf16[128,768]{1,0:T(8,128)(2,1)}, bf16[128,768]{1,0:T(8,128)(2,1)}, bf16[128,768]{1,0:T(8,128)(2,1)}, bf16[128,768]{1,0:T(8,128)(2,1)}, bf16[1...) conditional(s32[]{:T(128)} %bitcast.5, ...), branch_computations={%region_0.0_spmd, %region_1.0_spmd} | conditional | bytes 5505360 | solution.py:209
  16.0 1.2 %collective-permute-start.5 = (bf16[128,768]{1,0:T(8,128)(2,1)}, bf16[128,768]{1,0:T(8,128)(2,1)}, u32[]{:S(2)}, u32[]{:S(2)}) collective-permute-start(bf16[128,768]{1,0:T(8,128)(2,1)} %param.1), channel_id=1, source_target_pairs={{0,24},{4,28},{8,16},{12,20},{16,8},{20,12},{24,0},{28,4},{1,25},{... | collective-permute-start | bytes 589832 | tf_op jit(solution)/shard_map/cond/branch_1_fun/ppermute | solution.py:196
  17.2 0.8 %collective-permute-start.3 = (bf16[128,768]{1,0:T(8,128)(2,1)}, bf16[128,768]{1,0:T(8,128)(2,1)}, u32[]{:S(2)}, u32[]{:S(2)}) collective-permute-start(bf16[128,768]{1,0:T(8,128)(2,1)} %param.1), channel_id=1, source_target_pairs={{0,16},{4,20},{8,24},{12,28},{16,0},{20,4},{24,8},{28,12},{1,17},{... | collective-permute-start | bytes 589832 | tf_op jit(solution)/shard_map/cond/branch_1_fun/ppermute | solution.py:196
  18.0 1.5 %collective-permute-start.1 = (bf16[128,768]{1,0:T(8,128)(2,1)}, bf16[128,768]{1,0:T(8,128)(2,1)}, u32[]{:S(2)}, u32[]{:S(2)}) collective-permute-start(bf16[128,768]{1,0:T(8,128)(2,1)} %param.1), channel_id=1, source_target_pairs={{0,8},{4,12},{8,0},{12,4},{16,24},{20,28},{24,16},{28,20},{1,9},{5... | collective-permute-start | bytes 589832 | tf_op jit(solution)/shard_map/cond/branch_1_fun/ppermute | solution.py:196
  19.5 5.5 %collective-permute-done.5 = bf16[128,768]{1,0:T(8,128)(2,1)} collective-permute-done((bf16[128,768]{1,0:T(8,128)(2,1)}, bf16[128,768]{1,0:T(8,128)(2,1)}, u32[]{:S(2)}, u32[]{:S(2)}) %collective-permute-start.5) | collective-permute-done | bytes 196640 | tf_op jit(solution)/shard_map/cond/branch_1_fun/ppermute | solution.py:196
  25.0 3.3 %collective-permute-done.3 = bf16[128,768]{1,0:T(8,128)(2,1)} collective-permute-done((bf16[128,768]{1,0:T(8,128)(2,1)}, bf16[128,768]{1,0:T(8,128)(2,1)}, u32[]{:S(2)}, u32[]{:S(2)}) %collective-permute-start.3) | collective-permute-done | bytes 196640 | tf_op jit(solution)/shard_map/cond/branch_1_fun/ppermute | solution.py:196
  28.3 0.5 collective-permute-start.2
  28.8 1.3 %collective-permute-done.4 = bf16[128,768]{1,0:T(8,128)(2,1)} collective-permute-done((bf16[128,768]{1,0:T(8,128)(2,1)}, bf16[128,768]{1,0:T(8,128)(2,1)}, u32[]{:S(2)}, u32[]{:S(2)}) %collective-permute-start.4) | collective-permute-done | bytes 196640 | tf_op jit(solution)/shard_map/cond/branch_1_fun/ppermute | solution.py:202
  30.4 3.0 %project_3.1 = (bf16[256,768]{1,0:T(8,128)(2,1)S(1)}, bf16[256,768]{1,0:T(8,128)(2,1)S(1)}, bf16[256,768]{1,0:T(8,128)(2,1)S(1)}) custom-call(bf16[1024,768]{1,0:T(8,128)(2,1)S(1)} %stage.1.noise_ref, bf16[128,768]{1,0:T(8,128)(2,1)} %pad_maximum_fusion.refs_0_, bf16[128,768]{1,0:T(8,128)(2,1)} %get-tuple-element.37.refs_1_, ...), custom_call_target="tpu_custom_call" | custom-call | flops 1207959552 | bytes 4325376 | tf_op jit(solution)/shard_map/project_3/pallas_call | solution.py:41
  33.4 0.7 copy-done.2
  34.2 17.3 %conditional.3 = (bf16[128,1024]{1,0:T(8,128)(2,1)}, bf16[128,1024]{1,0:T(8,128)(2,1)}, bf16[128,1024]{1,0:T(8,128)(2,1)}, bf16[128,1024]{1,0:T(8,128)(2,1)}, bf...) conditional(s32[]{:T(128)} %bitcast.5, ...), branch_computations={%region_2.0_spmd, %region_3.0_spmd} | conditional | bytes 7340368 | solution.py:209
  34.2 1.2 %collective-permute-start.12 = (bf16[128,1024]{1,0:T(8,128)(2,1)S(1)}, bf16[128,1024]{1,0:T(8,128)(2,1)}, u32[]{:S(2)}, u32[]{:S(2)}) collective-permute-start(bf16[128,1024]{1,0:T(8,128)(2,1)S(1)} %param.3), channel_id=1, source_target_pairs={{0,24},{4,28},{8,16},{12,20},{16,8},{20,12},{24,0},{28,4},{1,25},{... | collective-permute-start | bytes 786440 | tf_op jit(solution)/shard_map/cond/branch_1_fun/ppermute | solution.py:196
  35.4 0.8 %collective-permute-start.10 = (bf16[128,1024]{1,0:T(8,128)(2,1)S(1)}, bf16[128,1024]{1,0:T(8,128)(2,1)}, u32[]{:S(2)}, u32[]{:S(2)}) collective-permute-start(bf16[128,1024]{1,0:T(8,128)(2,1)S(1)} %param.3), channel_id=1, source_target_pairs={{0,16},{4,20},{8,24},{12,28},{16,0},{20,4},{24,8},{28,12},{1,17},{... | collective-permute-start | bytes 786440 | tf_op jit(solution)/shard_map/cond/branch_1_fun/ppermute | solution.py:196
  36.2 1.5 %collective-permute-start.8 = (bf16[128,1024]{1,0:T(8,128)(2,1)S(1)}, bf16[128,1024]{1,0:T(8,128)(2,1)}, u32[]{:S(2)}, u32[]{:S(2)}) collective-permute-start(bf16[128,1024]{1,0:T(8,128)(2,1)S(1)} %param.3), channel_id=1, source_target_pairs={{0,8},{4,12},{8,0},{12,4},{16,24},{20,28},{24,16},{28,20},{1,9},{5... | collective-permute-start | bytes 786440 | tf_op jit(solution)/shard_map/cond/branch_1_fun/ppermute | solution.py:196
  37.7 6.7 %collective-permute-done.12 = bf16[128,1024]{1,0:T(8,128)(2,1)} collective-permute-done((bf16[128,1024]{1,0:T(8,128)(2,1)S(1)}, bf16[128,1024]{1,0:T(8,128)(2,1)}, u32[]{:S(2)}, u32[]{:S(2)}) %collective-permute-start.12) | collective-permute-done | bytes 262176 | tf_op jit(solution)/shard_map/cond/branch_1_fun/ppermute | solution.py:196
  44.4 4.9 %collective-permute-done.10 = bf16[128,1024]{1,0:T(8,128)(2,1)} collective-permute-done((bf16[128,1024]{1,0:T(8,128)(2,1)S(1)}, bf16[128,1024]{1,0:T(8,128)(2,1)}, u32[]{:S(2)}, u32[]{:S(2)}) %collective-permute-start.10) | collective-permute-done | bytes 262176 | tf_op jit(solution)/shard_map/cond/branch_1_fun/ppermute | solution.py:196
  49.8 1.4 %collective-permute-done.11 = bf16[128,1024]{1,0:T(8,128)(2,1)} collective-permute-done((bf16[128,1024]{1,0:T(8,128)(2,1)}, bf16[128,1024]{1,0:T(8,128)(2,1)}, u32[]{:S(2)}, u32[]{:S(2)}) %collective-permute-start.11) | collective-permute-done | bytes 262176 | tf_op jit(solution)/shard_map/cond/branch_1_fun/ppermute | solution.py:202
  51.5 1.4 %collective-permute-start.23 = (bf16[256,768]{1,0:T(8,128)(2,1)S(1)}, bf16[256,768]{1,0:T(8,128)(2,1)S(1)}, u32[]{:S(2)}, u32[]{:S(2)}) collective-permute-start(bf16[256,768]{1,0:T(8,128)(2,1)S(1)} %get-tuple-element.56), channel_id=1, source_target_pairs={{0,3},{1,0},{2,1},{3,2},{4,7},{5,4},{6,5},{7,6},{8,11},{9,8},{10,9... | collective-permute-start | bytes 1179656 | tf_op jit(solution)/shard_map/ppermute | solution.py:219
  52.9 0.6 collective-permute-start.22
  54.0 1.0 %copy-done.3 = bf16[256,768]{1,0:T(8,128)(2,1)S(1)} copy-done((bf16[256,768]{1,0:T(8,128)(2,1)S(1)}, bf16[256,768]{1,0:T(8,128)(2,1)}, u32[]{:S(2)}) %copy-start.3) | copy-done | bytes 393240
  55.0 2.6 %accumulate.1 = (bf16[1024,1024]{1,0:T(8,128)(2,1)S(1)}, f32[1024,768]{1,0:T(8,128)S(1)}) custom-call(s32[4,4]{1,0:T(4,128)S(1)} %copy-done.1, bf16[128,1024]{1,0:T(8,128)(2,1)} %bitcast.12, bf16[128,1024]{1,0:T(8,128)(2,1)} %get-tuple-element.46.refs_1_, bf16[128,1024]{1,0:T(8,128)(2,1)} %get-tuple-element.47.refs_2_, ...), custom_call_target="tpu_custom_call" | custom-call | flops 805306368 | bytes 7340032 | tf_op jit(solution)/shard_map/accumulate/pallas_call | solution.py:121
  57.7 13.4 %collective-permute-done.23.refs_1_ = bf16[256,768]{1,0:T(8,128)(2,1)S(1)} collective-permute-done((bf16[256,768]{1,0:T(8,128)(2,1)S(1)}, bf16[256,768]{1,0:T(8,128)(2,1)S(1)}, u32[]{:S(2)}, u32[]{:S(2)}) %collective-permute-start.23) | collective-permute-done | bytes 393248 | tf_op jit(solution)/shard_map/ppermute | solution.py:219
  71.1 4.2 %finish.1 = f32[1024,768]{1,0:T(8,128)} custom-call(s32[4,4]{1,0:T(4,128)S(1)} %copy-done.1, bf16[1024,1024]{1,0:T(8,128)(2,1)S(1)} %get-tuple-element.54.u_ref, f32[1024,768]{1,0:T(8,128)S(1)} %get-tuple-element.55.sum_ref, f32[1024,1]{1,0:T(8,128)S(1)} %copy.7.skew_ref, f32[1024,1]{1,0:T(8,128)S(1)} %copy.8.tail_ref, ...), custom_call_target="tpu_custom_call" | custom-call | flops 805306368 | bytes 8388608 | tf_op jit(solution)/shard_map/finish/pallas_call | solution.py:170
  (42 shorter events, 2.9 us)
Async XLA Ops:
  0.0 11.5 %copy-start.1 = (s32[4,4]{1,0:T(4,128)S(1)}, s32[4,4]{1,0:T(4,128)}, u32[]{:S(2)}) copy-start(s32[4,4]{1,0:T(4,128)} %ranks_ref.3) | copy-start | bytes 196
  1.0 9.9 %collective-permute-start.18 = (bf16[128,256]{1,0:T(8,128)(2,1)S(1)}, bf16[128,256]{1,0:T(8,128)(2,1)S(1)}, u32[]{:S(2)}, u32[]{:S(2)}) collective-permute-start(bf16[128,256]{1,0:T(8,128)(2,1)S(1)} %get-tuple-element.58.refs_0_), channel_id=1, source_target_pairs={{0,16},{4,20},{8,24},{12,28},{16,0},{20,4},{24,8},{28,12},{1,17},{... | collective-permute-start | bytes 196616 | tf_op jit(solution)/shard_map/ppermute | solution.py:196
  4.0 6.9 %collective-permute-start.16 = (bf16[128,256]{1,0:T(8,128)(2,1)S(1)}, bf16[128,256]{1,0:T(8,128)(2,1)S(1)}, u32[]{:S(2)}, u32[]{:S(2)}) collective-permute-start(bf16[128,256]{1,0:T(8,128)(2,1)S(1)} %get-tuple-element.58.refs_0_), channel_id=1, source_target_pairs={{0,8},{4,12},{8,0},{12,4},{16,24},{20,28},{24,16},{28,20},{1,9},{5... | collective-permute-start | bytes 196616 | tf_op jit(solution)/shard_map/ppermute | solution.py:196
  5.5 7.1 %collective-permute-start.15 = (bf16[128,256]{1,0:T(8,128)(2,1)S(1)}, bf16[128,256]{1,0:T(8,128)(2,1)S(1)}, u32[]{:S(2)}, u32[]{:S(2)}) collective-permute-start(bf16[128,256]{1,0:T(8,128)(2,1)S(1)} %get-tuple-element.58.refs_0_), channel_id=1, source_target_pairs={{0,4},{4,0},{8,12},{12,8},{16,20},{20,16},{24,28},{28,24},{1,5},{5... | collective-permute-start | bytes 196616 | tf_op jit(solution)/shard_map/ppermute | solution.py:202
  5.5 5.4 %collective-permute-start.14 = (bf16[128,256]{1,0:T(8,128)(2,1)S(1)}, bf16[128,256]{1,0:T(8,128)(2,1)S(1)}, u32[]{:S(2)}, u32[]{:S(2)}) collective-permute-start(bf16[128,256]{1,0:T(8,128)(2,1)S(1)} %get-tuple-element.58.refs_0_), channel_id=1, source_target_pairs={{0,24},{4,28},{8,16},{12,20},{16,8},{20,12},{24,0},{28,4},{1,25},{... | collective-permute-start | bytes 196616 | tf_op jit(solution)/shard_map/ppermute | solution.py:196
  5.6 1.4 %copy-start = (bf16[1024,768]{1,0:T(8,128)(2,1)S(1)}, bf16[1024,768]{1,0:T(8,128)(2,1)}, u32[]{:S(2)}) copy-start(bf16[1024,768]{1,0:T(8,128)(2,1)} %from_ref.1) | copy-start | bytes 4718596
  10.9 1.7 %collective-permute-start.19 = (bf16[128,256]{1,0:T(8,128)(2,1)S(1)}, bf16[128,256]{1,0:T(8,128)(2,1)S(1)}, u32[]{:S(2)}, u32[]{:S(2)}) collective-permute-start(bf16[128,256]{1,0:T(8,128)(2,1)S(1)} %collective-permute-done.18.refs_4_), channel_id=1, source_target_pairs={{0,4},{4,0},{8,12},{12,8},{16,20},{20,16},{24,28},{28,24},{1,5},{5... | collective-permute-start | bytes 196616 | tf_op jit(solution)/shard_map/ppermute | solution.py:202
  10.9 1.7 %collective-permute-start.17 = (bf16[128,256]{1,0:T(8,128)(2,1)S(1)}, bf16[128,256]{1,0:T(8,128)(2,1)S(1)}, u32[]{:S(2)}, u32[]{:S(2)}) collective-permute-start(bf16[128,256]{1,0:T(8,128)(2,1)S(1)} %collective-permute-done.16.refs_2_), channel_id=1, source_target_pairs={{0,4},{4,0},{8,12},{12,8},{16,20},{20,16},{24,28},{28,24},{1,5},{5... | collective-permute-start | bytes 196616 | tf_op jit(solution)/shard_map/ppermute | solution.py:202
  11.4 1.3 %collective-permute-start.20 = (bf16[128,256]{1,0:T(8,128)(2,1)S(1)}, bf16[128,256]{1,0:T(8,128)(2,1)S(1)}, u32[]{:S(2)}, u32[]{:S(2)}) collective-permute-start(bf16[128,256]{1,0:T(8,128)(2,1)S(1)} %collective-permute-done.14.refs_6_), channel_id=1, source_target_pairs={{0,4},{4,0},{8,12},{12,8},{16,20},{20,16},{24,28},{28,24},{1,5},{5... | collective-permute-start | bytes 196616 | tf_op jit(solution)/shard_map/ppermute | solution.py:202
  13.3 40.7 %collective-permute-start.21 = (bf16[256,768]{1,0:T(8,128)(2,1)S(1)}, bf16[256,768]{1,0:T(8,128)(2,1)S(1)}, u32[]{:S(2)}, u32[]{:S(2)}) collective-permute-start(bf16[256,768]{1,0:T(8,128)(2,1)S(1)} %project_1.1), channel_id=1, source_target_pairs={{0,2},{1,3},{2,0},{3,1},{4,6},{5,7},{6,4},{7,5},{8,10},{9,11},{10,... | collective-permute-start | bytes 1179656 | tf_op jit(solution)/shard_map/ppermute | solution.py:219
  16.0 9.0 %collective-permute-start.5 = (bf16[128,768]{1,0:T(8,128)(2,1)}, bf16[128,768]{1,0:T(8,128)(2,1)}, u32[]{:S(2)}, u32[]{:S(2)}) collective-permute-start(bf16[128,768]{1,0:T(8,128)(2,1)} %param.1), channel_id=1, source_target_pairs={{0,24},{4,28},{8,16},{12,20},{16,8},{20,12},{24,0},{28,4},{1,25},{... | collective-permute-start | bytes 589832 | tf_op jit(solution)/shard_map/cond/branch_1_fun/ppermute | solution.py:196
  17.2 11.1 %collective-permute-start.3 = (bf16[128,768]{1,0:T(8,128)(2,1)}, bf16[128,768]{1,0:T(8,128)(2,1)}, u32[]{:S(2)}, u32[]{:S(2)}) collective-permute-start(bf16[128,768]{1,0:T(8,128)(2,1)} %param.1), channel_id=1, source_target_pairs={{0,16},{4,20},{8,24},{12,28},{16,0},{20,4},{24,8},{28,12},{1,17},{... | collective-permute-start | bytes 589832 | tf_op jit(solution)/shard_map/cond/branch_1_fun/ppermute | solution.py:196
  18.0 10.3 %collective-permute-start.1 = (bf16[128,768]{1,0:T(8,128)(2,1)}, bf16[128,768]{1,0:T(8,128)(2,1)}, u32[]{:S(2)}, u32[]{:S(2)}) collective-permute-start(bf16[128,768]{1,0:T(8,128)(2,1)} %param.1), channel_id=1, source_target_pairs={{0,8},{4,12},{8,0},{12,4},{16,24},{20,28},{24,16},{28,20},{1,9},{5... | collective-permute-start | bytes 589832 | tf_op jit(solution)/shard_map/cond/branch_1_fun/ppermute | solution.py:196
  19.5 9.3 %collective-permute-start = (bf16[128,768]{1,0:T(8,128)(2,1)}, bf16[128,768]{1,0:T(8,128)(2,1)}, u32[]{:S(2)}, u32[]{:S(2)}) collective-permute-start(bf16[128,768]{1,0:T(8,128)(2,1)} %param.1), channel_id=1, source_target_pairs={{0,4},{4,0},{8,12},{12,8},{16,20},{20,16},{24,28},{28,24},{1,5},{5... | collective-permute-start | bytes 589832 | tf_op jit(solution)/shard_map/cond/branch_1_fun/ppermute | solution.py:202
  25.0 3.8 %collective-permute-start.6 = (bf16[128,768]{1,0:T(8,128)(2,1)}, bf16[128,768]{1,0:T(8,128)(2,1)}, u32[]{:S(2)}, u32[]{:S(2)}) collective-permute-start(bf16[128,768]{1,0:T(8,128)(2,1)} %collective-permute-done.5), channel_id=1, source_target_pairs={{0,4},{4,0},{8,12},{12,8},{16,20},{20,16},{24,28},{28,24},{1,5},{5... | collective-permute-start | bytes 589832 | tf_op jit(solution)/shard_map/cond/branch_1_fun/ppermute | solution.py:202
  28.3 1.8 %collective-permute-start.4 = (bf16[128,768]{1,0:T(8,128)(2,1)}, bf16[128,768]{1,0:T(8,128)(2,1)}, u32[]{:S(2)}, u32[]{:S(2)}) collective-permute-start(bf16[128,768]{1,0:T(8,128)(2,1)} %collective-permute-done.3), channel_id=1, source_target_pairs={{0,4},{4,0},{8,12},{12,8},{16,20},{20,16},{24,28},{28,24},{1,5},{5... | collective-permute-start | bytes 589832 | tf_op jit(solution)/shard_map/cond/branch_1_fun/ppermute | solution.py:202
  28.3 2.1 %collective-permute-start.2 = (bf16[128,768]{1,0:T(8,128)(2,1)}, bf16[128,768]{1,0:T(8,128)(2,1)}, u32[]{:S(2)}, u32[]{:S(2)}) collective-permute-start(bf16[128,768]{1,0:T(8,128)(2,1)} %collective-permute-done.1), channel_id=1, source_target_pairs={{0,4},{4,0},{8,12},{12,8},{16,20},{20,16},{24,28},{28,24},{1,5},{5... | collective-permute-start | bytes 589832 | tf_op jit(solution)/shard_map/cond/branch_1_fun/ppermute | solution.py:202
  30.4 3.8 %copy-start.4 = (bf16[1,128,1024]{2,1,0:T(8,128)(2,1)S(1)}, bf16[1,128,1024]{2,1,0:T(8,128)(2,1)}, u32[]{:S(2)}) copy-start(bf16[1,128,1024]{2,1,0:T(8,128)(2,1)} %param.12) | copy-start | bytes 786436
  33.4 0.7 copy-start.2
  34.2 19.4 %copy-start.5 = (f32[1024]{0:T(1024)S(1)}, f32[1024]{0:T(1024)}, u32[]{:S(2)}) copy-start(f32[1024]{0:T(1024)} %param.14) | copy-start | bytes 12292
  34.2 19.6 %copy-start.6 = (f32[1024]{0:T(1024)S(1)}, f32[1024]{0:T(1024)}, u32[]{:S(2)}) copy-start(f32[1024]{0:T(1024)} %param.15) | copy-start | bytes 12292
  34.2 10.2 %collective-permute-start.12 = (bf16[128,1024]{1,0:T(8,128)(2,1)S(1)}, bf16[128,1024]{1,0:T(8,128)(2,1)}, u32[]{:S(2)}, u32[]{:S(2)}) collective-permute-start(bf16[128,1024]{1,0:T(8,128)(2,1)S(1)} %param.3), channel_id=1, source_target_pairs={{0,24},{4,28},{8,16},{12,20},{16,8},{20,12},{24,0},{28,4},{1,25},{... | collective-permute-start | bytes 786440 | tf_op jit(solution)/shard_map/cond/branch_1_fun/ppermute | solution.py:196
  35.4 13.9 %collective-permute-start.10 = (bf16[128,1024]{1,0:T(8,128)(2,1)S(1)}, bf16[128,1024]{1,0:T(8,128)(2,1)}, u32[]{:S(2)}, u32[]{:S(2)}) collective-permute-start(bf16[128,1024]{1,0:T(8,128)(2,1)S(1)} %param.3), channel_id=1, source_target_pairs={{0,16},{4,20},{8,24},{12,28},{16,0},{20,4},{24,8},{28,12},{1,17},{... | collective-permute-start | bytes 786440 | tf_op jit(solution)/shard_map/cond/branch_1_fun/ppermute | solution.py:196
  36.2 13.1 %collective-permute-start.8 = (bf16[128,1024]{1,0:T(8,128)(2,1)S(1)}, bf16[128,1024]{1,0:T(8,128)(2,1)}, u32[]{:S(2)}, u32[]{:S(2)}) collective-permute-start(bf16[128,1024]{1,0:T(8,128)(2,1)S(1)} %param.3), channel_id=1, source_target_pairs={{0,8},{4,12},{8,0},{12,4},{16,24},{20,28},{24,16},{28,20},{1,9},{5... | collective-permute-start | bytes 786440 | tf_op jit(solution)/shard_map/cond/branch_1_fun/ppermute | solution.py:196
  37.7 12.1 %collective-permute-start.7 = (bf16[128,1024]{1,0:T(8,128)(2,1)S(1)}, bf16[128,1024]{1,0:T(8,128)(2,1)}, u32[]{:S(2)}, u32[]{:S(2)}) collective-permute-start(bf16[128,1024]{1,0:T(8,128)(2,1)S(1)} %param.3), channel_id=1, source_target_pairs={{0,4},{4,0},{8,12},{12,8},{16,20},{20,16},{24,28},{28,24},{1,5},{5... | collective-permute-start | bytes 786440 | tf_op jit(solution)/shard_map/cond/branch_1_fun/ppermute | solution.py:202
  44.4 5.4 %collective-permute-start.13 = (bf16[128,1024]{1,0:T(8,128)(2,1)}, bf16[128,1024]{1,0:T(8,128)(2,1)}, u32[]{:S(2)}, u32[]{:S(2)}) collective-permute-start(bf16[128,1024]{1,0:T(8,128)(2,1)} %collective-permute-done.12), channel_id=1, source_target_pairs={{0,4},{4,0},{8,12},{12,8},{16,20},{20,16},{24,28},{28,24},{1,5},{5... | collective-permute-start | bytes 786440 | tf_op jit(solution)/shard_map/cond/branch_1_fun/ppermute | solution.py:202
  49.3 1.9 %collective-permute-start.11 = (bf16[128,1024]{1,0:T(8,128)(2,1)}, bf16[128,1024]{1,0:T(8,128)(2,1)}, u32[]{:S(2)}, u32[]{:S(2)}) collective-permute-start(bf16[128,1024]{1,0:T(8,128)(2,1)} %collective-permute-done.10), channel_id=1, source_target_pairs={{0,4},{4,0},{8,12},{12,8},{16,20},{20,16},{24,28},{28,24},{1,5},{5... | collective-permute-start | bytes 786440 | tf_op jit(solution)/shard_map/cond/branch_1_fun/ppermute | solution.py:202
  49.3 2.2 %collective-permute-start.9 = (bf16[128,1024]{1,0:T(8,128)(2,1)}, bf16[128,1024]{1,0:T(8,128)(2,1)}, u32[]{:S(2)}, u32[]{:S(2)}) collective-permute-start(bf16[128,1024]{1,0:T(8,128)(2,1)} %collective-permute-done.8), channel_id=1, source_target_pairs={{0,4},{4,0},{8,12},{12,8},{16,20},{20,16},{24,28},{28,24},{1,5},{5... | collective-permute-start | bytes 786440 | tf_op jit(solution)/shard_map/cond/branch_1_fun/ppermute | solution.py:202
  51.5 19.6 %collective-permute-start.23 = (bf16[256,768]{1,0:T(8,128)(2,1)S(1)}, bf16[256,768]{1,0:T(8,128)(2,1)S(1)}, u32[]{:S(2)}, u32[]{:S(2)}) collective-permute-start(bf16[256,768]{1,0:T(8,128)(2,1)S(1)} %get-tuple-element.56), channel_id=1, source_target_pairs={{0,3},{1,0},{2,1},{3,2},{4,7},{5,4},{6,5},{7,6},{8,11},{9,8},{10,9... | collective-permute-start | bytes 1179656 | tf_op jit(solution)/shard_map/ppermute | solution.py:219
  52.9 18.2 %collective-permute-start.22 = (bf16[256,768]{1,0:T(8,128)(2,1)S(1)}, bf16[256,768]{1,0:T(8,128)(2,1)S(1)}, u32[]{:S(2)}, u32[]{:S(2)}) collective-permute-start(bf16[256,768]{1,0:T(8,128)(2,1)S(1)} %get-tuple-element.44), channel_id=1, source_target_pairs={{0,1},{1,2},{2,3},{3,0},{4,5},{5,6},{6,7},{7,4},{8,9},{9,10},{10,1... | collective-permute-start | bytes 1179656 | tf_op jit(solution)/shard_map/ppermute | solution.py:219
  54.0 1.0 %copy-start.3 = (bf16[256,768]{1,0:T(8,128)(2,1)S(1)}, bf16[256,768]{1,0:T(8,128)(2,1)}, u32[]{:S(2)}) copy-start(bf16[256,768]{1,0:T(8,128)(2,1)} %copy-done.2) | copy-start | bytes 1179652

commit v4 on v3

v4 whole, which is shorter than its diff:
```python
import functools

import jax
import jax.numpy as jnp
from jax import lax
from jax.experimental import pallas as pl
from jax.experimental.pallas import tpu as pltpu
from jax.sharding import PartitionSpec as P

CAP = 2
LOG2E = 1.4426950408889634
VMEM = pl.BlockSpec(memory_space=pltpu.VMEM)
SMEM = pl.BlockSpec(memory_space=pltpu.SMEM)
SMALL = pl.CostEstimate(flops=1, bytes_accessed=1, transcendentals=0)
LIMIT = pltpu.CompilerParams(vmem_limit_bytes=44 * 2**20)


def stack_pieces(places, rows, pieces, whole):
    me = lax.axis_index("real")
    for (distance, row), piece in zip(places, pieces):
        height = piece.shape[0]
        start = pl.multiple_of((me ^ distance) * rows + row, height)
        whole[pl.ds(start, height), :] = piece[...]


def project_columns(v_columns, noise_ref):
    projected = lax.dot_general(
        v_columns, noise_ref[...], (((0,), (0,)), ((), ())), preferred_element_type=jnp.float32
    )
    return projected.astype(jnp.bfloat16)


def project_kernel(places, rows, noise_ref, *refs):
    pieces, outs, whole = refs[: len(places)], refs[len(places) : -1], refs[-1]
    stack_pieces(places, rows, pieces, whole)
    for place, out_ref in enumerate(outs):
        columns = out_ref.shape[0]
        out_ref[...] = project_columns(
            whole[:, place * columns : (place + 1) * columns], noise_ref
        )


def project(n_shifts, noise, gathered):
    sites, reals = noise.shape
    places, pieces = zip(*gathered)
    rows, columns = pieces[0].shape
    return pl.pallas_call(
        functools.partial(project_kernel, places, rows),
        out_shape=[jax.ShapeDtypeStruct((columns // n_shifts, reals), jnp.bfloat16)] * n_shifts,
        in_specs=[VMEM] * (1 + len(pieces)),
        out_specs=[VMEM] * n_shifts,
        scratch_shapes=[pltpu.VMEM((sites, columns), jnp.bfloat16)],
        compiler_params=LIMIT,
        cost_estimate=SMALL,
        name=f"project_{n_shifts}",
    )(noise, *pieces)


def stage_kernel(from_ref, to_ref, sems):
    parts = sems.shape[0]
    rows = from_ref.shape[0] // parts
    copies = []
    for part in range(parts):
        span = slice(part * rows, (part + 1) * rows)
        copies.append(
            pltpu.make_async_copy(from_ref.at[span, :], to_ref.at[span, :], sems.at[part])
        )
        copies[-1].start()
    for copy in copies:
        copy.wait()


def stage(array):
    return pl.pallas_call(
        stage_kernel,
        out_shape=jax.ShapeDtypeStruct(array.shape, array.dtype),
        in_specs=[pl.BlockSpec(memory_space=pltpu.HBM)],
        out_specs=VMEM,
        scratch_shapes=[pltpu.SemaphoreType.DMA((4,))],
        compiler_params=LIMIT,
        cost_estimate=SMALL,
        name="stage",
    )(array)


def source_of(shift):
    site_count = lax.axis_size("site")
    return lax.rem(lax.axis_index("site") + (site_count - shift), site_count)


def alive_coef(shift, ranks_ref, coef):
    rank = ranks_ref[lax.axis_index("site"), source_of(shift)]
    row = lax.broadcasted_iota(jnp.int32, coef.shape, 0)
    alive = row < rank * (coef.shape[0] // CAP)
    return jnp.where(alive, coef.astype(jnp.float32), 0.0).astype(coef.dtype)


def accumulate_kernel(shifts, places, rows, ranks_ref, noise_ref, *refs):
    pieces, coefs = refs[: len(places)], refs[len(places) : len(places) + len(shifts)]
    u_ref, sum_ref, whole = refs[-3:]
    stack_pieces(places, rows, pieces, whole)
    per_source = whole.shape[1] - u_ref.shape[1]
    u_ref[...] = whole[:, per_source:]
    own = project_columns(whole[:, :per_source], noise_ref)
    total = jnp.zeros(sum_ref.shape, jnp.float32)
    for shift, coef in zip((0,) + shifts, [own] + [coef_ref[...] for coef_ref in coefs]):
        start = pl.multiple_of(source_of(shift) * per_source, per_source)
        total += jnp.dot(
            u_ref[:, pl.ds(start, per_source)],
            alive_coef(shift, ranks_ref, coef),
            preferred_element_type=jnp.float32,
        )
    sum_ref[...] = total


def accumulate(shifts, ranks, noise, gathered, coefs):
    places, pieces = zip(*gathered)
    rows, columns = pieces[0].shape
    sites, reals = noise.shape
    return pl.pallas_call(
        functools.partial(accumulate_kernel, shifts, places, rows),
        out_shape=[
            jax.ShapeDtypeStruct((sites, columns - coefs[0].shape[0]), jnp.bfloat16),
            jax.ShapeDtypeStruct((sites, reals), jnp.float32),
        ],
        in_specs=[SMEM] + [VMEM] * (1 + len(pieces) + len(coefs)),
        out_specs=[VMEM] * 2,
        scratch_shapes=[pltpu.VMEM((sites, columns), jnp.bfloat16)],
        compiler_params=LIMIT,
        cost_estimate=SMALL,
        name="accumulate",
    )(ranks, noise, *pieces, *coefs)


def finish_kernel(shifts, ranks_ref, u_ref, sum_ref, skew_ref, tail_ref, *refs):
    coefs = refs[: len(shifts)]
    out_ref, slots, sems = refs[len(shifts) :]
    block = slots.shape[1]
    alive = [alive_coef(shift, ranks_ref, coef[...]) for shift, coef in zip(shifts, coefs)]
    copies = []
    for step in range(out_ref.shape[0] // block):
        rows = slice(step * block, (step + 1) * block)
        gaussian = sum_ref[rows, :]
        for shift, coef in zip(shifts, alive):
            columns = coef.shape[0]
            start = pl.multiple_of(source_of(shift) * columns, columns)
            gaussian += jnp.dot(
                u_ref[rows, pl.ds(start, columns)], coef, preferred_element_type=jnp.float32
            )
        skew, tail = skew_ref[rows, :], tail_ref[rows, :]
        grown = jnp.exp2((skew * LOG2E) * gaussian) + 1.0
        grown = grown * jnp.tanh((0.5 * skew) * gaussian) * (1.0 / skew)
        slots[step] = grown * jnp.exp2((0.5 * LOG2E * tail) * (gaussian * gaussian))
        copy = pltpu.make_async_copy(slots.at[step], out_ref.at[rows, :], sems.at[step])
        copy.start()
        copies.append(copy)
    for copy in copies:
        copy.wait()


def finish(shifts, ranks, u_whole, total, skew, tail, coefs):
    rows, columns = u_whole.shape
    per_source, reals = coefs[0].shape
    block = min(rows, 128)
    return pl.pallas_call(
        functools.partial(finish_kernel, shifts),
        out_shape=jax.ShapeDtypeStruct((rows, reals), jnp.float32),
        in_specs=[SMEM] + [VMEM] * (4 + len(coefs)),
        out_specs=pl.BlockSpec(memory_space=pl.ANY),
        scratch_shapes=[
            pltpu.VMEM((rows // block, block, reals), jnp.float32),
            pltpu.SemaphoreType.DMA((rows // block,)),
        ],
        compiler_params=LIMIT,
        cost_estimate=SMALL,
        name="finish",
    )(ranks, u_whole, total, skew, tail, *coefs)


def after(value, *before):
    return lax.optimization_barrier((value, before))[0]


def swap(array, distance):
    count = lax.axis_size("real")
    return lax.ppermute(array, "real", [(k, k ^ distance) for k in range(count)])


def with_other_core(pieces):
    both = dict(pieces)
    for (distance, row), piece in pieces.items():
        if (distance ^ 1, row) not in pieces:
            both[distance ^ 1, row] = swap(piece, 1)
    return both


def from_chips(own):
    pieces = {(0, 0): own}
    for distance in range(2, lax.axis_size("real"), 2):
        pieces[distance, 0] = swap(own, distance)
    return pieces


def relay_steps(count):
    if count != 8:
        return (lambda pieces: from_chips(pieces[0, 0]), with_other_core)

    def neighbours(pieces):
        own = pieces[0, 0]
        return {(2, 0): swap(own, 2), (4, 0): swap(own, 4), (1, 0): swap(own, 1)}

    def opposite(pieces):
        first, second = pieces[2, 0], pieces[4, 0]
        half = first.shape[0] // 2
        return {
            (6, 0): swap(second[:half], 2),
            (6, half): swap(first[half:], 4),
            (3, 0): swap(first, 1),
        }

    return (neighbours, opposite, with_other_core)


def at_once(present, gather, *arrays):
    shapes = jax.eval_shape(gather, *arrays)
    return lax.cond(
        present, gather, lambda *same: [same[0][: shape.shape[0]] for shape in shapes], *arrays
    )


def gather_at_once(present, own, steps):
    pieces = {(0, 0): own}
    for step in steps:
        places, arrays = list(pieces), list(pieces.values())
        new = []

        def added(*arrays):
            more = step(dict(zip(places, arrays)))
            new[:] = [place for place in more if place not in pieces]
            return [more[place] for place in new]

        results = at_once(present, added, *arrays)
        pieces.update(zip(new, results))
    return list(pieces.items())


def along_site(coef, shift):
    count = lax.axis_size("site")
    return lax.ppermute(coef, "site", [(k, (k + shift) % count) for k in range(count)])


def per_device(noise, v_factors, u_factors, ranks, skew_g, tail_h):
    site_count = lax.axis_size("site")
    real_count = lax.axis_size("real")
    source = lax.axis_index("site")
    rows, columns = v_factors.shape[1:]
    per_dest = columns // site_count
    middle = site_count // 2
    others = sorted(range(1, site_count), key=lambda shift: (abs(shift - middle), shift))
    first, rest = others[0], tuple(others[1:])

    def columns_for(shift):
        start = lax.rem(source + shift, site_count) * per_dest
        return lax.dynamic_slice(v_factors[0], (0, start), (rows, per_dest))

    v_first = columns_for(first)
    v_rest = jnp.concatenate([columns_for(shift) for shift in rest], axis=1)
    own_and_u = jnp.concatenate([columns_for(0), u_factors[0]], axis=1)
    present = ranks[0, 0] > 0
    v_first = from_chips(v_first)
    last = max(v_first)
    waiting = (v_first[last], stage(noise), v_rest, own_and_u, present)
    v_first[last], noise, v_rest, own_and_u, present = lax.optimization_barrier(waiting)
    coefs = {}
    [coefs[first]] = project(1, noise, list(with_other_core(v_first).items()))

    v_rest = after(v_rest, coefs[first])
    direct = (lambda pieces: with_other_core(from_chips(pieces[0, 0])),)
    v_rest = gather_at_once(present, v_rest, direct)
    coefs.update(zip(rest, project(len(rest), noise, v_rest)))
    received = {shift: along_site(coef, shift) for shift, coef in coefs.items()}

    own_and_u = after(own_and_u, coefs[rest[0]], received[first])
    own_and_u = gather_at_once(present, own_and_u, relay_steps(lax.axis_size("real")))
    u_whole, total = accumulate((first,), ranks, noise, own_and_u, [received[first]])
    return finish(
        rest, ranks, u_whole, total, skew_g[:, None], tail_h[:, None], [received[s] for s in rest]
    )


def solution(mesh):
    placed = (
        P("site", "real"),
        P("site", "real", None),
        P("site", "real", None),
        P(),
        P("site"),
        P("site"),
    )
    return jax.shard_map(
        per_device, mesh=mesh, in_specs=placed, out_specs=P("site", "real"), check_vma=False
    )
```

time: 75.6 us -> 71.5 us (0.946)
  waiting for transfers between devices: 39.7 us -> 22 us
  starting transfers between devices: 17.9 us -> 30.3 us
  Pallas kernels: 11.3 us -> 12.1 us
    ppermute x3, waiting for transfers between devices: 13.4 us -> 0.01 us  [along_site(): lax.ppermute(coef, 'site', [(k, (k + shift) % count) for k in range(count)])]
    ppermute x21 -> x23, starting transfers between devices: 13.2 us -> 23.5 us  [swap(): lax.ppermute(array, 'real', [(k, k ^ distance) for k in range(count)])]
    ppermute x21 -> x23, waiting for transfers between devices: 26.2 us -> 22 us  [swap(): lax.ppermute(array, 'real', [(k, k ^ distance) for k in range(count)])]
    ppermute x3, starting transfers between devices: 4.7 us -> 6.81 us  [along_site(): lax.ppermute(coef, 'site', [(k, (k + shift) % count) for k in range(count)])]
    slice x0 -> x2, local copies, waits for them, and re-layouts: none -> 1.85 us  [the longest x1 0.93 us: opposite(): first[half:]]
    unnamed x14 -> x10, local copies, waits for them, and re-layouts: 3.15 us -> 1.42 us
    pallas_call x3, Pallas kernels: 6.33 us -> 8.04 us  [the longest x2 4.52 us: project(): pl.pallas_call(functools.partial(project_kernel, places, rows), out_shape...]
    pallas_call x1, Pallas kernels: 4.22 us -> 3.27 us  [finish(): pl.pallas_call(functools.partial(finish_kernel, shifts), out_shape=jax.Sh...]
  transfers between devices with their start and end apart: 24 -> 26, of which waited for: 11 -> 12; matrix products, arithmetic and copies ran while one was open for 2% -> 5% of each run, Pallas kernels for 9% -> 10%
where the time goes in v4:
time: 71.5 us; the launch traced here: 71.2 us
  starting transfers between devices  30.3 us (42%)
  waiting for transfers between devices  22 us (31%)
  Pallas kernels  12.1 us (17%)
  local copies, waits for them, and re-layouts  5.23 us (7%)
  other arithmetic  0.76 us (1%)
  between operations  0.76 us (1%)
    ppermute x23, starting transfers between devices, swap(): lax.ppermute(array, 'real', [(k, k ^ distance) for k in range(count)])  23.5 us
    ppermute x23, waiting for transfers between devices, swap(): lax.ppermute(array, 'real', [(k, k ^ distance) for k in range(count)])  22 us
    ppermute x3, starting transfers between devices, along_site(): lax.ppermute(coef, 'site', [(k, (k + shift) % count) for k in range(count)])  6.81 us
    pallas_call x2, Pallas kernels, project(): pl.pallas_call(functools.partial(project_kernel, places, rows), out_shape...  4.52 us
    pallas_call x1, Pallas kernels, accumulate(): pl.pallas_call(functools.partial(accumulate_kernel, shifts, places, rows)...  3.51 us
    pallas_call x1, Pallas kernels, finish(): pl.pallas_call(functools.partial(finish_kernel, shifts), out_shape=jax.Sh...  3.27 us
  transfers between devices with their start and end apart: 26, of which 12 were waited for; matrix products, arithmetic and copies ran while one was open for 5% of the time, Pallas kernels for 10%

profile of v4, /device:TPU:0, one launch (start us, length us, event | category | flops | bytes accessed | tf_op | source)
XLA Modules:
  0.0 71.2 jit_solution(11629488485171445291)
XLA Ops:
  0.0 1.0 %dynamic-slice_bitcast_fusion = (bf16[128,256]{1,0:T(8,128)(2,1)S(1)}, bf16[128,256]{1,0:T(8,128)(2,1)S(1)}, bf16[128,256]{1,0:T(8,128)(2,1)S(1)}, bf16[128,256]{1,0:T(8,128)(2,1)S(1)}) fusion(bf16[1,128,1024]{2,1,0:T(8,128)(2,1)} %param.15, s32[]{:T(128)S(6)} %select_n.15, s32[]{:T(128)S(6)} %select_n.13, s32[]{:T(128)S(6)} %select_n.12, s32[]{:T(128)S(6)} %select_n.14), kind=kLoop, calls=%fused_computation.2 | loop fusion | bytes 524304 | tf_op jit(solution)/shard_map/dynamic_slice | solution.py:264
  1.0 4.0 %collective-permute-start.16 = (bf16[128,256]{1,0:T(8,128)(2,1)S(1)}, bf16[128,256]{1,0:T(8,128)(2,1)S(1)}, u32[]{:S(2)}, u32[]{:S(2)}) collective-permute-start(bf16[128,256]{1,0:T(8,128)(2,1)S(1)} %get-tuple-element.82.refs_0_), channel_id=1, source_target_pairs={{0,24},{4,28},{8,16},{12,20},{16,8},{20,12},{24,0},{28,4},{1,25},{... | collective-permute-start | bytes 196616 | tf_op jit(solution)/shard_map/ppermute | solution.py:186
  5.0 0.5 collective-permute-start.17
  5.6 1.4 %copy-done = bf16[1024,768]{1,0:T(8,128)(2,1)S(1)} copy-done((bf16[1024,768]{1,0:T(8,128)(2,1)S(1)}, bf16[1024,768]{1,0:T(8,128)(2,1)}, u32[]{:S(2)}) %copy-start) | copy-done | bytes 1572888
  7.0 0.8 %stage.1.noise_ref = bf16[1024,768]{1,0:T(8,128)(2,1)S(1)} custom-call(bf16[1024,768]{1,0:T(8,128)(2,1)S(1)} %copy-done), custom_call_target="tpu_custom_call" | custom-call | flops 1 | bytes 1 | tf_op jit(solution)/shard_map/stage/pallas_call | solution.py:74
  8.3 0.7 %pad_maximum_fusion.refs_0_ = bf16[128,1280]{1,0:T(8,128)(2,1)} fusion(bf16[128,1024]{1,0:T(8,128)(2,1)S(1)} %bitcast.12, bf16[128,256]{1,0:T(8,128)(2,1)S(1)} %get-tuple-element.80), kind=kLoop, calls=%fused_computation | loop fusion | flops 655360 | bytes 655360 | tf_op jit(solution)/shard_map/concatenate | solution.py:268
  9.8 0.6 collective-permute-start.22
  11.8 1.4 %project_1.1 = bf16[256,768]{1,0:T(8,128)(2,1)} custom-call(bf16[1024,768]{1,0:T(8,128)(2,1)S(1)} %stage.1.noise_ref, bf16[128,256]{1,0:T(8,128)(2,1)S(1)} %get-tuple-element.82.refs_0_, bf16[128,256]{1,0:T(8,128)(2,1)S(1)} %collective-permute-done.17.refs_1_, bf16[128,256]{1,0:T(8,128)(2,1)S(1)} %collective-permute-done.18.refs_2_, ...), custom_call_target="tpu_custom_call" | custom-call | flops 1 | bytes 1 | tf_op jit(solution)/shard_map/project_1/pallas_call | solution.py:47
  13.2 3.0 %collective-permute-start.23 = (bf16[256,768]{1,0:T(8,128)(2,1)}, bf16[256,768]{1,0:T(8,128)(2,1)}, u32[]{:S(2)}, u32[]{:S(2)}) collective-permute-start(bf16[256,768]{1,0:T(8,128)(2,1)} %project_1.1), channel_id=1, source_target_pairs={{0,2},{1,3},{2,0},{3,1},{4,6},{5,7},{6,4},{7,5},{8,10},{9,11},{10,... | collective-permute-start | bytes 1179656 | tf_op jit(solution)/shard_map/ppermute | solution.py:249
  16.2 11.5 %conditional.4 = (bf16[128,512]{1,0:T(8,128)(2,1)}, bf16[128,512]{1,0:T(8,128)(2,1)}, bf16[128,512]{1,0:T(8,128)(2,1)}, bf16[128,512]{1,0:T(8,128)(2,1)}, bf16[1...) conditional(s32[]{:T(128)} %convert_element_type.2, ...), branch_computations={%region_0.0_spmd, %region_1.0_spmd} | conditional | bytes 3670352 | solution.py:226
  16.2 1.5 %collective-permute-start = (bf16[128,512]{1,0:T(8,128)(2,1)S(1)}, bf16[128,512]{1,0:T(8,128)(2,1)}, u32[]{:S(2)}, u32[]{:S(2)}) collective-permute-start(bf16[128,512]{1,0:T(8,128)(2,1)S(1)} %param.1), channel_id=1, source_target_pairs={{0,8},{4,12},{8,0},{12,4},{16,24},{20,28},{24,16},{28,20},{1,9},{5... | collective-permute-start | bytes 393224 | tf_op jit(solution)/shard_map/cond/branch_1_fun/ppermute | solution.py:186
  17.7 1.5 %collective-permute-start.1 = (bf16[128,512]{1,0:T(8,128)(2,1)S(1)}, bf16[128,512]{1,0:T(8,128)(2,1)}, u32[]{:S(2)}, u32[]{:S(2)}) collective-permute-start(bf16[128,512]{1,0:T(8,128)(2,1)S(1)} %param.1), channel_id=1, source_target_pairs={{0,16},{4,20},{8,24},{12,28},{16,0},{20,4},{24,8},{28,12},{1,17},{... | collective-permute-start | bytes 393224 | tf_op jit(solution)/shard_map/cond/branch_1_fun/ppermute | solution.py:186
  19.7 2.4 %collective-permute-done = bf16[128,512]{1,0:T(8,128)(2,1)} collective-permute-done((bf16[128,512]{1,0:T(8,128)(2,1)S(1)}, bf16[128,512]{1,0:T(8,128)(2,1)}, u32[]{:S(2)}, u32[]{:S(2)}) %collective-permute-start) | collective-permute-done | bytes 131104 | tf_op jit(solution)/shard_map/cond/branch_1_fun/ppermute | solution.py:186
  22.1 3.7 %collective-permute-done.1 = bf16[128,512]{1,0:T(8,128)(2,1)} collective-permute-done((bf16[128,512]{1,0:T(8,128)(2,1)S(1)}, bf16[128,512]{1,0:T(8,128)(2,1)}, u32[]{:S(2)}, u32[]{:S(2)}) %collective-permute-start.1) | collective-permute-done | bytes 131104 | tf_op jit(solution)/shard_map/cond/branch_1_fun/ppermute | solution.py:186
  26.3 1.2 %collective-permute-done.5 = bf16[128,512]{1,0:T(8,128)(2,1)} collective-permute-done((bf16[128,512]{1,0:T(8,128)(2,1)}, bf16[128,512]{1,0:T(8,128)(2,1)}, u32[]{:S(2)}, u32[]{:S(2)}) %collective-permute-start.5) | collective-permute-done | bytes 131104 | tf_op jit(solution)/shard_map/cond/branch_1_fun/ppermute | solution.py:186
  27.7 3.1 %project_2.1 = (bf16[256,768]{1,0:T(8,128)(2,1)}, bf16[256,768]{1,0:T(8,128)(2,1)}) custom-call(bf16[1024,768]{1,0:T(8,128)(2,1)S(1)} %stage.1.noise_ref, bf16[128,512]{1,0:T(8,128)(2,1)S(1)} %pad_maximum_fusion.1.refs_0_, bf16[128,512]{1,0:T(8,128)(2,1)} %get-tuple-element.59.refs_1_, bf16[128,512]{1,0:T(8,128)(2,1)} %get-tuple-element.60.refs_2_, ...), custom_call_target="tpu_custom_call" | custom-call | flops 1 | bytes 1 | tf_op jit(solution)/shard_map/project_2/pallas_call | solution.py:47
  30.8 1.6 %collective-permute-start.24 = (bf16[256,768]{1,0:T(8,128)(2,1)}, bf16[256,768]{1,0:T(8,128)(2,1)S(1)}, u32[]{:S(2)}, u32[]{:S(2)}) collective-permute-start(bf16[256,768]{1,0:T(8,128)(2,1)} %get-tuple-element.66), channel_id=1, source_target_pairs={{0,1},{1,2},{2,3},{3,0},{4,5},{5,6},{6,7},{7,4},{8,9},{9,10},{10,1... | collective-permute-start | bytes 1179656 | tf_op jit(solution)/shard_map/ppermute | solution.py:249
  32.3 2.3 %collective-permute-start.25 = (bf16[256,768]{1,0:T(8,128)(2,1)}, bf16[256,768]{1,0:T(8,128)(2,1)S(1)}, u32[]{:S(2)}, u32[]{:S(2)}) collective-permute-start(bf16[256,768]{1,0:T(8,128)(2,1)} %get-tuple-element.79), channel_id=1, source_target_pairs={{0,3},{1,0},{2,1},{3,2},{4,7},{5,4},{6,5},{7,6},{8,11},{9,8},{10,9... | collective-permute-start | bytes 1179656 | tf_op jit(solution)/shard_map/ppermute | solution.py:249
  35.1 16.4 %conditional.5 = (bf16[128,1280]{1,0:T(8,128)(2,1)}, bf16[128,1280]{1,0:T(8,128)(2,1)}, bf16[128,1280]{1,0:T(8,128)(2,1)}) conditional(s32[]{:T(128)} %convert_element_type.2, bf16[128,1280]{1,0:T(8,128)(2,1)} %pad_maximum_fusion.refs_0_, bf16[128,1280]{1,0:T(8,128)(2,1)} %pad_maximum_fusion.refs_0_), branch_computations={%region_2.0_spmd, %region_3.0_spmd} | conditional | bytes 3932304 | solution.py:226
  35.1 1.1 %collective-permute-start.7 = (bf16[128,1280]{1,0:T(8,128)(2,1)}, bf16[128,1280]{1,0:T(8,128)(2,1)}, u32[]{:S(2)}, u32[]{:S(2)}) collective-permute-start(bf16[128,1280]{1,0:T(8,128)(2,1)} %param.3), channel_id=1, source_target_pairs={{0,8},{4,12},{8,0},{12,4},{16,24},{20,28},{24,16},{28,20},{1,9},{5... | collective-permute-start | bytes 983048 | tf_op jit(solution)/shard_map/cond/branch_1_fun/ppermute | solution.py:186
  36.2 9.9 %collective-permute-start.8 = (bf16[128,1280]{1,0:T(8,128)(2,1)}, bf16[128,1280]{1,0:T(8,128)(2,1)}, u32[]{:S(2)}, u32[]{:S(2)}) collective-permute-start(bf16[128,1280]{1,0:T(8,128)(2,1)} %param.3), channel_id=1, source_target_pairs={{0,16},{4,20},{8,24},{12,28},{16,0},{20,4},{24,8},{28,12},{1,17},{... | collective-permute-start | bytes 983048 | tf_op jit(solution)/shard_map/cond/branch_1_fun/ppermute | solution.py:186
  46.1 5.4 %collective-permute-done.8 = bf16[128,1280]{1,0:T(8,128)(2,1)} collective-permute-done((bf16[128,1280]{1,0:T(8,128)(2,1)}, bf16[128,1280]{1,0:T(8,128)(2,1)}, u32[]{:S(2)}, u32[]{:S(2)}) %collective-permute-start.8) | collective-permute-done | bytes 327712 | tf_op jit(solution)/shard_map/cond/branch_1_fun/ppermute | solution.py:186
  51.5 10.4 %conditional.6 = (bf16[64,1280]{1,0:T(8,128)(2,1)}, bf16[64,1280]{1,0:T(8,128)(2,1)}, bf16[128,1280]{1,0:T(8,128)(2,1)}) conditional(s32[]{:T(128)} %convert_element_type.2, bf16[128,1280]{1,0:T(8,128)(2,1)} %pad_maximum_fusion.refs_0_, (bf16[128,1280]{1,0:T(8,128)(2,1)}, bf16[128,1280]{1,0:T(8,128)(2,1)}) %tuple.43), branch_computations={%region_4.0_spmd, %region_5.0_spmd} | conditional | bytes 3276944 | solution.py:226
  51.5 0.9 %slice.14 = bf16[64,1280]{1,0:T(8,128)(2,1)S(1)} slice(bf16[128,1280]{1,0:T(8,128)(2,1)} %get-tuple-element.22), slice={[64:128], [0:1280]} | slice | bytes 327680 | tf_op jit(solution)/shard_map/cond/branch_1_fun/slice | solution.py:217
  52.4 2.1 %collective-permute-start.11 = (bf16[64,1280]{1,0:T(8,128)(2,1)S(1)}, bf16[64,1280]{1,0:T(8,128)(2,1)}, u32[]{:S(2)}, u32[]{:S(2)}) collective-permute-start(bf16[64,1280]{1,0:T(8,128)(2,1)S(1)} %slice.14), channel_id=1, source_target_pairs={{0,16},{4,20},{8,24},{12,28},{16,0},{20,4},{24,8},{28,12},{1,17},{... | collective-permute-start | bytes 491528 | tf_op jit(solution)/shard_map/cond/branch_1_fun/ppermute | solution.py:186
  54.5 0.9 %slice.10 = bf16[64,1280]{1,0:T(8,128)(2,1)S(1)} slice(bf16[128,1280]{1,0:T(8,128)(2,1)} %get-tuple-element.21), slice={[0:64], [0:1280]} | slice | bytes 327680 | tf_op jit(solution)/shard_map/cond/branch_1_fun/slice | solution.py:216
  55.6 3.9 %collective-permute-done.11 = bf16[64,1280]{1,0:T(8,128)(2,1)} collective-permute-done((bf16[64,1280]{1,0:T(8,128)(2,1)S(1)}, bf16[64,1280]{1,0:T(8,128)(2,1)}, u32[]{:S(2)}, u32[]{:S(2)}) %collective-permute-start.11) | collective-permute-done | bytes 163872 | tf_op jit(solution)/shard_map/cond/branch_1_fun/ppermute | solution.py:186
  59.5 2.5 %collective-permute-done.10 = bf16[64,1280]{1,0:T(8,128)(2,1)} collective-permute-done((bf16[64,1280]{1,0:T(8,128)(2,1)S(1)}, bf16[64,1280]{1,0:T(8,128)(2,1)}, u32[]{:S(2)}, u32[]{:S(2)}) %collective-permute-start.10) | collective-permute-done | bytes 163872 | tf_op jit(solution)/shard_map/cond/branch_1_fun/ppermute | solution.py:186
  61.9 2.4 %conditional.7 = (bf16[128,1280]{1,0:T(8,128)(2,1)}, bf16[64,1280]{1,0:T(8,128)(2,1)}, bf16[64,1280]{1,0:T(8,128)(2,1)}) conditional(s32[]{:T(128)} %convert_element_type.2, bf16[128,1280]{1,0:T(8,128)(2,1)} %pad_maximum_fusion.refs_0_, (bf16[128,1280]{1,0:T(8,128)(2,1)}, bf16[64,1280]{1,0:T(8,128)(2,1)}, bf16[64,1280]{1,0:T(8,128)(2,1)}) %tuple.44), branch_computations={%region_6.0_spmd, %region_7.0_spmd} | conditional | bytes 2621584 | solution.py:226
  62.5 1.6 %collective-permute-done.14 = bf16[64,1280]{1,0:T(8,128)(2,1)} collective-permute-done((bf16[64,1280]{1,0:T(8,128)(2,1)}, bf16[64,1280]{1,0:T(8,128)(2,1)}, u32[]{:S(2)}, u32[]{:S(2)}) %collective-permute-start.14) | collective-permute-done | bytes 163872 | tf_op jit(solution)/shard_map/cond/branch_1_fun/ppermute | solution.py:186
  64.4 3.5 %accumulate.1 = (bf16[1024,1024]{1,0:T(8,128)(2,1)S(1)}, f32[1024,768]{1,0:T(8,128)S(1)}) custom-call(s32[4,4]{1,0:T(4,128)S(1)} %copy-done.1, bf16[1024,768]{1,0:T(8,128)(2,1)S(1)} %stage.1.noise_ref, bf16[128,1280]{1,0:T(8,128)(2,1)} %pad_maximum_fusion.refs_0_, bf16[128,1280]{1,0:T(8,128)(2,1)} %get-tuple-element.68.refs_1_, ...), custom_call_target="tpu_custom_call" | custom-call | flops 1 | bytes 1 | tf_op jit(solution)/shard_map/accumulate/pallas_call | solution.py:120
  67.9 3.3 %finish.1 = f32[1024,768]{1,0:T(8,128)} custom-call(s32[4,4]{1,0:T(4,128)S(1)} %copy-done.1, bf16[1024,1024]{1,0:T(8,128)(2,1)S(1)} %get-tuple-element.77.u_ref, f32[1024,768]{1,0:T(8,128)S(1)} %get-tuple-element.78.sum_ref, f32[1024,1]{1,0:T(8,128)S(1)} %copy.7.skew_ref, f32[1024,1]{1,0:T(8,128)S(1)} %copy.8.tail_ref, ...), custom_call_target="tpu_custom_call" | custom-call | flops 1 | bytes 1 | tf_op jit(solution)/shard_map/finish/pallas_call | solution.py:165
  (47 shorter events, 4.7 us)
Async XLA Ops:
  0.0 7.8 %copy-start.1 = (s32[4,4]{1,0:T(4,128)S(1)}, s32[4,4]{1,0:T(4,128)}, u32[]{:S(2)}) copy-start(s32[4,4]{1,0:T(4,128)} %ranks_ref.3) | copy-start | bytes 196
  0.0 8.3 %copy-start.2 = (bf16[1,128,1024]{2,1,0:T(8,128)(2,1)S(1)}, bf16[1,128,1024]{2,1,0:T(8,128)(2,1)}, u32[]{:S(2)}) copy-start(bf16[1,128,1024]{2,1,0:T(8,128)(2,1)} %param.16) | copy-start | bytes 786436
  1.0 8.8 %collective-permute-start.16 = (bf16[128,256]{1,0:T(8,128)(2,1)S(1)}, bf16[128,256]{1,0:T(8,128)(2,1)S(1)}, u32[]{:S(2)}, u32[]{:S(2)}) collective-permute-start(bf16[128,256]{1,0:T(8,128)(2,1)S(1)} %get-tuple-element.82.refs_0_), channel_id=1, source_target_pairs={{0,24},{4,28},{8,16},{12,20},{16,8},{20,12},{24,0},{28,4},{1,25},{... | collective-permute-start | bytes 196616 | tf_op jit(solution)/shard_map/ppermute | solution.py:186
  5.0 5.4 %collective-permute-start.17 = (bf16[128,256]{1,0:T(8,128)(2,1)S(1)}, bf16[128,256]{1,0:T(8,128)(2,1)S(1)}, u32[]{:S(2)}, u32[]{:S(2)}) collective-permute-start(bf16[128,256]{1,0:T(8,128)(2,1)S(1)} %get-tuple-element.82.refs_0_), channel_id=1, source_target_pairs={{0,8},{4,12},{8,0},{12,4},{16,24},{20,28},{24,16},{28,20},{1,9},{5... | collective-permute-start | bytes 196616 | tf_op jit(solution)/shard_map/ppermute | solution.py:186
  5.5 4.9 %collective-permute-start.18 = (bf16[128,256]{1,0:T(8,128)(2,1)S(1)}, bf16[128,256]{1,0:T(8,128)(2,1)S(1)}, u32[]{:S(2)}, u32[]{:S(2)}) collective-permute-start(bf16[128,256]{1,0:T(8,128)(2,1)S(1)} %get-tuple-element.82.refs_0_), channel_id=1, source_target_pairs={{0,16},{4,20},{8,24},{12,28},{16,0},{20,4},{24,8},{28,12},{1,17},{... | collective-permute-start | bytes 196616 | tf_op jit(solution)/shard_map/ppermute | solution.py:186
  5.6 5.3 %collective-permute-start.19 = (bf16[128,256]{1,0:T(8,128)(2,1)S(1)}, bf16[128,256]{1,0:T(8,128)(2,1)S(1)}, u32[]{:S(2)}, u32[]{:S(2)}) collective-permute-start(bf16[128,256]{1,0:T(8,128)(2,1)S(1)} %get-tuple-element.82.refs_0_), channel_id=1, source_target_pairs={{0,4},{4,0},{8,12},{12,8},{16,20},{20,16},{24,28},{28,24},{1,5},{5... | collective-permute-start | bytes 196616 | tf_op jit(solution)/shard_map/ppermute | solution.py:186
  5.6 1.4 %copy-start = (bf16[1024,768]{1,0:T(8,128)(2,1)S(1)}, bf16[1024,768]{1,0:T(8,128)(2,1)}, u32[]{:S(2)}) copy-start(bf16[1024,768]{1,0:T(8,128)(2,1)} %from_ref.1) | copy-start | bytes 4718596
  9.8 1.5 %collective-permute-start.22 = (bf16[128,256]{1,0:T(8,128)(2,1)S(1)}, bf16[128,256]{1,0:T(8,128)(2,1)S(1)}, u32[]{:S(2)}, u32[]{:S(2)}) collective-permute-start(bf16[128,256]{1,0:T(8,128)(2,1)S(1)} %collective-permute-done.16.refs_3_), channel_id=1, source_target_pairs={{0,4},{4,0},{8,12},{12,8},{16,20},{20,16},{24,28},{28,24},{1,5},{5... | collective-permute-start | bytes 196616 | tf_op jit(solution)/shard_map/ppermute | solution.py:186
  10.3 1.3 %collective-permute-start.20 = (bf16[128,256]{1,0:T(8,128)(2,1)S(1)}, bf16[128,256]{1,0:T(8,128)(2,1)S(1)}, u32[]{:S(2)}, u32[]{:S(2)}) collective-permute-start(bf16[128,256]{1,0:T(8,128)(2,1)S(1)} %collective-permute-done.17.refs_1_), channel_id=1, source_target_pairs={{0,4},{4,0},{8,12},{12,8},{16,20},{20,16},{24,28},{28,24},{1,5},{5... | collective-permute-start | bytes 196616 | tf_op jit(solution)/shard_map/ppermute | solution.py:186
  10.4 1.3 %collective-permute-start.21 = (bf16[128,256]{1,0:T(8,128)(2,1)S(1)}, bf16[128,256]{1,0:T(8,128)(2,1)S(1)}, u32[]{:S(2)}, u32[]{:S(2)}) collective-permute-start(bf16[128,256]{1,0:T(8,128)(2,1)S(1)} %collective-permute-done.18.refs_2_), channel_id=1, source_target_pairs={{0,4},{4,0},{8,12},{12,8},{16,20},{20,16},{24,28},{28,24},{1,5},{5... | collective-permute-start | bytes 196616 | tf_op jit(solution)/shard_map/ppermute | solution.py:186
  13.2 21.9 %collective-permute-start.23 = (bf16[256,768]{1,0:T(8,128)(2,1)}, bf16[256,768]{1,0:T(8,128)(2,1)}, u32[]{:S(2)}, u32[]{:S(2)}) collective-permute-start(bf16[256,768]{1,0:T(8,128)(2,1)} %project_1.1), channel_id=1, source_target_pairs={{0,2},{1,3},{2,0},{3,1},{4,6},{5,7},{6,4},{7,5},{8,10},{9,11},{10,... | collective-permute-start | bytes 1179656 | tf_op jit(solution)/shard_map/ppermute | solution.py:249
  16.2 18.4 %copy-start.3 = (f32[1024]{0:T(1024)S(1)}, f32[1024]{0:T(1024)}, u32[]{:S(2)}) copy-start(f32[1024]{0:T(1024)} %param.18) | copy-start | bytes 12292
  16.2 18.6 %copy-start.4 = (f32[1024]{0:T(1024)S(1)}, f32[1024]{0:T(1024)}, u32[]{:S(2)}) copy-start(f32[1024]{0:T(1024)} %param.19) | copy-start | bytes 12292
  16.2 5.9 %collective-permute-start = (bf16[128,512]{1,0:T(8,128)(2,1)S(1)}, bf16[128,512]{1,0:T(8,128)(2,1)}, u32[]{:S(2)}, u32[]{:S(2)}) collective-permute-start(bf16[128,512]{1,0:T(8,128)(2,1)S(1)} %param.1), channel_id=1, source_target_pairs={{0,8},{4,12},{8,0},{12,4},{16,24},{20,28},{24,16},{28,20},{1,9},{5... | collective-permute-start | bytes 393224 | tf_op jit(solution)/shard_map/cond/branch_1_fun/ppermute | solution.py:186
  17.7 8.1 %collective-permute-start.1 = (bf16[128,512]{1,0:T(8,128)(2,1)S(1)}, bf16[128,512]{1,0:T(8,128)(2,1)}, u32[]{:S(2)}, u32[]{:S(2)}) collective-permute-start(bf16[128,512]{1,0:T(8,128)(2,1)S(1)} %param.1), channel_id=1, source_target_pairs={{0,16},{4,20},{8,24},{12,28},{16,0},{20,4},{24,8},{28,12},{1,17},{... | collective-permute-start | bytes 393224 | tf_op jit(solution)/shard_map/cond/branch_1_fun/ppermute | solution.py:186
  19.2 6.6 %collective-permute-start.2 = (bf16[128,512]{1,0:T(8,128)(2,1)S(1)}, bf16[128,512]{1,0:T(8,128)(2,1)}, u32[]{:S(2)}, u32[]{:S(2)}) collective-permute-start(bf16[128,512]{1,0:T(8,128)(2,1)S(1)} %param.1), channel_id=1, source_target_pairs={{0,24},{4,28},{8,16},{12,20},{16,8},{20,12},{24,0},{28,4},{1,25},{... | collective-permute-start | bytes 393224 | tf_op jit(solution)/shard_map/cond/branch_1_fun/ppermute | solution.py:186
  19.7 6.6 %collective-permute-start.3 = (bf16[128,512]{1,0:T(8,128)(2,1)S(1)}, bf16[128,512]{1,0:T(8,128)(2,1)}, u32[]{:S(2)}, u32[]{:S(2)}) collective-permute-start(bf16[128,512]{1,0:T(8,128)(2,1)S(1)} %param.1), channel_id=1, source_target_pairs={{0,4},{4,0},{8,12},{12,8},{16,20},{20,16},{24,28},{28,24},{1,5},{5... | collective-permute-start | bytes 393224 | tf_op jit(solution)/shard_map/cond/branch_1_fun/ppermute | solution.py:186
  22.1 4.2 %collective-permute-start.4 = (bf16[128,512]{1,0:T(8,128)(2,1)}, bf16[128,512]{1,0:T(8,128)(2,1)}, u32[]{:S(2)}, u32[]{:S(2)}) collective-permute-start(bf16[128,512]{1,0:T(8,128)(2,1)} %collective-permute-done), channel_id=1, source_target_pairs={{0,4},{4,0},{8,12},{12,8},{16,20},{20,16},{24,28},{28,24},{1,5},{5... | collective-permute-start | bytes 393224 | tf_op jit(solution)/shard_map/cond/branch_1_fun/ppermute | solution.py:186
  25.8 1.7 %collective-permute-start.5 = (bf16[128,512]{1,0:T(8,128)(2,1)}, bf16[128,512]{1,0:T(8,128)(2,1)}, u32[]{:S(2)}, u32[]{:S(2)}) collective-permute-start(bf16[128,512]{1,0:T(8,128)(2,1)} %collective-permute-done.1), channel_id=1, source_target_pairs={{0,4},{4,0},{8,12},{12,8},{16,20},{20,16},{24,28},{28,24},{1,5},{5... | collective-permute-start | bytes 393224 | tf_op jit(solution)/shard_map/cond/branch_1_fun/ppermute | solution.py:186
  25.8 1.9 %collective-permute-start.6 = (bf16[128,512]{1,0:T(8,128)(2,1)}, bf16[128,512]{1,0:T(8,128)(2,1)}, u32[]{:S(2)}, u32[]{:S(2)}) collective-permute-start(bf16[128,512]{1,0:T(8,128)(2,1)} %collective-permute-done.2), channel_id=1, source_target_pairs={{0,4},{4,0},{8,12},{12,8},{16,20},{20,16},{24,28},{28,24},{1,5},{5... | collective-permute-start | bytes 393224 | tf_op jit(solution)/shard_map/cond/branch_1_fun/ppermute | solution.py:186
  30.8 37.1 %collective-permute-start.24 = (bf16[256,768]{1,0:T(8,128)(2,1)}, bf16[256,768]{1,0:T(8,128)(2,1)S(1)}, u32[]{:S(2)}, u32[]{:S(2)}) collective-permute-start(bf16[256,768]{1,0:T(8,128)(2,1)} %get-tuple-element.66), channel_id=1, source_target_pairs={{0,1},{1,2},{2,3},{3,0},{4,5},{5,6},{6,7},{7,4},{8,9},{9,10},{10,1... | collective-permute-start | bytes 1179656 | tf_op jit(solution)/shard_map/ppermute | solution.py:249
  32.3 35.6 %collective-permute-start.25 = (bf16[256,768]{1,0:T(8,128)(2,1)}, bf16[256,768]{1,0:T(8,128)(2,1)S(1)}, u32[]{:S(2)}, u32[]{:S(2)}) collective-permute-start(bf16[256,768]{1,0:T(8,128)(2,1)} %get-tuple-element.79), channel_id=1, source_target_pairs={{0,3},{1,0},{2,1},{3,2},{4,7},{5,4},{6,5},{7,6},{8,11},{9,8},{10,9... | collective-permute-start | bytes 1179656 | tf_op jit(solution)/shard_map/ppermute | solution.py:249
  35.1 11.0 %collective-permute-start.7 = (bf16[128,1280]{1,0:T(8,128)(2,1)}, bf16[128,1280]{1,0:T(8,128)(2,1)}, u32[]{:S(2)}, u32[]{:S(2)}) collective-permute-start(bf16[128,1280]{1,0:T(8,128)(2,1)} %param.3), channel_id=1, source_target_pairs={{0,8},{4,12},{8,0},{12,4},{16,24},{20,28},{24,16},{28,20},{1,9},{5... | collective-permute-start | bytes 983048 | tf_op jit(solution)/shard_map/cond/branch_1_fun/ppermute | solution.py:186
  36.2 15.3 %collective-permute-start.8 = (bf16[128,1280]{1,0:T(8,128)(2,1)}, bf16[128,1280]{1,0:T(8,128)(2,1)}, u32[]{:S(2)}, u32[]{:S(2)}) collective-permute-start(bf16[128,1280]{1,0:T(8,128)(2,1)} %param.3), channel_id=1, source_target_pairs={{0,16},{4,20},{8,24},{12,28},{16,0},{20,4},{24,8},{28,12},{1,17},{... | collective-permute-start | bytes 983048 | tf_op jit(solution)/shard_map/cond/branch_1_fun/ppermute | solution.py:186
  46.1 5.4 %collective-permute-start.9 = (bf16[128,1280]{1,0:T(8,128)(2,1)}, bf16[128,1280]{1,0:T(8,128)(2,1)}, u32[]{:S(2)}, u32[]{:S(2)}) collective-permute-start(bf16[128,1280]{1,0:T(8,128)(2,1)} %param.3), channel_id=1, source_target_pairs={{0,4},{4,0},{8,12},{12,8},{16,20},{20,16},{24,28},{28,24},{1,5},{5... | collective-permute-start | bytes 983048 | tf_op jit(solution)/shard_map/cond/branch_1_fun/ppermute | solution.py:186
  51.5 10.4 %collective-permute-start.12 = (bf16[128,1280]{1,0:T(8,128)(2,1)}, bf16[128,1280]{1,0:T(8,128)(2,1)}, u32[]{:S(2)}, u32[]{:S(2)}) collective-permute-start(bf16[128,1280]{1,0:T(8,128)(2,1)} %get-tuple-element.22), channel_id=1, source_target_pairs={{0,4},{4,0},{8,12},{12,8},{16,20},{20,16},{24,28},{28,24},{1,5},{5... | collective-permute-start | bytes 983048 | tf_op jit(solution)/shard_map/cond/branch_1_fun/ppermute | solution.py:186
  52.4 7.0 %collective-permute-start.11 = (bf16[64,1280]{1,0:T(8,128)(2,1)S(1)}, bf16[64,1280]{1,0:T(8,128)(2,1)}, u32[]{:S(2)}, u32[]{:S(2)}) collective-permute-start(bf16[64,1280]{1,0:T(8,128)(2,1)S(1)} %slice.14), channel_id=1, source_target_pairs={{0,16},{4,20},{8,24},{12,28},{16,0},{20,4},{24,8},{28,12},{1,17},{... | collective-permute-start | bytes 491528 | tf_op jit(solution)/shard_map/cond/branch_1_fun/ppermute | solution.py:186
  55.4 6.5 %collective-permute-start.10 = (bf16[64,1280]{1,0:T(8,128)(2,1)S(1)}, bf16[64,1280]{1,0:T(8,128)(2,1)}, u32[]{:S(2)}, u32[]{:S(2)}) collective-permute-start(bf16[64,1280]{1,0:T(8,128)(2,1)S(1)} %slice.10), channel_id=1, source_target_pairs={{0,8},{4,12},{8,0},{12,4},{16,24},{20,28},{24,16},{28,20},{1,9},{5... | collective-permute-start | bytes 491528 | tf_op jit(solution)/shard_map/cond/branch_1_fun/ppermute | solution.py:186
  61.9 2.4 %collective-permute-start.13 = (bf16[128,1280]{1,0:T(8,128)(2,1)}, bf16[128,1280]{1,0:T(8,128)(2,1)}, u32[]{:S(2)}, u32[]{:S(2)}) collective-permute-start(bf16[128,1280]{1,0:T(8,128)(2,1)} %get-tuple-element.23), channel_id=1, source_target_pairs={{0,4},{4,0},{8,12},{12,8},{16,20},{20,16},{24,28},{28,24},{1,5},{5... | collective-permute-start | bytes 983048 | tf_op jit(solution)/shard_map/cond/branch_1_fun/ppermute | solution.py:186
  61.9 2.2 %collective-permute-start.14 = (bf16[64,1280]{1,0:T(8,128)(2,1)}, bf16[64,1280]{1,0:T(8,128)(2,1)}, u32[]{:S(2)}, u32[]{:S(2)}) collective-permute-start(bf16[64,1280]{1,0:T(8,128)(2,1)} %get-tuple-element.24), channel_id=1, source_target_pairs={{0,4},{4,0},{8,12},{12,8},{16,20},{20,16},{24,28},{28,24},{1,5},{5... | collective-permute-start | bytes 491528 | tf_op jit(solution)/shard_map/cond/branch_1_fun/ppermute | solution.py:186
  62.4 1.9 %collective-permute-start.15 = (bf16[64,1280]{1,0:T(8,128)(2,1)}, bf16[64,1280]{1,0:T(8,128)(2,1)}, u32[]{:S(2)}, u32[]{:S(2)}) collective-permute-start(bf16[64,1280]{1,0:T(8,128)(2,1)} %get-tuple-element.25), channel_id=1, source_target_pairs={{0,4},{4,0},{8,12},{12,8},{16,20},{20,16},{24,28},{28,24},{1,5},{5... | collective-permute-start | bytes 491528 | tf_op jit(solution)/shard_map/cond/branch_1_fun/ppermute | solution.py:186

commit v5 on v4

--- a/solution.py
+++ b/solution.py
@@ -11,8 +11,12 @@
 LOG2E = 1.4426950408889634
 VMEM = pl.BlockSpec(memory_space=pltpu.VMEM)
 SMEM = pl.BlockSpec(memory_space=pltpu.SMEM)
-SMALL = pl.CostEstimate(flops=1, bytes_accessed=1, transcendentals=0)
 LIMIT = pltpu.CompilerParams(vmem_limit_bytes=44 * 2**20)
+
+
+def cost(flops, *arrays):
+    touched = sum(array.size * array.dtype.itemsize for array in arrays)
+    return pl.CostEstimate(flops=flops, bytes_accessed=2 * touched, transcendentals=0)
 
 
 def stack_pieces(places, rows, pieces, whole):
@@ -51,7 +55,7 @@
         out_specs=[VMEM] * n_shifts,
         scratch_shapes=[pltpu.VMEM((sites, columns), jnp.bfloat16)],
         compiler_params=LIMIT,
-        cost_estimate=SMALL,
+        cost_estimate=cost(2 * sites * columns * reals, noise, *pieces),
         name=f"project_{n_shifts}",
     )(noise, *pieces)
 
@@ -78,7 +82,7 @@
         out_specs=VMEM,
         scratch_shapes=[pltpu.SemaphoreType.DMA((4,))],
         compiler_params=LIMIT,
-        cost_estimate=SMALL,
+        cost_estimate=cost(0, array),
         name="stage",
     )(array)
 
@@ -95,41 +99,39 @@
     return jnp.where(alive, coef.astype(jnp.float32), 0.0).astype(coef.dtype)
 
 
-def accumulate_kernel(shifts, places, rows, ranks_ref, noise_ref, *refs):
+def accumulate_kernel(shifts, places, rows, ranks_ref, *refs):
     pieces, coefs = refs[: len(places)], refs[len(places) : len(places) + len(shifts)]
-    u_ref, sum_ref, whole = refs[-3:]
-    stack_pieces(places, rows, pieces, whole)
-    per_source = whole.shape[1] - u_ref.shape[1]
-    u_ref[...] = whole[:, per_source:]
-    own = project_columns(whole[:, :per_source], noise_ref)
+    u_ref, sum_ref = refs[-2:]
+    stack_pieces(places, rows, pieces, u_ref)
     total = jnp.zeros(sum_ref.shape, jnp.float32)
-    for shift, coef in zip((0,) + shifts, [own] + [coef_ref[...] for coef_ref in coefs]):
+    for shift, coef_ref in zip(shifts, coefs):
+        per_source = coef_ref.shape[0]
         start = pl.multiple_of(source_of(shift) * per_source, per_source)
         total += jnp.dot(
             u_ref[:, pl.ds(start, per_source)],
-            alive_coef(shift, ranks_ref, coef),
+            alive_coef(shift, ranks_ref, coef_ref[...]),
             preferred_element_type=jnp.float32,
         )
     sum_ref[...] = total
 
 
-def accumulate(shifts, ranks, noise, gathered, coefs):
+def accumulate(shifts, ranks, gathered, coefs):
     places, pieces = zip(*gathered)
     rows, columns = pieces[0].shape
-    sites, reals = noise.shape
+    sites = rows * lax.axis_size("real")
+    per_source, reals = coefs[0].shape
     return pl.pallas_call(
         functools.partial(accumulate_kernel, shifts, places, rows),
         out_shape=[
-            jax.ShapeDtypeStruct((sites, columns - coefs[0].shape[0]), jnp.bfloat16),
+            jax.ShapeDtypeStruct((sites, columns), jnp.bfloat16),
             jax.ShapeDtypeStruct((sites, reals), jnp.float32),
         ],
-        in_specs=[SMEM] + [VMEM] * (1 + len(pieces) + len(coefs)),
+        in_specs=[SMEM] + [VMEM] * (len(pieces) + len(coefs)),
         out_specs=[VMEM] * 2,
-        scratch_shapes=[pltpu.VMEM((sites, columns), jnp.bfloat16)],
-        compiler_params=LIMIT,
-        cost_estimate=SMALL,
+        compiler_params=LIMIT,
+        cost_estimate=cost(2 * sites * len(coefs) * per_source * reals, *pieces, *coefs),
         name="accumulate",
-    )(ranks, noise, *pieces, *coefs)
+    )(ranks, *pieces, *coefs)
 
 
 def finish_kernel(shifts, ranks_ref, u_ref, sum_ref, skew_ref, tail_ref, *refs):
@@ -172,7 +174,7 @@
             pltpu.SemaphoreType.DMA((rows // block,)),
         ],
         compiler_params=LIMIT,
-        cost_estimate=SMALL,
+        cost_estimate=cost(2 * rows * len(coefs) * per_source * reals, u_whole, total, *coefs),
         name="finish",
     )(ranks, u_whole, total, skew, tail, *coefs)
 
@@ -201,47 +203,29 @@
     return pieces
 
 
-def relay_steps(count):
-    if count != 8:
-        return (lambda pieces: from_chips(pieces[0, 0]), with_other_core)
-
-    def neighbours(pieces):
-        own = pieces[0, 0]
-        return {(2, 0): swap(own, 2), (4, 0): swap(own, 4), (1, 0): swap(own, 1)}
-
-    def opposite(pieces):
-        first, second = pieces[2, 0], pieces[4, 0]
-        half = first.shape[0] // 2
-        return {
-            (6, 0): swap(second[:half], 2),
-            (6, half): swap(first[half:], 4),
-            (3, 0): swap(first, 1),
-        }
-
-    return (neighbours, opposite, with_other_core)
-
-
-def at_once(present, gather, *arrays):
-    shapes = jax.eval_shape(gather, *arrays)
-    return lax.cond(
-        present, gather, lambda *same: [same[0][: shape.shape[0]] for shape in shapes], *arrays
-    )
-
-
-def gather_at_once(present, own, steps):
-    pieces = {(0, 0): own}
-    for step in steps:
-        places, arrays = list(pieces), list(pieces.values())
-        new = []
-
-        def added(*arrays):
-            more = step(dict(zip(places, arrays)))
-            new[:] = [place for place in more if place not in pieces]
-            return [more[place] for place in new]
-
-        results = at_once(present, added, *arrays)
-        pieces.update(zip(new, results))
-    return list(pieces.items())
+def two_at_a_time(own):
+    distances = range(2, lax.axis_size("real"), 2)
+    pieces, tails = {(0, 0): own}, [own, own]
+    for turn, distance in enumerate(distances):
+        tails[turn % 2] = pieces[distance, 0] = swap(after(own, tails[turn % 2]), distance)
+    last, tail = distances[-1], tails[len(distances) % 2]
+    for distance in (0, *distances[:-1]):
+        tail = pieces[distance ^ 1, 0] = swap(after(pieces[distance, 0], tail), 1)
+    pieces[last ^ 1, 0] = swap(pieces[last, 0], 1)
+    return pieces
+
+
+def at_once(present, gather, pieces):
+    places, arrays, new = list(pieces), list(pieces.values()), []
+
+    def added(*arrays):
+        more = gather(dict(zip(places, arrays)))
+        new[:] = [place for place in more if place not in pieces]
+        return [more[place] for place in new]
+
+    count = len(jax.eval_shape(added, *arrays))
+    results = lax.cond(present, added, lambda *same: [same[0]] * count, *arrays)
+    return {**pieces, **dict(zip(new, results))}
 
 
 def along_site(coef, shift):
@@ -264,28 +248,26 @@
         return lax.dynamic_slice(v_factors[0], (0, start), (rows, per_dest))
 
     v_first = columns_for(first)
-    v_rest = jnp.concatenate([columns_for(shift) for shift in rest], axis=1)
-    own_and_u = jnp.concatenate([columns_for(0), u_factors[0]], axis=1)
+    v_rest = jnp.concatenate([columns_for(shift) for shift in rest + (0,)], axis=1)
     present = ranks[0, 0] > 0
     v_first = from_chips(v_first)
     last = max(v_first)
-    waiting = (v_first[last], stage(noise), v_rest, own_and_u, present)
-    v_first[last], noise, v_rest, own_and_u, present = lax.optimization_barrier(waiting)
-    coefs = {}
-    [coefs[first]] = project(1, noise, list(with_other_core(v_first).items()))
-
-    v_rest = after(v_rest, coefs[first])
-    direct = (lambda pieces: with_other_core(from_chips(pieces[0, 0])),)
-    v_rest = gather_at_once(present, v_rest, direct)
-    coefs.update(zip(rest, project(len(rest), noise, v_rest)))
-    received = {shift: along_site(coef, shift) for shift, coef in coefs.items()}
-
-    own_and_u = after(own_and_u, coefs[rest[0]], received[first])
-    own_and_u = gather_at_once(present, own_and_u, relay_steps(lax.axis_size("real")))
-    u_whole, total = accumulate((first,), ranks, noise, own_and_u, [received[first]])
-    return finish(
-        rest, ranks, u_whole, total, skew_g[:, None], tail_h[:, None], [received[s] for s in rest]
-    )
+    waiting = (v_first[last], stage(noise), v_rest, present)
+    v_first[last], noise, v_rest, present = lax.optimization_barrier(waiting)
+    v_first = with_other_core(v_first)
+    v_rest = from_chips(after(v_rest, *v_first.values()))
+    [far] = project(1, noise, v_first.items())
+
+    v_rest = at_once(present, with_other_core, after(v_rest, far))
+    *others, own = project(len(rest) + 1, noise, v_rest.items())
+    far = along_site(far, first)
+    others = [along_site(coef, shift) for coef, shift in zip(others, rest)]
+
+    u_pieces = at_once(
+        present, lambda pieces: two_at_a_time(pieces[0, 0]), {(0, 0): after(u_factors[0], own)}
+    )
+    u_whole, total = accumulate((0, first), ranks, u_pieces.items(), [own, far])
+    return finish(rest, ranks, u_whole, total, skew_g[:, None], tail_h[:, None], others)
 
 
 def solution(mesh):

time: 71.5 us -> 63.4 us (0.89)
  starting transfers between devices: 30.3 us -> 20.5 us
  waiting for transfers between devices: 22 us -> 25.1 us
  Pallas kernels: 12.1 us -> 10.2 us
    ppermute x23 -> x21, starting transfers between devices: 23.5 us -> 14 us  [swap(): lax.ppermute(array, 'real', [(k, k ^ distance) for k in range(count)])]
    ppermute x23 -> x21, waiting for transfers between devices: 22 us -> 25.1 us  [swap(): lax.ppermute(array, 'real', [(k, k ^ distance) for k in range(count)])]
    slice x2 -> x0, local copies, waits for them, and re-layouts: 1.85 us -> none  [the longest x1 0.93 us: opposite(): first[half:]]
    unnamed x10 -> x12, local copies, waits for them, and re-layouts: 1.42 us -> 3.16 us
    pallas_call x1, Pallas kernels: 3.51 us -> 2.63 us  [accumulate(): pl.pallas_call(functools.partial(accumulate_kernel, shifts, places, rows)...]
    pallas_call x2, Pallas kernels: 4.52 us -> 3.68 us  [project(): pl.pallas_call(functools.partial(project_kernel, places, rows), out_shape...]
  transfers between devices with their start and end apart: 26 -> 24, of which waited for: 12 -> 16; matrix products, arithmetic and copies ran while one was open for 5% -> 4% of each run, Pallas kernels for 10% -> 11%
where the time goes in v5:
time: 63.4 us; the launch traced here: 63.1 us
  waiting for transfers between devices  25.1 us (40%)
  starting transfers between devices  20.5 us (32%)
  Pallas kernels  10.2 us (16%)
  local copies, waits for them, and re-layouts  5.74 us (9%)
  between operations  0.77 us (1%)
  other arithmetic  0.69 us (1%)
    ppermute x21, waiting for transfers between devices, swap(): lax.ppermute(array, 'real', [(k, k ^ distance) for k in range(count)])  25.1 us
    ppermute x21, starting transfers between devices, swap(): lax.ppermute(array, 'real', [(k, k ^ distance) for k in range(count)])  14 us
    ppermute x3, starting transfers between devices, along_site(): lax.ppermute(coef, 'site', [(k, (k + shift) % count) for k in range(count)])  6.53 us
    pallas_call x2, Pallas kernels, project(): pl.pallas_call(functools.partial(project_kernel, places, rows), out_shape...  3.68 us
    unnamed x12, local copies, waits for them, and re-layouts  3.16 us
    pallas_call x1, Pallas kernels, finish(): pl.pallas_call(functools.partial(finish_kernel, shifts), out_shape=jax.Sh...  3.15 us
    pallas_call x1, Pallas kernels, accumulate(): pl.pallas_call(functools.partial(accumulate_kernel, shifts, places, rows)...  2.63 us
  transfers between devices with their start and end apart: 24, of which 16 were waited for; matrix products, arithmetic and copies ran while one was open for 4% of the time, Pallas kernels for 11%

profile of v5, /device:TPU:0, one launch (start us, length us, event | category | flops | bytes accessed | tf_op | source)
XLA Modules:
  0.0 63.1 jit_solution(15271121284428357642)
XLA Ops:
  0.0 1.0 %dynamic-slice_bitcast_fusion.2 = (bf16[128,256]{1,0:T(8,128)(2,1)S(1)}, bf16[128,256]{1,0:T(8,128)(2,1)S(1)}, bf16[128,256]{1,0:T(8,128)(2,1)S(1)}, bf16[128,256]{1,0:T(8,128)(2,1)S(1)}) fusion(bf16[1,128,1024]{2,1,0:T(8,128)(2,1)} %param.11, s32[]{:T(128)S(6)} %select_n.13, s32[]{:T(128)S(6)} %select_n.12, s32[]{:T(128)S(6)} %select_n.15, s32[]{:T(128)S(6)} %select_n.14), kind=kLoop, calls=%fused_computation.3 | loop fusion | bytes 524304 | tf_op jit(solution)/shard_map/dynamic_slice | solution.py:248
  1.0 0.5 collective-permute-start.14
  1.5 2.6 %collective-permute-start.13 = (bf16[128,256]{1,0:T(8,128)(2,1)S(1)}, bf16[128,256]{1,0:T(8,128)(2,1)S(1)}, u32[]{:S(2)}, u32[]{:S(2)}) collective-permute-start(bf16[128,256]{1,0:T(8,128)(2,1)S(1)} %get-tuple-element.78.refs_0_), channel_id=1, source_target_pairs={{0,16},{4,20},{8,24},{12,28},{16,0},{20,4},{24,8},{28,12},{1,17},{... | collective-permute-start | bytes 196616 | tf_op jit(solution)/shard_map/ppermute | solution.py:188
  4.1 1.5 %collective-permute-start.12 = (bf16[128,256]{1,0:T(8,128)(2,1)S(1)}, bf16[128,256]{1,0:T(8,128)(2,1)S(1)}, u32[]{:S(2)}, u32[]{:S(2)}) collective-permute-start(bf16[128,256]{1,0:T(8,128)(2,1)S(1)} %get-tuple-element.78.refs_0_), channel_id=1, source_target_pairs={{0,8},{4,12},{8,0},{12,4},{16,24},{20,28},{24,16},{28,20},{1,9},{5... | collective-permute-start | bytes 196616 | tf_op jit(solution)/shard_map/ppermute | solution.py:188
  5.6 1.2 %slice.3 = s32[1,1]{1,0:T(1,128)} slice(s32[4,4]{1,0:T(4,128)} %ranks_ref.3), slice={[0:1], [0:1]} | slice | bytes 8 | tf_op jit(solution)/shard_map/slice | solution.py:252
  6.8 1.4 %copy-done = bf16[1024,768]{1,0:T(8,128)(2,1)S(1)} copy-done((bf16[1024,768]{1,0:T(8,128)(2,1)S(1)}, bf16[1024,768]{1,0:T(8,128)(2,1)}, u32[]{:S(2)}) %copy-start) | copy-done | bytes 1572888
  8.2 0.8 %stage.1.noise_ref = bf16[1024,768]{1,0:T(8,128)(2,1)S(1)} custom-call(bf16[1024,768]{1,0:T(8,128)(2,1)S(1)} %copy-done), custom_call_target="tpu_custom_call" | custom-call | bytes 3145728 | tf_op jit(solution)/shard_map/stage/pallas_call | solution.py:78
  9.7 0.7 %pad_maximum_fusion.refs_0_ = bf16[128,768]{1,0:T(8,128)(2,1)} fusion(bf16[128,256]{1,0:T(8,128)(2,1)S(1)} %get-tuple-element.79, bf16[128,256]{1,0:T(8,128)(2,1)S(1)} %get-tuple-element.80, bf16[128,256]{1,0:T(8,128)(2,1)S(1)} %get-tuple-element.77), kind=kLoop, calls=%fused_computation | loop fusion | flops 589824 | bytes 393216 | tf_op jit(solution)/shard_map/concatenate | solution.py:251
  11.3 0.7 %collective-permute-done.16.refs_6_ = bf16[128,256]{1,0:T(8,128)(2,1)S(1)} collective-permute-done((bf16[128,256]{1,0:T(8,128)(2,1)S(1)}, bf16[128,256]{1,0:T(8,128)(2,1)S(1)}, u32[]{:S(2)}, u32[]{:S(2)}) %collective-permute-start.16) | collective-permute-done | bytes 65568 | tf_op jit(solution)/shard_map/ppermute | solution.py:188
  12.5 2.5 %collective-permute-start.20 = (bf16[128,768]{1,0:T(8,128)(2,1)}, bf16[128,768]{1,0:T(8,128)(2,1)}, u32[]{:S(2)}, u32[]{:S(2)}) collective-permute-start(bf16[128,768]{1,0:T(8,128)(2,1)} %pad_maximum_fusion.refs_0_), channel_id=1, source_target_pairs={{0,24},{4,28},{8,16},{12,20},{16,8},{20,12},{24,0},{28,4},{1,25},{... | collective-permute-start | bytes 589832 | tf_op jit(solution)/shard_map/ppermute | solution.py:188
  16.0 0.7 %project_1.1 = bf16[256,768]{1,0:T(8,128)(2,1)S(1)} custom-call(bf16[1024,768]{1,0:T(8,128)(2,1)S(1)} %stage.1.noise_ref, bf16[128,256]{1,0:T(8,128)(2,1)S(1)} %get-tuple-element.78.refs_0_, bf16[128,256]{1,0:T(8,128)(2,1)S(1)} %collective-permute-done.12.refs_1_, bf16[128,256]{1,0:T(8,128)(2,1)S(1)} %collective-permute-done.13.refs_2_, ...), custom_call_target="tpu_custom_call" | custom-call | flops 402653184 | bytes 4194304 | tf_op jit(solution)/shard_map/project_1/pallas_call | solution.py:51
  16.7 2.7 %collective-permute-start.21 = (bf16[256,768]{1,0:T(8,128)(2,1)S(1)}, bf16[256,768]{1,0:T(8,128)(2,1)S(1)}, u32[]{:S(2)}, u32[]{:S(2)}) collective-permute-start(bf16[256,768]{1,0:T(8,128)(2,1)S(1)} %project_1.1), channel_id=1, source_target_pairs={{0,2},{1,3},{2,0},{3,1},{4,6},{5,7},{6,4},{7,5},{8,10},{9,11},{10,... | collective-permute-start | bytes 1179656 | tf_op jit(solution)/shard_map/ppermute | solution.py:233
  19.4 2.1 %collective-permute-done.20.refs_3_ = bf16[128,768]{1,0:T(8,128)(2,1)} collective-permute-done((bf16[128,768]{1,0:T(8,128)(2,1)}, bf16[128,768]{1,0:T(8,128)(2,1)}, u32[]{:S(2)}, u32[]{:S(2)}) %collective-permute-start.20) | collective-permute-done | bytes 196640 | tf_op jit(solution)/shard_map/ppermute | solution.py:188
  21.5 3.4 %collective-permute-done.19.refs_2_ = bf16[128,768]{1,0:T(8,128)(2,1)} collective-permute-done((bf16[128,768]{1,0:T(8,128)(2,1)}, bf16[128,768]{1,0:T(8,128)(2,1)}, u32[]{:S(2)}, u32[]{:S(2)}) %collective-permute-start.19) | collective-permute-done | bytes 196640 | tf_op jit(solution)/shard_map/ppermute | solution.py:188
  25.0 2.6 %conditional.2 = (bf16[128,768]{1,0:T(8,128)(2,1)}, bf16[128,768]{1,0:T(8,128)(2,1)}, bf16[128,768]{1,0:T(8,128)(2,1)}, bf16[128,768]{1,0:T(8,128)(2,1)}) conditional(s32[]{:T(128)} %convert_element_type.4, bf16[128,768]{1,0:T(8,128)(2,1)} %pad_maximum_fusion.refs_0_, (bf16[128,768]{1,0:T(8,128)(2,1)}, bf16[128,768]{1,0:T(8,128)(2,1)}, ...), branch_computations={%region_0.0_spmd, %region_1.0_spmd} | conditional | bytes 3145920 | solution.py:227
  26.1 0.8 %collective-permute-done = bf16[128,768]{1,0:T(8,128)(2,1)} collective-permute-done((bf16[128,768]{1,0:T(8,128)(2,1)}, bf16[128,768]{1,0:T(8,128)(2,1)}, u32[]{:S(2)}, u32[]{:S(2)}) %collective-permute-start) | collective-permute-done | bytes 196640 | tf_op jit(solution)/shard_map/cond/branch_1_fun/ppermute | solution.py:188
  27.7 3.0 %project_3.1 = (bf16[256,768]{1,0:T(8,128)(2,1)S(1)}, bf16[256,768]{1,0:T(8,128)(2,1)S(1)}, bf16[256,768]{1,0:T(8,128)(2,1)S(1)}) custom-call(bf16[1024,768]{1,0:T(8,128)(2,1)S(1)} %stage.1.noise_ref, bf16[128,768]{1,0:T(8,128)(2,1)} %pad_maximum_fusion.refs_0_, bf16[128,768]{1,0:T(8,128)(2,1)} %collective-permute-done.18.refs_1_, ...), custom_call_target="tpu_custom_call" | custom-call | flops 1207959552 | bytes 6291456 | tf_op jit(solution)/shard_map/project_3/pallas_call | solution.py:51
  30.7 0.7 %copy-done.2 = bf16[256,768]{1,0:T(8,128)(2,1)} copy-done((bf16[256,768]{1,0:T(8,128)(2,1)}, bf16[256,768]{1,0:T(8,128)(2,1)S(1)}, u32[]{:S(2)}) %copy-start.2) | copy-done | bytes 393240
  31.5 1.6 %collective-permute-start.22 = (bf16[256,768]{1,0:T(8,128)(2,1)S(1)}, bf16[256,768]{1,0:T(8,128)(2,1)S(1)}, u32[]{:S(2)}, u32[]{:S(2)}) collective-permute-start(bf16[256,768]{1,0:T(8,128)(2,1)S(1)} %get-tuple-element.75), channel_id=1, source_target_pairs={{0,1},{1,2},{2,3},{3,0},{4,5},{5,6},{6,7},{7,4},{8,9},{9,10},{10,1... | collective-permute-start | bytes 1179656 | tf_op jit(solution)/shard_map/ppermute | solution.py:233
  33.0 2.2 %collective-permute-start.23 = (bf16[256,768]{1,0:T(8,128)(2,1)S(1)}, bf16[256,768]{1,0:T(8,128)(2,1)S(1)}, u32[]{:S(2)}, u32[]{:S(2)}) collective-permute-start(bf16[256,768]{1,0:T(8,128)(2,1)S(1)} %get-tuple-element.76), channel_id=1, source_target_pairs={{0,3},{1,0},{2,1},{3,2},{4,7},{5,4},{6,5},{7,6},{8,11},{9,8},{10,9... | collective-permute-start | bytes 1179656 | tf_op jit(solution)/shard_map/ppermute | solution.py:233
  35.8 20.5 %conditional.3 = (bf16[128,1024]{1,0:T(8,128)(2,1)}, bf16[128,1024]{1,0:T(8,128)(2,1)}, bf16[128,1024]{1,0:T(8,128)(2,1)}, bf16[128,1024]{1,0:T(8,128)(2,1)}, bf...) conditional(s32[]{:T(128)} %convert_element_type.4, ...), branch_computations={%region_2.0_spmd, %region_3.0_spmd} | conditional | bytes 7340368 | solution.py:227
  35.8 1.5 %collective-permute-start.5 = (bf16[128,1024]{1,0:T(8,128)(2,1)}, bf16[128,1024]{1,0:T(8,128)(2,1)}, u32[]{:S(2)}, u32[]{:S(2)}) collective-permute-start(bf16[128,1024]{1,0:T(8,128)(2,1)} %param.3), channel_id=1, source_target_pairs={{0,16},{4,20},{8,24},{12,28},{16,0},{20,4},{24,8},{28,12},{1,17},{... | collective-permute-start | bytes 786440 | tf_op jit(solution)/shard_map/cond/branch_1_fun/ppermute | solution.py:188
  37.3 0.7 %collective-permute-start.4 = (bf16[128,1024]{1,0:T(8,128)(2,1)}, bf16[128,1024]{1,0:T(8,128)(2,1)}, u32[]{:S(2)}, u32[]{:S(2)}) collective-permute-start(bf16[128,1024]{1,0:T(8,128)(2,1)} %param.3), channel_id=1, source_target_pairs={{0,8},{4,12},{8,0},{12,4},{16,24},{20,28},{24,16},{28,20},{1,9},{5... | collective-permute-start | bytes 786440 | tf_op jit(solution)/shard_map/cond/branch_1_fun/ppermute | solution.py:188
  38.0 6.1 %collective-permute-done.5 = bf16[128,1024]{1,0:T(8,128)(2,1)} collective-permute-done((bf16[128,1024]{1,0:T(8,128)(2,1)}, bf16[128,1024]{1,0:T(8,128)(2,1)}, u32[]{:S(2)}, u32[]{:S(2)}) %collective-permute-start.5) | collective-permute-done | bytes 262176 | tf_op jit(solution)/shard_map/cond/branch_1_fun/ppermute | solution.py:188
  44.1 1.1 %collective-permute-done.4 = bf16[128,1024]{1,0:T(8,128)(2,1)} collective-permute-done((bf16[128,1024]{1,0:T(8,128)(2,1)}, bf16[128,1024]{1,0:T(8,128)(2,1)}, u32[]{:S(2)}, u32[]{:S(2)}) %collective-permute-start.4) | collective-permute-done | bytes 262176 | tf_op jit(solution)/shard_map/cond/branch_1_fun/ppermute | solution.py:188
  45.2 1.5 %collective-permute-start.6 = (bf16[128,1024]{1,0:T(8,128)(2,1)}, bf16[128,1024]{1,0:T(8,128)(2,1)}, u32[]{:S(2)}, u32[]{:S(2)}) collective-permute-start(bf16[128,1024]{1,0:T(8,128)(2,1)} %param.3), channel_id=1, source_target_pairs={{0,24},{4,28},{8,16},{12,20},{16,8},{20,12},{24,0},{28,4},{1,25},{... | collective-permute-start | bytes 786440 | tf_op jit(solution)/shard_map/cond/branch_1_fun/ppermute | solution.py:188
  46.8 7.3 %collective-permute-done.6 = bf16[128,1024]{1,0:T(8,128)(2,1)} collective-permute-done((bf16[128,1024]{1,0:T(8,128)(2,1)}, bf16[128,1024]{1,0:T(8,128)(2,1)}, u32[]{:S(2)}, u32[]{:S(2)}) %collective-permute-start.6) | collective-permute-done | bytes 262176 | tf_op jit(solution)/shard_map/cond/branch_1_fun/ppermute | solution.py:188
  54.0 0.5 collective-permute-start.9
  54.6 1.4 %collective-permute-done.10 = bf16[128,1024]{1,0:T(8,128)(2,1)} collective-permute-done((bf16[128,1024]{1,0:T(8,128)(2,1)}, bf16[128,1024]{1,0:T(8,128)(2,1)}, u32[]{:S(2)}, u32[]{:S(2)}) %collective-permute-start.10) | collective-permute-done | bytes 262176 | tf_op jit(solution)/shard_map/cond/branch_1_fun/ppermute | solution.py:188
  56.3 1.0 %copy-done.3 = bf16[256,768]{1,0:T(8,128)(2,1)S(1)} copy-done((bf16[256,768]{1,0:T(8,128)(2,1)S(1)}, bf16[256,768]{1,0:T(8,128)(2,1)}, u32[]{:S(2)}) %copy-start.3) | copy-done | bytes 393240
  57.3 2.6 %accumulate.1 = (bf16[1024,1024]{1,0:T(8,128)(2,1)S(1)}, f32[1024,768]{1,0:T(8,128)S(1)}) custom-call(s32[4,4]{1,0:T(4,128)S(1)} %copy-done.1, bf16[128,1024]{1,0:T(8,128)(2,1)} %bitcast.14, bf16[128,1024]{1,0:T(8,128)(2,1)} %get-tuple-element.66.refs_1_, bf16[128,1024]{1,0:T(8,128)(2,1)} %get-tuple-element.67.refs_2_, ...), custom_call_target="tpu_custom_call" | custom-call | flops 805306368 | bytes 5767168 | tf_op jit(solution)/shard_map/accumulate/pallas_call | solution.py:123
  60.0 3.1 %finish.1 = f32[1024,768]{1,0:T(8,128)} custom-call(s32[4,4]{1,0:T(4,128)S(1)} %copy-done.1, bf16[1024,1024]{1,0:T(8,128)(2,1)S(1)} %get-tuple-element.73.u_ref, f32[1024,768]{1,0:T(8,128)S(1)} %get-tuple-element.74.sum_ref, f32[1024,1]{1,0:T(8,128)S(1)} %copy.7.skew_ref, f32[1024,1]{1,0:T(8,128)S(1)} %copy.8.tail_ref, ...), custom_call_target="tpu_custom_call" | custom-call | flops 805306368 | bytes 12058624 | tf_op jit(solution)/shard_map/finish/pallas_call | solution.py:167
  (40 shorter events, 5.4 us)
Async XLA Ops:
  1.0 10.4 %collective-permute-start.14 = (bf16[128,256]{1,0:T(8,128)(2,1)S(1)}, bf16[128,256]{1,0:T(8,128)(2,1)S(1)}, u32[]{:S(2)}, u32[]{:S(2)}) collective-permute-start(bf16[128,256]{1,0:T(8,128)(2,1)S(1)} %get-tuple-element.78.refs_0_), channel_id=1, source_target_pairs={{0,4},{4,0},{8,12},{12,8},{16,20},{20,16},{24,28},{28,24},{1,5},{5... | collective-permute-start | bytes 196616 | tf_op jit(solution)/shard_map/ppermute | solution.py:188
  1.5 9.3 %collective-permute-start.13 = (bf16[128,256]{1,0:T(8,128)(2,1)S(1)}, bf16[128,256]{1,0:T(8,128)(2,1)S(1)}, u32[]{:S(2)}, u32[]{:S(2)}) collective-permute-start(bf16[128,256]{1,0:T(8,128)(2,1)S(1)} %get-tuple-element.78.refs_0_), channel_id=1, source_target_pairs={{0,16},{4,20},{8,24},{12,28},{16,0},{20,4},{24,8},{28,12},{1,17},{... | collective-permute-start | bytes 196616 | tf_op jit(solution)/shard_map/ppermute | solution.py:188
  4.1 6.7 %collective-permute-start.12 = (bf16[128,256]{1,0:T(8,128)(2,1)S(1)}, bf16[128,256]{1,0:T(8,128)(2,1)S(1)}, u32[]{:S(2)}, u32[]{:S(2)}) collective-permute-start(bf16[128,256]{1,0:T(8,128)(2,1)S(1)} %get-tuple-element.78.refs_0_), channel_id=1, source_target_pairs={{0,8},{4,12},{8,0},{12,4},{16,24},{20,28},{24,16},{28,20},{1,9},{5... | collective-permute-start | bytes 196616 | tf_op jit(solution)/shard_map/ppermute | solution.py:188
  5.6 5.2 %collective-permute-start.11 = (bf16[128,256]{1,0:T(8,128)(2,1)S(1)}, bf16[128,256]{1,0:T(8,128)(2,1)S(1)}, u32[]{:S(2)}, u32[]{:S(2)}) collective-permute-start(bf16[128,256]{1,0:T(8,128)(2,1)S(1)} %get-tuple-element.78.refs_0_), channel_id=1, source_target_pairs={{0,24},{4,28},{8,16},{12,20},{16,8},{20,12},{24,0},{28,4},{1,25},{... | collective-permute-start | bytes 196616 | tf_op jit(solution)/shard_map/ppermute | solution.py:188
  6.8 1.4 %copy-start = (bf16[1024,768]{1,0:T(8,128)(2,1)S(1)}, bf16[1024,768]{1,0:T(8,128)(2,1)}, u32[]{:S(2)}) copy-start(bf16[1024,768]{1,0:T(8,128)(2,1)} %from_ref.1) | copy-start | bytes 4718596
  10.7 1.3 %collective-permute-start.16 = (bf16[128,256]{1,0:T(8,128)(2,1)S(1)}, bf16[128,256]{1,0:T(8,128)(2,1)S(1)}, u32[]{:S(2)}, u32[]{:S(2)}) collective-permute-start(bf16[128,256]{1,0:T(8,128)(2,1)S(1)} %collective-permute-done.13.refs_2_), channel_id=1, source_target_pairs={{0,4},{4,0},{8,12},{12,8},{16,20},{20,16},{24,28},{28,24},{1,5},{5... | collective-permute-start | bytes 196616 | tf_op jit(solution)/shard_map/ppermute | solution.py:188
  10.7 1.4 %collective-permute-start.15 = (bf16[128,256]{1,0:T(8,128)(2,1)S(1)}, bf16[128,256]{1,0:T(8,128)(2,1)S(1)}, u32[]{:S(2)}, u32[]{:S(2)}) collective-permute-start(bf16[128,256]{1,0:T(8,128)(2,1)S(1)} %collective-permute-done.12.refs_1_), channel_id=1, source_target_pairs={{0,4},{4,0},{8,12},{12,8},{16,20},{20,16},{24,28},{28,24},{1,5},{5... | collective-permute-start | bytes 196616 | tf_op jit(solution)/shard_map/ppermute | solution.py:188
  11.2 1.3 %collective-permute-start.17 = (bf16[128,256]{1,0:T(8,128)(2,1)S(1)}, bf16[128,256]{1,0:T(8,128)(2,1)S(1)}, u32[]{:S(2)}, u32[]{:S(2)}) collective-permute-start(bf16[128,256]{1,0:T(8,128)(2,1)S(1)} %collective-permute-done.11.refs_3_), channel_id=1, source_target_pairs={{0,4},{4,0},{8,12},{12,8},{16,20},{20,16},{24,28},{28,24},{1,5},{5... | collective-permute-start | bytes 196616 | tf_op jit(solution)/shard_map/ppermute | solution.py:188
  12.5 9.0 %collective-permute-start.20 = (bf16[128,768]{1,0:T(8,128)(2,1)}, bf16[128,768]{1,0:T(8,128)(2,1)}, u32[]{:S(2)}, u32[]{:S(2)}) collective-permute-start(bf16[128,768]{1,0:T(8,128)(2,1)} %pad_maximum_fusion.refs_0_), channel_id=1, source_target_pairs={{0,24},{4,28},{8,16},{12,20},{16,8},{20,12},{24,0},{28,4},{1,25},{... | collective-permute-start | bytes 589832 | tf_op jit(solution)/shard_map/ppermute | solution.py:188
  15.0 9.9 %collective-permute-start.19 = (bf16[128,768]{1,0:T(8,128)(2,1)}, bf16[128,768]{1,0:T(8,128)(2,1)}, u32[]{:S(2)}, u32[]{:S(2)}) collective-permute-start(bf16[128,768]{1,0:T(8,128)(2,1)} %pad_maximum_fusion.refs_0_), channel_id=1, source_target_pairs={{0,16},{4,20},{8,24},{12,28},{16,0},{20,4},{24,8},{28,12},{1,17},{... | collective-permute-start | bytes 589832 | tf_op jit(solution)/shard_map/ppermute | solution.py:188
  15.5 9.5 %collective-permute-start.18 = (bf16[128,768]{1,0:T(8,128)(2,1)}, bf16[128,768]{1,0:T(8,128)(2,1)}, u32[]{:S(2)}, u32[]{:S(2)}) collective-permute-start(bf16[128,768]{1,0:T(8,128)(2,1)} %pad_maximum_fusion.refs_0_), channel_id=1, source_target_pairs={{0,8},{4,12},{8,0},{12,4},{16,24},{20,28},{24,16},{28,20},{1,9},{5... | collective-permute-start | bytes 589832 | tf_op jit(solution)/shard_map/ppermute | solution.py:188
  16.7 39.6 %collective-permute-start.21 = (bf16[256,768]{1,0:T(8,128)(2,1)S(1)}, bf16[256,768]{1,0:T(8,128)(2,1)S(1)}, u32[]{:S(2)}, u32[]{:S(2)}) collective-permute-start(bf16[256,768]{1,0:T(8,128)(2,1)S(1)} %project_1.1), channel_id=1, source_target_pairs={{0,2},{1,3},{2,0},{3,1},{4,6},{5,7},{6,4},{7,5},{8,10},{9,11},{10,... | collective-permute-start | bytes 1179656 | tf_op jit(solution)/shard_map/ppermute | solution.py:233
  25.0 1.8 %collective-permute-start = (bf16[128,768]{1,0:T(8,128)(2,1)}, bf16[128,768]{1,0:T(8,128)(2,1)}, u32[]{:S(2)}, u32[]{:S(2)}) collective-permute-start(bf16[128,768]{1,0:T(8,128)(2,1)} %get-tuple-element.16), channel_id=1, source_target_pairs={{0,4},{4,0},{8,12},{12,8},{16,20},{20,16},{24,28},{28,24},{1,5},{5... | collective-permute-start | bytes 589832 | tf_op jit(solution)/shard_map/cond/branch_1_fun/ppermute | solution.py:188
  25.0 2.1 %collective-permute-start.1 = (bf16[128,768]{1,0:T(8,128)(2,1)}, bf16[128,768]{1,0:T(8,128)(2,1)}, u32[]{:S(2)}, u32[]{:S(2)}) collective-permute-start(bf16[128,768]{1,0:T(8,128)(2,1)} %get-tuple-element.17), channel_id=1, source_target_pairs={{0,4},{4,0},{8,12},{12,8},{16,20},{20,16},{24,28},{28,24},{1,5},{5... | collective-permute-start | bytes 589832 | tf_op jit(solution)/shard_map/cond/branch_1_fun/ppermute | solution.py:188
  25.6 1.8 %collective-permute-start.2 = (bf16[128,768]{1,0:T(8,128)(2,1)}, bf16[128,768]{1,0:T(8,128)(2,1)}, u32[]{:S(2)}, u32[]{:S(2)}) collective-permute-start(bf16[128,768]{1,0:T(8,128)(2,1)} %get-tuple-element.18), channel_id=1, source_target_pairs={{0,4},{4,0},{8,12},{12,8},{16,20},{20,16},{24,28},{28,24},{1,5},{5... | collective-permute-start | bytes 589832 | tf_op jit(solution)/shard_map/cond/branch_1_fun/ppermute | solution.py:188
  25.6 2.1 %collective-permute-start.3 = (bf16[128,768]{1,0:T(8,128)(2,1)}, bf16[128,768]{1,0:T(8,128)(2,1)}, u32[]{:S(2)}, u32[]{:S(2)}) collective-permute-start(bf16[128,768]{1,0:T(8,128)(2,1)} %get-tuple-element.19), channel_id=1, source_target_pairs={{0,4},{4,0},{8,12},{12,8},{16,20},{20,16},{24,28},{28,24},{1,5},{5... | collective-permute-start | bytes 589832 | tf_op jit(solution)/shard_map/cond/branch_1_fun/ppermute | solution.py:188
  27.7 7.6 %copy-start.5 = (f32[1024]{0:T(1024)S(1)}, f32[1024]{0:T(1024)}, u32[]{:S(2)}) copy-start(f32[1024]{0:T(1024)} %param.14) | copy-start | bytes 12292
  27.7 7.8 %copy-start.6 = (f32[1024]{0:T(1024)S(1)}, f32[1024]{0:T(1024)}, u32[]{:S(2)}) copy-start(f32[1024]{0:T(1024)} %param.15) | copy-start | bytes 12292
  30.7 0.7 %copy-start.2 = (bf16[256,768]{1,0:T(8,128)(2,1)}, bf16[256,768]{1,0:T(8,128)(2,1)S(1)}, u32[]{:S(2)}) copy-start(bf16[256,768]{1,0:T(8,128)(2,1)S(1)} %get-tuple-element.64.refs_8_) | copy-start | bytes 1179652
  31.5 28.5 %collective-permute-start.22 = (bf16[256,768]{1,0:T(8,128)(2,1)S(1)}, bf16[256,768]{1,0:T(8,128)(2,1)S(1)}, u32[]{:S(2)}, u32[]{:S(2)}) collective-permute-start(bf16[256,768]{1,0:T(8,128)(2,1)S(1)} %get-tuple-element.75), channel_id=1, source_target_pairs={{0,1},{1,2},{2,3},{3,0},{4,5},{5,6},{6,7},{7,4},{8,9},{9,10},{10,1... | collective-permute-start | bytes 1179656 | tf_op jit(solution)/shard_map/ppermute | solution.py:233
  33.0 26.9 %collective-permute-start.23 = (bf16[256,768]{1,0:T(8,128)(2,1)S(1)}, bf16[256,768]{1,0:T(8,128)(2,1)S(1)}, u32[]{:S(2)}, u32[]{:S(2)}) collective-permute-start(bf16[256,768]{1,0:T(8,128)(2,1)S(1)} %get-tuple-element.76), channel_id=1, source_target_pairs={{0,3},{1,0},{2,1},{3,2},{4,7},{5,4},{6,5},{7,6},{8,11},{9,8},{10,9... | collective-permute-start | bytes 1179656 | tf_op jit(solution)/shard_map/ppermute | solution.py:233
  35.5 20.8 %copy-start.1 = (s32[4,4]{1,0:T(4,128)S(1)}, s32[4,4]{1,0:T(4,128)}, u32[]{:S(2)}) copy-start(s32[4,4]{1,0:T(4,128)} %ranks_ref.3) | copy-start | bytes 196
  35.8 8.3 %collective-permute-start.5 = (bf16[128,1024]{1,0:T(8,128)(2,1)}, bf16[128,1024]{1,0:T(8,128)(2,1)}, u32[]{:S(2)}, u32[]{:S(2)}) collective-permute-start(bf16[128,1024]{1,0:T(8,128)(2,1)} %param.3), channel_id=1, source_target_pairs={{0,16},{4,20},{8,24},{12,28},{16,0},{20,4},{24,8},{28,12},{1,17},{... | collective-permute-start | bytes 786440 | tf_op jit(solution)/shard_map/cond/branch_1_fun/ppermute | solution.py:188
  37.3 8.0 %collective-permute-start.4 = (bf16[128,1024]{1,0:T(8,128)(2,1)}, bf16[128,1024]{1,0:T(8,128)(2,1)}, u32[]{:S(2)}, u32[]{:S(2)}) collective-permute-start(bf16[128,1024]{1,0:T(8,128)(2,1)} %param.3), channel_id=1, source_target_pairs={{0,8},{4,12},{8,0},{12,4},{16,24},{20,28},{24,16},{28,20},{1,9},{5... | collective-permute-start | bytes 786440 | tf_op jit(solution)/shard_map/cond/branch_1_fun/ppermute | solution.py:188
  44.1 2.7 %collective-permute-start.7 = (bf16[128,1024]{1,0:T(8,128)(2,1)}, bf16[128,1024]{1,0:T(8,128)(2,1)}, u32[]{:S(2)}, u32[]{:S(2)}) collective-permute-start(bf16[128,1024]{1,0:T(8,128)(2,1)} %param.3), channel_id=1, source_target_pairs={{0,4},{4,0},{8,12},{12,8},{16,20},{20,16},{24,28},{28,24},{1,5},{5... | collective-permute-start | bytes 786440 | tf_op jit(solution)/shard_map/cond/branch_1_fun/ppermute | solution.py:188
  45.2 8.8 %collective-permute-start.6 = (bf16[128,1024]{1,0:T(8,128)(2,1)}, bf16[128,1024]{1,0:T(8,128)(2,1)}, u32[]{:S(2)}, u32[]{:S(2)}) collective-permute-start(bf16[128,1024]{1,0:T(8,128)(2,1)} %param.3), channel_id=1, source_target_pairs={{0,24},{4,28},{8,16},{12,20},{16,8},{20,12},{24,0},{28,4},{1,25},{... | collective-permute-start | bytes 786440 | tf_op jit(solution)/shard_map/cond/branch_1_fun/ppermute | solution.py:188
  46.8 7.3 %collective-permute-start.8 = (bf16[128,1024]{1,0:T(8,128)(2,1)}, bf16[128,1024]{1,0:T(8,128)(2,1)}, u32[]{:S(2)}, u32[]{:S(2)}) collective-permute-start(bf16[128,1024]{1,0:T(8,128)(2,1)} %collective-permute-done.4), channel_id=1, source_target_pairs={{0,4},{4,0},{8,12},{12,8},{16,20},{20,16},{24,28},{28,24},{1,5},{5... | collective-permute-start | bytes 786440 | tf_op jit(solution)/shard_map/cond/branch_1_fun/ppermute | solution.py:188
  54.0 1.9 %collective-permute-start.10 = (bf16[128,1024]{1,0:T(8,128)(2,1)}, bf16[128,1024]{1,0:T(8,128)(2,1)}, u32[]{:S(2)}, u32[]{:S(2)}) collective-permute-start(bf16[128,1024]{1,0:T(8,128)(2,1)} %collective-permute-done.6), channel_id=1, source_target_pairs={{0,4},{4,0},{8,12},{12,8},{16,20},{20,16},{24,28},{28,24},{1,5},{5... | collective-permute-start | bytes 786440 | tf_op jit(solution)/shard_map/cond/branch_1_fun/ppermute | solution.py:188
  54.0 2.2 %collective-permute-start.9 = (bf16[128,1024]{1,0:T(8,128)(2,1)}, bf16[128,1024]{1,0:T(8,128)(2,1)}, u32[]{:S(2)}, u32[]{:S(2)}) collective-permute-start(bf16[128,1024]{1,0:T(8,128)(2,1)} %collective-permute-done.5), channel_id=1, source_target_pairs={{0,4},{4,0},{8,12},{12,8},{16,20},{20,16},{24,28},{28,24},{1,5},{5... | collective-permute-start | bytes 786440 | tf_op jit(solution)/shard_map/cond/branch_1_fun/ppermute | solution.py:188
  56.3 1.0 %copy-start.3 = (bf16[256,768]{1,0:T(8,128)(2,1)S(1)}, bf16[256,768]{1,0:T(8,128)(2,1)}, u32[]{:S(2)}) copy-start(bf16[256,768]{1,0:T(8,128)(2,1)} %copy-done.2) | copy-start | bytes 1179652

commit v6 on v5

--- a/solution.py
+++ b/solution.py
@@ -99,39 +99,42 @@
     return jnp.where(alive, coef.astype(jnp.float32), 0.0).astype(coef.dtype)
 
 
-def accumulate_kernel(shifts, places, rows, ranks_ref, *refs):
+def accumulate_kernel(shifts, places, rows, ranks_ref, noise_ref, *refs):
     pieces, coefs = refs[: len(places)], refs[len(places) : len(places) + len(shifts)]
-    u_ref, sum_ref = refs[-2:]
-    stack_pieces(places, rows, pieces, u_ref)
+    u_ref, sum_ref, whole = refs[-3:]
+    stack_pieces(places, rows, pieces, whole)
+    per_source = whole.shape[1] - u_ref.shape[1]
+    u_ref[...] = whole[:, per_source:]
+    own = project_columns(whole[:, :per_source], noise_ref)
     total = jnp.zeros(sum_ref.shape, jnp.float32)
-    for shift, coef_ref in zip(shifts, coefs):
-        per_source = coef_ref.shape[0]
+    for shift, coef in zip((0,) + shifts, [own] + [coef_ref[...] for coef_ref in coefs]):
         start = pl.multiple_of(source_of(shift) * per_source, per_source)
         total += jnp.dot(
             u_ref[:, pl.ds(start, per_source)],
-            alive_coef(shift, ranks_ref, coef_ref[...]),
+            alive_coef(shift, ranks_ref, coef),
             preferred_element_type=jnp.float32,
         )
     sum_ref[...] = total
 
 
-def accumulate(shifts, ranks, gathered, coefs):
+def accumulate(shifts, ranks, noise, gathered, coefs):
     places, pieces = zip(*gathered)
     rows, columns = pieces[0].shape
-    sites = rows * lax.axis_size("real")
-    per_source, reals = coefs[0].shape
+    sites, reals = noise.shape
+    per_source = coefs[0].shape[0]
     return pl.pallas_call(
         functools.partial(accumulate_kernel, shifts, places, rows),
         out_shape=[
-            jax.ShapeDtypeStruct((sites, columns), jnp.bfloat16),
+            jax.ShapeDtypeStruct((sites, columns - per_source), jnp.bfloat16),
             jax.ShapeDtypeStruct((sites, reals), jnp.float32),
         ],
-        in_specs=[SMEM] + [VMEM] * (len(pieces) + len(coefs)),
+        in_specs=[SMEM] + [VMEM] * (1 + len(pieces) + len(coefs)),
         out_specs=[VMEM] * 2,
+        scratch_shapes=[pltpu.VMEM((sites, columns), jnp.bfloat16)],
         compiler_params=LIMIT,
-        cost_estimate=cost(2 * sites * len(coefs) * per_source * reals, *pieces, *coefs),
+        cost_estimate=cost(6 * sites * per_source * reals, noise, *pieces, *coefs),
         name="accumulate",
-    )(ranks, *pieces, *coefs)
+    )(ranks, noise, *pieces, *coefs)
 
 
 def finish_kernel(shifts, ranks_ref, u_ref, sum_ref, skew_ref, tail_ref, *refs):
@@ -203,29 +206,46 @@
     return pieces
 
 
-def two_at_a_time(own):
-    distances = range(2, lax.axis_size("real"), 2)
-    pieces, tails = {(0, 0): own}, [own, own]
+def neighbour_distances():
+    return (2, 4) if lax.axis_size("real") == 8 else ()
+
+
+def chunk_and_neighbours(chunk, later):
+    pieces, tail = from_chips(chunk), chunk
+    for distance, _ in list(pieces):
+        tail = pieces[distance ^ 1, 0] = swap(after(pieces[distance, 0], tail), 1)
+    near = {}
+    for distance in neighbour_distances():
+        near[distance, 0] = swap(after(later, pieces[distance, 0]), distance)
+    return {place: pieces[place] for place in pieces if place != (0, 0)}, near
+
+
+def two_at_a_time(pieces):
+    known, pieces = pieces, dict(pieces)
+    own = pieces[0, 0]
+    distances = [d for d in range(2, lax.axis_size("real"), 2) if (d, 0) not in pieces]
+    tails = [own, own]
     for turn, distance in enumerate(distances):
         tails[turn % 2] = pieces[distance, 0] = swap(after(own, tails[turn % 2]), distance)
     last, tail = distances[-1], tails[len(distances) % 2]
-    for distance in (0, *distances[:-1]):
-        tail = pieces[distance ^ 1, 0] = swap(after(pieces[distance, 0], tail), 1)
+    for distance in range(0, lax.axis_size("real"), 2):
+        if distance != last:
+            tail = pieces[distance ^ 1, 0] = swap(after(pieces[distance, 0], tail), 1)
     pieces[last ^ 1, 0] = swap(pieces[last, 0], 1)
-    return pieces
-
-
-def at_once(present, gather, pieces):
-    places, arrays, new = list(pieces), list(pieces.values()), []
-
-    def added(*arrays):
-        more = gather(dict(zip(places, arrays)))
-        new[:] = [place for place in more if place not in pieces]
-        return [more[place] for place in new]
-
-    count = len(jax.eval_shape(added, *arrays))
-    results = lax.cond(present, added, lambda *same: [same[0]] * count, *arrays)
-    return {**pieces, **dict(zip(new, results))}
+    return {place: pieces[place] for place in pieces if place not in known}
+
+
+def at_once(present, gather, *args):
+    shapes, tree = [], []
+
+    def flat(*args):
+        leaves, structure = jax.tree.flatten(gather(*args))
+        tree[:] = [structure]
+        return leaves
+
+    shapes = jax.eval_shape(flat, *args)
+    nothing = lambda *_: [jnp.zeros(leaf.shape, leaf.dtype) for leaf in shapes]
+    return jax.tree.unflatten(tree[0], lax.cond(present, flat, nothing, *args))
 
 
 def along_site(coef, shift):
@@ -248,25 +268,22 @@
         return lax.dynamic_slice(v_factors[0], (0, start), (rows, per_dest))
 
     v_first = columns_for(first)
-    v_rest = jnp.concatenate([columns_for(shift) for shift in rest + (0,)], axis=1)
-    present = ranks[0, 0] > 0
+    v_rest = jnp.concatenate([columns_for(shift) for shift in rest], axis=1)
+    own_and_u = jnp.concatenate([columns_for(0), u_factors[0]], axis=1)
     v_first = from_chips(v_first)
     last = max(v_first)
-    waiting = (v_first[last], stage(noise), v_rest, present)
-    v_first[last], noise, v_rest, present = lax.optimization_barrier(waiting)
-    v_first = with_other_core(v_first)
-    v_rest = from_chips(after(v_rest, *v_first.values()))
-    [far] = project(1, noise, v_first.items())
-
-    v_rest = at_once(present, with_other_core, after(v_rest, far))
-    *others, own = project(len(rest) + 1, noise, v_rest.items())
+    waiting = (v_first[last], stage(noise), v_rest, own_and_u)
+    v_first[last], noise, v_rest, own_and_u = lax.optimization_barrier(waiting)
+    present = ranks[0, 0] > 0
+    [far] = project(1, noise, with_other_core(v_first).items())
+    v_rest = after(v_rest, far)
+    v_pieces, u_pieces = at_once(present, chunk_and_neighbours, v_rest, own_and_u)
+    others = project(len(rest), noise, {(0, 0): v_rest, **v_pieces}.items())
     far = along_site(far, first)
+    u_pieces = after({(0, 0): own_and_u, **u_pieces}, others[0])
+    u_pieces.update(at_once(present, two_at_a_time, u_pieces))
     others = [along_site(coef, shift) for coef, shift in zip(others, rest)]
-
-    u_pieces = at_once(
-        present, lambda pieces: two_at_a_time(pieces[0, 0]), {(0, 0): after(u_factors[0], own)}
-    )
-    u_whole, total = accumulate((0, first), ranks, u_pieces.items(), [own, far])
+    u_whole, total = accumulate((first,), ranks, noise, u_pieces.items(), [far])
     return finish(rest, ranks, u_whole, total, skew_g[:, None], tail_h[:, None], others)
 
 

time: 63.4 us -> 65.2 us (1.028)
  waiting for transfers between devices: 25.1 us -> 28.6 us
  local copies, waits for them, and re-layouts: 5.74 us -> 3.35 us
  Pallas kernels: 10.2 us -> 12.1 us
  other arithmetic: 0.69 us -> 0.03 us
    ppermute x21, waiting for transfers between devices: 25.1 us -> 28.6 us  [swap(): lax.ppermute(array, 'real', [(k, k ^ distance) for k in range(count)])]
    unnamed x12, local copies, waits for them, and re-layouts: 3.16 us -> 1.43 us
    pallas_call x1, Pallas kernels: 2.63 us -> 3.51 us  [accumulate(): pl.pallas_call(functools.partial(accumulate_kernel, shifts, places, rows)...]
    pallas_call x2, Pallas kernels: 3.68 us -> 4.54 us  [project(): pl.pallas_call(functools.partial(project_kernel, places, rows), out_shape...]
    slice x1, local copies, waits for them, and re-layouts: 1.19 us -> 0.48 us  [per_device(): present = ranks[0, 0] > 0]
    concatenate x1 -> x2, other arithmetic: 0.69 us -> 0.03 us  [the longest x1 0.02 us: per_device(): own_and_u = jnp.concatenate([columns_for(0), u_factors[0]], axis=1)]
  transfers between devices with their start and end apart: 24 -> 24, of which waited for: 16 -> 12; matrix products, arithmetic and copies ran while one was open for 4% -> 1% of each run, Pallas kernels for 11% -> 11%
where the time goes in v6:
time: 65.2 us; the launch traced here: 64.9 us
  waiting for transfers between devices  28.6 us (44%)
  starting transfers between devices  20.1 us (31%)
  Pallas kernels  12.1 us (19%)
  local copies, waits for them, and re-layouts  3.35 us (5%)
  between operations  0.7 us (1%)
    ppermute x21, waiting for transfers between devices, swap(): lax.ppermute(array, 'real', [(k, k ^ distance) for k in range(count)])  28.6 us
    ppermute x21, starting transfers between devices, swap(): lax.ppermute(array, 'real', [(k, k ^ distance) for k in range(count)])  13.7 us
    ppermute x3, starting transfers between devices, along_site(): lax.ppermute(coef, 'site', [(k, (k + shift) % count) for k in range(count)])  6.41 us
    pallas_call x2, Pallas kernels, project(): pl.pallas_call(functools.partial(project_kernel, places, rows), out_shape...  4.54 us
    pallas_call x1, Pallas kernels, accumulate(): pl.pallas_call(functools.partial(accumulate_kernel, shifts, places, rows)...  3.51 us
    pallas_call x1, Pallas kernels, finish(): pl.pallas_call(functools.partial(finish_kernel, shifts), out_shape=jax.Sh...  3.25 us
    unnamed x12, local copies, waits for them, and re-layouts  1.43 us
  transfers between devices with their start and end apart: 24, of which 12 were waited for; matrix products, arithmetic and copies ran while one was open for 1% of the time, Pallas kernels for 11%

profile of v6, /device:TPU:0, one launch (start us, length us, event | category | flops | bytes accessed | tf_op | source)
XLA Modules:
  0.0 64.9 jit_solution(1055013015378853041)
XLA Ops:
  0.0 1.0 %dynamic-slice_bitcast_fusion = (bf16[128,256]{1,0:T(8,128)(2,1)S(1)}, bf16[128,256]{1,0:T(8,128)(2,1)S(1)}, bf16[128,256]{1,0:T(8,128)(2,1)S(1)}, bf16[128,256]{1,0:T(8,128)(2,1)S(1)}) fusion(bf16[1,128,1024]{2,1,0:T(8,128)(2,1)} %param.11, s32[]{:T(128)S(6)} %select_n.15, s32[]{:T(128)S(6)} %select_n.13, s32[]{:T(128)S(6)} %select_n.12, s32[]{:T(128)S(6)} %select_n.14), kind=kLoop, calls=%fused_computation.2 | loop fusion | bytes 524304 | tf_op jit(solution)/shard_map/dynamic_slice | solution.py:268
  1.0 4.0 %collective-permute-start.14 = (bf16[128,256]{1,0:T(8,128)(2,1)S(1)}, bf16[128,256]{1,0:T(8,128)(2,1)S(1)}, u32[]{:S(2)}, u32[]{:S(2)}) collective-permute-start(bf16[128,256]{1,0:T(8,128)(2,1)S(1)} %get-tuple-element.82.refs_0_), channel_id=1, source_target_pairs={{0,24},{4,28},{8,16},{12,20},{16,8},{20,12},{24,0},{28,4},{1,25},{... | collective-permute-start | bytes 196616 | tf_op jit(solution)/shard_map/ppermute | solution.py:191
  5.0 0.5 collective-permute-start.15
  5.6 1.4 %copy-done = bf16[1024,768]{1,0:T(8,128)(2,1)S(1)} copy-done((bf16[1024,768]{1,0:T(8,128)(2,1)S(1)}, bf16[1024,768]{1,0:T(8,128)(2,1)}, u32[]{:S(2)}) %copy-start) | copy-done | bytes 1572888
  7.0 0.8 %stage.1.noise_ref = bf16[1024,768]{1,0:T(8,128)(2,1)S(1)} custom-call(bf16[1024,768]{1,0:T(8,128)(2,1)S(1)} %copy-done), custom_call_target="tpu_custom_call" | custom-call | bytes 3145728 | tf_op jit(solution)/shard_map/stage/pallas_call | solution.py:78
  7.9 0.6 collective-permute-start.20
  8.5 0.8 %collective-permute-done.15.refs_1_ = bf16[128,256]{1,0:T(8,128)(2,1)S(1)} collective-permute-done((bf16[128,256]{1,0:T(8,128)(2,1)S(1)}, bf16[128,256]{1,0:T(8,128)(2,1)S(1)}, u32[]{:S(2)}, u32[]{:S(2)}) %collective-permute-start.15) | collective-permute-done | bytes 65568 | tf_op jit(solution)/shard_map/ppermute | solution.py:191
  9.2 0.5 collective-permute-done.16.refs_2_
  9.8 0.7 %collective-permute-done.18.refs_5_ = bf16[128,256]{1,0:T(8,128)(2,1)S(1)} collective-permute-done((bf16[128,256]{1,0:T(8,128)(2,1)S(1)}, bf16[128,256]{1,0:T(8,128)(2,1)S(1)}, u32[]{:S(2)}, u32[]{:S(2)}) %collective-permute-start.18) | collective-permute-done | bytes 65568 | tf_op jit(solution)/shard_map/ppermute | solution.py:191
  10.5 0.5 collective-permute-done.19.refs_6_
  11.0 1.4 %project_1.1 = bf16[256,768]{1,0:T(8,128)(2,1)} custom-call(bf16[1024,768]{1,0:T(8,128)(2,1)S(1)} %stage.1.noise_ref, bf16[128,256]{1,0:T(8,128)(2,1)S(1)} %get-tuple-element.82.refs_0_, bf16[128,256]{1,0:T(8,128)(2,1)S(1)} %collective-permute-done.15.refs_1_, bf16[128,256]{1,0:T(8,128)(2,1)S(1)} %collective-permute-done.16.refs_2_, ...), custom_call_target="tpu_custom_call" | custom-call | flops 402653184 | bytes 4194304 | tf_op jit(solution)/shard_map/project_1/pallas_call | solution.py:51
  12.4 2.6 %collective-permute-start.21 = (bf16[256,768]{1,0:T(8,128)(2,1)}, bf16[256,768]{1,0:T(8,128)(2,1)}, u32[]{:S(2)}, u32[]{:S(2)}) collective-permute-start(bf16[256,768]{1,0:T(8,128)(2,1)} %project_1.1), channel_id=1, source_target_pairs={{0,2},{1,3},{2,0},{3,1},{4,6},{5,7},{6,4},{7,5},{8,10},{9,11},{10,... | collective-permute-start | bytes 1179656 | tf_op jit(solution)/shard_map/ppermute | solution.py:253
  16.1 20.7 %conditional.2 = (bf16[128,512]{1,0:T(8,128)(2,1)}, bf16[128,512]{1,0:T(8,128)(2,1)}, bf16[128,512]{1,0:T(8,128)(2,1)}, bf16[128,512]{1,0:T(8,128)(2,1)}, bf16[1...) conditional(s32[]{:T(128)} %bitcast.5, () %tuple.34, ...), branch_computations={%region_0.0_spmd, %region_1.0_spmd} | conditional | bytes 6291888 | solution.py:248
  16.1 1.6 %collective-permute-start.1 = (bf16[128,512]{1,0:T(8,128)(2,1)S(1)}, bf16[128,512]{1,0:T(8,128)(2,1)}, u32[]{:S(2)}, u32[]{:S(2)}) collective-permute-start(bf16[128,512]{1,0:T(8,128)(2,1)S(1)} %get-tuple-element.16), channel_id=1, source_target_pairs={{0,8},{4,12},{8,0},{12,4},{16,24},{20,28},{24,16},{28,20},{1,9},{5... | collective-permute-start | bytes 393224 | tf_op jit(solution)/shard_map/cond/branch_1_fun/ppermute | solution.py:191
  17.7 0.8 %collective-permute-start.3 = (bf16[128,512]{1,0:T(8,128)(2,1)S(1)}, bf16[128,512]{1,0:T(8,128)(2,1)}, u32[]{:S(2)}, u32[]{:S(2)}) collective-permute-start(bf16[128,512]{1,0:T(8,128)(2,1)S(1)} %get-tuple-element.16), channel_id=1, source_target_pairs={{0,16},{4,20},{8,24},{12,28},{16,0},{20,4},{24,8},{28,12},{1,17},{... | collective-permute-start | bytes 393224 | tf_op jit(solution)/shard_map/cond/branch_1_fun/ppermute | solution.py:191
  18.5 3.1 %collective-permute-done.1 = bf16[128,512]{1,0:T(8,128)(2,1)} collective-permute-done((bf16[128,512]{1,0:T(8,128)(2,1)S(1)}, bf16[128,512]{1,0:T(8,128)(2,1)}, u32[]{:S(2)}, u32[]{:S(2)}) %collective-permute-start.1) | collective-permute-done | bytes 131104 | tf_op jit(solution)/shard_map/cond/branch_1_fun/ppermute | solution.py:191
  21.6 1.5 %collective-permute-start.7 = (bf16[128,1280]{1,0:T(8,128)(2,1)S(1)}, bf16[128,1280]{1,0:T(8,128)(2,1)}, u32[]{:S(2)}, u32[]{:S(2)}) collective-permute-start(bf16[128,1280]{1,0:T(8,128)(2,1)S(1)} %get-tuple-element.22), channel_id=1, source_target_pairs={{0,8},{4,12},{8,0},{12,4},{16,24},{20,28},{24,16},{28,20},{1,9},{5... | collective-permute-start | bytes 983048 | tf_op jit(solution)/shard_map/cond/branch_1_fun/ppermute | solution.py:191
  23.1 0.6 collective-permute-done.3
  23.7 0.8 %collective-permute-start.8 = (bf16[128,1280]{1,0:T(8,128)(2,1)S(1)}, bf16[128,1280]{1,0:T(8,128)(2,1)}, u32[]{:S(2)}, u32[]{:S(2)}) collective-permute-start(bf16[128,1280]{1,0:T(8,128)(2,1)S(1)} %get-tuple-element.22), channel_id=1, source_target_pairs={{0,16},{4,20},{8,24},{12,28},{16,0},{20,4},{24,8},{28,12},{1,17},{... | collective-permute-start | bytes 983048 | tf_op jit(solution)/shard_map/cond/branch_1_fun/ppermute | solution.py:191
  24.5 1.2 %collective-permute-start.5 = (bf16[128,512]{1,0:T(8,128)(2,1)S(1)}, bf16[128,512]{1,0:T(8,128)(2,1)}, u32[]{:S(2)}, u32[]{:S(2)}) collective-permute-start(bf16[128,512]{1,0:T(8,128)(2,1)S(1)} %get-tuple-element.16), channel_id=1, source_target_pairs={{0,24},{4,28},{8,16},{12,20},{16,8},{20,12},{24,0},{28,4},{1,25},{... | collective-permute-start | bytes 393224 | tf_op jit(solution)/shard_map/cond/branch_1_fun/ppermute | solution.py:191
  25.7 9.4 %collective-permute-done.5 = bf16[128,512]{1,0:T(8,128)(2,1)} collective-permute-done((bf16[128,512]{1,0:T(8,128)(2,1)S(1)}, bf16[128,512]{1,0:T(8,128)(2,1)}, u32[]{:S(2)}, u32[]{:S(2)}) %collective-permute-start.5) | collective-permute-done | bytes 131104 | tf_op jit(solution)/shard_map/cond/branch_1_fun/ppermute | solution.py:191
  35.2 0.8 %collective-permute-done.8 = bf16[128,1280]{1,0:T(8,128)(2,1)} collective-permute-done((bf16[128,1280]{1,0:T(8,128)(2,1)S(1)}, bf16[128,1280]{1,0:T(8,128)(2,1)}, u32[]{:S(2)}, u32[]{:S(2)}) %collective-permute-start.8) | collective-permute-done | bytes 327712 | tf_op jit(solution)/shard_map/cond/branch_1_fun/ppermute | solution.py:191
  35.9 0.9 %collective-permute-done.6 = bf16[128,512]{1,0:T(8,128)(2,1)} collective-permute-done((bf16[128,512]{1,0:T(8,128)(2,1)}, bf16[128,512]{1,0:T(8,128)(2,1)}, u32[]{:S(2)}, u32[]{:S(2)}) %collective-permute-start.6) | collective-permute-done | bytes 131104 | tf_op jit(solution)/shard_map/cond/branch_1_fun/ppermute | solution.py:191
  36.8 3.1 %project_2.1 = (bf16[256,768]{1,0:T(8,128)(2,1)}, bf16[256,768]{1,0:T(8,128)(2,1)}) custom-call(bf16[1024,768]{1,0:T(8,128)(2,1)S(1)} %stage.1.noise_ref, bf16[128,512]{1,0:T(8,128)(2,1)S(1)} %pad_maximum_fusion.1.refs_0_, bf16[128,512]{1,0:T(8,128)(2,1)} %get-tuple-element.61.refs_1_, bf16[128,512]{1,0:T(8,128)(2,1)} %get-tuple-element.62.refs_2_, ...), custom_call_target="tpu_custom_call" | custom-call | flops 805306368 | bytes 5242880 | tf_op jit(solution)/shard_map/project_2/pallas_call | solution.py:51
  40.0 1.6 %collective-permute-start.22 = (bf16[256,768]{1,0:T(8,128)(2,1)}, bf16[256,768]{1,0:T(8,128)(2,1)S(1)}, u32[]{:S(2)}, u32[]{:S(2)}) collective-permute-start(bf16[256,768]{1,0:T(8,128)(2,1)} %get-tuple-element.68), channel_id=1, source_target_pairs={{0,1},{1,2},{2,3},{3,0},{4,5},{5,6},{6,7},{7,4},{8,9},{9,10},{10,1... | collective-permute-start | bytes 1179656 | tf_op jit(solution)/shard_map/ppermute | solution.py:253
  41.5 2.3 %collective-permute-start.23 = (bf16[256,768]{1,0:T(8,128)(2,1)}, bf16[256,768]{1,0:T(8,128)(2,1)S(1)}, u32[]{:S(2)}, u32[]{:S(2)}) collective-permute-start(bf16[256,768]{1,0:T(8,128)(2,1)} %get-tuple-element.79), channel_id=1, source_target_pairs={{0,3},{1,0},{2,1},{3,2},{4,7},{5,4},{6,5},{7,6},{8,11},{9,8},{10,9... | collective-permute-start | bytes 1179656 | tf_op jit(solution)/shard_map/ppermute | solution.py:253
  44.3 13.9 %conditional.3 = (bf16[128,1280]{1,0:T(8,128)(2,1)}, bf16[128,1280]{1,0:T(8,128)(2,1)}, bf16[128,1280]{1,0:T(8,128)(2,1)}, bf16[128,1280]{1,0:T(8,128)(2,1)}, bf16[128,1280]{1,0:T(8,128)(2,1)}) conditional(s32[]{:T(128)} %bitcast.5, () %tuple.38, (bf16[128,1280]{1,0:T(8,128)(2,1)}, bf16[128,1280]{1,0:T(8,128)(2,1)}, bf16[128,1280]{1,0:T(8,128)(2,1)}) %tuple.47), branch_computations={%region_2.0_spmd, %region_3.0_spmd} | conditional | bytes 6553840 | solution.py:248
  44.4 1.9 %collective-permute-start.12 = (bf16[128,1280]{1,0:T(8,128)(2,1)}, bf16[128,1280]{1,0:T(8,128)(2,1)}, u32[]{:S(2)}, u32[]{:S(2)}) collective-permute-start(bf16[128,1280]{1,0:T(8,128)(2,1)} %get-tuple-element.23), channel_id=1, source_target_pairs={{0,24},{4,28},{8,16},{12,20},{16,8},{20,12},{24,0},{28,4},{1,25},{... | collective-permute-start | bytes 983048 | tf_op jit(solution)/shard_map/cond/branch_1_fun/ppermute | solution.py:191
  46.4 9.2 %collective-permute-done.12 = bf16[128,1280]{1,0:T(8,128)(2,1)} collective-permute-done((bf16[128,1280]{1,0:T(8,128)(2,1)}, bf16[128,1280]{1,0:T(8,128)(2,1)}, u32[]{:S(2)}, u32[]{:S(2)}) %collective-permute-start.12) | collective-permute-done | bytes 327712 | tf_op jit(solution)/shard_map/cond/branch_1_fun/ppermute | solution.py:191
  56.2 1.5 %collective-permute-done.13 = bf16[128,1280]{1,0:T(8,128)(2,1)} collective-permute-done((bf16[128,1280]{1,0:T(8,128)(2,1)}, bf16[128,1280]{1,0:T(8,128)(2,1)}, u32[]{:S(2)}, u32[]{:S(2)}) %collective-permute-start.13) | collective-permute-done | bytes 327712 | tf_op jit(solution)/shard_map/cond/branch_1_fun/ppermute | solution.py:191
  58.1 3.5 %accumulate.1 = (bf16[1024,1024]{1,0:T(8,128)(2,1)S(1)}, f32[1024,768]{1,0:T(8,128)S(1)}) custom-call(s32[4,4]{1,0:T(4,128)S(1)} %copy-done.1, bf16[1024,768]{1,0:T(8,128)(2,1)S(1)} %stage.1.noise_ref, bf16[128,1280]{1,0:T(8,128)(2,1)} %copy-done.2, bf16[128,1280]{1,0:T(8,128)(2,1)} %get-tuple-element.70.refs_1_, ...), custom_call_target="tpu_custom_call" | custom-call | flops 1207959552 | bytes 9175040 | tf_op jit(solution)/shard_map/accumulate/pallas_call | solution.py:125
  61.7 3.2 %finish.1 = f32[1024,768]{1,0:T(8,128)} custom-call(s32[4,4]{1,0:T(4,128)S(1)} %copy-done.1, bf16[1024,1024]{1,0:T(8,128)(2,1)S(1)} %get-tuple-element.77.u_ref, f32[1024,768]{1,0:T(8,128)S(1)} %get-tuple-element.78.sum_ref, f32[1024,1]{1,0:T(8,128)S(1)} %copy.7.skew_ref, f32[1024,1]{1,0:T(8,128)S(1)} %copy.8.tail_ref, ...), custom_call_target="tpu_custom_call" | custom-call | flops 805306368 | bytes 12058624 | tf_op jit(solution)/shard_map/finish/pallas_call | solution.py:170
  (41 shorter events, 2.4 us)
Async XLA Ops:
  0.0 7.8 %copy-start.3 = (bf16[1,128,1024]{2,1,0:T(8,128)(2,1)S(1)}, bf16[1,128,1024]{2,1,0:T(8,128)(2,1)}, u32[]{:S(2)}) copy-start(bf16[1,128,1024]{2,1,0:T(8,128)(2,1)} %param.12) | copy-start | bytes 786436
  1.0 6.9 %collective-permute-start.14 = (bf16[128,256]{1,0:T(8,128)(2,1)S(1)}, bf16[128,256]{1,0:T(8,128)(2,1)S(1)}, u32[]{:S(2)}, u32[]{:S(2)}) collective-permute-start(bf16[128,256]{1,0:T(8,128)(2,1)S(1)} %get-tuple-element.82.refs_0_), channel_id=1, source_target_pairs={{0,24},{4,28},{8,16},{12,20},{16,8},{20,12},{24,0},{28,4},{1,25},{... | collective-permute-start | bytes 196616 | tf_op jit(solution)/shard_map/ppermute | solution.py:191
  5.0 4.3 %collective-permute-start.15 = (bf16[128,256]{1,0:T(8,128)(2,1)S(1)}, bf16[128,256]{1,0:T(8,128)(2,1)S(1)}, u32[]{:S(2)}, u32[]{:S(2)}) collective-permute-start(bf16[128,256]{1,0:T(8,128)(2,1)S(1)} %get-tuple-element.82.refs_0_), channel_id=1, source_target_pairs={{0,8},{4,12},{8,0},{12,4},{16,24},{20,28},{24,16},{28,20},{1,9},{5... | collective-permute-start | bytes 196616 | tf_op jit(solution)/shard_map/ppermute | solution.py:191
  5.5 4.3 %collective-permute-start.16 = (bf16[128,256]{1,0:T(8,128)(2,1)S(1)}, bf16[128,256]{1,0:T(8,128)(2,1)S(1)}, u32[]{:S(2)}, u32[]{:S(2)}) collective-permute-start(bf16[128,256]{1,0:T(8,128)(2,1)S(1)} %get-tuple-element.82.refs_0_), channel_id=1, source_target_pairs={{0,16},{4,20},{8,24},{12,28},{16,0},{20,4},{24,8},{28,12},{1,17},{... | collective-permute-start | bytes 196616 | tf_op jit(solution)/shard_map/ppermute | solution.py:191
  5.6 4.2 %collective-permute-start.17 = (bf16[128,256]{1,0:T(8,128)(2,1)S(1)}, bf16[128,256]{1,0:T(8,128)(2,1)S(1)}, u32[]{:S(2)}, u32[]{:S(2)}) collective-permute-start(bf16[128,256]{1,0:T(8,128)(2,1)S(1)} %get-tuple-element.82.refs_0_), channel_id=1, source_target_pairs={{0,4},{4,0},{8,12},{12,8},{16,20},{20,16},{24,28},{28,24},{1,5},{5... | collective-permute-start | bytes 196616 | tf_op jit(solution)/shard_map/ppermute | solution.py:191
  5.6 1.4 %copy-start = (bf16[1024,768]{1,0:T(8,128)(2,1)S(1)}, bf16[1024,768]{1,0:T(8,128)(2,1)}, u32[]{:S(2)}) copy-start(bf16[1024,768]{1,0:T(8,128)(2,1)} %from_ref.1) | copy-start | bytes 4718596
  7.8 7.2 %copy-start.1 = (s32[4,4]{1,0:T(4,128)S(1)}, s32[4,4]{1,0:T(4,128)}, u32[]{:S(2)}) copy-start(s32[4,4]{1,0:T(4,128)} %ranks_ref.3) | copy-start | bytes 196
  7.9 8.2 %copy-start.2 = (bf16[128,1280]{1,0:T(8,128)(2,1)}, bf16[128,1280]{1,0:T(8,128)(2,1)S(1)}, u32[]{:S(2)}) copy-start(bf16[128,1280]{1,0:T(8,128)(2,1)S(1)} %pad_maximum_fusion.refs_0_) | copy-start | bytes 983044
  7.9 1.9 %collective-permute-start.20 = (bf16[128,256]{1,0:T(8,128)(2,1)S(1)}, bf16[128,256]{1,0:T(8,128)(2,1)S(1)}, u32[]{:S(2)}, u32[]{:S(2)}) collective-permute-start(bf16[128,256]{1,0:T(8,128)(2,1)S(1)} %collective-permute-done.14.refs_3_), channel_id=1, source_target_pairs={{0,4},{4,0},{8,12},{12,8},{16,20},{20,16},{24,28},{28,24},{1,5},{5... | collective-permute-start | bytes 196616 | tf_op jit(solution)/shard_map/ppermute | solution.py:191
  9.2 1.3 %collective-permute-start.18 = (bf16[128,256]{1,0:T(8,128)(2,1)S(1)}, bf16[128,256]{1,0:T(8,128)(2,1)S(1)}, u32[]{:S(2)}, u32[]{:S(2)}) collective-permute-start(bf16[128,256]{1,0:T(8,128)(2,1)S(1)} %collective-permute-done.15.refs_1_), channel_id=1, source_target_pairs={{0,4},{4,0},{8,12},{12,8},{16,20},{20,16},{24,28},{28,24},{1,5},{5... | collective-permute-start | bytes 196616 | tf_op jit(solution)/shard_map/ppermute | solution.py:191
  9.8 1.3 %collective-permute-start.19 = (bf16[128,256]{1,0:T(8,128)(2,1)S(1)}, bf16[128,256]{1,0:T(8,128)(2,1)S(1)}, u32[]{:S(2)}, u32[]{:S(2)}) collective-permute-start(bf16[128,256]{1,0:T(8,128)(2,1)S(1)} %collective-permute-done.16.refs_2_), channel_id=1, source_target_pairs={{0,4},{4,0},{8,12},{12,8},{16,20},{20,16},{24,28},{28,24},{1,5},{5... | collective-permute-start | bytes 196616 | tf_op jit(solution)/shard_map/ppermute | solution.py:191
  12.4 45.7 %collective-permute-start.21 = (bf16[256,768]{1,0:T(8,128)(2,1)}, bf16[256,768]{1,0:T(8,128)(2,1)}, u32[]{:S(2)}, u32[]{:S(2)}) collective-permute-start(bf16[256,768]{1,0:T(8,128)(2,1)} %project_1.1), channel_id=1, source_target_pairs={{0,2},{1,3},{2,0},{3,1},{4,6},{5,7},{6,4},{7,5},{8,10},{9,11},{10,... | collective-permute-start | bytes 1179656 | tf_op jit(solution)/shard_map/ppermute | solution.py:253
  16.1 27.7 %copy-start.4 = (f32[1024]{0:T(1024)S(1)}, f32[1024]{0:T(1024)}, u32[]{:S(2)}) copy-start(f32[1024]{0:T(1024)} %param.14) | copy-start | bytes 12292
  16.1 5.5 %collective-permute-start.1 = (bf16[128,512]{1,0:T(8,128)(2,1)S(1)}, bf16[128,512]{1,0:T(8,128)(2,1)}, u32[]{:S(2)}, u32[]{:S(2)}) collective-permute-start(bf16[128,512]{1,0:T(8,128)(2,1)S(1)} %get-tuple-element.16), channel_id=1, source_target_pairs={{0,8},{4,12},{8,0},{12,4},{16,24},{20,28},{24,16},{28,20},{1,9},{5... | collective-permute-start | bytes 393224 | tf_op jit(solution)/shard_map/cond/branch_1_fun/ppermute | solution.py:191
  17.7 3.9 %collective-permute-start = (bf16[128,512]{1,0:T(8,128)(2,1)S(1)}, bf16[128,512]{1,0:T(8,128)(2,1)}, u32[]{:S(2)}, u32[]{:S(2)}) collective-permute-start(bf16[128,512]{1,0:T(8,128)(2,1)S(1)} %get-tuple-element.16), channel_id=1, source_target_pairs={{0,4},{4,0},{8,12},{12,8},{16,20},{20,16},{24,28},{28,24},{1,5},{5... | collective-permute-start | bytes 393224 | tf_op jit(solution)/shard_map/cond/branch_1_fun/ppermute | solution.py:191
  17.7 6.0 %collective-permute-start.3 = (bf16[128,512]{1,0:T(8,128)(2,1)S(1)}, bf16[128,512]{1,0:T(8,128)(2,1)}, u32[]{:S(2)}, u32[]{:S(2)}) collective-permute-start(bf16[128,512]{1,0:T(8,128)(2,1)S(1)} %get-tuple-element.16), channel_id=1, source_target_pairs={{0,16},{4,20},{8,24},{12,28},{16,0},{20,4},{24,8},{28,12},{1,17},{... | collective-permute-start | bytes 393224 | tf_op jit(solution)/shard_map/cond/branch_1_fun/ppermute | solution.py:191
  21.6 4.1 %collective-permute-start.2 = (bf16[128,512]{1,0:T(8,128)(2,1)}, bf16[128,512]{1,0:T(8,128)(2,1)}, u32[]{:S(2)}, u32[]{:S(2)}) collective-permute-start(bf16[128,512]{1,0:T(8,128)(2,1)} %collective-permute-done.1), channel_id=1, source_target_pairs={{0,4},{4,0},{8,12},{12,8},{16,20},{20,16},{24,28},{28,24},{1,5},{5... | collective-permute-start | bytes 393224 | tf_op jit(solution)/shard_map/cond/branch_1_fun/ppermute | solution.py:191
  21.6 13.6 %collective-permute-start.7 = (bf16[128,1280]{1,0:T(8,128)(2,1)S(1)}, bf16[128,1280]{1,0:T(8,128)(2,1)}, u32[]{:S(2)}, u32[]{:S(2)}) collective-permute-start(bf16[128,1280]{1,0:T(8,128)(2,1)S(1)} %get-tuple-element.22), channel_id=1, source_target_pairs={{0,8},{4,12},{8,0},{12,4},{16,24},{20,28},{24,16},{28,20},{1,9},{5... | collective-permute-start | bytes 983048 | tf_op jit(solution)/shard_map/cond/branch_1_fun/ppermute | solution.py:191
  23.7 12.3 %collective-permute-start.8 = (bf16[128,1280]{1,0:T(8,128)(2,1)S(1)}, bf16[128,1280]{1,0:T(8,128)(2,1)}, u32[]{:S(2)}, u32[]{:S(2)}) collective-permute-start(bf16[128,1280]{1,0:T(8,128)(2,1)S(1)} %get-tuple-element.22), channel_id=1, source_target_pairs={{0,16},{4,20},{8,24},{12,28},{16,0},{20,4},{24,8},{28,12},{1,17},{... | collective-permute-start | bytes 983048 | tf_op jit(solution)/shard_map/cond/branch_1_fun/ppermute | solution.py:191
  24.5 10.7 %collective-permute-start.5 = (bf16[128,512]{1,0:T(8,128)(2,1)S(1)}, bf16[128,512]{1,0:T(8,128)(2,1)}, u32[]{:S(2)}, u32[]{:S(2)}) collective-permute-start(bf16[128,512]{1,0:T(8,128)(2,1)S(1)} %get-tuple-element.16), channel_id=1, source_target_pairs={{0,24},{4,28},{8,16},{12,20},{16,8},{20,12},{24,0},{28,4},{1,25},{... | collective-permute-start | bytes 393224 | tf_op jit(solution)/shard_map/cond/branch_1_fun/ppermute | solution.py:191
  25.7 9.5 %collective-permute-start.4 = (bf16[128,512]{1,0:T(8,128)(2,1)}, bf16[128,512]{1,0:T(8,128)(2,1)}, u32[]{:S(2)}, u32[]{:S(2)}) collective-permute-start(bf16[128,512]{1,0:T(8,128)(2,1)} %collective-permute-done.3), channel_id=1, source_target_pairs={{0,4},{4,0},{8,12},{12,8},{16,20},{20,16},{24,28},{28,24},{1,5},{5... | collective-permute-start | bytes 393224 | tf_op jit(solution)/shard_map/cond/branch_1_fun/ppermute | solution.py:191
  35.1 1.7 %collective-permute-start.6 = (bf16[128,512]{1,0:T(8,128)(2,1)}, bf16[128,512]{1,0:T(8,128)(2,1)}, u32[]{:S(2)}, u32[]{:S(2)}) collective-permute-start(bf16[128,512]{1,0:T(8,128)(2,1)} %collective-permute-done.5), channel_id=1, source_target_pairs={{0,4},{4,0},{8,12},{12,8},{16,20},{20,16},{24,28},{28,24},{1,5},{5... | collective-permute-start | bytes 393224 | tf_op jit(solution)/shard_map/cond/branch_1_fun/ppermute | solution.py:191
  36.8 7.2 %copy-start.5 = (f32[1024]{0:T(1024)S(1)}, f32[1024]{0:T(1024)}, u32[]{:S(2)}) copy-start(f32[1024]{0:T(1024)} %param.15) | copy-start | bytes 12292
  40.0 21.7 %collective-permute-start.22 = (bf16[256,768]{1,0:T(8,128)(2,1)}, bf16[256,768]{1,0:T(8,128)(2,1)S(1)}, u32[]{:S(2)}, u32[]{:S(2)}) collective-permute-start(bf16[256,768]{1,0:T(8,128)(2,1)} %get-tuple-element.68), channel_id=1, source_target_pairs={{0,1},{1,2},{2,3},{3,0},{4,5},{5,6},{6,7},{7,4},{8,9},{9,10},{10,1... | collective-permute-start | bytes 1179656 | tf_op jit(solution)/shard_map/ppermute | solution.py:253
  41.5 20.1 %collective-permute-start.23 = (bf16[256,768]{1,0:T(8,128)(2,1)}, bf16[256,768]{1,0:T(8,128)(2,1)S(1)}, u32[]{:S(2)}, u32[]{:S(2)}) collective-permute-start(bf16[256,768]{1,0:T(8,128)(2,1)} %get-tuple-element.79), channel_id=1, source_target_pairs={{0,3},{1,0},{2,1},{3,2},{4,7},{5,4},{6,5},{7,6},{8,11},{9,8},{10,9... | collective-permute-start | bytes 1179656 | tf_op jit(solution)/shard_map/ppermute | solution.py:253
  44.3 2.0 %collective-permute-start.9 = (bf16[128,1280]{1,0:T(8,128)(2,1)}, bf16[128,1280]{1,0:T(8,128)(2,1)}, u32[]{:S(2)}, u32[]{:S(2)}) collective-permute-start(bf16[128,1280]{1,0:T(8,128)(2,1)} %get-tuple-element.23), channel_id=1, source_target_pairs={{0,4},{4,0},{8,12},{12,8},{16,20},{20,16},{24,28},{28,24},{1,5},{5... | collective-permute-start | bytes 983048 | tf_op jit(solution)/shard_map/cond/branch_1_fun/ppermute | solution.py:191
  44.4 11.3 %collective-permute-start.12 = (bf16[128,1280]{1,0:T(8,128)(2,1)}, bf16[128,1280]{1,0:T(8,128)(2,1)}, u32[]{:S(2)}, u32[]{:S(2)}) collective-permute-start(bf16[128,1280]{1,0:T(8,128)(2,1)} %get-tuple-element.23), channel_id=1, source_target_pairs={{0,24},{4,28},{8,16},{12,20},{16,8},{20,12},{24,0},{28,4},{1,25},{... | collective-permute-start | bytes 983048 | tf_op jit(solution)/shard_map/cond/branch_1_fun/ppermute | solution.py:191
  46.3 9.4 %collective-permute-start.10 = (bf16[128,1280]{1,0:T(8,128)(2,1)}, bf16[128,1280]{1,0:T(8,128)(2,1)}, u32[]{:S(2)}, u32[]{:S(2)}) collective-permute-start(bf16[128,1280]{1,0:T(8,128)(2,1)} %get-tuple-element.25), channel_id=1, source_target_pairs={{0,4},{4,0},{8,12},{12,8},{16,20},{20,16},{24,28},{28,24},{1,5},{5... | collective-permute-start | bytes 983048 | tf_op jit(solution)/shard_map/cond/branch_1_fun/ppermute | solution.py:191
  55.7 2.0 %collective-permute-start.13 = (bf16[128,1280]{1,0:T(8,128)(2,1)}, bf16[128,1280]{1,0:T(8,128)(2,1)}, u32[]{:S(2)}, u32[]{:S(2)}) collective-permute-start(bf16[128,1280]{1,0:T(8,128)(2,1)} %collective-permute-done.12), channel_id=1, source_target_pairs={{0,4},{4,0},{8,12},{12,8},{16,20},{20,16},{24,28},{28,24},{1,5},{5... | collective-permute-start | bytes 983048 | tf_op jit(solution)/shard_map/cond/branch_1_fun/ppermute | solution.py:191
  55.7 2.4 %collective-permute-start.11 = (bf16[128,1280]{1,0:T(8,128)(2,1)}, bf16[128,1280]{1,0:T(8,128)(2,1)}, u32[]{:S(2)}, u32[]{:S(2)}) collective-permute-start(bf16[128,1280]{1,0:T(8,128)(2,1)} %get-tuple-element.27), channel_id=1, source_target_pairs={{0,4},{4,0},{8,12},{12,8},{16,20},{20,16},{24,28},{28,24},{1,5},{5... | collective-permute-start | bytes 983048 | tf_op jit(solution)/shard_map/cond/branch_1_fun/ppermute | solution.py:191

commit v7 on v6

--- a/solution.py
+++ b/solution.py
@@ -1,4 +1,5 @@
 import functools
+import math
 
 import jax
 import jax.numpy as jnp
@@ -11,7 +12,11 @@
 LOG2E = 1.4426950408889634
 VMEM = pl.BlockSpec(memory_space=pltpu.VMEM)
 SMEM = pl.BlockSpec(memory_space=pltpu.SMEM)
-LIMIT = pltpu.CompilerParams(vmem_limit_bytes=44 * 2**20)
+
+
+def vmem(*shapes):
+    held = sum(4 * math.prod(shape) for shape in shapes)
+    return pltpu.CompilerParams(vmem_limit_bytes=held + 6 * 2**20)
 
 
 def cost(flops, *arrays):
@@ -54,7 +59,7 @@
         in_specs=[VMEM] * (1 + len(pieces)),
         out_specs=[VMEM] * n_shifts,
         scratch_shapes=[pltpu.VMEM((sites, columns), jnp.bfloat16)],
-        compiler_params=LIMIT,
+        compiler_params=vmem(noise.shape, (sites, 2 * columns)),
         cost_estimate=cost(2 * sites * columns * reals, noise, *pieces),
         name=f"project_{n_shifts}",
     )(noise, *pieces)
@@ -81,7 +86,7 @@
         in_specs=[pl.BlockSpec(memory_space=pltpu.HBM)],
         out_specs=VMEM,
         scratch_shapes=[pltpu.SemaphoreType.DMA((4,))],
-        compiler_params=LIMIT,
+        compiler_params=vmem(array.shape),
         cost_estimate=cost(0, array),
         name="stage",
     )(array)
@@ -119,8 +124,8 @@
 
 def accumulate(shifts, ranks, noise, gathered, coefs):
     places, pieces = zip(*gathered)
-    rows, columns = pieces[0].shape
     sites, reals = noise.shape
+    rows, columns = sites // lax.axis_size("real"), pieces[0].shape[1]
     per_source = coefs[0].shape[0]
     return pl.pallas_call(
         functools.partial(accumulate_kernel, shifts, places, rows),
@@ -131,7 +136,7 @@
         in_specs=[SMEM] + [VMEM] * (1 + len(pieces) + len(coefs)),
         out_specs=[VMEM] * 2,
         scratch_shapes=[pltpu.VMEM((sites, columns), jnp.bfloat16)],
-        compiler_params=LIMIT,
+        compiler_params=vmem((sites, 3 * reals), (sites, 2 * columns)),
         cost_estimate=cost(6 * sites * per_source * reals, noise, *pieces, *coefs),
         name="accumulate",
     )(ranks, noise, *pieces, *coefs)
@@ -176,7 +181,7 @@
             pltpu.VMEM((rows // block, block, reals), jnp.float32),
             pltpu.SemaphoreType.DMA((rows // block,)),
         ],
-        compiler_params=LIMIT,
+        compiler_params=vmem((rows, 4 * reals), u_whole.shape),
         cost_estimate=cost(2 * rows * len(coefs) * per_source * reals, u_whole, total, *coefs),
         name="finish",
     )(ranks, u_whole, total, skew, tail, *coefs)
@@ -210,26 +215,34 @@
     return (2, 4) if lax.axis_size("real") == 8 else ()
 
 
-def chunk_and_neighbours(chunk, later):
-    pieces, tail = from_chips(chunk), chunk
-    for distance, _ in list(pieces):
-        tail = pieces[distance ^ 1, 0] = swap(after(pieces[distance, 0], tail), 1)
-    near = {}
-    for distance in neighbour_distances():
-        near[distance, 0] = swap(after(later, pieces[distance, 0]), distance)
-    return {place: pieces[place] for place in pieces if place != (0, 0)}, near
+def direct_rest(chunk):
+    pieces = with_other_core(from_chips(chunk))
+    del pieces[0, 0]
+    return pieces
+
+
+def relayed_rest(pieces):
+    if (2, 0) not in pieces:
+        return two_at_a_time(pieces)
+    first, second = pieces[2, 0], pieces[4, 0]
+    half = first.shape[0] // 2
+    one, two = swap(second[:half], 2), swap(first[half:], 4)
+    more = {(6, 0): one, (6, half): two}
+    more[3, 0], more[5, 0] = swap(after(first, one), 1), swap(after(second, two), 1)
+    more[7, 0], more[7, half] = swap(after(one, more[3, 0]), 1), swap(after(two, more[5, 0]), 1)
+    return more
 
 
 def two_at_a_time(pieces):
     known, pieces = pieces, dict(pieces)
     own = pieces[0, 0]
-    distances = [d for d in range(2, lax.axis_size("real"), 2) if (d, 0) not in pieces]
+    distances = range(2, lax.axis_size("real"), 2)
     tails = [own, own]
     for turn, distance in enumerate(distances):
         tails[turn % 2] = pieces[distance, 0] = swap(after(own, tails[turn % 2]), distance)
     last, tail = distances[-1], tails[len(distances) % 2]
-    for distance in range(0, lax.axis_size("real"), 2):
-        if distance != last:
+    for distance in (0, *distances):
+        if distance != last and (distance ^ 1, 0) not in known:
             tail = pieces[distance ^ 1, 0] = swap(after(pieces[distance, 0], tail), 1)
     pieces[last ^ 1, 0] = swap(pieces[last, 0], 1)
     return {place: pieces[place] for place in pieces if place not in known}
@@ -277,11 +290,15 @@
     present = ranks[0, 0] > 0
     [far] = project(1, noise, with_other_core(v_first).items())
     v_rest = after(v_rest, far)
-    v_pieces, u_pieces = at_once(present, chunk_and_neighbours, v_rest, own_and_u)
-    others = project(len(rest), noise, {(0, 0): v_rest, **v_pieces}.items())
+    u_pieces = {(0, 0): own_and_u, (1, 0): swap(after(own_and_u, far), 1)}
+    v_pieces = {(0, 0): after(v_rest, u_pieces[1, 0])}
+    v_pieces.update(at_once(present, direct_rest, v_pieces[0, 0]))
+    for distance in neighbour_distances():
+        u_pieces[distance, 0] = swap(after(own_and_u, v_pieces), distance)
+    others = project(len(rest), noise, v_pieces.items())
     far = along_site(far, first)
-    u_pieces = after({(0, 0): own_and_u, **u_pieces}, others[0])
-    u_pieces.update(at_once(present, two_at_a_time, u_pieces))
+    u_pieces = after(u_pieces, others[0])
+    u_pieces.update(at_once(present, relayed_rest, u_pieces))
     others = [along_site(coef, shift) for coef, shift in zip(others, rest)]
     u_whole, total = accumulate((first,), ranks, noise, u_pieces.items(), [far])
     return finish(rest, ranks, u_whole, total, skew_g[:, None], tail_h[:, None], others)

time: 65.2 us -> 59.2 us (0.908)
  waiting for transfers between devices: 28.6 us -> 18.8 us
  local copies, waits for them, and re-layouts: 3.35 us -> 6.29 us
    ppermute x21 -> x23, waiting for transfers between devices: 28.6 us -> 18.8 us  [swap(): lax.ppermute(array, 'real', [(k, k ^ distance) for k in range(count)])]
    slice x0 -> x2, local copies, waits for them, and re-layouts: none -> 1.85 us  [relayed_rest(): one, two = (swap(second[:half], 2), swap(first[half:], 4))]
    unnamed x12 -> x14, local copies, waits for them, and re-layouts: 1.43 us -> 2.41 us
    ppermute x21 -> x23, starting transfers between devices: 13.7 us -> 14.3 us  [swap(): lax.ppermute(array, 'real', [(k, k ^ distance) for k in range(count)])]
  transfers between devices with their start and end apart: 24 -> 26, of which waited for: 12 -> 14; matrix products, arithmetic and copies ran while one was open for 1% -> 5% of each run, Pallas kernels for 11% -> 12%
where the time goes in v7:
time: 59.2 us; the launch traced here: 58.9 us
  starting transfers between devices  20.7 us (35%)
  waiting for transfers between devices  18.8 us (32%)
  Pallas kernels  12.2 us (21%)
  local copies, waits for them, and re-layouts  6.29 us (11%)
  between operations  0.84 us (1%)
    ppermute x23, waiting for transfers between devices, swap(): lax.ppermute(array, 'real', [(k, k ^ distance) for k in range(count)])  18.8 us
    ppermute x23, starting transfers between devices, swap(): lax.ppermute(array, 'real', [(k, k ^ distance) for k in range(count)])  14.3 us
    ppermute x3, starting transfers between devices, along_site(): lax.ppermute(coef, 'site', [(k, (k + shift) % count) for k in range(count)])  6.41 us
    pallas_call x2, Pallas kernels, project(): pl.pallas_call(functools.partial(project_kernel, places, rows), out_shape...  4.51 us
    pallas_call x1, Pallas kernels, finish(): pl.pallas_call(functools.partial(finish_kernel, shifts), out_shape=jax.Sh...  3.59 us
    pallas_call x1, Pallas kernels, accumulate(): pl.pallas_call(functools.partial(accumulate_kernel, shifts, places, rows)...  3.31 us
    unnamed x14, local copies, waits for them, and re-layouts  2.41 us
    slice x2, local copies, waits for them, and re-layouts, relayed_rest(): one, two = (swap(second[:half], 2), swap(first[half:], 4))  1.85 us
  transfers between devices with their start and end apart: 26, of which 14 were waited for; matrix products, arithmetic and copies ran while one was open for 5% of the time, Pallas kernels for 12%

profile of v7, /device:TPU:0, one launch (start us, length us, event | category | flops | bytes accessed | tf_op | source)
XLA Modules:
  0.0 58.9 jit_solution(5741445044506235237)
XLA Ops:
  0.0 1.0 %dynamic-slice_bitcast_fusion = (bf16[128,256]{1,0:T(8,128)(2,1)S(1)}, bf16[128,256]{1,0:T(8,128)(2,1)S(1)}, bf16[128,256]{1,0:T(8,128)(2,1)S(1)}, bf16[128,256]{1,0:T(8,128)(2,1)S(1)}) fusion(bf16[1,128,1024]{2,1,0:T(8,128)(2,1)} %param.11, s32[]{:T(128)S(6)} %select_n.15, s32[]{:T(128)S(6)} %select_n.13, s32[]{:T(128)S(6)} %select_n.12, s32[]{:T(128)S(6)} %select_n.14), kind=kLoop, calls=%fused_computation.2 | loop fusion | bytes 524304 | tf_op jit(solution)/shard_map/dynamic_slice | solution.py:281
  1.0 4.0 %collective-permute-start.13 = (bf16[128,256]{1,0:T(8,128)(2,1)S(1)}, bf16[128,256]{1,0:T(8,128)(2,1)S(1)}, u32[]{:S(2)}, u32[]{:S(2)}) collective-permute-start(bf16[128,256]{1,0:T(8,128)(2,1)S(1)} %get-tuple-element.76.refs_0_), channel_id=1, source_target_pairs={{0,24},{4,28},{8,16},{12,20},{16,8},{20,12},{24,0},{28,4},{1,25},{... | collective-permute-start | bytes 196616 | tf_op jit(solution)/shard_map/ppermute | solution.py:196
  5.6 1.4 %copy-done = bf16[1024,768]{1,0:T(8,128)(2,1)S(1)} copy-done((bf16[1024,768]{1,0:T(8,128)(2,1)S(1)}, bf16[1024,768]{1,0:T(8,128)(2,1)}, u32[]{:S(2)}) %copy-start) | copy-done | bytes 1572888
  7.0 0.8 %stage.1.noise_ref = bf16[1024,768]{1,0:T(8,128)(2,1)S(1)} custom-call(bf16[1024,768]{1,0:T(8,128)(2,1)S(1)} %copy-done), custom_call_target="tpu_custom_call" | custom-call | bytes 3145728 | tf_op jit(solution)/shard_map/stage/pallas_call | solution.py:83
  8.5 0.8 %collective-permute-done.14.refs_1_ = bf16[128,256]{1,0:T(8,128)(2,1)S(1)} collective-permute-done((bf16[128,256]{1,0:T(8,128)(2,1)S(1)}, bf16[128,256]{1,0:T(8,128)(2,1)S(1)}, u32[]{:S(2)}, u32[]{:S(2)}) %collective-permute-start.14) | collective-permute-done | bytes 65568 | tf_op jit(solution)/shard_map/ppermute | solution.py:196
  9.8 0.7 %collective-permute-done.17.refs_5_ = bf16[128,256]{1,0:T(8,128)(2,1)S(1)} collective-permute-done((bf16[128,256]{1,0:T(8,128)(2,1)S(1)}, bf16[128,256]{1,0:T(8,128)(2,1)S(1)}, u32[]{:S(2)}, u32[]{:S(2)}) %collective-permute-start.17) | collective-permute-done | bytes 65568 | tf_op jit(solution)/shard_map/ppermute | solution.py:196
  11.0 1.4 %project_1.1 = bf16[256,768]{1,0:T(8,128)(2,1)} custom-call(bf16[1024,768]{1,0:T(8,128)(2,1)S(1)} %stage.1.noise_ref, bf16[128,256]{1,0:T(8,128)(2,1)S(1)} %get-tuple-element.76.refs_0_, bf16[128,256]{1,0:T(8,128)(2,1)S(1)} %collective-permute-done.14.refs_1_, bf16[128,256]{1,0:T(8,128)(2,1)S(1)} %collective-permute-done.15.refs_2_, ...), custom_call_target="tpu_custom_call" | custom-call | flops 402653184 | bytes 4194304 | tf_op jit(solution)/shard_map/project_1/pallas_call | solution.py:56
  12.6 2.6 %collective-permute-start.23 = (bf16[256,768]{1,0:T(8,128)(2,1)}, bf16[256,768]{1,0:T(8,128)(2,1)}, u32[]{:S(2)}, u32[]{:S(2)}) collective-permute-start(bf16[256,768]{1,0:T(8,128)(2,1)} %project_1.1), channel_id=1, source_target_pairs={{0,2},{1,3},{2,0},{3,1},{4,6},{5,7},{6,4},{7,5},{8,10},{9,11},{10,... | collective-permute-start | bytes 1179656 | tf_op jit(solution)/shard_map/ppermute | solution.py:266
  16.5 11.6 %conditional.2 = (bf16[128,512]{1,0:T(8,128)(2,1)}, bf16[128,512]{1,0:T(8,128)(2,1)}, bf16[128,512]{1,0:T(8,128)(2,1)}, bf16[128,512]{1,0:T(8,128)(2,1)}, bf16[1...) conditional(s32[]{:T(128)} %bitcast.5, () %tuple.35, ...), branch_computations={%region_0.0_spmd, %region_1.0_spmd} | conditional | bytes 3670352 | solution.py:261
  16.5 1.6 %collective-permute-start.1 = (bf16[128,512]{1,0:T(8,128)(2,1)S(1)}, bf16[128,512]{1,0:T(8,128)(2,1)}, u32[]{:S(2)}, u32[]{:S(2)}) collective-permute-start(bf16[128,512]{1,0:T(8,128)(2,1)S(1)} %param.1), channel_id=1, source_target_pairs={{0,8},{4,12},{8,0},{12,4},{16,24},{20,28},{24,16},{28,20},{1,9},{5... | collective-permute-start | bytes 393224 | tf_op jit(solution)/shard_map/cond/branch_1_fun/ppermute | solution.py:196
  18.1 1.0 %collective-permute-start.3 = (bf16[128,512]{1,0:T(8,128)(2,1)S(1)}, bf16[128,512]{1,0:T(8,128)(2,1)}, u32[]{:S(2)}, u32[]{:S(2)}) collective-permute-start(bf16[128,512]{1,0:T(8,128)(2,1)S(1)} %param.1), channel_id=1, source_target_pairs={{0,16},{4,20},{8,24},{12,28},{16,0},{20,4},{24,8},{28,12},{1,17},{... | collective-permute-start | bytes 393224 | tf_op jit(solution)/shard_map/cond/branch_1_fun/ppermute | solution.py:196
  19.1 1.0 %collective-permute-start.5 = (bf16[128,512]{1,0:T(8,128)(2,1)S(1)}, bf16[128,512]{1,0:T(8,128)(2,1)}, u32[]{:S(2)}, u32[]{:S(2)}) collective-permute-start(bf16[128,512]{1,0:T(8,128)(2,1)S(1)} %param.1), channel_id=1, source_target_pairs={{0,24},{4,28},{8,16},{12,20},{16,8},{20,12},{24,0},{28,4},{1,25},{... | collective-permute-start | bytes 393224 | tf_op jit(solution)/shard_map/cond/branch_1_fun/ppermute | solution.py:196
  20.1 2.4 %collective-permute-done.1 = bf16[128,512]{1,0:T(8,128)(2,1)} collective-permute-done((bf16[128,512]{1,0:T(8,128)(2,1)S(1)}, bf16[128,512]{1,0:T(8,128)(2,1)}, u32[]{:S(2)}, u32[]{:S(2)}) %collective-permute-start.1) | collective-permute-done | bytes 131104 | tf_op jit(solution)/shard_map/cond/branch_1_fun/ppermute | solution.py:196
  22.5 3.7 %collective-permute-done.3 = bf16[128,512]{1,0:T(8,128)(2,1)} collective-permute-done((bf16[128,512]{1,0:T(8,128)(2,1)S(1)}, bf16[128,512]{1,0:T(8,128)(2,1)}, u32[]{:S(2)}, u32[]{:S(2)}) %collective-permute-start.3) | collective-permute-done | bytes 131104 | tf_op jit(solution)/shard_map/cond/branch_1_fun/ppermute | solution.py:196
  26.7 1.2 %collective-permute-done.4 = bf16[128,512]{1,0:T(8,128)(2,1)} collective-permute-done((bf16[128,512]{1,0:T(8,128)(2,1)}, bf16[128,512]{1,0:T(8,128)(2,1)}, u32[]{:S(2)}, u32[]{:S(2)}) %collective-permute-start.4) | collective-permute-done | bytes 131104 | tf_op jit(solution)/shard_map/cond/branch_1_fun/ppermute | solution.py:196
  28.4 1.2 %collective-permute-start.22 = (bf16[128,1280]{1,0:T(8,128)(2,1)S(1)}, bf16[128,1280]{1,0:T(8,128)(2,1)}, u32[]{:S(2)}, u32[]{:S(2)}) collective-permute-start(bf16[128,1280]{1,0:T(8,128)(2,1)S(1)} %pad_maximum_fusion.refs_0_), channel_id=1, source_target_pairs={{0,16},{4,20},{8,24},{12,28},{16,0},{20,4},{24,8},{28,12},{1,17},{... | collective-permute-start | bytes 983048 | tf_op jit(solution)/shard_map/ppermute | solution.py:196
  29.6 3.1 %project_2.1 = (bf16[256,768]{1,0:T(8,128)(2,1)}, bf16[256,768]{1,0:T(8,128)(2,1)}) custom-call(bf16[1024,768]{1,0:T(8,128)(2,1)S(1)} %stage.1.noise_ref, bf16[128,512]{1,0:T(8,128)(2,1)S(1)} %pad_maximum_fusion.1.refs_0_, bf16[128,512]{1,0:T(8,128)(2,1)} %get-tuple-element.52.refs_1_, bf16[128,512]{1,0:T(8,128)(2,1)} %get-tuple-element.53.refs_2_, ...), custom_call_target="tpu_custom_call" | custom-call | flops 805306368 | bytes 5242880 | tf_op jit(solution)/shard_map/project_2/pallas_call | solution.py:56
  32.7 1.6 %collective-permute-start.24 = (bf16[256,768]{1,0:T(8,128)(2,1)}, bf16[256,768]{1,0:T(8,128)(2,1)S(1)}, u32[]{:S(2)}, u32[]{:S(2)}) collective-permute-start(bf16[256,768]{1,0:T(8,128)(2,1)} %get-tuple-element.60), channel_id=1, source_target_pairs={{0,1},{1,2},{2,3},{3,0},{4,5},{5,6},{6,7},{7,4},{8,9},{9,10},{10,1... | collective-permute-start | bytes 1179656 | tf_op jit(solution)/shard_map/ppermute | solution.py:266
  34.3 2.3 %collective-permute-start.25 = (bf16[256,768]{1,0:T(8,128)(2,1)}, bf16[256,768]{1,0:T(8,128)(2,1)}, u32[]{:S(2)}, u32[]{:S(2)}) collective-permute-start(bf16[256,768]{1,0:T(8,128)(2,1)} %get-tuple-element.73), channel_id=1, source_target_pairs={{0,3},{1,0},{2,1},{3,2},{4,7},{5,4},{6,5},{7,6},{8,11},{9,8},{10,9... | collective-permute-start | bytes 1179656 | tf_op jit(solution)/shard_map/ppermute | solution.py:266
  37.0 1.1 %collective-permute-done.21.refs_2_ = bf16[128,1280]{1,0:T(8,128)(2,1)} collective-permute-done((bf16[128,1280]{1,0:T(8,128)(2,1)S(1)}, bf16[128,1280]{1,0:T(8,128)(2,1)}, u32[]{:S(2)}, u32[]{:S(2)}) %collective-permute-start.21) | collective-permute-done | bytes 327712 | tf_op jit(solution)/shard_map/ppermute | solution.py:196
  38.1 12.9 %conditional.3 = (bf16[128,1280]{1,0:T(8,128)(2,1)}, bf16[128,1280]{1,0:T(8,128)(2,1)}, bf16[64,1280]{1,0:T(8,128)(2,1)}, bf16[64,1280]{1,0:T(8,128)(2,1)}, bf16...) conditional(s32[]{:T(128)} %bitcast.5, () %tuple.38, (bf16[128,1280]{1,0:T(8,128)(2,1)}, ...), branch_computations={%region_2.0_spmd, %region_3.0_spmd} | conditional | bytes 5898528 | solution.py:261
  38.1 0.9 %slice.6 = bf16[64,1280]{1,0:T(8,128)(2,1)S(1)} slice(bf16[128,1280]{1,0:T(8,128)(2,1)} %get-tuple-element.13), slice={[0:64], [0:1280]} | slice | bytes 327680 | tf_op jit(solution)/shard_map/cond/branch_1_fun/slice | solution.py:229
  39.1 1.8 %collective-permute-start.7 = (bf16[64,1280]{1,0:T(8,128)(2,1)S(1)}, bf16[64,1280]{1,0:T(8,128)(2,1)}, u32[]{:S(2)}, u32[]{:S(2)}) collective-permute-start(bf16[64,1280]{1,0:T(8,128)(2,1)S(1)} %slice.6), channel_id=1, source_target_pairs={{0,8},{4,12},{8,0},{12,4},{16,24},{20,28},{24,16},{28,20},{1,9},{5... | collective-permute-start | bytes 491528 | tf_op jit(solution)/shard_map/cond/branch_1_fun/ppermute | solution.py:196
  40.9 0.9 %slice.7 = bf16[64,1280]{1,0:T(8,128)(2,1)S(1)} slice(bf16[128,1280]{1,0:T(8,128)(2,1)} %get-tuple-element.12), slice={[64:128], [0:1280]} | slice | bytes 327680 | tf_op jit(solution)/shard_map/cond/branch_1_fun/slice | solution.py:229
  41.8 0.8 %collective-permute-start.9 = (bf16[64,1280]{1,0:T(8,128)(2,1)S(1)}, bf16[64,1280]{1,0:T(8,128)(2,1)}, u32[]{:S(2)}, u32[]{:S(2)}) collective-permute-start(bf16[64,1280]{1,0:T(8,128)(2,1)S(1)} %slice.7), channel_id=1, source_target_pairs={{0,16},{4,20},{8,24},{12,28},{16,0},{20,4},{24,8},{28,12},{1,17},{... | collective-permute-start | bytes 491528 | tf_op jit(solution)/shard_map/cond/branch_1_fun/ppermute | solution.py:196
  42.6 2.2 %collective-permute-done.7 = bf16[64,1280]{1,0:T(8,128)(2,1)} collective-permute-done((bf16[64,1280]{1,0:T(8,128)(2,1)S(1)}, bf16[64,1280]{1,0:T(8,128)(2,1)}, u32[]{:S(2)}, u32[]{:S(2)}) %collective-permute-start.7) | collective-permute-done | bytes 163872 | tf_op jit(solution)/shard_map/cond/branch_1_fun/ppermute | solution.py:196
  44.9 2.4 %collective-permute-done.9 = bf16[64,1280]{1,0:T(8,128)(2,1)} collective-permute-done((bf16[64,1280]{1,0:T(8,128)(2,1)S(1)}, bf16[64,1280]{1,0:T(8,128)(2,1)}, u32[]{:S(2)}, u32[]{:S(2)}) %collective-permute-start.9) | collective-permute-done | bytes 163872 | tf_op jit(solution)/shard_map/cond/branch_1_fun/ppermute | solution.py:196
  47.8 1.5 %collective-permute-done.10 = bf16[128,1280]{1,0:T(8,128)(2,1)} collective-permute-done((bf16[128,1280]{1,0:T(8,128)(2,1)}, bf16[128,1280]{1,0:T(8,128)(2,1)}, u32[]{:S(2)}, u32[]{:S(2)}) %collective-permute-start.10) | collective-permute-done | bytes 327712 | tf_op jit(solution)/shard_map/cond/branch_1_fun/ppermute | solution.py:196
  49.5 1.5 %collective-permute-done.12 = bf16[64,1280]{1,0:T(8,128)(2,1)} collective-permute-done((bf16[64,1280]{1,0:T(8,128)(2,1)}, bf16[64,1280]{1,0:T(8,128)(2,1)}, u32[]{:S(2)}, u32[]{:S(2)}) %collective-permute-start.12) | collective-permute-done | bytes 163872 | tf_op jit(solution)/shard_map/cond/branch_1_fun/ppermute | solution.py:196
  51.0 1.0 %copy-done.2 = bf16[128,1280]{1,0:T(8,128)(2,1)S(1)} copy-done((bf16[128,1280]{1,0:T(8,128)(2,1)S(1)}, bf16[128,1280]{1,0:T(8,128)(2,1)}, u32[]{:S(2)}) %copy-start.2) | copy-done | bytes 327704
  52.0 3.3 %accumulate.1 = (bf16[1024,1024]{1,0:T(8,128)(2,1)S(1)}, f32[1024,768]{1,0:T(8,128)S(1)}) custom-call(s32[4,4]{1,0:T(4,128)S(1)} %copy-done.3, bf16[1024,768]{1,0:T(8,128)(2,1)S(1)} %stage.1.noise_ref, bf16[128,1280]{1,0:T(8,128)(2,1)S(1)} %pad_maximum_fusion.refs_0_, bf16[128,1280]{1,0:T(8,128)(2,1)S(1)} %copy-done.2, ...), custom_call_target="tpu_custom_call" | custom-call | flops 1207959552 | bytes 9175040 | tf_op jit(solution)/shard_map/accumulate/pallas_call | solution.py:130
  55.3 3.6 %finish.1 = f32[1024,768]{1,0:T(8,128)} custom-call(s32[4,4]{1,0:T(4,128)S(1)} %copy-done.3, bf16[1024,1024]{1,0:T(8,128)(2,1)S(1)} %get-tuple-element.71.u_ref, f32[1024,768]{1,0:T(8,128)S(1)} %get-tuple-element.72.sum_ref, f32[1024,1]{1,0:T(8,128)S(1)} %copy.7.skew_ref, f32[1024,1]{1,0:T(8,128)S(1)} %copy.8.tail_ref, ...), custom_call_target="tpu_custom_call" | custom-call | flops 805306368 | bytes 12058624 | tf_op jit(solution)/shard_map/finish/pallas_call | solution.py:175
  (49 shorter events, 5.4 us)
Async XLA Ops:
  0.0 7.8 %copy-start.4 = (bf16[1,128,1024]{2,1,0:T(8,128)(2,1)S(1)}, bf16[1,128,1024]{2,1,0:T(8,128)(2,1)}, u32[]{:S(2)}) copy-start(bf16[1,128,1024]{2,1,0:T(8,128)(2,1)} %param.12) | copy-start | bytes 786436
  1.0 6.9 %collective-permute-start.13 = (bf16[128,256]{1,0:T(8,128)(2,1)S(1)}, bf16[128,256]{1,0:T(8,128)(2,1)S(1)}, u32[]{:S(2)}, u32[]{:S(2)}) collective-permute-start(bf16[128,256]{1,0:T(8,128)(2,1)S(1)} %get-tuple-element.76.refs_0_), channel_id=1, source_target_pairs={{0,24},{4,28},{8,16},{12,20},{16,8},{20,12},{24,0},{28,4},{1,25},{... | collective-permute-start | bytes 196616 | tf_op jit(solution)/shard_map/ppermute | solution.py:196
  5.0 4.3 %collective-permute-start.14 = (bf16[128,256]{1,0:T(8,128)(2,1)S(1)}, bf16[128,256]{1,0:T(8,128)(2,1)S(1)}, u32[]{:S(2)}, u32[]{:S(2)}) collective-permute-start(bf16[128,256]{1,0:T(8,128)(2,1)S(1)} %get-tuple-element.76.refs_0_), channel_id=1, source_target_pairs={{0,8},{4,12},{8,0},{12,4},{16,24},{20,28},{24,16},{28,20},{1,9},{5... | collective-permute-start | bytes 196616 | tf_op jit(solution)/shard_map/ppermute | solution.py:196
  5.5 4.3 %collective-permute-start.15 = (bf16[128,256]{1,0:T(8,128)(2,1)S(1)}, bf16[128,256]{1,0:T(8,128)(2,1)S(1)}, u32[]{:S(2)}, u32[]{:S(2)}) collective-permute-start(bf16[128,256]{1,0:T(8,128)(2,1)S(1)} %get-tuple-element.76.refs_0_), channel_id=1, source_target_pairs={{0,16},{4,20},{8,24},{12,28},{16,0},{20,4},{24,8},{28,12},{1,17},{... | collective-permute-start | bytes 196616 | tf_op jit(solution)/shard_map/ppermute | solution.py:196
  5.6 4.2 %collective-permute-start.16 = (bf16[128,256]{1,0:T(8,128)(2,1)S(1)}, bf16[128,256]{1,0:T(8,128)(2,1)S(1)}, u32[]{:S(2)}, u32[]{:S(2)}) collective-permute-start(bf16[128,256]{1,0:T(8,128)(2,1)S(1)} %get-tuple-element.76.refs_0_), channel_id=1, source_target_pairs={{0,4},{4,0},{8,12},{12,8},{16,20},{20,16},{24,28},{28,24},{1,5},{5... | collective-permute-start | bytes 196616 | tf_op jit(solution)/shard_map/ppermute | solution.py:196
  5.6 1.4 %copy-start = (bf16[1024,768]{1,0:T(8,128)(2,1)S(1)}, bf16[1024,768]{1,0:T(8,128)(2,1)}, u32[]{:S(2)}) copy-start(bf16[1024,768]{1,0:T(8,128)(2,1)} %from_ref.1) | copy-start | bytes 4718596
  7.8 7.4 %copy-start.3 = (s32[4,4]{1,0:T(4,128)S(1)}, s32[4,4]{1,0:T(4,128)}, u32[]{:S(2)}) copy-start(s32[4,4]{1,0:T(4,128)} %ranks_ref.3) | copy-start | bytes 196
  7.9 1.9 %collective-permute-start.19 = (bf16[128,256]{1,0:T(8,128)(2,1)S(1)}, bf16[128,256]{1,0:T(8,128)(2,1)S(1)}, u32[]{:S(2)}, u32[]{:S(2)}) collective-permute-start(bf16[128,256]{1,0:T(8,128)(2,1)S(1)} %collective-permute-done.13.refs_3_), channel_id=1, source_target_pairs={{0,4},{4,0},{8,12},{12,8},{16,20},{20,16},{24,28},{28,24},{1,5},{5... | collective-permute-start | bytes 196616 | tf_op jit(solution)/shard_map/ppermute | solution.py:196
  9.2 1.3 %collective-permute-start.17 = (bf16[128,256]{1,0:T(8,128)(2,1)S(1)}, bf16[128,256]{1,0:T(8,128)(2,1)S(1)}, u32[]{:S(2)}, u32[]{:S(2)}) collective-permute-start(bf16[128,256]{1,0:T(8,128)(2,1)S(1)} %collective-permute-done.14.refs_1_), channel_id=1, source_target_pairs={{0,4},{4,0},{8,12},{12,8},{16,20},{20,16},{24,28},{28,24},{1,5},{5... | collective-permute-start | bytes 196616 | tf_op jit(solution)/shard_map/ppermute | solution.py:196
  9.8 1.3 %collective-permute-start.18 = (bf16[128,256]{1,0:T(8,128)(2,1)S(1)}, bf16[128,256]{1,0:T(8,128)(2,1)S(1)}, u32[]{:S(2)}, u32[]{:S(2)}) collective-permute-start(bf16[128,256]{1,0:T(8,128)(2,1)S(1)} %collective-permute-done.15.refs_2_), channel_id=1, source_target_pairs={{0,4},{4,0},{8,12},{12,8},{16,20},{20,16},{24,28},{28,24},{1,5},{5... | collective-permute-start | bytes 196616 | tf_op jit(solution)/shard_map/ppermute | solution.py:196
  12.4 24.1 %copy-start.5 = (f32[1024]{0:T(1024)S(1)}, f32[1024]{0:T(1024)}, u32[]{:S(2)}) copy-start(f32[1024]{0:T(1024)} %param.14) | copy-start | bytes 12292
  12.4 4.0 %collective-permute-start.20 = (bf16[128,1280]{1,0:T(8,128)(2,1)S(1)}, bf16[128,1280]{1,0:T(8,128)(2,1)S(1)}, u32[]{:S(2)}, u32[]{:S(2)}) collective-permute-start(bf16[128,1280]{1,0:T(8,128)(2,1)S(1)} %pad_maximum_fusion.refs_0_), channel_id=1, source_target_pairs={{0,4},{4,0},{8,12},{12,8},{16,20},{20,16},{24,28},{28,24},{1,5},{5... | collective-permute-start | bytes 983048 | tf_op jit(solution)/shard_map/ppermute | solution.py:196
  12.6 38.4 %collective-permute-start.23 = (bf16[256,768]{1,0:T(8,128)(2,1)}, bf16[256,768]{1,0:T(8,128)(2,1)}, u32[]{:S(2)}, u32[]{:S(2)}) collective-permute-start(bf16[256,768]{1,0:T(8,128)(2,1)} %project_1.1), channel_id=1, source_target_pairs={{0,2},{1,3},{2,0},{3,1},{4,6},{5,7},{6,4},{7,5},{8,10},{9,11},{10,... | collective-permute-start | bytes 1179656 | tf_op jit(solution)/shard_map/ppermute | solution.py:266
  16.5 20.1 %copy-start.1 = (bf16[128,1280]{1,0:T(8,128)(2,1)}, bf16[128,1280]{1,0:T(8,128)(2,1)S(1)}, u32[]{:S(2)}) copy-start(bf16[128,1280]{1,0:T(8,128)(2,1)S(1)} %collective-permute-done.20.refs_1_) | copy-start | bytes 983044
  16.5 20.3 %copy-start.6 = (f32[1024]{0:T(1024)S(1)}, f32[1024]{0:T(1024)}, u32[]{:S(2)}) copy-start(f32[1024]{0:T(1024)} %param.15) | copy-start | bytes 12292
  16.5 6.0 %collective-permute-start.1 = (bf16[128,512]{1,0:T(8,128)(2,1)S(1)}, bf16[128,512]{1,0:T(8,128)(2,1)}, u32[]{:S(2)}, u32[]{:S(2)}) collective-permute-start(bf16[128,512]{1,0:T(8,128)(2,1)S(1)} %param.1), channel_id=1, source_target_pairs={{0,8},{4,12},{8,0},{12,4},{16,24},{20,28},{24,16},{28,20},{1,9},{5... | collective-permute-start | bytes 393224 | tf_op jit(solution)/shard_map/cond/branch_1_fun/ppermute | solution.py:196
  18.1 8.1 %collective-permute-start.3 = (bf16[128,512]{1,0:T(8,128)(2,1)S(1)}, bf16[128,512]{1,0:T(8,128)(2,1)}, u32[]{:S(2)}, u32[]{:S(2)}) collective-permute-start(bf16[128,512]{1,0:T(8,128)(2,1)S(1)} %param.1), channel_id=1, source_target_pairs={{0,16},{4,20},{8,24},{12,28},{16,0},{20,4},{24,8},{28,12},{1,17},{... | collective-permute-start | bytes 393224 | tf_op jit(solution)/shard_map/cond/branch_1_fun/ppermute | solution.py:196
  19.1 7.1 %collective-permute-start.5 = (bf16[128,512]{1,0:T(8,128)(2,1)S(1)}, bf16[128,512]{1,0:T(8,128)(2,1)}, u32[]{:S(2)}, u32[]{:S(2)}) collective-permute-start(bf16[128,512]{1,0:T(8,128)(2,1)S(1)} %param.1), channel_id=1, source_target_pairs={{0,24},{4,28},{8,16},{12,20},{16,8},{20,12},{24,0},{28,4},{1,25},{... | collective-permute-start | bytes 393224 | tf_op jit(solution)/shard_map/cond/branch_1_fun/ppermute | solution.py:196
  20.1 6.6 %collective-permute-start = (bf16[128,512]{1,0:T(8,128)(2,1)S(1)}, bf16[128,512]{1,0:T(8,128)(2,1)}, u32[]{:S(2)}, u32[]{:S(2)}) collective-permute-start(bf16[128,512]{1,0:T(8,128)(2,1)S(1)} %param.1), channel_id=1, source_target_pairs={{0,4},{4,0},{8,12},{12,8},{16,20},{20,16},{24,28},{28,24},{1,5},{5... | collective-permute-start | bytes 393224 | tf_op jit(solution)/shard_map/cond/branch_1_fun/ppermute | solution.py:196
  22.5 4.2 %collective-permute-start.2 = (bf16[128,512]{1,0:T(8,128)(2,1)}, bf16[128,512]{1,0:T(8,128)(2,1)}, u32[]{:S(2)}, u32[]{:S(2)}) collective-permute-start(bf16[128,512]{1,0:T(8,128)(2,1)} %collective-permute-done.1), channel_id=1, source_target_pairs={{0,4},{4,0},{8,12},{12,8},{16,20},{20,16},{24,28},{28,24},{1,5},{5... | collective-permute-start | bytes 393224 | tf_op jit(solution)/shard_map/cond/branch_1_fun/ppermute | solution.py:196
  26.2 1.7 %collective-permute-start.4 = (bf16[128,512]{1,0:T(8,128)(2,1)}, bf16[128,512]{1,0:T(8,128)(2,1)}, u32[]{:S(2)}, u32[]{:S(2)}) collective-permute-start(bf16[128,512]{1,0:T(8,128)(2,1)} %collective-permute-done.3), channel_id=1, source_target_pairs={{0,4},{4,0},{8,12},{12,8},{16,20},{20,16},{24,28},{28,24},{1,5},{5... | collective-permute-start | bytes 393224 | tf_op jit(solution)/shard_map/cond/branch_1_fun/ppermute | solution.py:196
  26.2 1.9 %collective-permute-start.6 = (bf16[128,512]{1,0:T(8,128)(2,1)}, bf16[128,512]{1,0:T(8,128)(2,1)}, u32[]{:S(2)}, u32[]{:S(2)}) collective-permute-start(bf16[128,512]{1,0:T(8,128)(2,1)} %collective-permute-done.5), channel_id=1, source_target_pairs={{0,4},{4,0},{8,12},{12,8},{16,20},{20,16},{24,28},{28,24},{1,5},{5... | collective-permute-start | bytes 393224 | tf_op jit(solution)/shard_map/cond/branch_1_fun/ppermute | solution.py:196
  28.1 10.0 %collective-permute-start.21 = (bf16[128,1280]{1,0:T(8,128)(2,1)S(1)}, bf16[128,1280]{1,0:T(8,128)(2,1)}, u32[]{:S(2)}, u32[]{:S(2)}) collective-permute-start(bf16[128,1280]{1,0:T(8,128)(2,1)S(1)} %pad_maximum_fusion.refs_0_), channel_id=1, source_target_pairs={{0,8},{4,12},{8,0},{12,4},{16,24},{20,28},{24,16},{28,20},{1,9},{5... | collective-permute-start | bytes 983048 | tf_op jit(solution)/shard_map/ppermute | solution.py:196
  28.4 9.7 %collective-permute-start.22 = (bf16[128,1280]{1,0:T(8,128)(2,1)S(1)}, bf16[128,1280]{1,0:T(8,128)(2,1)}, u32[]{:S(2)}, u32[]{:S(2)}) collective-permute-start(bf16[128,1280]{1,0:T(8,128)(2,1)S(1)} %pad_maximum_fusion.refs_0_), channel_id=1, source_target_pairs={{0,16},{4,20},{8,24},{12,28},{16,0},{20,4},{24,8},{28,12},{1,17},{... | collective-permute-start | bytes 983048 | tf_op jit(solution)/shard_map/ppermute | solution.py:196
  32.7 22.6 %collective-permute-start.24 = (bf16[256,768]{1,0:T(8,128)(2,1)}, bf16[256,768]{1,0:T(8,128)(2,1)S(1)}, u32[]{:S(2)}, u32[]{:S(2)}) collective-permute-start(bf16[256,768]{1,0:T(8,128)(2,1)} %get-tuple-element.60), channel_id=1, source_target_pairs={{0,1},{1,2},{2,3},{3,0},{4,5},{5,6},{6,7},{7,4},{8,9},{9,10},{10,1... | collective-permute-start | bytes 1179656 | tf_op jit(solution)/shard_map/ppermute | solution.py:266
  34.3 21.0 %collective-permute-start.25 = (bf16[256,768]{1,0:T(8,128)(2,1)}, bf16[256,768]{1,0:T(8,128)(2,1)}, u32[]{:S(2)}, u32[]{:S(2)}) collective-permute-start(bf16[256,768]{1,0:T(8,128)(2,1)} %get-tuple-element.73), channel_id=1, source_target_pairs={{0,3},{1,0},{2,1},{3,2},{4,7},{5,4},{6,5},{7,6},{8,11},{9,8},{10,9... | collective-permute-start | bytes 1179656 | tf_op jit(solution)/shard_map/ppermute | solution.py:266
  39.1 5.8 %collective-permute-start.7 = (bf16[64,1280]{1,0:T(8,128)(2,1)S(1)}, bf16[64,1280]{1,0:T(8,128)(2,1)}, u32[]{:S(2)}, u32[]{:S(2)}) collective-permute-start(bf16[64,1280]{1,0:T(8,128)(2,1)S(1)} %slice.6), channel_id=1, source_target_pairs={{0,8},{4,12},{8,0},{12,4},{16,24},{20,28},{24,16},{28,20},{1,9},{5... | collective-permute-start | bytes 491528 | tf_op jit(solution)/shard_map/cond/branch_1_fun/ppermute | solution.py:196
  41.8 5.5 %collective-permute-start.9 = (bf16[64,1280]{1,0:T(8,128)(2,1)S(1)}, bf16[64,1280]{1,0:T(8,128)(2,1)}, u32[]{:S(2)}, u32[]{:S(2)}) collective-permute-start(bf16[64,1280]{1,0:T(8,128)(2,1)S(1)} %slice.7), channel_id=1, source_target_pairs={{0,16},{4,20},{8,24},{12,28},{16,0},{20,4},{24,8},{28,12},{1,17},{... | collective-permute-start | bytes 491528 | tf_op jit(solution)/shard_map/cond/branch_1_fun/ppermute | solution.py:196
  44.9 2.4 %collective-permute-start.8 = (bf16[128,1280]{1,0:T(8,128)(2,1)}, bf16[128,1280]{1,0:T(8,128)(2,1)}, u32[]{:S(2)}, u32[]{:S(2)}) collective-permute-start(bf16[128,1280]{1,0:T(8,128)(2,1)} %get-tuple-element.12), channel_id=1, source_target_pairs={{0,4},{4,0},{8,12},{12,8},{16,20},{20,16},{24,28},{28,24},{1,5},{5... | collective-permute-start | bytes 983048 | tf_op jit(solution)/shard_map/cond/branch_1_fun/ppermute | solution.py:196
  47.3 2.0 %collective-permute-start.10 = (bf16[128,1280]{1,0:T(8,128)(2,1)}, bf16[128,1280]{1,0:T(8,128)(2,1)}, u32[]{:S(2)}, u32[]{:S(2)}) collective-permute-start(bf16[128,1280]{1,0:T(8,128)(2,1)} %get-tuple-element.13), channel_id=1, source_target_pairs={{0,4},{4,0},{8,12},{12,8},{16,20},{20,16},{24,28},{28,24},{1,5},{5... | collective-permute-start | bytes 983048 | tf_op jit(solution)/shard_map/cond/branch_1_fun/ppermute | solution.py:196
  47.3 2.2 %collective-permute-start.11 = (bf16[64,1280]{1,0:T(8,128)(2,1)}, bf16[64,1280]{1,0:T(8,128)(2,1)}, u32[]{:S(2)}, u32[]{:S(2)}) collective-permute-start(bf16[64,1280]{1,0:T(8,128)(2,1)} %collective-permute-done.7), channel_id=1, source_target_pairs={{0,4},{4,0},{8,12},{12,8},{16,20},{20,16},{24,28},{28,24},{1,5},{5... | collective-permute-start | bytes 491528 | tf_op jit(solution)/shard_map/cond/branch_1_fun/ppermute | solution.py:196
  49.3 1.7 %collective-permute-start.12 = (bf16[64,1280]{1,0:T(8,128)(2,1)}, bf16[64,1280]{1,0:T(8,128)(2,1)}, u32[]{:S(2)}, u32[]{:S(2)}) collective-permute-start(bf16[64,1280]{1,0:T(8,128)(2,1)} %collective-permute-done.9), channel_id=1, source_target_pairs={{0,4},{4,0},{8,12},{12,8},{16,20},{20,16},{24,28},{28,24},{1,5},{5... | collective-permute-start | bytes 491528 | tf_op jit(solution)/shard_map/cond/branch_1_fun/ppermute | solution.py:196
  (1 other events, 1.0 us)

commit v8 on v7

--- a/solution.py
+++ b/solution.py
@@ -211,41 +211,14 @@
     return pieces
 
 
-def neighbour_distances():
-    return (2, 4) if lax.axis_size("real") == 8 else ()
-
-
 def direct_rest(chunk):
     pieces = with_other_core(from_chips(chunk))
     del pieces[0, 0]
     return pieces
 
 
-def relayed_rest(pieces):
-    if (2, 0) not in pieces:
-        return two_at_a_time(pieces)
-    first, second = pieces[2, 0], pieces[4, 0]
-    half = first.shape[0] // 2
-    one, two = swap(second[:half], 2), swap(first[half:], 4)
-    more = {(6, 0): one, (6, half): two}
-    more[3, 0], more[5, 0] = swap(after(first, one), 1), swap(after(second, two), 1)
-    more[7, 0], more[7, half] = swap(after(one, more[3, 0]), 1), swap(after(two, more[5, 0]), 1)
-    return more
-
-
-def two_at_a_time(pieces):
-    known, pieces = pieces, dict(pieces)
-    own = pieces[0, 0]
-    distances = range(2, lax.axis_size("real"), 2)
-    tails = [own, own]
-    for turn, distance in enumerate(distances):
-        tails[turn % 2] = pieces[distance, 0] = swap(after(own, tails[turn % 2]), distance)
-    last, tail = distances[-1], tails[len(distances) % 2]
-    for distance in (0, *distances):
-        if distance != last and (distance ^ 1, 0) not in known:
-            tail = pieces[distance ^ 1, 0] = swap(after(pieces[distance, 0], tail), 1)
-    pieces[last ^ 1, 0] = swap(pieces[last, 0], 1)
-    return {place: pieces[place] for place in pieces if place not in known}
+def from_other_core(pieces):
+    return {place: array for place, array in with_other_core(pieces).items() if place not in pieces}
 
 
 def at_once(present, gather, *args):
@@ -286,19 +259,20 @@
     v_first = from_chips(v_first)
     last = max(v_first)
     waiting = (v_first[last], stage(noise), v_rest, own_and_u)
-    v_first[last], noise, v_rest, own_and_u = lax.optimization_barrier(waiting)
+    v_first[last], noise_here, v_rest, own_and_u = lax.optimization_barrier(waiting)
     present = ranks[0, 0] > 0
-    [far] = project(1, noise, with_other_core(v_first).items())
-    v_rest = after(v_rest, far)
-    u_pieces = {(0, 0): own_and_u, (1, 0): swap(after(own_and_u, far), 1)}
-    v_pieces = {(0, 0): after(v_rest, u_pieces[1, 0])}
-    v_pieces.update(at_once(present, direct_rest, v_pieces[0, 0]))
-    for distance in neighbour_distances():
-        u_pieces[distance, 0] = swap(after(own_and_u, v_pieces), distance)
-    others = project(len(rest), noise, v_pieces.items())
+    noise_here, present = lax.optimization_barrier((noise_here, present))
+    [far] = project(1, noise_here, with_other_core(v_first).items())
+
+    u_swapped = swap(after(own_and_u, far), 1)
+    v_rest = after(v_rest, far, u_swapped)
+    v_pieces = {(0, 0): v_rest, **at_once(present, direct_rest, v_rest)}
+    u_pieces = from_chips(after(own_and_u, v_pieces))
+    others = project(len(rest), noise_here, v_pieces.items())
     far = along_site(far, first)
-    u_pieces = after(u_pieces, others[0])
-    u_pieces.update(at_once(present, relayed_rest, u_pieces))
+    others = after(others, far)
+    u_pieces = {**u_pieces, (1, 0): u_swapped}
+    u_pieces.update(at_once(present, from_other_core, u_pieces))
     others = [along_site(coef, shift) for coef, shift in zip(others, rest)]
     u_whole, total = accumulate((first,), ranks, noise, u_pieces.items(), [far])
     return finish(rest, ranks, u_whole, total, skew_g[:, None], tail_h[:, None], others)

time: 59.2 us -> 59.2 us (level)
  local copies, waits for them, and re-layouts: 6.29 us -> 4.35 us
  waiting for transfers between devices: 18.8 us -> 20.7 us
  other arithmetic: 0.03 us -> 0.68 us
    ppermute x3, waiting for transfers between devices: 0.01 us -> 2.34 us  [along_site(): lax.ppermute(coef, 'site', [(k, (k + shift) % count) for k in range(count)])]
    slice x2 -> x0, local copies, waits for them, and re-layouts: 1.85 us -> none  [relayed_rest(): one, two = (swap(second[:half], 2), swap(first[half:], 4))]
    concatenate x1, other arithmetic: 0.01 us -> 0.65 us  [per_device(): v_rest = jnp.concatenate([columns_for(shift) for shift in rest], axis=1)]
    ppermute x23 -> x21, starting transfers between devices: 14.3 us -> 13.8 us  [swap(): lax.ppermute(array, 'real', [(k, k ^ distance) for k in range(count)])]
    ppermute x23 -> x21, waiting for transfers between devices: 18.8 us -> 18.4 us  [swap(): lax.ppermute(array, 'real', [(k, k ^ distance) for k in range(count)])]
    unnamed x14 -> x16, local copies, waits for them, and re-layouts: 2.41 us -> 2.4 us
  transfers between devices with their start and end apart: 26 -> 24, of which waited for: 14 -> 12; matrix products, arithmetic and copies ran while one was open for 5% -> 3% of each run, Pallas kernels for 12% -> 12%
where the time goes in v8:
time: 59.2 us; the launch traced here: 59 us
  waiting for transfers between devices  20.7 us (35%)
  starting transfers between devices  20.2 us (34%)
  Pallas kernels  12.2 us (21%)
  local copies, waits for them, and re-layouts  4.35 us (7%)
  between operations  0.78 us (1%)
  other arithmetic  0.68 us (1%)
    ppermute x21, waiting for transfers between devices, swap(): lax.ppermute(array, 'real', [(k, k ^ distance) for k in range(count)])  18.4 us
    ppermute x21, starting transfers between devices, swap(): lax.ppermute(array, 'real', [(k, k ^ distance) for k in range(count)])  13.8 us
    ppermute x3, starting transfers between devices, along_site(): lax.ppermute(coef, 'site', [(k, (k + shift) % count) for k in range(count)])  6.41 us
    pallas_call x2, Pallas kernels, project(): pl.pallas_call(functools.partial(project_kernel, places, rows), out_shape...  4.55 us
    pallas_call x1, Pallas kernels, finish(): pl.pallas_call(functools.partial(finish_kernel, shifts), out_shape=jax.Sh...  3.58 us
    pallas_call x1, Pallas kernels, accumulate(): pl.pallas_call(functools.partial(accumulate_kernel, shifts, places, rows)...  3.31 us
    unnamed x16, local copies, waits for them, and re-layouts  2.4 us
    ppermute x3, waiting for transfers between devices, along_site(): lax.ppermute(coef, 'site', [(k, (k + shift) % count) for k in range(count)])  2.34 us
  transfers between devices with their start and end apart: 24, of which 12 were waited for; matrix products, arithmetic and copies ran while one was open for 3% of the time, Pallas kernels for 12%

profile of v8, /device:TPU:0, one launch (start us, length us, event | category | flops | bytes accessed | tf_op | source)
XLA Modules:
  0.0 59.0 jit_solution(17292496701011972145)
XLA Ops:
  0.0 1.0 %dynamic-slice_bitcast_fusion = (bf16[128,256]{1,0:T(8,128)(2,1)S(1)}, bf16[128,256]{1,0:T(8,128)(2,1)S(1)}, bf16[128,256]{1,0:T(8,128)(2,1)S(1)}, bf16[128,256]{1,0:T(8,128)(2,1)S(1)}) fusion(bf16[1,128,1024]{2,1,0:T(8,128)(2,1)} %param.11, s32[]{:T(128)S(6)} %select_n.15, s32[]{:T(128)S(6)} %select_n.13, s32[]{:T(128)S(6)} %select_n.12, s32[]{:T(128)S(6)} %select_n.14), kind=kLoop, calls=%fused_computation.2 | loop fusion | bytes 524304 | tf_op jit(solution)/shard_map/dynamic_slice | solution.py:254
  1.0 0.5 collective-permute-start.13
  1.5 2.6 %collective-permute-start.12 = (bf16[128,256]{1,0:T(8,128)(2,1)S(1)}, bf16[128,256]{1,0:T(8,128)(2,1)S(1)}, u32[]{:S(2)}, u32[]{:S(2)}) collective-permute-start(bf16[128,256]{1,0:T(8,128)(2,1)S(1)} %get-tuple-element.67.refs_0_), channel_id=1, source_target_pairs={{0,16},{4,20},{8,24},{12,28},{16,0},{20,4},{24,8},{28,12},{1,17},{... | collective-permute-start | bytes 196616 | tf_op jit(solution)/shard_map/ppermute | solution.py:196
  4.1 1.5 %collective-permute-start.11 = (bf16[128,256]{1,0:T(8,128)(2,1)S(1)}, bf16[128,256]{1,0:T(8,128)(2,1)S(1)}, u32[]{:S(2)}, u32[]{:S(2)}) collective-permute-start(bf16[128,256]{1,0:T(8,128)(2,1)S(1)} %get-tuple-element.67.refs_0_), channel_id=1, source_target_pairs={{0,8},{4,12},{8,0},{12,4},{16,24},{20,28},{24,16},{28,20},{1,9},{5... | collective-permute-start | bytes 196616 | tf_op jit(solution)/shard_map/ppermute | solution.py:196
  5.7 1.4 %copy-done = bf16[1024,768]{1,0:T(8,128)(2,1)S(1)} copy-done((bf16[1024,768]{1,0:T(8,128)(2,1)S(1)}, bf16[1024,768]{1,0:T(8,128)(2,1)}, u32[]{:S(2)}) %copy-start) | copy-done | bytes 1572888
  7.1 0.8 %stage.1.noise_ref = bf16[1024,768]{1,0:T(8,128)(2,1)S(1)} custom-call(bf16[1024,768]{1,0:T(8,128)(2,1)S(1)} %copy-done), custom_call_target="tpu_custom_call" | custom-call | bytes 3145728 | tf_op jit(solution)/shard_map/stage/pallas_call | solution.py:83
  7.9 0.7 %pad_maximum_fusion.1.refs_0_ = bf16[128,512]{1,0:T(8,128)(2,1)} fusion(bf16[128,256]{1,0:T(8,128)(2,1)S(1)} %get-tuple-element.68, bf16[128,256]{1,0:T(8,128)(2,1)S(1)} %get-tuple-element.66), kind=kLoop, calls=%fused_computation.1 | loop fusion | flops 262144 | bytes 262144 | tf_op jit(solution)/shard_map/concatenate | solution.py:257
  8.6 2.2 %collective-permute-done.10.refs_3_ = bf16[128,256]{1,0:T(8,128)(2,1)S(1)} collective-permute-done((bf16[128,256]{1,0:T(8,128)(2,1)S(1)}, bf16[128,256]{1,0:T(8,128)(2,1)S(1)}, u32[]{:S(2)}, u32[]{:S(2)}) %collective-permute-start.10) | collective-permute-done | bytes 65568 | tf_op jit(solution)/shard_map/ppermute | solution.py:196
  10.8 0.5 collective-permute-start.14
  11.4 0.5 slice.3
  12.6 1.4 %project_1.1 = bf16[256,768]{1,0:T(8,128)(2,1)} custom-call(bf16[1024,768]{1,0:T(8,128)(2,1)S(1)} %stage.1.noise_ref, bf16[128,256]{1,0:T(8,128)(2,1)S(1)} %get-tuple-element.67.refs_0_, bf16[128,256]{1,0:T(8,128)(2,1)S(1)} %collective-permute-done.11.refs_1_, bf16[128,256]{1,0:T(8,128)(2,1)S(1)} %collective-permute-done.12.refs_2_, ...), custom_call_target="tpu_custom_call" | custom-call | flops 402653184 | bytes 4194304 | tf_op jit(solution)/shard_map/project_1/pallas_call | solution.py:56
  14.4 2.6 %collective-permute-start.21 = (bf16[256,768]{1,0:T(8,128)(2,1)}, bf16[256,768]{1,0:T(8,128)(2,1)}, u32[]{:S(2)}, u32[]{:S(2)}) collective-permute-start(bf16[256,768]{1,0:T(8,128)(2,1)} %project_1.1), channel_id=1, source_target_pairs={{0,2},{1,3},{2,0},{3,1},{4,6},{5,7},{6,4},{7,5},{8,10},{9,11},{10,... | collective-permute-start | bytes 1179656 | tf_op jit(solution)/shard_map/ppermute | solution.py:239
  17.0 11.2 %conditional.2 = (bf16[128,512]{1,0:T(8,128)(2,1)}, bf16[128,512]{1,0:T(8,128)(2,1)}, bf16[128,512]{1,0:T(8,128)(2,1)}, bf16[128,512]{1,0:T(8,128)(2,1)}, bf16[1...) conditional(s32[]{:T(128)} %convert_element_type.4, () %tuple.31, ...), branch_computations={%region_0.0_spmd, %region_1.0_spmd} | conditional | bytes 3670352 | solution.py:234
  17.0 1.4 %collective-permute-start.5 = (bf16[128,512]{1,0:T(8,128)(2,1)}, bf16[128,512]{1,0:T(8,128)(2,1)}, u32[]{:S(2)}, u32[]{:S(2)}) collective-permute-start(bf16[128,512]{1,0:T(8,128)(2,1)} %param.1), channel_id=1, source_target_pairs={{0,24},{4,28},{8,16},{12,20},{16,8},{20,12},{24,0},{28,4},{1,25},{... | collective-permute-start | bytes 393224 | tf_op jit(solution)/shard_map/cond/branch_1_fun/ppermute | solution.py:196
  18.4 0.7 %collective-permute-start.3 = (bf16[128,512]{1,0:T(8,128)(2,1)}, bf16[128,512]{1,0:T(8,128)(2,1)}, u32[]{:S(2)}, u32[]{:S(2)}) collective-permute-start(bf16[128,512]{1,0:T(8,128)(2,1)} %param.1), channel_id=1, source_target_pairs={{0,16},{4,20},{8,24},{12,28},{16,0},{20,4},{24,8},{28,12},{1,17},{... | collective-permute-start | bytes 393224 | tf_op jit(solution)/shard_map/cond/branch_1_fun/ppermute | solution.py:196
  19.1 1.5 %collective-permute-start.1 = (bf16[128,512]{1,0:T(8,128)(2,1)}, bf16[128,512]{1,0:T(8,128)(2,1)}, u32[]{:S(2)}, u32[]{:S(2)}) collective-permute-start(bf16[128,512]{1,0:T(8,128)(2,1)} %param.1), channel_id=1, source_target_pairs={{0,8},{4,12},{8,0},{12,4},{16,24},{20,28},{24,16},{28,20},{1,9},{5... | collective-permute-start | bytes 393224 | tf_op jit(solution)/shard_map/cond/branch_1_fun/ppermute | solution.py:196
  20.6 4.1 %collective-permute-done.5 = bf16[128,512]{1,0:T(8,128)(2,1)} collective-permute-done((bf16[128,512]{1,0:T(8,128)(2,1)}, bf16[128,512]{1,0:T(8,128)(2,1)}, u32[]{:S(2)}, u32[]{:S(2)}) %collective-permute-start.5) | collective-permute-done | bytes 131104 | tf_op jit(solution)/shard_map/cond/branch_1_fun/ppermute | solution.py:196
  24.7 1.6 %collective-permute-done.3 = bf16[128,512]{1,0:T(8,128)(2,1)} collective-permute-done((bf16[128,512]{1,0:T(8,128)(2,1)}, bf16[128,512]{1,0:T(8,128)(2,1)}, u32[]{:S(2)}, u32[]{:S(2)}) %collective-permute-start.3) | collective-permute-done | bytes 131104 | tf_op jit(solution)/shard_map/cond/branch_1_fun/ppermute | solution.py:196
  26.8 1.2 %collective-permute-done.4 = bf16[128,512]{1,0:T(8,128)(2,1)} collective-permute-done((bf16[128,512]{1,0:T(8,128)(2,1)}, bf16[128,512]{1,0:T(8,128)(2,1)}, u32[]{:S(2)}, u32[]{:S(2)}) %collective-permute-start.4) | collective-permute-done | bytes 131104 | tf_op jit(solution)/shard_map/cond/branch_1_fun/ppermute | solution.py:196
  28.2 1.3 %collective-permute-start.20 = (bf16[128,1280]{1,0:T(8,128)(2,1)S(1)}, bf16[128,1280]{1,0:T(8,128)(2,1)}, u32[]{:S(2)}, u32[]{:S(2)}) collective-permute-start(bf16[128,1280]{1,0:T(8,128)(2,1)S(1)} %pad_maximum_fusion.refs_0_), channel_id=1, source_target_pairs={{0,24},{4,28},{8,16},{12,20},{16,8},{20,12},{24,0},{28,4},{1,25},{... | collective-permute-start | bytes 983048 | tf_op jit(solution)/shard_map/ppermute | solution.py:196
  29.5 0.7 %collective-permute-start.19 = (bf16[128,1280]{1,0:T(8,128)(2,1)S(1)}, bf16[128,1280]{1,0:T(8,128)(2,1)}, u32[]{:S(2)}, u32[]{:S(2)}) collective-permute-start(bf16[128,1280]{1,0:T(8,128)(2,1)S(1)} %pad_maximum_fusion.refs_0_), channel_id=1, source_target_pairs={{0,16},{4,20},{8,24},{12,28},{16,0},{20,4},{24,8},{28,12},{1,17},{... | collective-permute-start | bytes 983048 | tf_op jit(solution)/shard_map/ppermute | solution.py:196
  30.2 1.5 %collective-permute-start.18 = (bf16[128,1280]{1,0:T(8,128)(2,1)S(1)}, bf16[128,1280]{1,0:T(8,128)(2,1)}, u32[]{:S(2)}, u32[]{:S(2)}) collective-permute-start(bf16[128,1280]{1,0:T(8,128)(2,1)S(1)} %pad_maximum_fusion.refs_0_), channel_id=1, source_target_pairs={{0,8},{4,12},{8,0},{12,4},{16,24},{20,28},{24,16},{28,20},{1,9},{5... | collective-permute-start | bytes 983048 | tf_op jit(solution)/shard_map/ppermute | solution.py:196
  31.7 3.1 %project_2.1 = (bf16[256,768]{1,0:T(8,128)(2,1)}, bf16[256,768]{1,0:T(8,128)(2,1)}) custom-call(bf16[1024,768]{1,0:T(8,128)(2,1)S(1)} %stage.1.noise_ref, bf16[128,512]{1,0:T(8,128)(2,1)} %pad_maximum_fusion.1.refs_0_, bf16[128,512]{1,0:T(8,128)(2,1)} %get-tuple-element.48.refs_1_, bf16[128,512]{1,0:T(8,128)(2,1)} %get-tuple-element.49.refs_2_, ...), custom_call_target="tpu_custom_call" | custom-call | flops 805306368 | bytes 5242880 | tf_op jit(solution)/shard_map/project_2/pallas_call | solution.py:56
  35.2 1.2 %collective-permute-start.22 = (bf16[256,768]{1,0:T(8,128)(2,1)}, bf16[256,768]{1,0:T(8,128)(2,1)S(1)}, u32[]{:S(2)}, u32[]{:S(2)}) collective-permute-start(bf16[256,768]{1,0:T(8,128)(2,1)} %get-tuple-element.63), channel_id=1, source_target_pairs={{0,1},{1,2},{2,3},{3,0},{4,5},{5,6},{6,7},{7,4},{8,9},{9,10},{10,1... | collective-permute-start | bytes 1179656 | tf_op jit(solution)/shard_map/ppermute | solution.py:239
  36.4 2.6 %collective-permute-start.23 = (bf16[256,768]{1,0:T(8,128)(2,1)}, bf16[256,768]{1,0:T(8,128)(2,1)}, u32[]{:S(2)}, u32[]{:S(2)}) collective-permute-start(bf16[256,768]{1,0:T(8,128)(2,1)} %get-tuple-element.64), channel_id=1, source_target_pairs={{0,3},{1,0},{2,1},{3,2},{4,7},{5,4},{6,5},{7,6},{8,11},{9,8},{10,9... | collective-permute-start | bytes 1179656 | tf_op jit(solution)/shard_map/ppermute | solution.py:239
  39.8 6.4 %collective-permute-done.19.refs_2_ = bf16[128,1280]{1,0:T(8,128)(2,1)} collective-permute-done((bf16[128,1280]{1,0:T(8,128)(2,1)S(1)}, bf16[128,1280]{1,0:T(8,128)(2,1)}, u32[]{:S(2)}, u32[]{:S(2)}) %collective-permute-start.19) | collective-permute-done | bytes 327712 | tf_op jit(solution)/shard_map/ppermute | solution.py:196
  46.2 2.9 %conditional.3 = (bf16[128,1280]{1,0:T(8,128)(2,1)}, bf16[128,1280]{1,0:T(8,128)(2,1)}, bf16[128,1280]{1,0:T(8,128)(2,1)}) conditional(s32[]{:T(128)} %convert_element_type.4, () %tuple.33, (bf16[128,1280]{1,0:T(8,128)(2,1)}, bf16[128,1280]{1,0:T(8,128)(2,1)}, bf16[128,1280]{1,0:T(8,128)(2,1)}) %tuple.34), branch_computations={%region_2.0_spmd, %region_3.0_spmd} | conditional | bytes 3932304 | solution.py:234
  46.7 1.4 %collective-permute-done.7 = bf16[128,1280]{1,0:T(8,128)(2,1)} collective-permute-done((bf16[128,1280]{1,0:T(8,128)(2,1)}, bf16[128,1280]{1,0:T(8,128)(2,1)}, u32[]{:S(2)}, u32[]{:S(2)}) %collective-permute-start.7) | collective-permute-done | bytes 327712 | tf_op jit(solution)/shard_map/cond/branch_1_fun/ppermute | solution.py:196
  49.1 1.0 %copy-done.3 = bf16[128,1280]{1,0:T(8,128)(2,1)S(1)} copy-done((bf16[128,1280]{1,0:T(8,128)(2,1)S(1)}, bf16[128,1280]{1,0:T(8,128)(2,1)}, u32[]{:S(2)}) %copy-start.3) | copy-done | bytes 327704
  50.1 3.3 %accumulate.1 = (bf16[1024,1024]{1,0:T(8,128)(2,1)S(1)}, f32[1024,768]{1,0:T(8,128)S(1)}) custom-call(s32[4,4]{1,0:T(4,128)S(1)} %copy-done.4, bf16[1024,768]{1,0:T(8,128)(2,1)S(1)} %copy-done.1, bf16[128,1280]{1,0:T(8,128)(2,1)S(1)} %pad_maximum_fusion.refs_0_, bf16[128,1280]{1,0:T(8,128)(2,1)} %collective-permute-done.18.refs_1_, ...), custom_call_target="tpu_custom_call" | custom-call | flops 1207959552 | bytes 9175040 | tf_op jit(solution)/shard_map/accumulate/pallas_call | solution.py:130
  53.4 2.0 %collective-permute-done.23.refs_1_ = bf16[256,768]{1,0:T(8,128)(2,1)} collective-permute-done((bf16[256,768]{1,0:T(8,128)(2,1)}, bf16[256,768]{1,0:T(8,128)(2,1)}, u32[]{:S(2)}, u32[]{:S(2)}) %collective-permute-start.23) | collective-permute-done | bytes 393248 | tf_op jit(solution)/shard_map/ppermute | solution.py:239
  55.4 3.6 %finish.1 = f32[1024,768]{1,0:T(8,128)} custom-call(s32[4,4]{1,0:T(4,128)S(1)} %copy-done.4, bf16[1024,1024]{1,0:T(8,128)(2,1)S(1)} %get-tuple-element.59.u_ref, f32[1024,768]{1,0:T(8,128)S(1)} %get-tuple-element.60.sum_ref, f32[1024,1]{1,0:T(8,128)S(1)} %copy.7.skew_ref, f32[1024,1]{1,0:T(8,128)S(1)} %copy.8.tail_ref, ...), custom_call_target="tpu_custom_call" | custom-call | flops 805306368 | bytes 12058624 | tf_op jit(solution)/shard_map/finish/pallas_call | solution.py:175
  (45 shorter events, 3.9 us)
Async XLA Ops:
  0.0 7.9 %copy-start.5 = (bf16[1,128,1024]{2,1,0:T(8,128)(2,1)S(1)}, bf16[1,128,1024]{2,1,0:T(8,128)(2,1)}, u32[]{:S(2)}) copy-start(bf16[1,128,1024]{2,1,0:T(8,128)(2,1)} %param.12) | copy-start | bytes 786436
  0.0 11.4 %copy-start.4 = (s32[4,4]{1,0:T(4,128)S(1)}, s32[4,4]{1,0:T(4,128)}, u32[]{:S(2)}) copy-start(s32[4,4]{1,0:T(4,128)} %ranks_ref.3) | copy-start | bytes 196
  1.0 11.5 %collective-permute-start.13 = (bf16[128,256]{1,0:T(8,128)(2,1)S(1)}, bf16[128,256]{1,0:T(8,128)(2,1)S(1)}, u32[]{:S(2)}, u32[]{:S(2)}) collective-permute-start(bf16[128,256]{1,0:T(8,128)(2,1)S(1)} %get-tuple-element.67.refs_0_), channel_id=1, source_target_pairs={{0,4},{4,0},{8,12},{12,8},{16,20},{20,16},{24,28},{28,24},{1,5},{5... | collective-permute-start | bytes 196616 | tf_op jit(solution)/shard_map/ppermute | solution.py:196
  1.5 9.3 %collective-permute-start.12 = (bf16[128,256]{1,0:T(8,128)(2,1)S(1)}, bf16[128,256]{1,0:T(8,128)(2,1)S(1)}, u32[]{:S(2)}, u32[]{:S(2)}) collective-permute-start(bf16[128,256]{1,0:T(8,128)(2,1)S(1)} %get-tuple-element.67.refs_0_), channel_id=1, source_target_pairs={{0,16},{4,20},{8,24},{12,28},{16,0},{20,4},{24,8},{28,12},{1,17},{... | collective-permute-start | bytes 196616 | tf_op jit(solution)/shard_map/ppermute | solution.py:196
  4.1 6.7 %collective-permute-start.11 = (bf16[128,256]{1,0:T(8,128)(2,1)S(1)}, bf16[128,256]{1,0:T(8,128)(2,1)S(1)}, u32[]{:S(2)}, u32[]{:S(2)}) collective-permute-start(bf16[128,256]{1,0:T(8,128)(2,1)S(1)} %get-tuple-element.67.refs_0_), channel_id=1, source_target_pairs={{0,8},{4,12},{8,0},{12,4},{16,24},{20,28},{24,16},{28,20},{1,9},{5... | collective-permute-start | bytes 196616 | tf_op jit(solution)/shard_map/ppermute | solution.py:196
  5.6 5.2 %collective-permute-start.10 = (bf16[128,256]{1,0:T(8,128)(2,1)S(1)}, bf16[128,256]{1,0:T(8,128)(2,1)S(1)}, u32[]{:S(2)}, u32[]{:S(2)}) collective-permute-start(bf16[128,256]{1,0:T(8,128)(2,1)S(1)} %get-tuple-element.67.refs_0_), channel_id=1, source_target_pairs={{0,24},{4,28},{8,16},{12,20},{16,8},{20,12},{24,0},{28,4},{1,25},{... | collective-permute-start | bytes 196616 | tf_op jit(solution)/shard_map/ppermute | solution.py:196
  5.7 1.4 %copy-start = (bf16[1024,768]{1,0:T(8,128)(2,1)S(1)}, bf16[1024,768]{1,0:T(8,128)(2,1)}, u32[]{:S(2)}) copy-start(bf16[1024,768]{1,0:T(8,128)(2,1)} %noise_ref.1) | copy-start | bytes 4718596
  10.8 1.8 %collective-permute-start.15 = (bf16[128,256]{1,0:T(8,128)(2,1)S(1)}, bf16[128,256]{1,0:T(8,128)(2,1)S(1)}, u32[]{:S(2)}, u32[]{:S(2)}) collective-permute-start(bf16[128,256]{1,0:T(8,128)(2,1)S(1)} %collective-permute-done.12.refs_2_), channel_id=1, source_target_pairs={{0,4},{4,0},{8,12},{12,8},{16,20},{20,16},{24,28},{28,24},{1,5},{5... | collective-permute-start | bytes 196616 | tf_op jit(solution)/shard_map/ppermute | solution.py:196
  10.8 1.8 %collective-permute-start.14 = (bf16[128,256]{1,0:T(8,128)(2,1)S(1)}, bf16[128,256]{1,0:T(8,128)(2,1)S(1)}, u32[]{:S(2)}, u32[]{:S(2)}) collective-permute-start(bf16[128,256]{1,0:T(8,128)(2,1)S(1)} %collective-permute-done.11.refs_1_), channel_id=1, source_target_pairs={{0,4},{4,0},{8,12},{12,8},{16,20},{20,16},{24,28},{28,24},{1,5},{5... | collective-permute-start | bytes 196616 | tf_op jit(solution)/shard_map/ppermute | solution.py:196
  11.3 1.3 %collective-permute-start.16 = (bf16[128,256]{1,0:T(8,128)(2,1)S(1)}, bf16[128,256]{1,0:T(8,128)(2,1)S(1)}, u32[]{:S(2)}, u32[]{:S(2)}) collective-permute-start(bf16[128,256]{1,0:T(8,128)(2,1)S(1)} %collective-permute-done.10.refs_3_), channel_id=1, source_target_pairs={{0,4},{4,0},{8,12},{12,8},{16,20},{20,16},{24,28},{28,24},{1,5},{5... | collective-permute-start | bytes 196616 | tf_op jit(solution)/shard_map/ppermute | solution.py:196
  14.0 25.0 %copy-start.6 = (f32[1024]{0:T(1024)S(1)}, f32[1024]{0:T(1024)}, u32[]{:S(2)}) copy-start(f32[1024]{0:T(1024)} %param.14) | copy-start | bytes 12292
  14.0 3.0 %collective-permute-start.17 = (bf16[128,1280]{1,0:T(8,128)(2,1)S(1)}, bf16[128,1280]{1,0:T(8,128)(2,1)S(1)}, u32[]{:S(2)}, u32[]{:S(2)}) collective-permute-start(bf16[128,1280]{1,0:T(8,128)(2,1)S(1)} %pad_maximum_fusion.refs_0_), channel_id=1, source_target_pairs={{0,4},{4,0},{8,12},{12,8},{16,20},{20,16},{24,28},{28,24},{1,5},{5... | collective-permute-start | bytes 983048 | tf_op jit(solution)/shard_map/ppermute | solution.py:196
  14.4 20.7 %collective-permute-start.21 = (bf16[256,768]{1,0:T(8,128)(2,1)}, bf16[256,768]{1,0:T(8,128)(2,1)}, u32[]{:S(2)}, u32[]{:S(2)}) collective-permute-start(bf16[256,768]{1,0:T(8,128)(2,1)} %project_1.1), channel_id=1, source_target_pairs={{0,2},{1,3},{2,0},{3,1},{4,6},{5,7},{6,4},{7,5},{8,10},{9,11},{10,... | collective-permute-start | bytes 1179656 | tf_op jit(solution)/shard_map/ppermute | solution.py:239
  17.0 22.2 %copy-start.7 = (f32[1024]{0:T(1024)S(1)}, f32[1024]{0:T(1024)}, u32[]{:S(2)}) copy-start(f32[1024]{0:T(1024)} %param.15) | copy-start | bytes 12292
  17.0 11.2 %copy-start.2 = (bf16[128,1280]{1,0:T(8,128)(2,1)}, bf16[128,1280]{1,0:T(8,128)(2,1)S(1)}, u32[]{:S(2)}) copy-start(bf16[128,1280]{1,0:T(8,128)(2,1)S(1)} %collective-permute-done.17.refs_4_) | copy-start | bytes 983044
  17.0 7.7 %collective-permute-start.5 = (bf16[128,512]{1,0:T(8,128)(2,1)}, bf16[128,512]{1,0:T(8,128)(2,1)}, u32[]{:S(2)}, u32[]{:S(2)}) collective-permute-start(bf16[128,512]{1,0:T(8,128)(2,1)} %param.1), channel_id=1, source_target_pairs={{0,24},{4,28},{8,16},{12,20},{16,8},{20,12},{24,0},{28,4},{1,25},{... | collective-permute-start | bytes 393224 | tf_op jit(solution)/shard_map/cond/branch_1_fun/ppermute | solution.py:196
  18.4 7.9 %collective-permute-start.3 = (bf16[128,512]{1,0:T(8,128)(2,1)}, bf16[128,512]{1,0:T(8,128)(2,1)}, u32[]{:S(2)}, u32[]{:S(2)}) collective-permute-start(bf16[128,512]{1,0:T(8,128)(2,1)} %param.1), channel_id=1, source_target_pairs={{0,16},{4,20},{8,24},{12,28},{16,0},{20,4},{24,8},{28,12},{1,17},{... | collective-permute-start | bytes 393224 | tf_op jit(solution)/shard_map/cond/branch_1_fun/ppermute | solution.py:196
  19.1 7.2 %collective-permute-start.1 = (bf16[128,512]{1,0:T(8,128)(2,1)}, bf16[128,512]{1,0:T(8,128)(2,1)}, u32[]{:S(2)}, u32[]{:S(2)}) collective-permute-start(bf16[128,512]{1,0:T(8,128)(2,1)} %param.1), channel_id=1, source_target_pairs={{0,8},{4,12},{8,0},{12,4},{16,24},{20,28},{24,16},{28,20},{1,9},{5... | collective-permute-start | bytes 393224 | tf_op jit(solution)/shard_map/cond/branch_1_fun/ppermute | solution.py:196
  20.6 6.2 %collective-permute-start = (bf16[128,512]{1,0:T(8,128)(2,1)}, bf16[128,512]{1,0:T(8,128)(2,1)}, u32[]{:S(2)}, u32[]{:S(2)}) collective-permute-start(bf16[128,512]{1,0:T(8,128)(2,1)} %param.1), channel_id=1, source_target_pairs={{0,4},{4,0},{8,12},{12,8},{16,20},{20,16},{24,28},{28,24},{1,5},{5... | collective-permute-start | bytes 393224 | tf_op jit(solution)/shard_map/cond/branch_1_fun/ppermute | solution.py:196
  24.7 2.1 %collective-permute-start.6 = (bf16[128,512]{1,0:T(8,128)(2,1)}, bf16[128,512]{1,0:T(8,128)(2,1)}, u32[]{:S(2)}, u32[]{:S(2)}) collective-permute-start(bf16[128,512]{1,0:T(8,128)(2,1)} %collective-permute-done.5), channel_id=1, source_target_pairs={{0,4},{4,0},{8,12},{12,8},{16,20},{20,16},{24,28},{28,24},{1,5},{5... | collective-permute-start | bytes 393224 | tf_op jit(solution)/shard_map/cond/branch_1_fun/ppermute | solution.py:196
  26.3 1.7 %collective-permute-start.4 = (bf16[128,512]{1,0:T(8,128)(2,1)}, bf16[128,512]{1,0:T(8,128)(2,1)}, u32[]{:S(2)}, u32[]{:S(2)}) collective-permute-start(bf16[128,512]{1,0:T(8,128)(2,1)} %collective-permute-done.3), channel_id=1, source_target_pairs={{0,4},{4,0},{8,12},{12,8},{16,20},{20,16},{24,28},{28,24},{1,5},{5... | collective-permute-start | bytes 393224 | tf_op jit(solution)/shard_map/cond/branch_1_fun/ppermute | solution.py:196
  26.3 1.9 %collective-permute-start.2 = (bf16[128,512]{1,0:T(8,128)(2,1)}, bf16[128,512]{1,0:T(8,128)(2,1)}, u32[]{:S(2)}, u32[]{:S(2)}) collective-permute-start(bf16[128,512]{1,0:T(8,128)(2,1)} %collective-permute-done.1), channel_id=1, source_target_pairs={{0,4},{4,0},{8,12},{12,8},{16,20},{20,16},{24,28},{28,24},{1,5},{5... | collective-permute-start | bytes 393224 | tf_op jit(solution)/shard_map/cond/branch_1_fun/ppermute | solution.py:196
  28.2 20.9 %copy-start.1 = (bf16[1024,768]{1,0:T(8,128)(2,1)S(1)}, bf16[1024,768]{1,0:T(8,128)(2,1)}, u32[]{:S(2)}) copy-start(bf16[1024,768]{1,0:T(8,128)(2,1)} %noise_ref.1) | copy-start | bytes 4718596
  28.2 11.6 %collective-permute-start.20 = (bf16[128,1280]{1,0:T(8,128)(2,1)S(1)}, bf16[128,1280]{1,0:T(8,128)(2,1)}, u32[]{:S(2)}, u32[]{:S(2)}) collective-permute-start(bf16[128,1280]{1,0:T(8,128)(2,1)S(1)} %pad_maximum_fusion.refs_0_), channel_id=1, source_target_pairs={{0,24},{4,28},{8,16},{12,20},{16,8},{20,12},{24,0},{28,4},{1,25},{... | collective-permute-start | bytes 983048 | tf_op jit(solution)/shard_map/ppermute | solution.py:196
  29.5 16.7 %collective-permute-start.19 = (bf16[128,1280]{1,0:T(8,128)(2,1)S(1)}, bf16[128,1280]{1,0:T(8,128)(2,1)}, u32[]{:S(2)}, u32[]{:S(2)}) collective-permute-start(bf16[128,1280]{1,0:T(8,128)(2,1)S(1)} %pad_maximum_fusion.refs_0_), channel_id=1, source_target_pairs={{0,16},{4,20},{8,24},{12,28},{16,0},{20,4},{24,8},{28,12},{1,17},{... | collective-permute-start | bytes 983048 | tf_op jit(solution)/shard_map/ppermute | solution.py:196
  30.2 16.0 %collective-permute-start.18 = (bf16[128,1280]{1,0:T(8,128)(2,1)S(1)}, bf16[128,1280]{1,0:T(8,128)(2,1)}, u32[]{:S(2)}, u32[]{:S(2)}) collective-permute-start(bf16[128,1280]{1,0:T(8,128)(2,1)S(1)} %pad_maximum_fusion.refs_0_), channel_id=1, source_target_pairs={{0,8},{4,12},{8,0},{12,4},{16,24},{20,28},{24,16},{28,20},{1,9},{5... | collective-permute-start | bytes 983048 | tf_op jit(solution)/shard_map/ppermute | solution.py:196
  35.2 18.2 %collective-permute-start.22 = (bf16[256,768]{1,0:T(8,128)(2,1)}, bf16[256,768]{1,0:T(8,128)(2,1)S(1)}, u32[]{:S(2)}, u32[]{:S(2)}) collective-permute-start(bf16[256,768]{1,0:T(8,128)(2,1)} %get-tuple-element.63), channel_id=1, source_target_pairs={{0,1},{1,2},{2,3},{3,0},{4,5},{5,6},{6,7},{7,4},{8,9},{9,10},{10,1... | collective-permute-start | bytes 1179656 | tf_op jit(solution)/shard_map/ppermute | solution.py:239
  36.4 19.0 %collective-permute-start.23 = (bf16[256,768]{1,0:T(8,128)(2,1)}, bf16[256,768]{1,0:T(8,128)(2,1)}, u32[]{:S(2)}, u32[]{:S(2)}) collective-permute-start(bf16[256,768]{1,0:T(8,128)(2,1)} %get-tuple-element.64), channel_id=1, source_target_pairs={{0,3},{1,0},{2,1},{3,2},{4,7},{5,4},{6,5},{7,6},{8,11},{9,8},{10,9... | collective-permute-start | bytes 1179656 | tf_op jit(solution)/shard_map/ppermute | solution.py:239
  46.2 2.0 %collective-permute-start.7 = (bf16[128,1280]{1,0:T(8,128)(2,1)}, bf16[128,1280]{1,0:T(8,128)(2,1)}, u32[]{:S(2)}, u32[]{:S(2)}) collective-permute-start(bf16[128,1280]{1,0:T(8,128)(2,1)} %get-tuple-element.12), channel_id=1, source_target_pairs={{0,4},{4,0},{8,12},{12,8},{16,20},{20,16},{24,28},{28,24},{1,5},{5... | collective-permute-start | bytes 983048 | tf_op jit(solution)/shard_map/cond/branch_1_fun/ppermute | solution.py:196
  46.2 2.4 %collective-permute-start.8 = (bf16[128,1280]{1,0:T(8,128)(2,1)}, bf16[128,1280]{1,0:T(8,128)(2,1)}, u32[]{:S(2)}, u32[]{:S(2)}) collective-permute-start(bf16[128,1280]{1,0:T(8,128)(2,1)} %get-tuple-element.13), channel_id=1, source_target_pairs={{0,4},{4,0},{8,12},{12,8},{16,20},{20,16},{24,28},{28,24},{1,5},{5... | collective-permute-start | bytes 983048 | tf_op jit(solution)/shard_map/cond/branch_1_fun/ppermute | solution.py:196
  46.7 2.4 %collective-permute-start.9 = (bf16[128,1280]{1,0:T(8,128)(2,1)}, bf16[128,1280]{1,0:T(8,128)(2,1)}, u32[]{:S(2)}, u32[]{:S(2)}) collective-permute-start(bf16[128,1280]{1,0:T(8,128)(2,1)} %get-tuple-element.14), channel_id=1, source_target_pairs={{0,4},{4,0},{8,12},{12,8},{16,20},{20,16},{24,28},{28,24},{1,5},{5... | collective-permute-start | bytes 983048 | tf_op jit(solution)/shard_map/cond/branch_1_fun/ppermute | solution.py:196
  49.1 1.0 %copy-start.3 = (bf16[128,1280]{1,0:T(8,128)(2,1)S(1)}, bf16[128,1280]{1,0:T(8,128)(2,1)}, u32[]{:S(2)}) copy-start(bf16[128,1280]{1,0:T(8,128)(2,1)} %copy-done.2) | copy-start | bytes 983044

commit v9 on v8

--- a/solution.py
+++ b/solution.py
@@ -55,7 +55,7 @@
     rows, columns = pieces[0].shape
     return pl.pallas_call(
         functools.partial(project_kernel, places, rows),
-        out_shape=[jax.ShapeDtypeStruct((columns // n_shifts, reals), jnp.bfloat16)] * n_shifts,
+        out_shape=[pltpu.VMEM((columns // n_shifts, reals), jnp.bfloat16)] * n_shifts,
         in_specs=[VMEM] * (1 + len(pieces)),
         out_specs=[VMEM] * n_shifts,
         scratch_shapes=[pltpu.VMEM((sites, columns), jnp.bfloat16)],
@@ -204,9 +204,9 @@
     return both
 
 
-def from_chips(own):
+def from_chips(own, end=None):
     pieces = {(0, 0): own}
-    for distance in range(2, lax.axis_size("real"), 2):
+    for distance in range(2, end or lax.axis_size("real"), 2):
         pieces[distance, 0] = swap(own, distance)
     return pieces
 
@@ -262,16 +262,18 @@
     v_first[last], noise_here, v_rest, own_and_u = lax.optimization_barrier(waiting)
     present = ranks[0, 0] > 0
     noise_here, present = lax.optimization_barrier((noise_here, present))
+    opposite = max(v_first)
+    u_opposite = swap(after(own_and_u, v_first), opposite[0])
     [far] = project(1, noise_here, with_other_core(v_first).items())
 
     u_swapped = swap(after(own_and_u, far), 1)
-    v_rest = after(v_rest, far, u_swapped)
+    v_rest = after(v_rest, far, u_opposite, u_swapped)
     v_pieces = {(0, 0): v_rest, **at_once(present, direct_rest, v_rest)}
-    u_pieces = from_chips(after(own_and_u, v_pieces))
+    u_pieces = {**from_chips(after(own_and_u, v_pieces), opposite[0]), opposite: u_opposite}
+    u_pieces[1, 0] = u_swapped
     others = project(len(rest), noise_here, v_pieces.items())
     far = along_site(far, first)
-    others = after(others, far)
-    u_pieces = {**u_pieces, (1, 0): u_swapped}
+    others = [others[0], *after(others[1:], far)]
     u_pieces.update(at_once(present, from_other_core, u_pieces))
     others = [along_site(coef, shift) for coef, shift in zip(others, rest)]
     u_whole, total = accumulate((first,), ranks, noise, u_pieces.items(), [far])

time: 59.2 us -> 64.6 us (1.091)
  waiting for transfers between devices: 20.7 us -> 26.5 us
    ppermute x3, waiting for transfers between devices: 2.34 us -> 8.36 us  [along_site(): lax.ppermute(coef, 'site', [(k, (k + shift) % count) for k in range(count)])]
    unnamed x16 -> x18, local copies, waits for them, and re-layouts: 2.4 us -> 2.41 us
  transfers between devices with their start and end apart: 24 -> 24, of which waited for: 12 -> 13; matrix products, arithmetic and copies ran while one was open for 3% -> 3% of each run, Pallas kernels for 12% -> 13%
where the time goes in v9:
time: 64.6 us; the launch traced here: 64.3 us
  waiting for transfers between devices  26.5 us (41%)
  starting transfers between devices  19.7 us (30%)
  Pallas kernels  12.3 us (19%)
  local copies, waits for them, and re-layouts  4.36 us (7%)
  between operations  0.75 us (1%)
  other arithmetic  0.68 us (1%)
    ppermute x21, waiting for transfers between devices, swap(): lax.ppermute(array, 'real', [(k, k ^ distance) for k in range(count)])  18.1 us
    ppermute x21, starting transfers between devices, swap(): lax.ppermute(array, 'real', [(k, k ^ distance) for k in range(count)])  13.3 us
    ppermute x3, waiting for transfers between devices, along_site(): lax.ppermute(coef, 'site', [(k, (k + shift) % count) for k in range(count)])  8.36 us
    ppermute x3, starting transfers between devices, along_site(): lax.ppermute(coef, 'site', [(k, (k + shift) % count) for k in range(count)])  6.41 us
    pallas_call x2, Pallas kernels, project(): pl.pallas_call(functools.partial(project_kernel, places, rows), out_shape...  4.57 us
    pallas_call x1, Pallas kernels, finish(): pl.pallas_call(functools.partial(finish_kernel, shifts), out_shape=jax.Sh...  3.66 us
    pallas_call x1, Pallas kernels, accumulate(): pl.pallas_call(functools.partial(accumulate_kernel, shifts, places, rows)...  3.31 us
    unnamed x18, local copies, waits for them, and re-layouts  2.41 us
  transfers between devices with their start and end apart: 24, of which 13 were waited for; matrix products, arithmetic and copies ran while one was open for 3% of the time, Pallas kernels for 13%

profile of v9, /device:TPU:0, one launch (start us, length us, event | category | flops | bytes accessed | tf_op | source)
XLA Modules:
  0.0 64.3 jit_solution(17056497555745681813)
XLA Ops:
  0.0 1.0 %dynamic-slice_bitcast_fusion = (bf16[128,256]{1,0:T(8,128)(2,1)S(1)}, bf16[128,256]{1,0:T(8,128)(2,1)S(1)}, bf16[128,256]{1,0:T(8,128)(2,1)S(1)}, bf16[128,256]{1,0:T(8,128)(2,1)S(1)}) fusion(bf16[1,128,1024]{2,1,0:T(8,128)(2,1)} %param.11, s32[]{:T(128)S(6)} %select_n.15, s32[]{:T(128)S(6)} %select_n.13, s32[]{:T(128)S(6)} %select_n.12, s32[]{:T(128)S(6)} %select_n.14), kind=kLoop, calls=%fused_computation.2 | loop fusion | bytes 524304 | tf_op jit(solution)/shard_map/dynamic_slice | solution.py:254
  1.0 0.5 collective-permute-start.13
  1.5 2.6 %collective-permute-start.12 = (bf16[128,256]{1,0:T(8,128)(2,1)S(1)}, bf16[128,256]{1,0:T(8,128)(2,1)S(1)}, u32[]{:S(2)}, u32[]{:S(2)}) collective-permute-start(bf16[128,256]{1,0:T(8,128)(2,1)S(1)} %get-tuple-element.67.refs_0_), channel_id=1, source_target_pairs={{0,16},{4,20},{8,24},{12,28},{16,0},{20,4},{24,8},{28,12},{1,17},{... | collective-permute-start | bytes 196616 | tf_op jit(solution)/shard_map/ppermute | solution.py:196
  4.1 1.5 %collective-permute-start.11 = (bf16[128,256]{1,0:T(8,128)(2,1)S(1)}, bf16[128,256]{1,0:T(8,128)(2,1)S(1)}, u32[]{:S(2)}, u32[]{:S(2)}) collective-permute-start(bf16[128,256]{1,0:T(8,128)(2,1)S(1)} %get-tuple-element.67.refs_0_), channel_id=1, source_target_pairs={{0,8},{4,12},{8,0},{12,4},{16,24},{20,28},{24,16},{28,20},{1,9},{5... | collective-permute-start | bytes 196616 | tf_op jit(solution)/shard_map/ppermute | solution.py:196
  5.7 1.4 %copy-done = bf16[1024,768]{1,0:T(8,128)(2,1)S(1)} copy-done((bf16[1024,768]{1,0:T(8,128)(2,1)S(1)}, bf16[1024,768]{1,0:T(8,128)(2,1)}, u32[]{:S(2)}) %copy-start) | copy-done | bytes 1572888
  7.1 0.8 %stage.1.noise_ref = bf16[1024,768]{1,0:T(8,128)(2,1)S(1)} custom-call(bf16[1024,768]{1,0:T(8,128)(2,1)S(1)} %copy-done), custom_call_target="tpu_custom_call" | custom-call | bytes 3145728 | tf_op jit(solution)/shard_map/stage/pallas_call | solution.py:83
  7.9 0.7 %pad_maximum_fusion.1.refs_0_ = bf16[128,512]{1,0:T(8,128)(2,1)} fusion(bf16[128,256]{1,0:T(8,128)(2,1)S(1)} %get-tuple-element.68, bf16[128,256]{1,0:T(8,128)(2,1)S(1)} %get-tuple-element.66), kind=kLoop, calls=%fused_computation.1 | loop fusion | flops 262144 | bytes 262144 | tf_op jit(solution)/shard_map/concatenate | solution.py:257
  8.6 2.2 %collective-permute-done.10.refs_3_ = bf16[128,256]{1,0:T(8,128)(2,1)S(1)} collective-permute-done((bf16[128,256]{1,0:T(8,128)(2,1)S(1)}, bf16[128,256]{1,0:T(8,128)(2,1)S(1)}, u32[]{:S(2)}, u32[]{:S(2)}) %collective-permute-start.10) | collective-permute-done | bytes 65568 | tf_op jit(solution)/shard_map/ppermute | solution.py:196
  12.5 1.4 %collective-permute-start.17 = (bf16[128,1280]{1,0:T(8,128)(2,1)S(1)}, bf16[128,1280]{1,0:T(8,128)(2,1)S(1)}, u32[]{:S(2)}, u32[]{:S(2)}) collective-permute-start(bf16[128,1280]{1,0:T(8,128)(2,1)S(1)} %pad_maximum_fusion.refs_0_), channel_id=1, source_target_pairs={{0,24},{4,28},{8,16},{12,20},{16,8},{20,12},{24,0},{28,4},{1,25},{... | collective-permute-start | bytes 983048 | tf_op jit(solution)/shard_map/ppermute | solution.py:196
  13.9 1.4 %project_1.1 = bf16[256,768]{1,0:T(8,128)(2,1)} custom-call(bf16[1024,768]{1,0:T(8,128)(2,1)S(1)} %stage.1.noise_ref, bf16[128,256]{1,0:T(8,128)(2,1)S(1)} %get-tuple-element.67.refs_0_, bf16[128,256]{1,0:T(8,128)(2,1)S(1)} %collective-permute-done.11.refs_1_, bf16[128,256]{1,0:T(8,128)(2,1)S(1)} %collective-permute-done.12.refs_2_, ...), custom_call_target="tpu_custom_call" | custom-call | flops 402653184 | bytes 4194304 | tf_op jit(solution)/shard_map/project_1/pallas_call | solution.py:56
  15.5 2.6 %collective-permute-start.21 = (bf16[256,768]{1,0:T(8,128)(2,1)}, bf16[256,768]{1,0:T(8,128)(2,1)}, u32[]{:S(2)}, u32[]{:S(2)}) collective-permute-start(bf16[256,768]{1,0:T(8,128)(2,1)} %project_1.1), channel_id=1, source_target_pairs={{0,2},{1,3},{2,0},{3,1},{4,6},{5,7},{6,4},{7,5},{8,10},{9,11},{10,... | collective-permute-start | bytes 1179656 | tf_op jit(solution)/shard_map/ppermute | solution.py:239
  18.1 5.5 %collective-permute-done.17.refs_3_ = bf16[128,1280]{1,0:T(8,128)(2,1)S(1)} collective-permute-done((bf16[128,1280]{1,0:T(8,128)(2,1)S(1)}, bf16[128,1280]{1,0:T(8,128)(2,1)S(1)}, u32[]{:S(2)}, u32[]{:S(2)}) %collective-permute-start.17) | collective-permute-done | bytes 327712 | tf_op jit(solution)/shard_map/ppermute | solution.py:196
  23.6 11.1 %conditional.2 = (bf16[128,512]{1,0:T(8,128)(2,1)}, bf16[128,512]{1,0:T(8,128)(2,1)}, bf16[128,512]{1,0:T(8,128)(2,1)}, bf16[128,512]{1,0:T(8,128)(2,1)}, bf16[1...) conditional(s32[]{:T(128)} %convert_element_type.4, () %tuple.33, ...), branch_computations={%region_0.0_spmd, %region_1.0_spmd} | conditional | bytes 3670352 | solution.py:234
  23.6 1.4 %collective-permute-start.5 = (bf16[128,512]{1,0:T(8,128)(2,1)}, bf16[128,512]{1,0:T(8,128)(2,1)}, u32[]{:S(2)}, u32[]{:S(2)}) collective-permute-start(bf16[128,512]{1,0:T(8,128)(2,1)} %param.1), channel_id=1, source_target_pairs={{0,24},{4,28},{8,16},{12,20},{16,8},{20,12},{24,0},{28,4},{1,25},{... | collective-permute-start | bytes 393224 | tf_op jit(solution)/shard_map/cond/branch_1_fun/ppermute | solution.py:196
  24.9 0.7 %collective-permute-start.3 = (bf16[128,512]{1,0:T(8,128)(2,1)}, bf16[128,512]{1,0:T(8,128)(2,1)}, u32[]{:S(2)}, u32[]{:S(2)}) collective-permute-start(bf16[128,512]{1,0:T(8,128)(2,1)} %param.1), channel_id=1, source_target_pairs={{0,16},{4,20},{8,24},{12,28},{16,0},{20,4},{24,8},{28,12},{1,17},{... | collective-permute-start | bytes 393224 | tf_op jit(solution)/shard_map/cond/branch_1_fun/ppermute | solution.py:196
  25.6 1.5 %collective-permute-start.1 = (bf16[128,512]{1,0:T(8,128)(2,1)}, bf16[128,512]{1,0:T(8,128)(2,1)}, u32[]{:S(2)}, u32[]{:S(2)}) collective-permute-start(bf16[128,512]{1,0:T(8,128)(2,1)} %param.1), channel_id=1, source_target_pairs={{0,8},{4,12},{8,0},{12,4},{16,24},{20,28},{24,16},{28,20},{1,9},{5... | collective-permute-start | bytes 393224 | tf_op jit(solution)/shard_map/cond/branch_1_fun/ppermute | solution.py:196
  27.1 4.1 %collective-permute-done.5 = bf16[128,512]{1,0:T(8,128)(2,1)} collective-permute-done((bf16[128,512]{1,0:T(8,128)(2,1)}, bf16[128,512]{1,0:T(8,128)(2,1)}, u32[]{:S(2)}, u32[]{:S(2)}) %collective-permute-start.5) | collective-permute-done | bytes 131104 | tf_op jit(solution)/shard_map/cond/branch_1_fun/ppermute | solution.py:196
  31.3 1.6 %collective-permute-done.3 = bf16[128,512]{1,0:T(8,128)(2,1)} collective-permute-done((bf16[128,512]{1,0:T(8,128)(2,1)}, bf16[128,512]{1,0:T(8,128)(2,1)}, u32[]{:S(2)}, u32[]{:S(2)}) %collective-permute-start.3) | collective-permute-done | bytes 131104 | tf_op jit(solution)/shard_map/cond/branch_1_fun/ppermute | solution.py:196
  33.3 1.2 %collective-permute-done.4 = bf16[128,512]{1,0:T(8,128)(2,1)} collective-permute-done((bf16[128,512]{1,0:T(8,128)(2,1)}, bf16[128,512]{1,0:T(8,128)(2,1)}, u32[]{:S(2)}, u32[]{:S(2)}) %collective-permute-start.4) | collective-permute-done | bytes 131104 | tf_op jit(solution)/shard_map/cond/branch_1_fun/ppermute | solution.py:196
  34.7 0.6 collective-permute-start.20
  35.3 1.4 %collective-permute-start.19 = (bf16[128,1280]{1,0:T(8,128)(2,1)S(1)}, bf16[128,1280]{1,0:T(8,128)(2,1)}, u32[]{:S(2)}, u32[]{:S(2)}) collective-permute-start(bf16[128,1280]{1,0:T(8,128)(2,1)S(1)} %pad_maximum_fusion.refs_0_), channel_id=1, source_target_pairs={{0,8},{4,12},{8,0},{12,4},{16,24},{20,28},{24,16},{28,20},{1,9},{5... | collective-permute-start | bytes 983048 | tf_op jit(solution)/shard_map/ppermute | solution.py:196
  36.6 3.1 %project_2.1 = (bf16[256,768]{1,0:T(8,128)(2,1)}, bf16[256,768]{1,0:T(8,128)(2,1)}) custom-call(bf16[1024,768]{1,0:T(8,128)(2,1)S(1)} %stage.1.noise_ref, bf16[128,512]{1,0:T(8,128)(2,1)} %pad_maximum_fusion.1.refs_0_, bf16[128,512]{1,0:T(8,128)(2,1)} %get-tuple-element.49.refs_1_, bf16[128,512]{1,0:T(8,128)(2,1)} %get-tuple-element.50.refs_2_, ...), custom_call_target="tpu_custom_call" | custom-call | flops 805306368 | bytes 5242880 | tf_op jit(solution)/shard_map/project_2/pallas_call | solution.py:56
  39.8 1.6 %collective-permute-start.22 = (bf16[256,768]{1,0:T(8,128)(2,1)}, bf16[256,768]{1,0:T(8,128)(2,1)S(1)}, u32[]{:S(2)}, u32[]{:S(2)}) collective-permute-start(bf16[256,768]{1,0:T(8,128)(2,1)} %get-tuple-element.62), channel_id=1, source_target_pairs={{0,1},{1,2},{2,3},{3,0},{4,5},{5,6},{6,7},{7,4},{8,9},{9,10},{10,1... | collective-permute-start | bytes 1179656 | tf_op jit(solution)/shard_map/ppermute | solution.py:239
  41.4 2.2 %collective-permute-start.23 = (bf16[256,768]{1,0:T(8,128)(2,1)}, bf16[256,768]{1,0:T(8,128)(2,1)}, u32[]{:S(2)}, u32[]{:S(2)}) collective-permute-start(bf16[256,768]{1,0:T(8,128)(2,1)} %get-tuple-element.64), channel_id=1, source_target_pairs={{0,3},{1,0},{2,1},{3,2},{4,7},{5,4},{6,5},{7,6},{8,11},{9,8},{10,9... | collective-permute-start | bytes 1179656 | tf_op jit(solution)/shard_map/ppermute | solution.py:239
  44.1 0.7 %collective-permute-done.20.refs_2_ = bf16[128,1280]{1,0:T(8,128)(2,1)} collective-permute-done((bf16[128,1280]{1,0:T(8,128)(2,1)S(1)}, bf16[128,1280]{1,0:T(8,128)(2,1)}, u32[]{:S(2)}, u32[]{:S(2)}) %collective-permute-start.20) | collective-permute-done | bytes 327712 | tf_op jit(solution)/shard_map/ppermute | solution.py:196
  45.1 2.9 %conditional.3 = (bf16[128,1280]{1,0:T(8,128)(2,1)}, bf16[128,1280]{1,0:T(8,128)(2,1)}, bf16[128,1280]{1,0:T(8,128)(2,1)}) conditional(s32[]{:T(128)} %convert_element_type.4, () %tuple.35, (bf16[128,1280]{1,0:T(8,128)(2,1)}, bf16[128,1280]{1,0:T(8,128)(2,1)}, bf16[128,1280]{1,0:T(8,128)(2,1)}) %tuple.45), branch_computations={%region_2.0_spmd, %region_3.0_spmd} | conditional | bytes 3932304 | solution.py:234
  45.6 1.5 %collective-permute-done.7 = bf16[128,1280]{1,0:T(8,128)(2,1)} collective-permute-done((bf16[128,1280]{1,0:T(8,128)(2,1)}, bf16[128,1280]{1,0:T(8,128)(2,1)}, u32[]{:S(2)}, u32[]{:S(2)}) %collective-permute-start.7) | collective-permute-done | bytes 327712 | tf_op jit(solution)/shard_map/cond/branch_1_fun/ppermute | solution.py:196
  48.0 1.0 %copy-done.3 = bf16[128,1280]{1,0:T(8,128)(2,1)S(1)} copy-done((bf16[128,1280]{1,0:T(8,128)(2,1)S(1)}, bf16[128,1280]{1,0:T(8,128)(2,1)}, u32[]{:S(2)}) %copy-start.3) | copy-done | bytes 327704
  48.9 3.3 %accumulate.1 = (bf16[1024,1024]{1,0:T(8,128)(2,1)S(1)}, f32[1024,768]{1,0:T(8,128)S(1)}) custom-call(s32[4,4]{1,0:T(4,128)S(1)} %copy-done.4, bf16[1024,768]{1,0:T(8,128)(2,1)S(1)} %copy-done.1, bf16[128,1280]{1,0:T(8,128)(2,1)S(1)} %pad_maximum_fusion.refs_0_, bf16[128,1280]{1,0:T(8,128)(2,1)} %collective-permute-done.19.refs_1_, ...), custom_call_target="tpu_custom_call" | custom-call | flops 1207959552 | bytes 9175040 | tf_op jit(solution)/shard_map/accumulate/pallas_call | solution.py:130
  52.3 1.6 %collective-permute-done.22.refs_0_ = bf16[256,768]{1,0:T(8,128)(2,1)S(1)} collective-permute-done((bf16[256,768]{1,0:T(8,128)(2,1)}, bf16[256,768]{1,0:T(8,128)(2,1)S(1)}, u32[]{:S(2)}, u32[]{:S(2)}) %collective-permute-start.22) | collective-permute-done | bytes 393248 | tf_op jit(solution)/shard_map/ppermute | solution.py:239
  53.8 6.8 %collective-permute-done.23.refs_1_ = bf16[256,768]{1,0:T(8,128)(2,1)} collective-permute-done((bf16[256,768]{1,0:T(8,128)(2,1)}, bf16[256,768]{1,0:T(8,128)(2,1)}, u32[]{:S(2)}, u32[]{:S(2)}) %collective-permute-start.23) | collective-permute-done | bytes 393248 | tf_op jit(solution)/shard_map/ppermute | solution.py:239
  60.6 3.7 %finish.1 = f32[1024,768]{1,0:T(8,128)} custom-call(s32[4,4]{1,0:T(4,128)S(1)} %copy-done.4, bf16[1024,1024]{1,0:T(8,128)(2,1)S(1)} %get-tuple-element.60.u_ref, f32[1024,768]{1,0:T(8,128)S(1)} %get-tuple-element.61.sum_ref, f32[1024,1]{1,0:T(8,128)S(1)} %copy.7.skew_ref, f32[1024,1]{1,0:T(8,128)S(1)} %copy.8.tail_ref, ...), custom_call_target="tpu_custom_call" | custom-call | flops 805306368 | bytes 12058624 | tf_op jit(solution)/shard_map/finish/pallas_call | solution.py:175
  (47 shorter events, 4.2 us)
Async XLA Ops:
  0.0 7.9 %copy-start.6 = (bf16[1,128,1024]{2,1,0:T(8,128)(2,1)S(1)}, bf16[1,128,1024]{2,1,0:T(8,128)(2,1)}, u32[]{:S(2)}) copy-start(bf16[1,128,1024]{2,1,0:T(8,128)(2,1)} %param.12) | copy-start | bytes 786436
  0.0 11.4 %copy-start.4 = (s32[4,4]{1,0:T(4,128)S(1)}, s32[4,4]{1,0:T(4,128)}, u32[]{:S(2)}) copy-start(s32[4,4]{1,0:T(4,128)} %ranks_ref.3) | copy-start | bytes 196
  1.0 12.9 %collective-permute-start.13 = (bf16[128,256]{1,0:T(8,128)(2,1)S(1)}, bf16[128,256]{1,0:T(8,128)(2,1)S(1)}, u32[]{:S(2)}, u32[]{:S(2)}) collective-permute-start(bf16[128,256]{1,0:T(8,128)(2,1)S(1)} %get-tuple-element.67.refs_0_), channel_id=1, source_target_pairs={{0,4},{4,0},{8,12},{12,8},{16,20},{20,16},{24,28},{28,24},{1,5},{5... | collective-permute-start | bytes 196616 | tf_op jit(solution)/shard_map/ppermute | solution.py:196
  1.5 9.3 %collective-permute-start.12 = (bf16[128,256]{1,0:T(8,128)(2,1)S(1)}, bf16[128,256]{1,0:T(8,128)(2,1)S(1)}, u32[]{:S(2)}, u32[]{:S(2)}) collective-permute-start(bf16[128,256]{1,0:T(8,128)(2,1)S(1)} %get-tuple-element.67.refs_0_), channel_id=1, source_target_pairs={{0,16},{4,20},{8,24},{12,28},{16,0},{20,4},{24,8},{28,12},{1,17},{... | collective-permute-start | bytes 196616 | tf_op jit(solution)/shard_map/ppermute | solution.py:196
  4.1 6.7 %collective-permute-start.11 = (bf16[128,256]{1,0:T(8,128)(2,1)S(1)}, bf16[128,256]{1,0:T(8,128)(2,1)S(1)}, u32[]{:S(2)}, u32[]{:S(2)}) collective-permute-start(bf16[128,256]{1,0:T(8,128)(2,1)S(1)} %get-tuple-element.67.refs_0_), channel_id=1, source_target_pairs={{0,8},{4,12},{8,0},{12,4},{16,24},{20,28},{24,16},{28,20},{1,9},{5... | collective-permute-start | bytes 196616 | tf_op jit(solution)/shard_map/ppermute | solution.py:196
  5.6 5.2 %collective-permute-start.10 = (bf16[128,256]{1,0:T(8,128)(2,1)S(1)}, bf16[128,256]{1,0:T(8,128)(2,1)S(1)}, u32[]{:S(2)}, u32[]{:S(2)}) collective-permute-start(bf16[128,256]{1,0:T(8,128)(2,1)S(1)} %get-tuple-element.67.refs_0_), channel_id=1, source_target_pairs={{0,24},{4,28},{8,16},{12,20},{16,8},{20,12},{24,0},{28,4},{1,25},{... | collective-permute-start | bytes 196616 | tf_op jit(solution)/shard_map/ppermute | solution.py:196
  5.7 1.4 %copy-start = (bf16[1024,768]{1,0:T(8,128)(2,1)S(1)}, bf16[1024,768]{1,0:T(8,128)(2,1)}, u32[]{:S(2)}) copy-start(bf16[1024,768]{1,0:T(8,128)(2,1)} %noise_ref.1) | copy-start | bytes 4718596
  10.8 3.1 %collective-permute-start.15 = (bf16[128,256]{1,0:T(8,128)(2,1)S(1)}, bf16[128,256]{1,0:T(8,128)(2,1)S(1)}, u32[]{:S(2)}, u32[]{:S(2)}) collective-permute-start(bf16[128,256]{1,0:T(8,128)(2,1)S(1)} %collective-permute-done.12.refs_2_), channel_id=1, source_target_pairs={{0,4},{4,0},{8,12},{12,8},{16,20},{20,16},{24,28},{28,24},{1,5},{5... | collective-permute-start | bytes 196616 | tf_op jit(solution)/shard_map/ppermute | solution.py:196
  10.8 3.1 %collective-permute-start.14 = (bf16[128,256]{1,0:T(8,128)(2,1)S(1)}, bf16[128,256]{1,0:T(8,128)(2,1)S(1)}, u32[]{:S(2)}, u32[]{:S(2)}) collective-permute-start(bf16[128,256]{1,0:T(8,128)(2,1)S(1)} %collective-permute-done.11.refs_1_), channel_id=1, source_target_pairs={{0,4},{4,0},{8,12},{12,8},{16,20},{20,16},{24,28},{28,24},{1,5},{5... | collective-permute-start | bytes 196616 | tf_op jit(solution)/shard_map/ppermute | solution.py:196
  11.3 2.6 %collective-permute-start.16 = (bf16[128,256]{1,0:T(8,128)(2,1)S(1)}, bf16[128,256]{1,0:T(8,128)(2,1)S(1)}, u32[]{:S(2)}, u32[]{:S(2)}) collective-permute-start(bf16[128,256]{1,0:T(8,128)(2,1)S(1)} %collective-permute-done.10.refs_3_), channel_id=1, source_target_pairs={{0,4},{4,0},{8,12},{12,8},{16,20},{20,16},{24,28},{28,24},{1,5},{5... | collective-permute-start | bytes 196616 | tf_op jit(solution)/shard_map/ppermute | solution.py:196
  12.5 11.0 %collective-permute-start.17 = (bf16[128,1280]{1,0:T(8,128)(2,1)S(1)}, bf16[128,1280]{1,0:T(8,128)(2,1)S(1)}, u32[]{:S(2)}, u32[]{:S(2)}) collective-permute-start(bf16[128,1280]{1,0:T(8,128)(2,1)S(1)} %pad_maximum_fusion.refs_0_), channel_id=1, source_target_pairs={{0,24},{4,28},{8,16},{12,20},{16,8},{20,12},{24,0},{28,4},{1,25},{... | collective-permute-start | bytes 983048 | tf_op jit(solution)/shard_map/ppermute | solution.py:196
  15.3 28.3 %copy-start.7 = (f32[1024]{0:T(1024)S(1)}, f32[1024]{0:T(1024)}, u32[]{:S(2)}) copy-start(f32[1024]{0:T(1024)} %param.14) | copy-start | bytes 12292
  15.3 8.2 %collective-permute-start.18 = (bf16[128,1280]{1,0:T(8,128)(2,1)S(1)}, bf16[128,1280]{1,0:T(8,128)(2,1)S(1)}, u32[]{:S(2)}, u32[]{:S(2)}) collective-permute-start(bf16[128,1280]{1,0:T(8,128)(2,1)S(1)} %pad_maximum_fusion.refs_0_), channel_id=1, source_target_pairs={{0,4},{4,0},{8,12},{12,8},{16,20},{20,16},{24,28},{28,24},{1,5},{5... | collective-permute-start | bytes 983048 | tf_op jit(solution)/shard_map/ppermute | solution.py:196
  15.5 25.9 %collective-permute-start.21 = (bf16[256,768]{1,0:T(8,128)(2,1)}, bf16[256,768]{1,0:T(8,128)(2,1)}, u32[]{:S(2)}, u32[]{:S(2)}) collective-permute-start(bf16[256,768]{1,0:T(8,128)(2,1)} %project_1.1), channel_id=1, source_target_pairs={{0,2},{1,3},{2,0},{3,1},{4,6},{5,7},{6,4},{7,5},{8,10},{9,11},{10,... | collective-permute-start | bytes 1179656 | tf_op jit(solution)/shard_map/ppermute | solution.py:239
  18.1 25.8 %copy-start.8 = (f32[1024]{0:T(1024)S(1)}, f32[1024]{0:T(1024)}, u32[]{:S(2)}) copy-start(f32[1024]{0:T(1024)} %param.15) | copy-start | bytes 12292
  23.6 11.2 %copy-start.5 = (bf16[128,1280]{1,0:T(8,128)(2,1)}, bf16[128,1280]{1,0:T(8,128)(2,1)S(1)}, u32[]{:S(2)}) copy-start(bf16[128,1280]{1,0:T(8,128)(2,1)S(1)} %collective-permute-done.17.refs_3_) | copy-start | bytes 983044
  23.6 11.1 %copy-start.2 = (bf16[128,1280]{1,0:T(8,128)(2,1)}, bf16[128,1280]{1,0:T(8,128)(2,1)S(1)}, u32[]{:S(2)}) copy-start(bf16[128,1280]{1,0:T(8,128)(2,1)S(1)} %collective-permute-done.18.refs_4_) | copy-start | bytes 983044
  23.6 7.7 %collective-permute-start.5 = (bf16[128,512]{1,0:T(8,128)(2,1)}, bf16[128,512]{1,0:T(8,128)(2,1)}, u32[]{:S(2)}, u32[]{:S(2)}) collective-permute-start(bf16[128,512]{1,0:T(8,128)(2,1)} %param.1), channel_id=1, source_target_pairs={{0,24},{4,28},{8,16},{12,20},{16,8},{20,12},{24,0},{28,4},{1,25},{... | collective-permute-start | bytes 393224 | tf_op jit(solution)/shard_map/cond/branch_1_fun/ppermute | solution.py:196
  24.9 7.9 %collective-permute-start.3 = (bf16[128,512]{1,0:T(8,128)(2,1)}, bf16[128,512]{1,0:T(8,128)(2,1)}, u32[]{:S(2)}, u32[]{:S(2)}) collective-permute-start(bf16[128,512]{1,0:T(8,128)(2,1)} %param.1), channel_id=1, source_target_pairs={{0,16},{4,20},{8,24},{12,28},{16,0},{20,4},{24,8},{28,12},{1,17},{... | collective-permute-start | bytes 393224 | tf_op jit(solution)/shard_map/cond/branch_1_fun/ppermute | solution.py:196
  25.6 7.2 %collective-permute-start.1 = (bf16[128,512]{1,0:T(8,128)(2,1)}, bf16[128,512]{1,0:T(8,128)(2,1)}, u32[]{:S(2)}, u32[]{:S(2)}) collective-permute-start(bf16[128,512]{1,0:T(8,128)(2,1)} %param.1), channel_id=1, source_target_pairs={{0,8},{4,12},{8,0},{12,4},{16,24},{20,28},{24,16},{28,20},{1,9},{5... | collective-permute-start | bytes 393224 | tf_op jit(solution)/shard_map/cond/branch_1_fun/ppermute | solution.py:196
  27.1 6.2 %collective-permute-start = (bf16[128,512]{1,0:T(8,128)(2,1)}, bf16[128,512]{1,0:T(8,128)(2,1)}, u32[]{:S(2)}, u32[]{:S(2)}) collective-permute-start(bf16[128,512]{1,0:T(8,128)(2,1)} %param.1), channel_id=1, source_target_pairs={{0,4},{4,0},{8,12},{12,8},{16,20},{20,16},{24,28},{28,24},{1,5},{5... | collective-permute-start | bytes 393224 | tf_op jit(solution)/shard_map/cond/branch_1_fun/ppermute | solution.py:196
  31.3 2.1 %collective-permute-start.6 = (bf16[128,512]{1,0:T(8,128)(2,1)}, bf16[128,512]{1,0:T(8,128)(2,1)}, u32[]{:S(2)}, u32[]{:S(2)}) collective-permute-start(bf16[128,512]{1,0:T(8,128)(2,1)} %collective-permute-done.5), channel_id=1, source_target_pairs={{0,4},{4,0},{8,12},{12,8},{16,20},{20,16},{24,28},{28,24},{1,5},{5... | collective-permute-start | bytes 393224 | tf_op jit(solution)/shard_map/cond/branch_1_fun/ppermute | solution.py:196
  32.8 1.7 %collective-permute-start.4 = (bf16[128,512]{1,0:T(8,128)(2,1)}, bf16[128,512]{1,0:T(8,128)(2,1)}, u32[]{:S(2)}, u32[]{:S(2)}) collective-permute-start(bf16[128,512]{1,0:T(8,128)(2,1)} %collective-permute-done.3), channel_id=1, source_target_pairs={{0,4},{4,0},{8,12},{12,8},{16,20},{20,16},{24,28},{28,24},{1,5},{5... | collective-permute-start | bytes 393224 | tf_op jit(solution)/shard_map/cond/branch_1_fun/ppermute | solution.py:196
  32.8 1.9 %collective-permute-start.2 = (bf16[128,512]{1,0:T(8,128)(2,1)}, bf16[128,512]{1,0:T(8,128)(2,1)}, u32[]{:S(2)}, u32[]{:S(2)}) collective-permute-start(bf16[128,512]{1,0:T(8,128)(2,1)} %collective-permute-done.1), channel_id=1, source_target_pairs={{0,4},{4,0},{8,12},{12,8},{16,20},{20,16},{24,28},{28,24},{1,5},{5... | collective-permute-start | bytes 393224 | tf_op jit(solution)/shard_map/cond/branch_1_fun/ppermute | solution.py:196
  34.7 13.3 %copy-start.1 = (bf16[1024,768]{1,0:T(8,128)(2,1)S(1)}, bf16[1024,768]{1,0:T(8,128)(2,1)}, u32[]{:S(2)}) copy-start(bf16[1024,768]{1,0:T(8,128)(2,1)} %noise_ref.1) | copy-start | bytes 4718596
  34.7 10.1 %collective-permute-start.20 = (bf16[128,1280]{1,0:T(8,128)(2,1)S(1)}, bf16[128,1280]{1,0:T(8,128)(2,1)}, u32[]{:S(2)}, u32[]{:S(2)}) collective-permute-start(bf16[128,1280]{1,0:T(8,128)(2,1)S(1)} %pad_maximum_fusion.refs_0_), channel_id=1, source_target_pairs={{0,16},{4,20},{8,24},{12,28},{16,0},{20,4},{24,8},{28,12},{1,17},{... | collective-permute-start | bytes 983048 | tf_op jit(solution)/shard_map/ppermute | solution.py:196
  35.3 9.8 %collective-permute-start.19 = (bf16[128,1280]{1,0:T(8,128)(2,1)S(1)}, bf16[128,1280]{1,0:T(8,128)(2,1)}, u32[]{:S(2)}, u32[]{:S(2)}) collective-permute-start(bf16[128,1280]{1,0:T(8,128)(2,1)S(1)} %pad_maximum_fusion.refs_0_), channel_id=1, source_target_pairs={{0,8},{4,12},{8,0},{12,4},{16,24},{20,28},{24,16},{28,20},{1,9},{5... | collective-permute-start | bytes 983048 | tf_op jit(solution)/shard_map/ppermute | solution.py:196
  39.8 14.1 %collective-permute-start.22 = (bf16[256,768]{1,0:T(8,128)(2,1)}, bf16[256,768]{1,0:T(8,128)(2,1)S(1)}, u32[]{:S(2)}, u32[]{:S(2)}) collective-permute-start(bf16[256,768]{1,0:T(8,128)(2,1)} %get-tuple-element.62), channel_id=1, source_target_pairs={{0,1},{1,2},{2,3},{3,0},{4,5},{5,6},{6,7},{7,4},{8,9},{9,10},{10,1... | collective-permute-start | bytes 1179656 | tf_op jit(solution)/shard_map/ppermute | solution.py:239
  41.4 19.2 %collective-permute-start.23 = (bf16[256,768]{1,0:T(8,128)(2,1)}, bf16[256,768]{1,0:T(8,128)(2,1)}, u32[]{:S(2)}, u32[]{:S(2)}) collective-permute-start(bf16[256,768]{1,0:T(8,128)(2,1)} %get-tuple-element.64), channel_id=1, source_target_pairs={{0,3},{1,0},{2,1},{3,2},{4,7},{5,4},{6,5},{7,6},{8,11},{9,8},{10,9... | collective-permute-start | bytes 1179656 | tf_op jit(solution)/shard_map/ppermute | solution.py:239
  45.1 2.0 %collective-permute-start.7 = (bf16[128,1280]{1,0:T(8,128)(2,1)}, bf16[128,1280]{1,0:T(8,128)(2,1)}, u32[]{:S(2)}, u32[]{:S(2)}) collective-permute-start(bf16[128,1280]{1,0:T(8,128)(2,1)} %get-tuple-element.12), channel_id=1, source_target_pairs={{0,4},{4,0},{8,12},{12,8},{16,20},{20,16},{24,28},{28,24},{1,5},{5... | collective-permute-start | bytes 983048 | tf_op jit(solution)/shard_map/cond/branch_1_fun/ppermute | solution.py:196
  45.1 2.4 %collective-permute-start.8 = (bf16[128,1280]{1,0:T(8,128)(2,1)}, bf16[128,1280]{1,0:T(8,128)(2,1)}, u32[]{:S(2)}, u32[]{:S(2)}) collective-permute-start(bf16[128,1280]{1,0:T(8,128)(2,1)} %get-tuple-element.13), channel_id=1, source_target_pairs={{0,4},{4,0},{8,12},{12,8},{16,20},{20,16},{24,28},{28,24},{1,5},{5... | collective-permute-start | bytes 983048 | tf_op jit(solution)/shard_map/cond/branch_1_fun/ppermute | solution.py:196
  45.6 2.4 %collective-permute-start.9 = (bf16[128,1280]{1,0:T(8,128)(2,1)}, bf16[128,1280]{1,0:T(8,128)(2,1)}, u32[]{:S(2)}, u32[]{:S(2)}) collective-permute-start(bf16[128,1280]{1,0:T(8,128)(2,1)} %get-tuple-element.14), channel_id=1, source_target_pairs={{0,4},{4,0},{8,12},{12,8},{16,20},{20,16},{24,28},{28,24},{1,5},{5... | collective-permute-start | bytes 983048 | tf_op jit(solution)/shard_map/cond/branch_1_fun/ppermute | solution.py:196
  (1 other events, 1.0 us)

commit v10 on v8

--- a/solution.py
+++ b/solution.py
@@ -142,6 +142,11 @@
     )(ranks, noise, *pieces, *coefs)
 
 
+def as_rows(ref, rows):
+    values = ref[:, rows]
+    return jnp.transpose(jnp.broadcast_to(values, (values.shape[1], values.shape[1])))
+
+
 def finish_kernel(shifts, ranks_ref, u_ref, sum_ref, skew_ref, tail_ref, *refs):
     coefs = refs[: len(shifts)]
     out_ref, slots, sems = refs[len(shifts) :]
@@ -157,10 +162,14 @@
             gaussian += jnp.dot(
                 u_ref[rows, pl.ds(start, columns)], coef, preferred_element_type=jnp.float32
             )
-        skew, tail = skew_ref[rows, :], tail_ref[rows, :]
-        grown = jnp.exp2((skew * LOG2E) * gaussian) + 1.0
-        grown = grown * jnp.tanh((0.5 * skew) * gaussian) * (1.0 / skew)
-        slots[step] = grown * jnp.exp2((0.5 * LOG2E * tail) * (gaussian * gaussian))
+        skew, tail = as_rows(skew_ref, rows), as_rows(tail_ref, rows)
+        growth, turn, scale = LOG2E * skew, 0.5 * skew, 1.0 / skew
+        spread = (0.5 * LOG2E) * tail
+        lanes = skew.shape[1]
+        for start in range(0, gaussian.shape[1], lanes):
+            at = gaussian[:, start : start + lanes]
+            grown = (jnp.exp2(growth * at) + 1.0) * jnp.tanh(turn * at) * scale
+            slots[step, :, start : start + lanes] = grown * jnp.exp2(spread * (at * at))
         copy = pltpu.make_async_copy(slots.at[step], out_ref.at[rows, :], sems.at[step])
         copy.start()
         copies.append(copy)
@@ -270,12 +279,12 @@
     u_pieces = from_chips(after(own_and_u, v_pieces))
     others = project(len(rest), noise_here, v_pieces.items())
     far = along_site(far, first)
-    others = after(others, far)
+    others = [others[0], *after(others[1:], far)]
     u_pieces = {**u_pieces, (1, 0): u_swapped}
     u_pieces.update(at_once(present, from_other_core, u_pieces))
     others = [along_site(coef, shift) for coef, shift in zip(others, rest)]
     u_whole, total = accumulate((first,), ranks, noise, u_pieces.items(), [far])
-    return finish(rest, ranks, u_whole, total, skew_g[:, None], tail_h[:, None], others)
+    return finish(rest, ranks, u_whole, total, skew_g[None], tail_h[None], others)
 
 
 def solution(mesh):

time: 59.2 us -> 59.6 us (level)
    unnamed x16 -> x18, local copies, waits for them, and re-layouts: 2.4 us -> 3.12 us
  transfers between devices with their start and end apart: 24 -> 24, of which waited for: 12 -> 11; matrix products, arithmetic and copies ran while one was open for 3% -> 2% of each run, Pallas kernels for 12% -> 12%
where the time goes in v10:
time: 59.6 us; the launch traced here: 59.3 us
  waiting for transfers between devices  21 us (35%)
  starting transfers between devices  20.2 us (34%)
  Pallas kernels  12.1 us (20%)
  local copies, waits for them, and re-layouts  4.63 us (8%)
  between operations  0.75 us (1%)
  other arithmetic  0.69 us (1%)
    ppermute x21, waiting for transfers between devices, swap(): lax.ppermute(array, 'real', [(k, k ^ distance) for k in range(count)])  18.9 us
    ppermute x21, starting transfers between devices, swap(): lax.ppermute(array, 'real', [(k, k ^ distance) for k in range(count)])  13.7 us
    ppermute x3, starting transfers between devices, along_site(): lax.ppermute(coef, 'site', [(k, (k + shift) % count) for k in range(count)])  6.41 us
    pallas_call x2, Pallas kernels, project(): pl.pallas_call(functools.partial(project_kernel, places, rows), out_shape...  4.57 us
    pallas_call x1, Pallas kernels, finish(): pl.pallas_call(functools.partial(finish_kernel, shifts), out_shape=jax.Sh...  3.41 us
    pallas_call x1, Pallas kernels, accumulate(): pl.pallas_call(functools.partial(accumulate_kernel, shifts, places, rows)...  3.34 us
    unnamed x18, local copies, waits for them, and re-layouts  3.12 us
    ppermute x3, waiting for transfers between devices, along_site(): lax.ppermute(coef, 'site', [(k, (k + shift) % count) for k in range(count)])  2.07 us
  transfers between devices with their start and end apart: 24, of which 11 were waited for; matrix products, arithmetic and copies ran while one was open for 2% of the time, Pallas kernels for 12%

profile of v10, /device:TPU:0, one launch (start us, length us, event | category | flops | bytes accessed | tf_op | source)
XLA Modules:
  0.0 59.3 jit_solution(11451204392371490328)
XLA Ops:
  0.0 1.0 %dynamic-slice_bitcast_fusion = (bf16[128,256]{1,0:T(8,128)(2,1)S(1)}, bf16[128,256]{1,0:T(8,128)(2,1)S(1)}, bf16[128,256]{1,0:T(8,128)(2,1)S(1)}, bf16[128,256]{1,0:T(8,128)(2,1)S(1)}) fusion(bf16[1,128,1024]{2,1,0:T(8,128)(2,1)} %param.11, s32[]{:T(128)S(6)} %select_n.15, s32[]{:T(128)S(6)} %select_n.13, s32[]{:T(128)S(6)} %select_n.12, s32[]{:T(128)S(6)} %select_n.14), kind=kLoop, calls=%fused_computation.2 | loop fusion | bytes 524304 | tf_op jit(solution)/shard_map/dynamic_slice | solution.py:263
  1.0 0.5 collective-permute-start.13
  1.5 2.6 %collective-permute-start.12 = (bf16[128,256]{1,0:T(8,128)(2,1)S(1)}, bf16[128,256]{1,0:T(8,128)(2,1)S(1)}, u32[]{:S(2)}, u32[]{:S(2)}) collective-permute-start(bf16[128,256]{1,0:T(8,128)(2,1)S(1)} %get-tuple-element.65.refs_0_), channel_id=1, source_target_pairs={{0,16},{4,20},{8,24},{12,28},{16,0},{20,4},{24,8},{28,12},{1,17},{... | collective-permute-start | bytes 196616 | tf_op jit(solution)/shard_map/ppermute | solution.py:205
  4.1 1.5 %collective-permute-start.11 = (bf16[128,256]{1,0:T(8,128)(2,1)S(1)}, bf16[128,256]{1,0:T(8,128)(2,1)S(1)}, u32[]{:S(2)}, u32[]{:S(2)}) collective-permute-start(bf16[128,256]{1,0:T(8,128)(2,1)S(1)} %get-tuple-element.65.refs_0_), channel_id=1, source_target_pairs={{0,8},{4,12},{8,0},{12,4},{16,24},{20,28},{24,16},{28,20},{1,9},{5... | collective-permute-start | bytes 196616 | tf_op jit(solution)/shard_map/ppermute | solution.py:205
  5.7 1.4 %copy-done = bf16[1024,768]{1,0:T(8,128)(2,1)S(1)} copy-done((bf16[1024,768]{1,0:T(8,128)(2,1)S(1)}, bf16[1024,768]{1,0:T(8,128)(2,1)}, u32[]{:S(2)}) %copy-start) | copy-done | bytes 1572888
  7.1 0.8 %stage.1.noise_ref = bf16[1024,768]{1,0:T(8,128)(2,1)S(1)} custom-call(bf16[1024,768]{1,0:T(8,128)(2,1)S(1)} %copy-done), custom_call_target="tpu_custom_call" | custom-call | bytes 3145728 | tf_op jit(solution)/shard_map/stage/pallas_call | solution.py:83
  7.9 0.7 %pad_maximum_fusion.1.refs_0_ = bf16[128,512]{1,0:T(8,128)(2,1)} fusion(bf16[128,256]{1,0:T(8,128)(2,1)S(1)} %get-tuple-element.66, bf16[128,256]{1,0:T(8,128)(2,1)S(1)} %get-tuple-element.64), kind=kLoop, calls=%fused_computation.1 | loop fusion | flops 262144 | bytes 262144 | tf_op jit(solution)/shard_map/concatenate | solution.py:266
  8.6 2.2 %collective-permute-done.10.refs_3_ = bf16[128,256]{1,0:T(8,128)(2,1)S(1)} collective-permute-done((bf16[128,256]{1,0:T(8,128)(2,1)S(1)}, bf16[128,256]{1,0:T(8,128)(2,1)S(1)}, u32[]{:S(2)}, u32[]{:S(2)}) %collective-permute-start.10) | collective-permute-done | bytes 65568 | tf_op jit(solution)/shard_map/ppermute | solution.py:205
  12.6 1.4 %project_1.1 = bf16[256,768]{1,0:T(8,128)(2,1)} custom-call(bf16[1024,768]{1,0:T(8,128)(2,1)S(1)} %stage.1.noise_ref, bf16[128,256]{1,0:T(8,128)(2,1)S(1)} %get-tuple-element.65.refs_0_, bf16[128,256]{1,0:T(8,128)(2,1)S(1)} %collective-permute-done.11.refs_1_, bf16[128,256]{1,0:T(8,128)(2,1)S(1)} %collective-permute-done.12.refs_2_, ...), custom_call_target="tpu_custom_call" | custom-call | flops 402653184 | bytes 4194304 | tf_op jit(solution)/shard_map/project_1/pallas_call | solution.py:56
  14.4 2.6 %collective-permute-start.21 = (bf16[256,768]{1,0:T(8,128)(2,1)}, bf16[256,768]{1,0:T(8,128)(2,1)}, u32[]{:S(2)}, u32[]{:S(2)}) collective-permute-start(bf16[256,768]{1,0:T(8,128)(2,1)} %project_1.1), channel_id=1, source_target_pairs={{0,2},{1,3},{2,0},{3,1},{4,6},{5,7},{6,4},{7,5},{8,10},{9,11},{10,... | collective-permute-start | bytes 1179656 | tf_op jit(solution)/shard_map/ppermute | solution.py:248
  17.0 0.7 %copy-done.2 = bf16[128,1280]{1,0:T(8,128)(2,1)} copy-done((bf16[128,1280]{1,0:T(8,128)(2,1)}, bf16[128,1280]{1,0:T(8,128)(2,1)S(1)}, u32[]{:S(2)}) %copy-start.2) | copy-done | bytes 327704
  17.8 11.1 %conditional.2 = (bf16[128,512]{1,0:T(8,128)(2,1)}, bf16[128,512]{1,0:T(8,128)(2,1)}, bf16[128,512]{1,0:T(8,128)(2,1)}, bf16[128,512]{1,0:T(8,128)(2,1)}, bf16[1...) conditional(s32[]{:T(128)} %convert_element_type.4, () %tuple.31, ...), branch_computations={%region_0.0_spmd, %region_1.0_spmd} | conditional | bytes 3670352 | solution.py:243
  17.8 1.3 %collective-permute-start.5 = (bf16[128,512]{1,0:T(8,128)(2,1)}, bf16[128,512]{1,0:T(8,128)(2,1)}, u32[]{:S(2)}, u32[]{:S(2)}) collective-permute-start(bf16[128,512]{1,0:T(8,128)(2,1)} %param.1), channel_id=1, source_target_pairs={{0,24},{4,28},{8,16},{12,20},{16,8},{20,12},{24,0},{28,4},{1,25},{... | collective-permute-start | bytes 393224 | tf_op jit(solution)/shard_map/cond/branch_1_fun/ppermute | solution.py:205
  19.1 0.7 %collective-permute-start.3 = (bf16[128,512]{1,0:T(8,128)(2,1)}, bf16[128,512]{1,0:T(8,128)(2,1)}, u32[]{:S(2)}, u32[]{:S(2)}) collective-permute-start(bf16[128,512]{1,0:T(8,128)(2,1)} %param.1), channel_id=1, source_target_pairs={{0,16},{4,20},{8,24},{12,28},{16,0},{20,4},{24,8},{28,12},{1,17},{... | collective-permute-start | bytes 393224 | tf_op jit(solution)/shard_map/cond/branch_1_fun/ppermute | solution.py:205
  19.7 1.5 %collective-permute-start.1 = (bf16[128,512]{1,0:T(8,128)(2,1)}, bf16[128,512]{1,0:T(8,128)(2,1)}, u32[]{:S(2)}, u32[]{:S(2)}) collective-permute-start(bf16[128,512]{1,0:T(8,128)(2,1)} %param.1), channel_id=1, source_target_pairs={{0,8},{4,12},{8,0},{12,4},{16,24},{20,28},{24,16},{28,20},{1,9},{5... | collective-permute-start | bytes 393224 | tf_op jit(solution)/shard_map/cond/branch_1_fun/ppermute | solution.py:205
  21.2 4.1 %collective-permute-done.5 = bf16[128,512]{1,0:T(8,128)(2,1)} collective-permute-done((bf16[128,512]{1,0:T(8,128)(2,1)}, bf16[128,512]{1,0:T(8,128)(2,1)}, u32[]{:S(2)}, u32[]{:S(2)}) %collective-permute-start.5) | collective-permute-done | bytes 131104 | tf_op jit(solution)/shard_map/cond/branch_1_fun/ppermute | solution.py:205
  25.4 1.6 %collective-permute-done.3 = bf16[128,512]{1,0:T(8,128)(2,1)} collective-permute-done((bf16[128,512]{1,0:T(8,128)(2,1)}, bf16[128,512]{1,0:T(8,128)(2,1)}, u32[]{:S(2)}, u32[]{:S(2)}) %collective-permute-start.3) | collective-permute-done | bytes 131104 | tf_op jit(solution)/shard_map/cond/branch_1_fun/ppermute | solution.py:205
  27.5 1.2 %collective-permute-done.4 = bf16[128,512]{1,0:T(8,128)(2,1)} collective-permute-done((bf16[128,512]{1,0:T(8,128)(2,1)}, bf16[128,512]{1,0:T(8,128)(2,1)}, u32[]{:S(2)}, u32[]{:S(2)}) %collective-permute-start.4) | collective-permute-done | bytes 131104 | tf_op jit(solution)/shard_map/cond/branch_1_fun/ppermute | solution.py:205
  28.8 1.3 %collective-permute-start.20 = (bf16[128,1280]{1,0:T(8,128)(2,1)S(1)}, bf16[128,1280]{1,0:T(8,128)(2,1)S(1)}, u32[]{:S(2)}, u32[]{:S(2)}) collective-permute-start(bf16[128,1280]{1,0:T(8,128)(2,1)S(1)} %pad_maximum_fusion.refs_0_), channel_id=1, source_target_pairs={{0,24},{4,28},{8,16},{12,20},{16,8},{20,12},{24,0},{28,4},{1,25},{... | collective-permute-start | bytes 983048 | tf_op jit(solution)/shard_map/ppermute | solution.py:205
  30.1 0.7 %collective-permute-start.19 = (bf16[128,1280]{1,0:T(8,128)(2,1)S(1)}, bf16[128,1280]{1,0:T(8,128)(2,1)}, u32[]{:S(2)}, u32[]{:S(2)}) collective-permute-start(bf16[128,1280]{1,0:T(8,128)(2,1)S(1)} %pad_maximum_fusion.refs_0_), channel_id=1, source_target_pairs={{0,16},{4,20},{8,24},{12,28},{16,0},{20,4},{24,8},{28,12},{1,17},{... | collective-permute-start | bytes 983048 | tf_op jit(solution)/shard_map/ppermute | solution.py:205
  30.8 1.5 %collective-permute-start.18 = (bf16[128,1280]{1,0:T(8,128)(2,1)S(1)}, bf16[128,1280]{1,0:T(8,128)(2,1)}, u32[]{:S(2)}, u32[]{:S(2)}) collective-permute-start(bf16[128,1280]{1,0:T(8,128)(2,1)S(1)} %pad_maximum_fusion.refs_0_), channel_id=1, source_target_pairs={{0,8},{4,12},{8,0},{12,4},{16,24},{20,28},{24,16},{28,20},{1,9},{5... | collective-permute-start | bytes 983048 | tf_op jit(solution)/shard_map/ppermute | solution.py:205
  32.3 3.1 %project_2.1 = (bf16[256,768]{1,0:T(8,128)(2,1)}, bf16[256,768]{1,0:T(8,128)(2,1)}) custom-call(bf16[1024,768]{1,0:T(8,128)(2,1)S(1)} %stage.1.noise_ref, bf16[128,512]{1,0:T(8,128)(2,1)} %pad_maximum_fusion.1.refs_0_, bf16[128,512]{1,0:T(8,128)(2,1)} %get-tuple-element.47.refs_1_, bf16[128,512]{1,0:T(8,128)(2,1)} %get-tuple-element.48.refs_2_, ...), custom_call_target="tpu_custom_call" | custom-call | flops 805306368 | bytes 5242880 | tf_op jit(solution)/shard_map/project_2/pallas_call | solution.py:56
  35.5 1.6 %collective-permute-start.22 = (bf16[256,768]{1,0:T(8,128)(2,1)}, bf16[256,768]{1,0:T(8,128)(2,1)S(1)}, u32[]{:S(2)}, u32[]{:S(2)}) collective-permute-start(bf16[256,768]{1,0:T(8,128)(2,1)} %get-tuple-element.60), channel_id=1, source_target_pairs={{0,1},{1,2},{2,3},{3,0},{4,5},{5,6},{6,7},{7,4},{8,9},{9,10},{10,1... | collective-permute-start | bytes 1179656 | tf_op jit(solution)/shard_map/ppermute | solution.py:248
  37.1 2.2 %collective-permute-start.23 = (bf16[256,768]{1,0:T(8,128)(2,1)}, bf16[256,768]{1,0:T(8,128)(2,1)S(1)}, u32[]{:S(2)}, u32[]{:S(2)}) collective-permute-start(bf16[256,768]{1,0:T(8,128)(2,1)} %get-tuple-element.62), channel_id=1, source_target_pairs={{0,3},{1,0},{2,1},{3,2},{4,7},{5,4},{6,5},{7,6},{8,11},{9,8},{10,9... | collective-permute-start | bytes 1179656 | tf_op jit(solution)/shard_map/ppermute | solution.py:248
  39.3 1.0 %collective-permute-done.20.refs_3_ = bf16[128,1280]{1,0:T(8,128)(2,1)S(1)} collective-permute-done((bf16[128,1280]{1,0:T(8,128)(2,1)S(1)}, bf16[128,1280]{1,0:T(8,128)(2,1)S(1)}, u32[]{:S(2)}, u32[]{:S(2)}) %collective-permute-start.20) | collective-permute-done | bytes 327712 | tf_op jit(solution)/shard_map/ppermute | solution.py:205
  40.3 6.5 %collective-permute-done.19.refs_2_ = bf16[128,1280]{1,0:T(8,128)(2,1)} collective-permute-done((bf16[128,1280]{1,0:T(8,128)(2,1)S(1)}, bf16[128,1280]{1,0:T(8,128)(2,1)}, u32[]{:S(2)}, u32[]{:S(2)}) %collective-permute-start.19) | collective-permute-done | bytes 327712 | tf_op jit(solution)/shard_map/ppermute | solution.py:205
  46.8 2.7 %conditional.3 = (bf16[128,1280]{1,0:T(8,128)(2,1)}, bf16[128,1280]{1,0:T(8,128)(2,1)}, bf16[128,1280]{1,0:T(8,128)(2,1)}) conditional(s32[]{:T(128)} %convert_element_type.4, () %tuple.33, (bf16[128,1280]{1,0:T(8,128)(2,1)}, bf16[128,1280]{1,0:T(8,128)(2,1)}, bf16[128,1280]{1,0:T(8,128)(2,1)S(1)}) %tuple.34), branch_computations={%region_2.0_spmd, %region_3.0_spmd} | conditional | bytes 3932304 | solution.py:243
  47.4 1.4 %collective-permute-done.7 = bf16[128,1280]{1,0:T(8,128)(2,1)} collective-permute-done((bf16[128,1280]{1,0:T(8,128)(2,1)}, bf16[128,1280]{1,0:T(8,128)(2,1)}, u32[]{:S(2)}, u32[]{:S(2)}) %collective-permute-start.7) | collective-permute-done | bytes 327712 | tf_op jit(solution)/shard_map/cond/branch_1_fun/ppermute | solution.py:205
  49.5 1.0 %copy-done.3 = bf16[128,1280]{1,0:T(8,128)(2,1)S(1)} copy-done((bf16[128,1280]{1,0:T(8,128)(2,1)S(1)}, bf16[128,1280]{1,0:T(8,128)(2,1)}, u32[]{:S(2)}) %copy-start.3) | copy-done | bytes 327704
  50.5 3.3 %accumulate.1 = (bf16[1024,1024]{1,0:T(8,128)(2,1)S(1)}, f32[1024,768]{1,0:T(8,128)S(1)}) custom-call(s32[4,4]{1,0:T(4,128)S(1)} %copy-done.4, bf16[1024,768]{1,0:T(8,128)(2,1)S(1)} %copy-done.1, bf16[128,1280]{1,0:T(8,128)(2,1)S(1)} %pad_maximum_fusion.refs_0_, bf16[128,1280]{1,0:T(8,128)(2,1)} %collective-permute-done.18.refs_1_, ...), custom_call_target="tpu_custom_call" | custom-call | flops 1207959552 | bytes 9175040 | tf_op jit(solution)/shard_map/accumulate/pallas_call | solution.py:130
  53.9 2.1 %collective-permute-done.23.refs_1_ = bf16[256,768]{1,0:T(8,128)(2,1)S(1)} collective-permute-done((bf16[256,768]{1,0:T(8,128)(2,1)}, bf16[256,768]{1,0:T(8,128)(2,1)S(1)}, u32[]{:S(2)}, u32[]{:S(2)}) %collective-permute-start.23) | collective-permute-done | bytes 393248 | tf_op jit(solution)/shard_map/ppermute | solution.py:248
  55.9 3.4 %finish.1 = f32[1024,768]{1,0:T(8,128)} custom-call(s32[4,4]{1,0:T(4,128)S(1)} %copy-done.4, bf16[1024,1024]{1,0:T(8,128)(2,1)S(1)} %get-tuple-element.58.u_ref, f32[1024,768]{1,0:T(8,128)S(1)} %get-tuple-element.59.sum_ref, f32[1,1024]{1,0:T(1,128)S(1)} %bitcast.12, f32[1,1024]{1,0:T(1,128)S(1)} %bitcast.13, ...), custom_call_target="tpu_custom_call" | custom-call | flops 805306368 | bytes 12058624 | tf_op jit(solution)/shard_map/finish/pallas_call | solution.py:184
  (45 shorter events, 3.7 us)
Async XLA Ops:
  0.0 7.9 %copy-start.8 = (bf16[1,128,1024]{2,1,0:T(8,128)(2,1)S(1)}, bf16[1,128,1024]{2,1,0:T(8,128)(2,1)}, u32[]{:S(2)}) copy-start(bf16[1,128,1024]{2,1,0:T(8,128)(2,1)} %param.12) | copy-start | bytes 786436
  0.0 11.4 %copy-start.4 = (s32[4,4]{1,0:T(4,128)S(1)}, s32[4,4]{1,0:T(4,128)}, u32[]{:S(2)}) copy-start(s32[4,4]{1,0:T(4,128)} %ranks_ref.3) | copy-start | bytes 196
  1.0 11.5 %collective-permute-start.13 = (bf16[128,256]{1,0:T(8,128)(2,1)S(1)}, bf16[128,256]{1,0:T(8,128)(2,1)S(1)}, u32[]{:S(2)}, u32[]{:S(2)}) collective-permute-start(bf16[128,256]{1,0:T(8,128)(2,1)S(1)} %get-tuple-element.65.refs_0_), channel_id=1, source_target_pairs={{0,4},{4,0},{8,12},{12,8},{16,20},{20,16},{24,28},{28,24},{1,5},{5... | collective-permute-start | bytes 196616 | tf_op jit(solution)/shard_map/ppermute | solution.py:205
  1.5 9.3 %collective-permute-start.12 = (bf16[128,256]{1,0:T(8,128)(2,1)S(1)}, bf16[128,256]{1,0:T(8,128)(2,1)S(1)}, u32[]{:S(2)}, u32[]{:S(2)}) collective-permute-start(bf16[128,256]{1,0:T(8,128)(2,1)S(1)} %get-tuple-element.65.refs_0_), channel_id=1, source_target_pairs={{0,16},{4,20},{8,24},{12,28},{16,0},{20,4},{24,8},{28,12},{1,17},{... | collective-permute-start | bytes 196616 | tf_op jit(solution)/shard_map/ppermute | solution.py:205
  4.1 6.7 %collective-permute-start.11 = (bf16[128,256]{1,0:T(8,128)(2,1)S(1)}, bf16[128,256]{1,0:T(8,128)(2,1)S(1)}, u32[]{:S(2)}, u32[]{:S(2)}) collective-permute-start(bf16[128,256]{1,0:T(8,128)(2,1)S(1)} %get-tuple-element.65.refs_0_), channel_id=1, source_target_pairs={{0,8},{4,12},{8,0},{12,4},{16,24},{20,28},{24,16},{28,20},{1,9},{5... | collective-permute-start | bytes 196616 | tf_op jit(solution)/shard_map/ppermute | solution.py:205
  5.6 5.2 %collective-permute-start.10 = (bf16[128,256]{1,0:T(8,128)(2,1)S(1)}, bf16[128,256]{1,0:T(8,128)(2,1)S(1)}, u32[]{:S(2)}, u32[]{:S(2)}) collective-permute-start(bf16[128,256]{1,0:T(8,128)(2,1)S(1)} %get-tuple-element.65.refs_0_), channel_id=1, source_target_pairs={{0,24},{4,28},{8,16},{12,20},{16,8},{20,12},{24,0},{28,4},{1,25},{... | collective-permute-start | bytes 196616 | tf_op jit(solution)/shard_map/ppermute | solution.py:205
  5.7 1.4 %copy-start = (bf16[1024,768]{1,0:T(8,128)(2,1)S(1)}, bf16[1024,768]{1,0:T(8,128)(2,1)}, u32[]{:S(2)}) copy-start(bf16[1024,768]{1,0:T(8,128)(2,1)} %noise_ref.1) | copy-start | bytes 4718596
  10.8 1.8 %collective-permute-start.15 = (bf16[128,256]{1,0:T(8,128)(2,1)S(1)}, bf16[128,256]{1,0:T(8,128)(2,1)S(1)}, u32[]{:S(2)}, u32[]{:S(2)}) collective-permute-start(bf16[128,256]{1,0:T(8,128)(2,1)S(1)} %collective-permute-done.12.refs_2_), channel_id=1, source_target_pairs={{0,4},{4,0},{8,12},{12,8},{16,20},{20,16},{24,28},{28,24},{1,5},{5... | collective-permute-start | bytes 196616 | tf_op jit(solution)/shard_map/ppermute | solution.py:205
  10.8 1.8 %collective-permute-start.14 = (bf16[128,256]{1,0:T(8,128)(2,1)S(1)}, bf16[128,256]{1,0:T(8,128)(2,1)S(1)}, u32[]{:S(2)}, u32[]{:S(2)}) collective-permute-start(bf16[128,256]{1,0:T(8,128)(2,1)S(1)} %collective-permute-done.11.refs_1_), channel_id=1, source_target_pairs={{0,4},{4,0},{8,12},{12,8},{16,20},{20,16},{24,28},{28,24},{1,5},{5... | collective-permute-start | bytes 196616 | tf_op jit(solution)/shard_map/ppermute | solution.py:205
  11.3 1.3 %collective-permute-start.16 = (bf16[128,256]{1,0:T(8,128)(2,1)S(1)}, bf16[128,256]{1,0:T(8,128)(2,1)S(1)}, u32[]{:S(2)}, u32[]{:S(2)}) collective-permute-start(bf16[128,256]{1,0:T(8,128)(2,1)S(1)} %collective-permute-done.10.refs_3_), channel_id=1, source_target_pairs={{0,4},{4,0},{8,12},{12,8},{16,20},{20,16},{24,28},{28,24},{1,5},{5... | collective-permute-start | bytes 196616 | tf_op jit(solution)/shard_map/ppermute | solution.py:205
  14.0 3.0 %collective-permute-start.17 = (bf16[128,1280]{1,0:T(8,128)(2,1)S(1)}, bf16[128,1280]{1,0:T(8,128)(2,1)S(1)}, u32[]{:S(2)}, u32[]{:S(2)}) collective-permute-start(bf16[128,1280]{1,0:T(8,128)(2,1)S(1)} %pad_maximum_fusion.refs_0_), channel_id=1, source_target_pairs={{0,4},{4,0},{8,12},{12,8},{16,20},{20,16},{24,28},{28,24},{1,5},{5... | collective-permute-start | bytes 983048 | tf_op jit(solution)/shard_map/ppermute | solution.py:205
  14.4 22.6 %collective-permute-start.21 = (bf16[256,768]{1,0:T(8,128)(2,1)}, bf16[256,768]{1,0:T(8,128)(2,1)}, u32[]{:S(2)}, u32[]{:S(2)}) collective-permute-start(bf16[256,768]{1,0:T(8,128)(2,1)} %project_1.1), channel_id=1, source_target_pairs={{0,2},{1,3},{2,0},{3,1},{4,6},{5,7},{6,4},{7,5},{8,10},{9,11},{10,... | collective-permute-start | bytes 1179656 | tf_op jit(solution)/shard_map/ppermute | solution.py:248
  17.8 7.6 %collective-permute-start.5 = (bf16[128,512]{1,0:T(8,128)(2,1)}, bf16[128,512]{1,0:T(8,128)(2,1)}, u32[]{:S(2)}, u32[]{:S(2)}) collective-permute-start(bf16[128,512]{1,0:T(8,128)(2,1)} %param.1), channel_id=1, source_target_pairs={{0,24},{4,28},{8,16},{12,20},{16,8},{20,12},{24,0},{28,4},{1,25},{... | collective-permute-start | bytes 393224 | tf_op jit(solution)/shard_map/cond/branch_1_fun/ppermute | solution.py:205
  19.1 7.9 %collective-permute-start.3 = (bf16[128,512]{1,0:T(8,128)(2,1)}, bf16[128,512]{1,0:T(8,128)(2,1)}, u32[]{:S(2)}, u32[]{:S(2)}) collective-permute-start(bf16[128,512]{1,0:T(8,128)(2,1)} %param.1), channel_id=1, source_target_pairs={{0,16},{4,20},{8,24},{12,28},{16,0},{20,4},{24,8},{28,12},{1,17},{... | collective-permute-start | bytes 393224 | tf_op jit(solution)/shard_map/cond/branch_1_fun/ppermute | solution.py:205
  19.7 7.2 %collective-permute-start.1 = (bf16[128,512]{1,0:T(8,128)(2,1)}, bf16[128,512]{1,0:T(8,128)(2,1)}, u32[]{:S(2)}, u32[]{:S(2)}) collective-permute-start(bf16[128,512]{1,0:T(8,128)(2,1)} %param.1), channel_id=1, source_target_pairs={{0,8},{4,12},{8,0},{12,4},{16,24},{20,28},{24,16},{28,20},{1,9},{5... | collective-permute-start | bytes 393224 | tf_op jit(solution)/shard_map/cond/branch_1_fun/ppermute | solution.py:205
  21.2 6.2 %collective-permute-start = (bf16[128,512]{1,0:T(8,128)(2,1)}, bf16[128,512]{1,0:T(8,128)(2,1)}, u32[]{:S(2)}, u32[]{:S(2)}) collective-permute-start(bf16[128,512]{1,0:T(8,128)(2,1)} %param.1), channel_id=1, source_target_pairs={{0,4},{4,0},{8,12},{12,8},{16,20},{20,16},{24,28},{28,24},{1,5},{5... | collective-permute-start | bytes 393224 | tf_op jit(solution)/shard_map/cond/branch_1_fun/ppermute | solution.py:205
  25.4 2.1 %collective-permute-start.6 = (bf16[128,512]{1,0:T(8,128)(2,1)}, bf16[128,512]{1,0:T(8,128)(2,1)}, u32[]{:S(2)}, u32[]{:S(2)}) collective-permute-start(bf16[128,512]{1,0:T(8,128)(2,1)} %collective-permute-done.5), channel_id=1, source_target_pairs={{0,4},{4,0},{8,12},{12,8},{16,20},{20,16},{24,28},{28,24},{1,5},{5... | collective-permute-start | bytes 393224 | tf_op jit(solution)/shard_map/cond/branch_1_fun/ppermute | solution.py:205
  27.0 1.7 %collective-permute-start.4 = (bf16[128,512]{1,0:T(8,128)(2,1)}, bf16[128,512]{1,0:T(8,128)(2,1)}, u32[]{:S(2)}, u32[]{:S(2)}) collective-permute-start(bf16[128,512]{1,0:T(8,128)(2,1)} %collective-permute-done.3), channel_id=1, source_target_pairs={{0,4},{4,0},{8,12},{12,8},{16,20},{20,16},{24,28},{28,24},{1,5},{5... | collective-permute-start | bytes 393224 | tf_op jit(solution)/shard_map/cond/branch_1_fun/ppermute | solution.py:205
  27.0 1.9 %collective-permute-start.2 = (bf16[128,512]{1,0:T(8,128)(2,1)}, bf16[128,512]{1,0:T(8,128)(2,1)}, u32[]{:S(2)}, u32[]{:S(2)}) collective-permute-start(bf16[128,512]{1,0:T(8,128)(2,1)} %collective-permute-done.1), channel_id=1, source_target_pairs={{0,4},{4,0},{8,12},{12,8},{16,20},{20,16},{24,28},{28,24},{1,5},{5... | collective-permute-start | bytes 393224 | tf_op jit(solution)/shard_map/cond/branch_1_fun/ppermute | solution.py:205
  28.8 20.7 %copy-start.1 = (bf16[1024,768]{1,0:T(8,128)(2,1)S(1)}, bf16[1024,768]{1,0:T(8,128)(2,1)}, u32[]{:S(2)}) copy-start(bf16[1024,768]{1,0:T(8,128)(2,1)} %noise_ref.1) | copy-start | bytes 4718596
  28.8 11.5 %collective-permute-start.20 = (bf16[128,1280]{1,0:T(8,128)(2,1)S(1)}, bf16[128,1280]{1,0:T(8,128)(2,1)S(1)}, u32[]{:S(2)}, u32[]{:S(2)}) collective-permute-start(bf16[128,1280]{1,0:T(8,128)(2,1)S(1)} %pad_maximum_fusion.refs_0_), channel_id=1, source_target_pairs={{0,24},{4,28},{8,16},{12,20},{16,8},{20,12},{24,0},{28,4},{1,25},{... | collective-permute-start | bytes 983048 | tf_op jit(solution)/shard_map/ppermute | solution.py:205
  30.1 16.7 %collective-permute-start.19 = (bf16[128,1280]{1,0:T(8,128)(2,1)S(1)}, bf16[128,1280]{1,0:T(8,128)(2,1)}, u32[]{:S(2)}, u32[]{:S(2)}) collective-permute-start(bf16[128,1280]{1,0:T(8,128)(2,1)S(1)} %pad_maximum_fusion.refs_0_), channel_id=1, source_target_pairs={{0,16},{4,20},{8,24},{12,28},{16,0},{20,4},{24,8},{28,12},{1,17},{... | collective-permute-start | bytes 983048 | tf_op jit(solution)/shard_map/ppermute | solution.py:205
  30.8 16.0 %collective-permute-start.18 = (bf16[128,1280]{1,0:T(8,128)(2,1)S(1)}, bf16[128,1280]{1,0:T(8,128)(2,1)}, u32[]{:S(2)}, u32[]{:S(2)}) collective-permute-start(bf16[128,1280]{1,0:T(8,128)(2,1)S(1)} %pad_maximum_fusion.refs_0_), channel_id=1, source_target_pairs={{0,8},{4,12},{8,0},{12,4},{16,24},{20,28},{24,16},{28,20},{1,9},{5... | collective-permute-start | bytes 983048 | tf_op jit(solution)/shard_map/ppermute | solution.py:205
  35.5 18.4 %collective-permute-start.22 = (bf16[256,768]{1,0:T(8,128)(2,1)}, bf16[256,768]{1,0:T(8,128)(2,1)S(1)}, u32[]{:S(2)}, u32[]{:S(2)}) collective-permute-start(bf16[256,768]{1,0:T(8,128)(2,1)} %get-tuple-element.60), channel_id=1, source_target_pairs={{0,1},{1,2},{2,3},{3,0},{4,5},{5,6},{6,7},{7,4},{8,9},{9,10},{10,1... | collective-permute-start | bytes 1179656 | tf_op jit(solution)/shard_map/ppermute | solution.py:248
  37.1 18.9 %collective-permute-start.23 = (bf16[256,768]{1,0:T(8,128)(2,1)}, bf16[256,768]{1,0:T(8,128)(2,1)S(1)}, u32[]{:S(2)}, u32[]{:S(2)}) collective-permute-start(bf16[256,768]{1,0:T(8,128)(2,1)} %get-tuple-element.62), channel_id=1, source_target_pairs={{0,3},{1,0},{2,1},{3,2},{4,7},{5,4},{6,5},{7,6},{8,11},{9,8},{10,9... | collective-permute-start | bytes 1179656 | tf_op jit(solution)/shard_map/ppermute | solution.py:248
  40.3 6.5 %copy-start.7 = (bf16[128,1280]{1,0:T(8,128)(2,1)}, bf16[128,1280]{1,0:T(8,128)(2,1)S(1)}, u32[]{:S(2)}) copy-start(bf16[128,1280]{1,0:T(8,128)(2,1)S(1)} %collective-permute-done.20.refs_3_) | copy-start | bytes 983044
  46.8 2.0 %collective-permute-start.7 = (bf16[128,1280]{1,0:T(8,128)(2,1)}, bf16[128,1280]{1,0:T(8,128)(2,1)}, u32[]{:S(2)}, u32[]{:S(2)}) collective-permute-start(bf16[128,1280]{1,0:T(8,128)(2,1)} %get-tuple-element.12), channel_id=1, source_target_pairs={{0,4},{4,0},{8,12},{12,8},{16,20},{20,16},{24,28},{28,24},{1,5},{5... | collective-permute-start | bytes 983048 | tf_op jit(solution)/shard_map/cond/branch_1_fun/ppermute | solution.py:205
  46.9 2.4 %collective-permute-start.8 = (bf16[128,1280]{1,0:T(8,128)(2,1)}, bf16[128,1280]{1,0:T(8,128)(2,1)}, u32[]{:S(2)}, u32[]{:S(2)}) collective-permute-start(bf16[128,1280]{1,0:T(8,128)(2,1)} %get-tuple-element.13), channel_id=1, source_target_pairs={{0,4},{4,0},{8,12},{12,8},{16,20},{20,16},{24,28},{28,24},{1,5},{5... | collective-permute-start | bytes 983048 | tf_op jit(solution)/shard_map/cond/branch_1_fun/ppermute | solution.py:205
  47.3 2.2 %collective-permute-start.9 = (bf16[128,1280]{1,0:T(8,128)(2,1)S(1)}, bf16[128,1280]{1,0:T(8,128)(2,1)}, u32[]{:S(2)}, u32[]{:S(2)}) collective-permute-start(bf16[128,1280]{1,0:T(8,128)(2,1)S(1)} %get-tuple-element.14), channel_id=1, source_target_pairs={{0,4},{4,0},{8,12},{12,8},{16,20},{20,16},{24,28},{28,24},{1,5},{5... | collective-permute-start | bytes 983048 | tf_op jit(solution)/shard_map/cond/branch_1_fun/ppermute | solution.py:205
  49.5 1.0 %copy-start.3 = (bf16[128,1280]{1,0:T(8,128)(2,1)S(1)}, bf16[128,1280]{1,0:T(8,128)(2,1)}, u32[]{:S(2)}) copy-start(bf16[128,1280]{1,0:T(8,128)(2,1)} %copy-done.2) | copy-start | bytes 983044
  50.5 5.4 %copy-start.5 = (f32[1024]{0:T(1024)S(1)}, f32[1024]{0:T(1024)}, u32[]{:S(2)}) copy-start(f32[1024]{0:T(1024)} %param.14) | copy-start | bytes 12292
  50.5 5.4 %copy-start.6 = (f32[1024]{0:T(1024)S(1)}, f32[1024]{0:T(1024)}, u32[]{:S(2)}) copy-start(f32[1024]{0:T(1024)} %param.15) | copy-start | bytes 12292
  (1 other events, 0.7 us)

commit v11 on v10

--- a/solution.py
+++ b/solution.py
@@ -220,27 +220,21 @@
     return pieces
 
 
-def direct_rest(chunk):
-    pieces = with_other_core(from_chips(chunk))
-    del pieces[0, 0]
-    return pieces
-
-
 def from_other_core(pieces):
     return {place: array for place, array in with_other_core(pieces).items() if place not in pieces}
 
 
-def at_once(present, gather, *args):
-    shapes, tree = [], []
-
-    def flat(*args):
-        leaves, structure = jax.tree.flatten(gather(*args))
-        tree[:] = [structure]
-        return leaves
-
-    shapes = jax.eval_shape(flat, *args)
-    nothing = lambda *_: [jnp.zeros(leaf.shape, leaf.dtype) for leaf in shapes]
-    return jax.tree.unflatten(tree[0], lax.cond(present, flat, nothing, *args))
+def at_once(present, gather, pieces):
+    places, arrays, new = list(pieces), list(pieces.values()), []
+
+    def added(*arrays):
+        more = gather(dict(zip(places, arrays)))
+        new[:] = [place for place in more if place not in pieces]
+        return [more[place] for place in new]
+
+    count = len(jax.eval_shape(added, *arrays))
+    results = lax.cond(present, added, lambda *same: [same[0]] * count, *arrays)
+    return dict(zip(new, results))
 
 
 def along_site(coef, shift):
@@ -275,7 +269,8 @@
 
     u_swapped = swap(after(own_and_u, far), 1)
     v_rest = after(v_rest, far, u_swapped)
-    v_pieces = {(0, 0): v_rest, **at_once(present, direct_rest, v_rest)}
+    v_pieces = {(0, 0): v_rest}
+    v_pieces.update(at_once(present, lambda own: with_other_core(from_chips(own[0, 0])), v_pieces))
     u_pieces = from_chips(after(own_and_u, v_pieces))
     others = project(len(rest), noise_here, v_pieces.items())
     far = along_site(far, first)

time: 59.6 us -> 59 us (0.990)
  local copies, waits for them, and re-layouts: 4.63 us -> 2.96 us
  waiting for transfers between devices: 21 us -> 21.8 us
    unnamed x18 -> x22, local copies, waits for them, and re-layouts: 3.12 us -> 1.45 us
    ppermute x3, waiting for transfers between devices: 2.07 us -> 2.76 us  [along_site(): lax.ppermute(coef, 'site', [(k, (k + shift) % count) for k in range(count)])]
where the time goes in v11:
time: 59 us; the launch traced here: 58.8 us
  waiting for transfers between devices  21.8 us (37%)
  starting transfers between devices  20.4 us (35%)
  Pallas kernels  12.1 us (21%)
  local copies, waits for them, and re-layouts  2.96 us (5%)
  between operations  0.78 us (1%)
  other arithmetic  0.74 us (1%)
    ppermute x21, waiting for transfers between devices, swap(): lax.ppermute(array, 'real', [(k, k ^ distance) for k in range(count)])  19.1 us
    ppermute x21, starting transfers between devices, swap(): lax.ppermute(array, 'real', [(k, k ^ distance) for k in range(count)])  13.9 us
    ppermute x3, starting transfers between devices, along_site(): lax.ppermute(coef, 'site', [(k, (k + shift) % count) for k in range(count)])  6.41 us
    pallas_call x2, Pallas kernels, project(): pl.pallas_call(functools.partial(project_kernel, places, rows), out_shape...  4.57 us
    pallas_call x1, Pallas kernels, finish(): pl.pallas_call(functools.partial(finish_kernel, shifts), out_shape=jax.Sh...  3.41 us
    pallas_call x1, Pallas kernels, accumulate(): pl.pallas_call(functools.partial(accumulate_kernel, shifts, places, rows)...  3.3 us
    ppermute x3, waiting for transfers between devices, along_site(): lax.ppermute(coef, 'site', [(k, (k + shift) % count) for k in range(count)])  2.76 us
    unnamed x22, local copies, waits for them, and re-layouts  1.45 us
  transfers between devices with their start and end apart: 24, of which 11 were waited for; matrix products, arithmetic and copies ran while one was open for 2% of the time, Pallas kernels for 12%

profile of v11, /device:TPU:0, one launch (start us, length us, event | category | flops | bytes accessed | tf_op | source)
XLA Modules:
  0.0 58.8 jit_solution(15356073275640532860)
XLA Ops:
  0.0 1.0 %dynamic-slice_bitcast_fusion = (bf16[128,256]{1,0:T(8,128)(2,1)S(1)}, bf16[128,256]{1,0:T(8,128)(2,1)S(1)}, bf16[128,256]{1,0:T(8,128)(2,1)S(1)}, bf16[128,256]{1,0:T(8,128)(2,1)S(1)}) fusion(bf16[1,128,1024]{2,1,0:T(8,128)(2,1)} %param.11, s32[]{:T(128)S(6)} %select_n.15, s32[]{:T(128)S(6)} %select_n.13, s32[]{:T(128)S(6)} %select_n.12, s32[]{:T(128)S(6)} %select_n.14), kind=kLoop, calls=%fused_computation.2 | loop fusion | bytes 524304 | tf_op jit(solution)/shard_map/dynamic_slice | solution.py:257
  1.0 0.5 collective-permute-start.13
  1.5 2.6 %collective-permute-start.12 = (bf16[128,256]{1,0:T(8,128)(2,1)S(1)}, bf16[128,256]{1,0:T(8,128)(2,1)S(1)}, u32[]{:S(2)}, u32[]{:S(2)}) collective-permute-start(bf16[128,256]{1,0:T(8,128)(2,1)S(1)} %get-tuple-element.67.refs_0_), channel_id=1, source_target_pairs={{0,16},{4,20},{8,24},{12,28},{16,0},{20,4},{24,8},{28,12},{1,17},{... | collective-permute-start | bytes 196616 | tf_op jit(solution)/shard_map/ppermute | solution.py:205
  4.1 1.5 %collective-permute-start.11 = (bf16[128,256]{1,0:T(8,128)(2,1)S(1)}, bf16[128,256]{1,0:T(8,128)(2,1)S(1)}, u32[]{:S(2)}, u32[]{:S(2)}) collective-permute-start(bf16[128,256]{1,0:T(8,128)(2,1)S(1)} %get-tuple-element.67.refs_0_), channel_id=1, source_target_pairs={{0,8},{4,12},{8,0},{12,4},{16,24},{20,28},{24,16},{28,20},{1,9},{5... | collective-permute-start | bytes 196616 | tf_op jit(solution)/shard_map/ppermute | solution.py:205
  5.7 1.4 %copy-done = bf16[1024,768]{1,0:T(8,128)(2,1)S(1)} copy-done((bf16[1024,768]{1,0:T(8,128)(2,1)S(1)}, bf16[1024,768]{1,0:T(8,128)(2,1)}, u32[]{:S(2)}) %copy-start) | copy-done | bytes 1572888
  7.1 0.8 %stage.1.noise_ref = bf16[1024,768]{1,0:T(8,128)(2,1)S(1)} custom-call(bf16[1024,768]{1,0:T(8,128)(2,1)S(1)} %copy-done), custom_call_target="tpu_custom_call" | custom-call | bytes 3145728 | tf_op jit(solution)/shard_map/stage/pallas_call | solution.py:83
  7.9 0.7 %pad_maximum_fusion.1.refs_0_ = bf16[128,512]{1,0:T(8,128)(2,1)} fusion(bf16[128,256]{1,0:T(8,128)(2,1)S(1)} %get-tuple-element.68, bf16[128,256]{1,0:T(8,128)(2,1)S(1)} %get-tuple-element.66), kind=kLoop, calls=%fused_computation.1 | loop fusion | flops 262144 | bytes 262144 | tf_op jit(solution)/shard_map/concatenate | solution.py:260
  8.6 2.2 %collective-permute-done.10.refs_3_ = bf16[128,256]{1,0:T(8,128)(2,1)S(1)} collective-permute-done((bf16[128,256]{1,0:T(8,128)(2,1)S(1)}, bf16[128,256]{1,0:T(8,128)(2,1)S(1)}, u32[]{:S(2)}, u32[]{:S(2)}) %collective-permute-start.10) | collective-permute-done | bytes 65568 | tf_op jit(solution)/shard_map/ppermute | solution.py:205
  10.8 0.5 collective-permute-start.14
  11.4 0.5 slice.3
  12.6 1.4 %project_1.1 = bf16[256,768]{1,0:T(8,128)(2,1)} custom-call(bf16[1024,768]{1,0:T(8,128)(2,1)S(1)} %stage.1.noise_ref, bf16[128,256]{1,0:T(8,128)(2,1)S(1)} %get-tuple-element.67.refs_0_, bf16[128,256]{1,0:T(8,128)(2,1)S(1)} %collective-permute-done.11.refs_1_, bf16[128,256]{1,0:T(8,128)(2,1)S(1)} %collective-permute-done.12.refs_2_, ...), custom_call_target="tpu_custom_call" | custom-call | flops 402653184 | bytes 4194304 | tf_op jit(solution)/shard_map/project_1/pallas_call | solution.py:56
  14.4 2.6 %collective-permute-start.21 = (bf16[256,768]{1,0:T(8,128)(2,1)}, bf16[256,768]{1,0:T(8,128)(2,1)S(1)}, u32[]{:S(2)}, u32[]{:S(2)}) collective-permute-start(bf16[256,768]{1,0:T(8,128)(2,1)} %project_1.1), channel_id=1, source_target_pairs={{0,2},{1,3},{2,0},{3,1},{4,6},{5,7},{6,4},{7,5},{8,10},{9,11},{10,... | collective-permute-start | bytes 1179656 | tf_op jit(solution)/shard_map/ppermute | solution.py:242
  17.0 11.2 %conditional.2 = (bf16[128,512]{1,0:T(8,128)(2,1)}, bf16[128,512]{1,0:T(8,128)(2,1)}, bf16[128,512]{1,0:T(8,128)(2,1)}, bf16[128,512]{1,0:T(8,128)(2,1)}, bf16[1...) conditional(s32[]{:T(128)} %convert_element_type.4, ...), branch_computations={%region_0.0_spmd, %region_1.0_spmd} | conditional | bytes 3670352 | solution.py:236
  17.1 1.4 %collective-permute-start.2 = (bf16[128,512]{1,0:T(8,128)(2,1)}, bf16[128,512]{1,0:T(8,128)(2,1)}, u32[]{:S(2)}, u32[]{:S(2)}) collective-permute-start(bf16[128,512]{1,0:T(8,128)(2,1)} %param.1), channel_id=1, source_target_pairs={{0,24},{4,28},{8,16},{12,20},{16,8},{20,12},{24,0},{28,4},{1,25},{... | collective-permute-start | bytes 393224 | tf_op jit(solution)/shard_map/cond/branch_1_fun/ppermute | solution.py:205
  18.4 0.7 %collective-permute-start.1 = (bf16[128,512]{1,0:T(8,128)(2,1)}, bf16[128,512]{1,0:T(8,128)(2,1)}, u32[]{:S(2)}, u32[]{:S(2)}) collective-permute-start(bf16[128,512]{1,0:T(8,128)(2,1)} %param.1), channel_id=1, source_target_pairs={{0,16},{4,20},{8,24},{12,28},{16,0},{20,4},{24,8},{28,12},{1,17},{... | collective-permute-start | bytes 393224 | tf_op jit(solution)/shard_map/cond/branch_1_fun/ppermute | solution.py:205
  19.1 1.5 %collective-permute-start = (bf16[128,512]{1,0:T(8,128)(2,1)}, bf16[128,512]{1,0:T(8,128)(2,1)}, u32[]{:S(2)}, u32[]{:S(2)}) collective-permute-start(bf16[128,512]{1,0:T(8,128)(2,1)} %param.1), channel_id=1, source_target_pairs={{0,8},{4,12},{8,0},{12,4},{16,24},{20,28},{24,16},{28,20},{1,9},{5... | collective-permute-start | bytes 393224 | tf_op jit(solution)/shard_map/cond/branch_1_fun/ppermute | solution.py:205
  20.6 4.1 %collective-permute-done.2 = bf16[128,512]{1,0:T(8,128)(2,1)} collective-permute-done((bf16[128,512]{1,0:T(8,128)(2,1)}, bf16[128,512]{1,0:T(8,128)(2,1)}, u32[]{:S(2)}, u32[]{:S(2)}) %collective-permute-start.2) | collective-permute-done | bytes 131104 | tf_op jit(solution)/shard_map/cond/branch_1_fun/ppermute | solution.py:205
  24.7 1.6 %collective-permute-done.1 = bf16[128,512]{1,0:T(8,128)(2,1)} collective-permute-done((bf16[128,512]{1,0:T(8,128)(2,1)}, bf16[128,512]{1,0:T(8,128)(2,1)}, u32[]{:S(2)}, u32[]{:S(2)}) %collective-permute-start.1) | collective-permute-done | bytes 131104 | tf_op jit(solution)/shard_map/cond/branch_1_fun/ppermute | solution.py:205
  26.9 1.2 %collective-permute-done.5 = bf16[128,512]{1,0:T(8,128)(2,1)} collective-permute-done((bf16[128,512]{1,0:T(8,128)(2,1)}, bf16[128,512]{1,0:T(8,128)(2,1)}, u32[]{:S(2)}, u32[]{:S(2)}) %collective-permute-start.5) | collective-permute-done | bytes 131104 | tf_op jit(solution)/shard_map/cond/branch_1_fun/ppermute | solution.py:205
  28.2 1.4 %collective-permute-start.20 = (bf16[128,1280]{1,0:T(8,128)(2,1)}, bf16[128,1280]{1,0:T(8,128)(2,1)S(1)}, u32[]{:S(2)}, u32[]{:S(2)}) collective-permute-start(bf16[128,1280]{1,0:T(8,128)(2,1)} %copy-done.7), channel_id=1, source_target_pairs={{0,24},{4,28},{8,16},{12,20},{16,8},{20,12},{24,0},{28,4},{1,25},{... | collective-permute-start | bytes 983048 | tf_op jit(solution)/shard_map/ppermute | solution.py:205
  29.6 0.7 %collective-permute-start.19 = (bf16[128,1280]{1,0:T(8,128)(2,1)}, bf16[128,1280]{1,0:T(8,128)(2,1)}, u32[]{:S(2)}, u32[]{:S(2)}) collective-permute-start(bf16[128,1280]{1,0:T(8,128)(2,1)} %copy-done.7), channel_id=1, source_target_pairs={{0,16},{4,20},{8,24},{12,28},{16,0},{20,4},{24,8},{28,12},{1,17},{... | collective-permute-start | bytes 983048 | tf_op jit(solution)/shard_map/ppermute | solution.py:205
  30.3 1.5 %collective-permute-start.18 = (bf16[128,1280]{1,0:T(8,128)(2,1)}, bf16[128,1280]{1,0:T(8,128)(2,1)}, u32[]{:S(2)}, u32[]{:S(2)}) collective-permute-start(bf16[128,1280]{1,0:T(8,128)(2,1)} %copy-done.7), channel_id=1, source_target_pairs={{0,8},{4,12},{8,0},{12,4},{16,24},{20,28},{24,16},{28,20},{1,9},{5... | collective-permute-start | bytes 983048 | tf_op jit(solution)/shard_map/ppermute | solution.py:205
  31.8 3.1 %project_2.1 = (bf16[256,768]{1,0:T(8,128)(2,1)}, bf16[256,768]{1,0:T(8,128)(2,1)}) custom-call(bf16[1024,768]{1,0:T(8,128)(2,1)S(1)} %stage.1.noise_ref, bf16[128,512]{1,0:T(8,128)(2,1)} %pad_maximum_fusion.1.refs_0_, bf16[128,512]{1,0:T(8,128)(2,1)} %get-tuple-element.50.refs_1_, bf16[128,512]{1,0:T(8,128)(2,1)} %get-tuple-element.52.refs_2_, ...), custom_call_target="tpu_custom_call" | custom-call | flops 805306368 | bytes 5242880 | tf_op jit(solution)/shard_map/project_2/pallas_call | solution.py:56
  34.9 1.6 %collective-permute-start.22 = (bf16[256,768]{1,0:T(8,128)(2,1)}, bf16[256,768]{1,0:T(8,128)(2,1)S(1)}, u32[]{:S(2)}, u32[]{:S(2)}) collective-permute-start(bf16[256,768]{1,0:T(8,128)(2,1)} %get-tuple-element.62), channel_id=1, source_target_pairs={{0,1},{1,2},{2,3},{3,0},{4,5},{5,6},{6,7},{7,4},{8,9},{9,10},{10,1... | collective-permute-start | bytes 1179656 | tf_op jit(solution)/shard_map/ppermute | solution.py:242
  36.5 2.2 %collective-permute-start.23 = (bf16[256,768]{1,0:T(8,128)(2,1)}, bf16[256,768]{1,0:T(8,128)(2,1)S(1)}, u32[]{:S(2)}, u32[]{:S(2)}) collective-permute-start(bf16[256,768]{1,0:T(8,128)(2,1)} %get-tuple-element.64), channel_id=1, source_target_pairs={{0,3},{1,0},{2,1},{3,2},{4,7},{5,4},{6,5},{7,6},{8,11},{9,8},{10,9... | collective-permute-start | bytes 1179656 | tf_op jit(solution)/shard_map/ppermute | solution.py:242
  38.7 1.2 %collective-permute-done.20.refs_3_ = bf16[128,1280]{1,0:T(8,128)(2,1)S(1)} collective-permute-done((bf16[128,1280]{1,0:T(8,128)(2,1)}, bf16[128,1280]{1,0:T(8,128)(2,1)S(1)}, u32[]{:S(2)}, u32[]{:S(2)}) %collective-permute-start.20) | collective-permute-done | bytes 327712 | tf_op jit(solution)/shard_map/ppermute | solution.py:205
  40.0 6.5 %collective-permute-done.19.refs_2_ = bf16[128,1280]{1,0:T(8,128)(2,1)} collective-permute-done((bf16[128,1280]{1,0:T(8,128)(2,1)}, bf16[128,1280]{1,0:T(8,128)(2,1)}, u32[]{:S(2)}, u32[]{:S(2)}) %collective-permute-start.19) | collective-permute-done | bytes 327712 | tf_op jit(solution)/shard_map/ppermute | solution.py:205
  46.5 2.8 %conditional.3 = (bf16[128,1280]{1,0:T(8,128)(2,1)}, bf16[128,1280]{1,0:T(8,128)(2,1)}, bf16[128,1280]{1,0:T(8,128)(2,1)}) conditional(s32[]{:T(128)} %convert_element_type.4, bf16[128,1280]{1,0:T(8,128)(2,1)S(1)} %copy-done.8, (bf16[128,1280]{1,0:T(8,128)(2,1)}, bf16[128,1280]{1,0:T(8,128)(2,1)}, bf16[128,1280]{1,0:T(8,128)(2,1)S(1)}) %tuple.32), branch_computations={%region_2.0_spmd, %region_3.0_spmd} | conditional | bytes 3932304 | solution.py:236
  47.1 1.4 %collective-permute-done.7 = bf16[128,1280]{1,0:T(8,128)(2,1)} collective-permute-done((bf16[128,1280]{1,0:T(8,128)(2,1)}, bf16[128,1280]{1,0:T(8,128)(2,1)}, u32[]{:S(2)}, u32[]{:S(2)}) %collective-permute-start.7) | collective-permute-done | bytes 327712 | tf_op jit(solution)/shard_map/cond/branch_1_fun/ppermute | solution.py:205
  49.3 3.3 %accumulate.1 = (bf16[1024,1024]{1,0:T(8,128)(2,1)S(1)}, f32[1024,768]{1,0:T(8,128)S(1)}) custom-call(s32[4,4]{1,0:T(4,128)S(1)} %copy-done.4, bf16[1024,768]{1,0:T(8,128)(2,1)S(1)} %copy-done.1, bf16[128,1280]{1,0:T(8,128)(2,1)} %copy-done.7, bf16[128,1280]{1,0:T(8,128)(2,1)} %collective-permute-done.18.refs_1_, ...), custom_call_target="tpu_custom_call" | custom-call | flops 1207959552 | bytes 9175040 | tf_op jit(solution)/shard_map/accumulate/pallas_call | solution.py:130
  52.6 2.8 %collective-permute-done.23.refs_1_ = bf16[256,768]{1,0:T(8,128)(2,1)S(1)} collective-permute-done((bf16[256,768]{1,0:T(8,128)(2,1)}, bf16[256,768]{1,0:T(8,128)(2,1)S(1)}, u32[]{:S(2)}, u32[]{:S(2)}) %collective-permute-start.23) | collective-permute-done | bytes 393248 | tf_op jit(solution)/shard_map/ppermute | solution.py:242
  55.4 3.4 %finish.1 = f32[1024,768]{1,0:T(8,128)} custom-call(s32[4,4]{1,0:T(4,128)S(1)} %copy-done.4, bf16[1024,1024]{1,0:T(8,128)(2,1)S(1)} %get-tuple-element.60.u_ref, f32[1024,768]{1,0:T(8,128)S(1)} %get-tuple-element.61.sum_ref, f32[1,1024]{1,0:T(1,128)S(1)} %bitcast.12, f32[1,1024]{1,0:T(1,128)S(1)} %bitcast.13, ...), custom_call_target="tpu_custom_call" | custom-call | flops 805306368 | bytes 12058624 | tf_op jit(solution)/shard_map/finish/pallas_call | solution.py:184
  (49 shorter events, 2.7 us)
Async XLA Ops:
  0.0 7.9 %copy-start.10 = (bf16[1,128,1024]{2,1,0:T(8,128)(2,1)S(1)}, bf16[1,128,1024]{2,1,0:T(8,128)(2,1)}, u32[]{:S(2)}) copy-start(bf16[1,128,1024]{2,1,0:T(8,128)(2,1)} %param.12) | copy-start | bytes 786436
  0.0 11.4 %copy-start.4 = (s32[4,4]{1,0:T(4,128)S(1)}, s32[4,4]{1,0:T(4,128)}, u32[]{:S(2)}) copy-start(s32[4,4]{1,0:T(4,128)} %ranks_ref.3) | copy-start | bytes 196
  1.0 11.5 %collective-permute-start.13 = (bf16[128,256]{1,0:T(8,128)(2,1)S(1)}, bf16[128,256]{1,0:T(8,128)(2,1)S(1)}, u32[]{:S(2)}, u32[]{:S(2)}) collective-permute-start(bf16[128,256]{1,0:T(8,128)(2,1)S(1)} %get-tuple-element.67.refs_0_), channel_id=1, source_target_pairs={{0,4},{4,0},{8,12},{12,8},{16,20},{20,16},{24,28},{28,24},{1,5},{5... | collective-permute-start | bytes 196616 | tf_op jit(solution)/shard_map/ppermute | solution.py:205
  1.5 9.3 %collective-permute-start.12 = (bf16[128,256]{1,0:T(8,128)(2,1)S(1)}, bf16[128,256]{1,0:T(8,128)(2,1)S(1)}, u32[]{:S(2)}, u32[]{:S(2)}) collective-permute-start(bf16[128,256]{1,0:T(8,128)(2,1)S(1)} %get-tuple-element.67.refs_0_), channel_id=1, source_target_pairs={{0,16},{4,20},{8,24},{12,28},{16,0},{20,4},{24,8},{28,12},{1,17},{... | collective-permute-start | bytes 196616 | tf_op jit(solution)/shard_map/ppermute | solution.py:205
  4.1 6.7 %collective-permute-start.11 = (bf16[128,256]{1,0:T(8,128)(2,1)S(1)}, bf16[128,256]{1,0:T(8,128)(2,1)S(1)}, u32[]{:S(2)}, u32[]{:S(2)}) collective-permute-start(bf16[128,256]{1,0:T(8,128)(2,1)S(1)} %get-tuple-element.67.refs_0_), channel_id=1, source_target_pairs={{0,8},{4,12},{8,0},{12,4},{16,24},{20,28},{24,16},{28,20},{1,9},{5... | collective-permute-start | bytes 196616 | tf_op jit(solution)/shard_map/ppermute | solution.py:205
  5.6 5.2 %collective-permute-start.10 = (bf16[128,256]{1,0:T(8,128)(2,1)S(1)}, bf16[128,256]{1,0:T(8,128)(2,1)S(1)}, u32[]{:S(2)}, u32[]{:S(2)}) collective-permute-start(bf16[128,256]{1,0:T(8,128)(2,1)S(1)} %get-tuple-element.67.refs_0_), channel_id=1, source_target_pairs={{0,24},{4,28},{8,16},{12,20},{16,8},{20,12},{24,0},{28,4},{1,25},{... | collective-permute-start | bytes 196616 | tf_op jit(solution)/shard_map/ppermute | solution.py:205
  7.9 9.1 %copy-start.7 = (bf16[128,1280]{1,0:T(8,128)(2,1)}, bf16[128,1280]{1,0:T(8,128)(2,1)S(1)}, u32[]{:S(2)}) copy-start(bf16[128,1280]{1,0:T(8,128)(2,1)S(1)} %pad_maximum_fusion.refs_0_) | copy-start | bytes 983044
  10.8 1.8 %collective-permute-start.15 = (bf16[128,256]{1,0:T(8,128)(2,1)S(1)}, bf16[128,256]{1,0:T(8,128)(2,1)S(1)}, u32[]{:S(2)}, u32[]{:S(2)}) collective-permute-start(bf16[128,256]{1,0:T(8,128)(2,1)S(1)} %collective-permute-done.12.refs_2_), channel_id=1, source_target_pairs={{0,4},{4,0},{8,12},{12,8},{16,20},{20,16},{24,28},{28,24},{1,5},{5... | collective-permute-start | bytes 196616 | tf_op jit(solution)/shard_map/ppermute | solution.py:205
  10.8 1.8 %collective-permute-start.14 = (bf16[128,256]{1,0:T(8,128)(2,1)S(1)}, bf16[128,256]{1,0:T(8,128)(2,1)S(1)}, u32[]{:S(2)}, u32[]{:S(2)}) collective-permute-start(bf16[128,256]{1,0:T(8,128)(2,1)S(1)} %collective-permute-done.11.refs_1_), channel_id=1, source_target_pairs={{0,4},{4,0},{8,12},{12,8},{16,20},{20,16},{24,28},{28,24},{1,5},{5... | collective-permute-start | bytes 196616 | tf_op jit(solution)/shard_map/ppermute | solution.py:205
  11.3 1.3 %collective-permute-start.16 = (bf16[128,256]{1,0:T(8,128)(2,1)S(1)}, bf16[128,256]{1,0:T(8,128)(2,1)S(1)}, u32[]{:S(2)}, u32[]{:S(2)}) collective-permute-start(bf16[128,256]{1,0:T(8,128)(2,1)S(1)} %collective-permute-done.10.refs_3_), channel_id=1, source_target_pairs={{0,4},{4,0},{8,12},{12,8},{16,20},{20,16},{24,28},{28,24},{1,5},{5... | collective-permute-start | bytes 196616 | tf_op jit(solution)/shard_map/ppermute | solution.py:205
  14.0 3.0 %collective-permute-start.17 = (bf16[128,1280]{1,0:T(8,128)(2,1)S(1)}, bf16[128,1280]{1,0:T(8,128)(2,1)S(1)}, u32[]{:S(2)}, u32[]{:S(2)}) collective-permute-start(bf16[128,1280]{1,0:T(8,128)(2,1)S(1)} %pad_maximum_fusion.refs_0_), channel_id=1, source_target_pairs={{0,4},{4,0},{8,12},{12,8},{16,20},{20,16},{24,28},{28,24},{1,5},{5... | collective-permute-start | bytes 983048 | tf_op jit(solution)/shard_map/ppermute | solution.py:205
  14.4 22.1 %collective-permute-start.21 = (bf16[256,768]{1,0:T(8,128)(2,1)}, bf16[256,768]{1,0:T(8,128)(2,1)S(1)}, u32[]{:S(2)}, u32[]{:S(2)}) collective-permute-start(bf16[256,768]{1,0:T(8,128)(2,1)} %project_1.1), channel_id=1, source_target_pairs={{0,2},{1,3},{2,0},{3,1},{4,6},{5,7},{6,4},{7,5},{8,10},{9,11},{10,... | collective-permute-start | bytes 1179656 | tf_op jit(solution)/shard_map/ppermute | solution.py:242
  17.0 11.2 %copy-start.2 = (bf16[128,1280]{1,0:T(8,128)(2,1)}, bf16[128,1280]{1,0:T(8,128)(2,1)S(1)}, u32[]{:S(2)}) copy-start(bf16[128,1280]{1,0:T(8,128)(2,1)S(1)} %collective-permute-done.17.refs_4_) | copy-start | bytes 983044
  17.1 7.7 %collective-permute-start.2 = (bf16[128,512]{1,0:T(8,128)(2,1)}, bf16[128,512]{1,0:T(8,128)(2,1)}, u32[]{:S(2)}, u32[]{:S(2)}) collective-permute-start(bf16[128,512]{1,0:T(8,128)(2,1)} %param.1), channel_id=1, source_target_pairs={{0,24},{4,28},{8,16},{12,20},{16,8},{20,12},{24,0},{28,4},{1,25},{... | collective-permute-start | bytes 393224 | tf_op jit(solution)/shard_map/cond/branch_1_fun/ppermute | solution.py:205
  18.4 7.9 %collective-permute-start.1 = (bf16[128,512]{1,0:T(8,128)(2,1)}, bf16[128,512]{1,0:T(8,128)(2,1)}, u32[]{:S(2)}, u32[]{:S(2)}) collective-permute-start(bf16[128,512]{1,0:T(8,128)(2,1)} %param.1), channel_id=1, source_target_pairs={{0,16},{4,20},{8,24},{12,28},{16,0},{20,4},{24,8},{28,12},{1,17},{... | collective-permute-start | bytes 393224 | tf_op jit(solution)/shard_map/cond/branch_1_fun/ppermute | solution.py:205
  19.1 7.2 %collective-permute-start = (bf16[128,512]{1,0:T(8,128)(2,1)}, bf16[128,512]{1,0:T(8,128)(2,1)}, u32[]{:S(2)}, u32[]{:S(2)}) collective-permute-start(bf16[128,512]{1,0:T(8,128)(2,1)} %param.1), channel_id=1, source_target_pairs={{0,8},{4,12},{8,0},{12,4},{16,24},{20,28},{24,16},{28,20},{1,9},{5... | collective-permute-start | bytes 393224 | tf_op jit(solution)/shard_map/cond/branch_1_fun/ppermute | solution.py:205
  20.6 6.2 %collective-permute-start.3 = (bf16[128,512]{1,0:T(8,128)(2,1)}, bf16[128,512]{1,0:T(8,128)(2,1)}, u32[]{:S(2)}, u32[]{:S(2)}) collective-permute-start(bf16[128,512]{1,0:T(8,128)(2,1)} %param.1), channel_id=1, source_target_pairs={{0,4},{4,0},{8,12},{12,8},{16,20},{20,16},{24,28},{28,24},{1,5},{5... | collective-permute-start | bytes 393224 | tf_op jit(solution)/shard_map/cond/branch_1_fun/ppermute | solution.py:205
  24.7 2.1 %collective-permute-start.6 = (bf16[128,512]{1,0:T(8,128)(2,1)}, bf16[128,512]{1,0:T(8,128)(2,1)}, u32[]{:S(2)}, u32[]{:S(2)}) collective-permute-start(bf16[128,512]{1,0:T(8,128)(2,1)} %collective-permute-done.2), channel_id=1, source_target_pairs={{0,4},{4,0},{8,12},{12,8},{16,20},{20,16},{24,28},{28,24},{1,5},{5... | collective-permute-start | bytes 393224 | tf_op jit(solution)/shard_map/cond/branch_1_fun/ppermute | solution.py:205
  26.3 1.7 %collective-permute-start.5 = (bf16[128,512]{1,0:T(8,128)(2,1)}, bf16[128,512]{1,0:T(8,128)(2,1)}, u32[]{:S(2)}, u32[]{:S(2)}) collective-permute-start(bf16[128,512]{1,0:T(8,128)(2,1)} %collective-permute-done.1), channel_id=1, source_target_pairs={{0,4},{4,0},{8,12},{12,8},{16,20},{20,16},{24,28},{28,24},{1,5},{5... | collective-permute-start | bytes 393224 | tf_op jit(solution)/shard_map/cond/branch_1_fun/ppermute | solution.py:205
  26.4 1.9 %collective-permute-start.4 = (bf16[128,512]{1,0:T(8,128)(2,1)}, bf16[128,512]{1,0:T(8,128)(2,1)}, u32[]{:S(2)}, u32[]{:S(2)}) collective-permute-start(bf16[128,512]{1,0:T(8,128)(2,1)} %collective-permute-done), channel_id=1, source_target_pairs={{0,4},{4,0},{8,12},{12,8},{16,20},{20,16},{24,28},{28,24},{1,5},{5... | collective-permute-start | bytes 393224 | tf_op jit(solution)/shard_map/cond/branch_1_fun/ppermute | solution.py:205
  28.2 18.3 %copy-start.8 = (bf16[128,1280]{1,0:T(8,128)(2,1)S(1)}, bf16[128,1280]{1,0:T(8,128)(2,1)}, u32[]{:S(2)}) copy-start(bf16[128,1280]{1,0:T(8,128)(2,1)} %copy-done.7) | copy-start | bytes 983044
  28.2 21.0 %copy-start.1 = (bf16[1024,768]{1,0:T(8,128)(2,1)S(1)}, bf16[1024,768]{1,0:T(8,128)(2,1)}, u32[]{:S(2)}) copy-start(bf16[1024,768]{1,0:T(8,128)(2,1)} %noise_ref.1) | copy-start | bytes 4718596
  28.2 11.7 %collective-permute-start.20 = (bf16[128,1280]{1,0:T(8,128)(2,1)}, bf16[128,1280]{1,0:T(8,128)(2,1)S(1)}, u32[]{:S(2)}, u32[]{:S(2)}) collective-permute-start(bf16[128,1280]{1,0:T(8,128)(2,1)} %copy-done.7), channel_id=1, source_target_pairs={{0,24},{4,28},{8,16},{12,20},{16,8},{20,12},{24,0},{28,4},{1,25},{... | collective-permute-start | bytes 983048 | tf_op jit(solution)/shard_map/ppermute | solution.py:205
  29.6 16.9 %collective-permute-start.19 = (bf16[128,1280]{1,0:T(8,128)(2,1)}, bf16[128,1280]{1,0:T(8,128)(2,1)}, u32[]{:S(2)}, u32[]{:S(2)}) collective-permute-start(bf16[128,1280]{1,0:T(8,128)(2,1)} %copy-done.7), channel_id=1, source_target_pairs={{0,16},{4,20},{8,24},{12,28},{16,0},{20,4},{24,8},{28,12},{1,17},{... | collective-permute-start | bytes 983048 | tf_op jit(solution)/shard_map/ppermute | solution.py:205
  30.3 16.2 %collective-permute-start.18 = (bf16[128,1280]{1,0:T(8,128)(2,1)}, bf16[128,1280]{1,0:T(8,128)(2,1)}, u32[]{:S(2)}, u32[]{:S(2)}) collective-permute-start(bf16[128,1280]{1,0:T(8,128)(2,1)} %copy-done.7), channel_id=1, source_target_pairs={{0,8},{4,12},{8,0},{12,4},{16,24},{20,28},{24,16},{28,20},{1,9},{5... | collective-permute-start | bytes 983048 | tf_op jit(solution)/shard_map/ppermute | solution.py:205
  34.9 14.3 %copy-start.3 = (bf16[128,1280]{1,0:T(8,128)(2,1)S(1)}, bf16[128,1280]{1,0:T(8,128)(2,1)}, u32[]{:S(2)}) copy-start(bf16[128,1280]{1,0:T(8,128)(2,1)} %copy-done.2) | copy-start | bytes 983044
  34.9 17.7 %collective-permute-start.22 = (bf16[256,768]{1,0:T(8,128)(2,1)}, bf16[256,768]{1,0:T(8,128)(2,1)S(1)}, u32[]{:S(2)}, u32[]{:S(2)}) collective-permute-start(bf16[256,768]{1,0:T(8,128)(2,1)} %get-tuple-element.62), channel_id=1, source_target_pairs={{0,1},{1,2},{2,3},{3,0},{4,5},{5,6},{6,7},{7,4},{8,9},{9,10},{10,1... | collective-permute-start | bytes 1179656 | tf_op jit(solution)/shard_map/ppermute | solution.py:242
  36.5 18.9 %collective-permute-start.23 = (bf16[256,768]{1,0:T(8,128)(2,1)}, bf16[256,768]{1,0:T(8,128)(2,1)S(1)}, u32[]{:S(2)}, u32[]{:S(2)}) collective-permute-start(bf16[256,768]{1,0:T(8,128)(2,1)} %get-tuple-element.64), channel_id=1, source_target_pairs={{0,3},{1,0},{2,1},{3,2},{4,7},{5,4},{6,5},{7,6},{8,11},{9,8},{10,9... | collective-permute-start | bytes 1179656 | tf_op jit(solution)/shard_map/ppermute | solution.py:242
  40.0 6.5 %copy-start.9 = (bf16[128,1280]{1,0:T(8,128)(2,1)}, bf16[128,1280]{1,0:T(8,128)(2,1)S(1)}, u32[]{:S(2)}) copy-start(bf16[128,1280]{1,0:T(8,128)(2,1)S(1)} %collective-permute-done.20.refs_3_) | copy-start | bytes 983044
  46.5 2.0 %collective-permute-start.7 = (bf16[128,1280]{1,0:T(8,128)(2,1)}, bf16[128,1280]{1,0:T(8,128)(2,1)}, u32[]{:S(2)}, u32[]{:S(2)}) collective-permute-start(bf16[128,1280]{1,0:T(8,128)(2,1)} %get-tuple-element.14), channel_id=1, source_target_pairs={{0,4},{4,0},{8,12},{12,8},{16,20},{20,16},{24,28},{28,24},{1,5},{5... | collective-permute-start | bytes 983048 | tf_op jit(solution)/shard_map/cond/branch_1_fun/ppermute | solution.py:205
  46.6 2.4 %collective-permute-start.8 = (bf16[128,1280]{1,0:T(8,128)(2,1)}, bf16[128,1280]{1,0:T(8,128)(2,1)}, u32[]{:S(2)}, u32[]{:S(2)}) collective-permute-start(bf16[128,1280]{1,0:T(8,128)(2,1)} %get-tuple-element.15), channel_id=1, source_target_pairs={{0,4},{4,0},{8,12},{12,8},{16,20},{20,16},{24,28},{28,24},{1,5},{5... | collective-permute-start | bytes 983048 | tf_op jit(solution)/shard_map/cond/branch_1_fun/ppermute | solution.py:205
  47.1 2.2 %collective-permute-start.9 = (bf16[128,1280]{1,0:T(8,128)(2,1)S(1)}, bf16[128,1280]{1,0:T(8,128)(2,1)}, u32[]{:S(2)}, u32[]{:S(2)}) collective-permute-start(bf16[128,1280]{1,0:T(8,128)(2,1)S(1)} %get-tuple-element.16), channel_id=1, source_target_pairs={{0,4},{4,0},{8,12},{12,8},{16,20},{20,16},{24,28},{28,24},{1,5},{5... | collective-permute-start | bytes 983048 | tf_op jit(solution)/shard_map/cond/branch_1_fun/ppermute | solution.py:205
  (3 other events, 13.6 us)

commit v12 on v11

--- a/solution.py
+++ b/solution.py
@@ -24,12 +24,13 @@
     return pl.CostEstimate(flops=flops, bytes_accessed=2 * touched, transcendentals=0)
 
 
-def stack_pieces(places, rows, pieces, whole):
-    me = lax.axis_index("real")
-    for (distance, row), piece in zip(places, pieces):
-        height = piece.shape[0]
-        start = pl.multiple_of((me ^ distance) * rows + row, height)
-        whole[pl.ds(start, height), :] = piece[...]
+def stack_pieces(mine, others, whole):
+    core = lax.rem(lax.axis_index("real"), 2)
+    chips, rows, _ = mine.shape
+    for chip in range(chips):
+        for place, pieces in ((core, mine), (1 - core, others)):
+            start = pl.multiple_of((2 * chip + place) * rows, rows)
+            whole[pl.ds(start, rows), :] = pieces[chip]
 
 
 def project_columns(v_columns, noise_ref):
@@ -39,9 +40,9 @@
     return projected.astype(jnp.bfloat16)
 
 
-def project_kernel(places, rows, noise_ref, *refs):
-    pieces, outs, whole = refs[: len(places)], refs[len(places) : -1], refs[-1]
-    stack_pieces(places, rows, pieces, whole)
+def project_kernel(noise_ref, mine, others, *refs):
+    outs, whole = refs[:-1], refs[-1]
+    stack_pieces(mine, others, whole)
     for place, out_ref in enumerate(outs):
         columns = out_ref.shape[0]
         out_ref[...] = project_columns(
@@ -49,20 +50,19 @@
         )
 
 
-def project(n_shifts, noise, gathered):
+def project(n_shifts, noise, mine, others):
     sites, reals = noise.shape
-    places, pieces = zip(*gathered)
-    rows, columns = pieces[0].shape
-    return pl.pallas_call(
-        functools.partial(project_kernel, places, rows),
+    columns = mine.shape[2]
+    return pl.pallas_call(
+        project_kernel,
         out_shape=[jax.ShapeDtypeStruct((columns // n_shifts, reals), jnp.bfloat16)] * n_shifts,
-        in_specs=[VMEM] * (1 + len(pieces)),
+        in_specs=[VMEM] * 3,
         out_specs=[VMEM] * n_shifts,
         scratch_shapes=[pltpu.VMEM((sites, columns), jnp.bfloat16)],
         compiler_params=vmem(noise.shape, (sites, 2 * columns)),
-        cost_estimate=cost(2 * sites * columns * reals, noise, *pieces),
+        cost_estimate=cost(2 * sites * columns * reals, noise, mine, others),
         name=f"project_{n_shifts}",
-    )(noise, *pieces)
+    )(noise, mine, others)
 
 
 def stage_kernel(from_ref, to_ref, sems):
@@ -104,10 +104,10 @@
     return jnp.where(alive, coef.astype(jnp.float32), 0.0).astype(coef.dtype)
 
 
-def accumulate_kernel(shifts, places, rows, ranks_ref, noise_ref, *refs):
-    pieces, coefs = refs[: len(places)], refs[len(places) : len(places) + len(shifts)]
+def accumulate_kernel(shifts, ranks_ref, noise_ref, mine, others, *refs):
+    coefs = refs[: len(shifts)]
     u_ref, sum_ref, whole = refs[-3:]
-    stack_pieces(places, rows, pieces, whole)
+    stack_pieces(mine, others, whole)
     per_source = whole.shape[1] - u_ref.shape[1]
     u_ref[...] = whole[:, per_source:]
     own = project_columns(whole[:, :per_source], noise_ref)
@@ -122,24 +122,23 @@
     sum_ref[...] = total
 
 
-def accumulate(shifts, ranks, noise, gathered, coefs):
-    places, pieces = zip(*gathered)
+def accumulate(shifts, ranks, noise, mine, others, coefs):
     sites, reals = noise.shape
-    rows, columns = sites // lax.axis_size("real"), pieces[0].shape[1]
+    columns = mine.shape[2]
     per_source = coefs[0].shape[0]
     return pl.pallas_call(
-        functools.partial(accumulate_kernel, shifts, places, rows),
+        functools.partial(accumulate_kernel, shifts),
         out_shape=[
             jax.ShapeDtypeStruct((sites, columns - per_source), jnp.bfloat16),
             jax.ShapeDtypeStruct((sites, reals), jnp.float32),
         ],
-        in_specs=[SMEM] + [VMEM] * (1 + len(pieces) + len(coefs)),
+        in_specs=[SMEM] + [VMEM] * (3 + len(coefs)),
         out_specs=[VMEM] * 2,
         scratch_shapes=[pltpu.VMEM((sites, columns), jnp.bfloat16)],
         compiler_params=vmem((sites, 3 * reals), (sites, 2 * columns)),
-        cost_estimate=cost(6 * sites * per_source * reals, noise, *pieces, *coefs),
+        cost_estimate=cost(6 * sites * per_source * reals, noise, mine, others, *coefs),
         name="accumulate",
-    )(ranks, noise, *pieces, *coefs)
+    )(ranks, noise, mine, others, *coefs)
 
 
 def as_rows(ref, rows):
@@ -200,41 +199,30 @@
     return lax.optimization_barrier((value, before))[0]
 
 
-def swap(array, distance):
+def repeated(own):
+    return jnp.broadcast_to(own, (lax.axis_size("real") // 2, *own.shape))
+
+
+def from_chips(copies):
     count = lax.axis_size("real")
-    return lax.ppermute(array, "real", [(k, k ^ distance) for k in range(count)])
-
-
-def with_other_core(pieces):
-    both = dict(pieces)
-    for (distance, row), piece in pieces.items():
-        if (distance ^ 1, row) not in pieces:
-            both[distance ^ 1, row] = swap(piece, 1)
-    return both
-
-
-def from_chips(own):
-    pieces = {(0, 0): own}
-    for distance in range(2, lax.axis_size("real"), 2):
-        pieces[distance, 0] = swap(own, distance)
-    return pieces
+    cores = [list(range(core, count, 2)) for core in range(2)]
+    return lax.all_to_all(copies, "real", 0, 0, axis_index_groups=cores, tiled=True)
 
 
 def from_other_core(pieces):
-    return {place: array for place, array in with_other_core(pieces).items() if place not in pieces}
-
-
-def at_once(present, gather, pieces):
-    places, arrays, new = list(pieces), list(pieces.values()), []
-
-    def added(*arrays):
-        more = gather(dict(zip(places, arrays)))
-        new[:] = [place for place in more if place not in pieces]
-        return [more[place] for place in new]
-
-    count = len(jax.eval_shape(added, *arrays))
-    results = lax.cond(present, added, lambda *same: [same[0]] * count, *arrays)
-    return dict(zip(new, results))
+    count = lax.axis_size("real")
+    return lax.ppermute(pieces, "real", [(k, k ^ 1) for k in range(count)])
+
+
+def both(copies):
+    mine = from_chips(copies)
+    return mine, from_other_core(mine)
+
+
+def at_once(present, gather, array):
+    shapes = jax.eval_shape(gather, array)
+    same = lambda array: jax.tree.map(lambda _: array, shapes)
+    return lax.cond(present, gather, same, array)
 
 
 def along_site(coef, shift):
@@ -256,29 +244,23 @@
         start = lax.rem(source + shift, site_count) * per_dest
         return lax.dynamic_slice(v_factors[0], (0, start), (rows, per_dest))
 
-    v_first = columns_for(first)
-    v_rest = jnp.concatenate([columns_for(shift) for shift in rest], axis=1)
-    own_and_u = jnp.concatenate([columns_for(0), u_factors[0]], axis=1)
-    v_first = from_chips(v_first)
-    last = max(v_first)
-    waiting = (v_first[last], stage(noise), v_rest, own_and_u)
-    v_first[last], noise_here, v_rest, own_and_u = lax.optimization_barrier(waiting)
+    v_first = from_chips(repeated(columns_for(first)))
+    v_rest = repeated(jnp.concatenate([columns_for(shift) for shift in rest], axis=1))
+    own_and_u = repeated(jnp.concatenate([columns_for(0), u_factors[0]], axis=1))
+    waiting = (v_first, stage(noise), v_rest, own_and_u)
+    v_first, noise_here, v_rest, own_and_u = lax.optimization_barrier(waiting)
     present = ranks[0, 0] > 0
     noise_here, present = lax.optimization_barrier((noise_here, present))
-    [far] = project(1, noise_here, with_other_core(v_first).items())
-
-    u_swapped = swap(after(own_and_u, far), 1)
-    v_rest = after(v_rest, far, u_swapped)
-    v_pieces = {(0, 0): v_rest}
-    v_pieces.update(at_once(present, lambda own: with_other_core(from_chips(own[0, 0])), v_pieces))
-    u_pieces = from_chips(after(own_and_u, v_pieces))
-    others = project(len(rest), noise_here, v_pieces.items())
+    [far] = project(1, noise_here, v_first, from_other_core(v_first))
+
+    v_pieces = at_once(present, both, after(v_rest, far))
+    u_mine = from_chips(after(own_and_u, v_pieces))
+    others = project(len(rest), noise_here, *v_pieces)
     far = along_site(far, first)
-    others = [others[0], *after(others[1:], far)]
-    u_pieces = {**u_pieces, (1, 0): u_swapped}
-    u_pieces.update(at_once(present, from_other_core, u_pieces))
+    u_mine = after(u_mine, others[0])
+    u_others = at_once(present, from_other_core, u_mine)
     others = [along_site(coef, shift) for coef, shift in zip(others, rest)]
-    u_whole, total = accumulate((first,), ranks, noise, u_pieces.items(), [far])
+    u_whole, total = accumulate((first,), ranks, noise, u_mine, u_others, [far])
     return finish(rest, ranks, u_whole, total, skew_g[None], tail_h[None], others)
 
 

time: 59 us -> 75.7 us (1.28)
  the two profiles are of different devices: /device:TPU:0 before, /device:TPU:19 now
where the time goes in v12:
time: 75.7 us; the launch traced here: 75.1 us
  waiting for transfers between devices  29.4 us (39%)
  starting transfers between devices  15.9 us (21%)
  blocking collectives  11.4 us (15%)
  Pallas kernels  11.1 us (15%)
  local copies, waits for them, and re-layouts  6.51 us (9%)
    ppermute x3, waiting for transfers between devices, along_site(): lax.ppermute(coef, 'site', [(k, (k + shift) % count) for k in range(count)])  13.6 us
    all_to_all x2, waiting for transfers between devices, from_chips(): lax.all_to_all(copies, 'real', 0, 0, axis_index_groups=cores, tiled=True)  12 us
    all_to_all x1, blocking collectives, from_chips(): lax.all_to_all(copies, 'real', 0, 0, axis_index_groups=cores, tiled=True)  11.4 us
    all_to_all x2, starting transfers between devices, from_chips(): lax.all_to_all(copies, 'real', 0, 0, axis_index_groups=cores, tiled=True)  8.91 us
    ppermute x3, starting transfers between devices, from_other_core(): return lax.ppermute(pieces, 'real', [(k, k ^ 1) for k in range(count)])  4.51 us
    ppermute x3, waiting for transfers between devices, from_other_core(): return lax.ppermute(pieces, 'real', [(k, k ^ 1) for k in range(count)])  3.89 us
    pallas_call x2, Pallas kernels, project(): pl.pallas_call(project_kernel, out_shape=[jax.ShapeDtypeStruct((columns /...  3.52 us
    pallas_call x1, Pallas kernels, accumulate(): pl.pallas_call(functools.partial(accumulate_kernel, shifts), out_shape=[j...  3.5 us
  transfers between devices with their start and end apart: 8, of which 6 were waited for; matrix products, arithmetic and copies ran while one was open for 2% of the time, Pallas kernels for 10%

profile of v12, /device:TPU:19, one launch (start us, length us, event | category | flops | bytes accessed | tf_op | source)
XLA Modules:
  0.0 75.1 jit_solution(9554420075801207352)
XLA Ops:
  0.0 1.0 %dynamic-slice_bitcast_fusion = (bf16[128,256]{1,0:T(8,128)(2,1)S(1)}, bf16[128,256]{1,0:T(8,128)(2,1)S(1)}, bf16[128,256]{1,0:T(8,128)(2,1)S(1)}, bf16[128,256]{1,0:T(8,128)(2,1)S(1)}) fusion(bf16[1,128,1024]{2,1,0:T(8,128)(2,1)} %param.11, s32[]{:T(128)S(6)} %select_n.15, s32[]{:T(128)S(6)} %select_n.13, s32[]{:T(128)S(6)} %select_n.12, s32[]{:T(128)S(6)} %select_n.14), kind=kLoop, calls=%fused_computation.2 | loop fusion | bytes 524304 | tf_op jit(solution)/shard_map/dynamic_slice | solution.py:245
  1.0 0.7 broadcast_in_dim.15
  1.7 3.7 %all-to-all-start.1 = ((bf16[4,128,256]{2,1,0:T(8,128)(2,1)}), bf16[4,128,256]{2,1,0:T(8,128)(2,1)S(1)}, u32[]{:S(2)}, u32[]{:S(2)}) async-start(bf16[4,128,256]{2,1,0:T(8,128)(2,1)} %broadcast_in_dim.15), calls=%async_computation.1 | async-start | bytes 524288 | tf_op jit(solution)/shard_map/all_to_all | solution.py:209
  5.4 1.4 %copy-done = bf16[1024,768]{1,0:T(8,128)(2,1)S(1)} copy-done((bf16[1024,768]{1,0:T(8,128)(2,1)S(1)}, bf16[1024,768]{1,0:T(8,128)(2,1)}, u32[]{:S(2)}) %copy-start) | copy-done | bytes 1572888
  6.8 0.8 %stage.1.noise_ref = bf16[1024,768]{1,0:T(8,128)(2,1)S(1)} custom-call(bf16[1024,768]{1,0:T(8,128)(2,1)S(1)} %copy-done), custom_call_target="tpu_custom_call" | custom-call | bytes 3145728 | tf_op jit(solution)/shard_map/stage/pallas_call | solution.py:83
  7.6 0.0 copy-start.2
  7.6 0.1 copy-done.6
  7.8 1.4 %all-to-all-done.1.mine = bf16[4,128,256]{2,1,0:T(8,128)(2,1)S(1)} async-done(((bf16[4,128,256]{2,1,0:T(8,128)(2,1)}), bf16[4,128,256]{2,1,0:T(8,128)(2,1)S(1)}, u32[]{:S(2)}, u32[]{:S(2)}) %all-to-all-start.1) | async-done | bytes 262176 | tf_op jit(solution)/shard_map/all_to_all | solution.py:209
  9.1 0.8 %broadcast_in_dim.16 = bf16[4,128,512]{2,1,0:T(8,128)(2,1)} broadcast(bf16[128,512]{1,0:T(8,128)(2,1)S(1)} %pad_maximum_fusion.1), dimensions={1,2} | broadcast | bytes 655360 | tf_op jit(solution)/shard_map/broadcast_in_dim | solution.py:203
  9.9 1.1 %broadcast_in_dim.17 = bf16[4,128,1280]{2,1,0:T(8,128)(2,1)} broadcast(bf16[128,1280]{1,0:T(8,128)(2,1)S(1)} %pad_maximum_fusion), dimensions={1,2} | broadcast | bytes 1638400 | tf_op jit(solution)/shard_map/broadcast_in_dim | solution.py:203
  11.1 2.1 %collective-permute-start.2 = (bf16[4,128,256]{2,1,0:T(8,128)(2,1)S(1)}, bf16[4,128,256]{2,1,0:T(8,128)(2,1)S(1)}, u32[]{:S(2)}, u32[]{:S(2)}) collective-permute-start(bf16[4,128,256]{2,1,0:T(8,128)(2,1)S(1)} %all-to-all-done.1.mine), channel_id=1, source_target_pairs={{0,4},{4,0},{8,12},{12,8},{16,20},{20,16},{24,28},{28,24},{1,5},{5... | collective-permute-start | bytes 786440 | tf_op jit(solution)/shard_map/ppermute | solution.py:214
  13.2 0.5 slice.3
  14.4 0.0 collective-permute-done.2.others
  14.4 0.7 project_1.1
  15.0 14.3 %conditional.2 = (bf16[4,128,512]{2,1,0:T(8,128)(2,1)}, bf16[4,128,512]{2,1,0:T(8,128)(2,1)}) conditional(s32[]{:T(128)} %convert_element_type.4, bf16[4,128,512]{2,1,0:T(8,128)(2,1)} %broadcast_in_dim.16, bf16[4,128,512]{2,1,0:T(8,128)(2,1)} %broadcast_in_dim.16), branch_computations={%region_0.0_spmd, %region_1.0_spmd} | conditional | bytes 4194360 | solution.py:225
  15.1 11.4 %all_to_all.14 = bf16[4,128,512]{2,1,0:T(8,128)(2,1)S(1)} all-to-all(bf16[4,128,512]{2,1,0:T(8,128)(2,1)} %param.1), channel_id=1, replica_groups={{0,8,16,24},{4,12,20,28},{1,9,17,25},{5,13,21,29},{2,10,18,26},{6,14,22..., dimensions={0} | all-to-all | bytes 1048576 | tf_op jit(solution)/shard_map/cond/branch_1_fun/all_to_all | solution.py:209
  26.4 1.2 %collective-permute-start = (bf16[4,128,512]{2,1,0:T(8,128)(2,1)S(1)}, bf16[4,128,512]{2,1,0:T(8,128)(2,1)}, u32[]{:S(2)}, u32[]{:S(2)}) collective-permute-start(bf16[4,128,512]{2,1,0:T(8,128)(2,1)S(1)} %all_to_all.14), channel_id=1, source_target_pairs={{0,4},{4,0},{8,12},{12,8},{16,20},{20,16},{24,28},{28,24},{1,5},{5... | collective-permute-start | bytes 1572872 | tf_op jit(solution)/shard_map/cond/branch_1_fun/ppermute | solution.py:214
  27.6 0.8 %copy.9 = bf16[4,128,512]{2,1,0:T(8,128)(2,1)} copy(bf16[4,128,512]{2,1,0:T(8,128)(2,1)S(1)} %all_to_all.14) | data formatting | bytes 1048576 | tf_op jit(solution)/shard_map/cond
  28.4 0.9 %collective-permute-done = bf16[4,128,512]{2,1,0:T(8,128)(2,1)} collective-permute-done((bf16[4,128,512]{2,1,0:T(8,128)(2,1)S(1)}, bf16[4,128,512]{2,1,0:T(8,128)(2,1)}, u32[]{:S(2)}, u32[]{:S(2)}) %collective-permute-start) | collective-permute-done | bytes 524320 | tf_op jit(solution)/shard_map/cond/branch_1_fun/ppermute | solution.py:214
  29.3 5.2 %all-to-all-start.2 = ((bf16[4,128,1280]{2,1,0:T(8,128)(2,1)}), bf16[4,128,1280]{2,1,0:T(8,128)(2,1)}, u32[]{:S(2)}, u32[]{:S(2)}) async-start(bf16[4,128,1280]{2,1,0:T(8,128)(2,1)} %broadcast_in_dim.17), calls=%async_computation.2 | async-start | bytes 2621440 | tf_op jit(solution)/shard_map/all_to_all | solution.py:209
  34.5 0.1 collective-permute-start.3
  34.6 2.9 %project_2.1 = (bf16[256,768]{1,0:T(8,128)(2,1)S(1)}, bf16[256,768]{1,0:T(8,128)(2,1)}) custom-call(bf16[1024,768]{1,0:T(8,128)(2,1)S(1)} %stage.1.noise_ref, bf16[4,128,512]{2,1,0:T(8,128)(2,1)S(1)} %copy-done.5, bf16[4,128,512]{2,1,0:T(8,128)(2,1)} %get-tuple-element.35.others), custom_call_target="tpu_custom_call" | custom-call | flops 805306368 | bytes 5242880 | tf_op jit(solution)/shard_map/project_2/pallas_call | solution.py:56
  37.5 2.4 %collective-permute-start.5 = (bf16[256,768]{1,0:T(8,128)(2,1)}, bf16[256,768]{1,0:T(8,128)(2,1)S(1)}, u32[]{:S(2)}, u32[]{:S(2)}) collective-permute-start(bf16[256,768]{1,0:T(8,128)(2,1)} %get-tuple-element.41), channel_id=1, source_target_pairs={{0,3},{1,0},{2,1},{3,2},{4,7},{5,4},{6,5},{7,6},{8,11},{9,8},{10,9... | collective-permute-start | bytes 1179656 | tf_op jit(solution)/shard_map/ppermute | solution.py:230
  39.9 10.6 %all-to-all-done.2.mine = bf16[4,128,1280]{2,1,0:T(8,128)(2,1)} async-done(((bf16[4,128,1280]{2,1,0:T(8,128)(2,1)}), bf16[4,128,1280]{2,1,0:T(8,128)(2,1)}, u32[]{:S(2)}, u32[]{:S(2)}) %all-to-all-start.2) | async-done | bytes 1310752 | tf_op jit(solution)/shard_map/all_to_all | solution.py:209
  50.5 4.2 %conditional.3 = (bf16[4,128,1280]{2,1,0:T(8,128)(2,1)}) conditional(s32[]{:T(128)} %convert_element_type.4, bf16[4,128,1280]{2,1,0:T(8,128)(2,1)} %all-to-all-done.2.mine, bf16[4,128,1280]{2,1,0:T(8,128)(2,1)} %all-to-all-done.2.mine), branch_computations={%region_2.0_spmd, %region_3.0_spmd} | conditional | bytes 5242928 | solution.py:225
  50.5 1.2 %collective-permute-start.1 = (bf16[4,128,1280]{2,1,0:T(8,128)(2,1)}, bf16[4,128,1280]{2,1,0:T(8,128)(2,1)}, u32[]{:S(2)}, u32[]{:S(2)}) collective-permute-start(bf16[4,128,1280]{2,1,0:T(8,128)(2,1)} %param.3), channel_id=1, source_target_pairs={{0,4},{4,0},{8,12},{12,8},{16,20},{20,16},{24,28},{28,24},{1,5},{5... | collective-permute-start | bytes 3932168 | tf_op jit(solution)/shard_map/cond/branch_1_fun/ppermute | solution.py:214
  51.7 3.0 %collective-permute-done.1 = bf16[4,128,1280]{2,1,0:T(8,128)(2,1)} collective-permute-done((bf16[4,128,1280]{2,1,0:T(8,128)(2,1)}, bf16[4,128,1280]{2,1,0:T(8,128)(2,1)}, u32[]{:S(2)}, u32[]{:S(2)}) %collective-permute-start.1) | collective-permute-done | bytes 1310752 | tf_op jit(solution)/shard_map/cond/branch_1_fun/ppermute | solution.py:214
  54.7 0.0 collective-permute-done.3.refs_0_
  54.7 3.5 %accumulate.1 = (bf16[1024,1024]{1,0:T(8,128)(2,1)S(1)}, f32[1024,768]{1,0:T(8,128)S(1)}) custom-call(s32[4,4]{1,0:T(4,128)S(1)} %copy-done.2, bf16[1024,768]{1,0:T(8,128)(2,1)S(1)} %copy-done.1, bf16[4,128,1280]{2,1,0:T(8,128)(2,1)} %all-to-all-done.2.mine, bf16[4,128,1280]{2,1,0:T(8,128)(2,1)} %get-tuple-element.50.others, ...), custom_call_target="tpu_custom_call" | custom-call | flops 1207959552 | bytes 9175040 | tf_op jit(solution)/shard_map/accumulate/pallas_call | solution.py:129
  58.2 9.6 %collective-permute-done.5.refs_1_ = bf16[256,768]{1,0:T(8,128)(2,1)S(1)} collective-permute-done((bf16[256,768]{1,0:T(8,128)(2,1)}, bf16[256,768]{1,0:T(8,128)(2,1)S(1)}, u32[]{:S(2)}, u32[]{:S(2)}) %collective-permute-start.5) | collective-permute-done | bytes 393248 | tf_op jit(solution)/shard_map/ppermute | solution.py:230
  67.8 4.0 %collective-permute-done.4.refs_0_ = bf16[256,768]{1,0:T(8,128)(2,1)S(1)} collective-permute-done((bf16[256,768]{1,0:T(8,128)(2,1)S(1)}, bf16[256,768]{1,0:T(8,128)(2,1)S(1)}, u32[]{:S(2)}, u32[]{:S(2)}) %collective-permute-start.4) | collective-permute-done | bytes 393248 | tf_op jit(solution)/shard_map/ppermute | solution.py:230
  71.8 3.3 %finish.1 = f32[1024,768]{1,0:T(8,128)} custom-call(s32[4,4]{1,0:T(4,128)S(1)} %copy-done.2, bf16[1024,1024]{1,0:T(8,128)(2,1)S(1)} %get-tuple-element.39.u_ref, f32[1024,768]{1,0:T(8,128)S(1)} %get-tuple-element.40.sum_ref, f32[1,1024]{1,0:T(1,128)S(1)} %bitcast.12, f32[1,1024]{1,0:T(1,128)S(1)} %bitcast.13, ...), custom_call_target="tpu_custom_call" | custom-call | flops 805306368 | bytes 12058624 | tf_op jit(solution)/shard_map/finish/pallas_call | solution.py:183
  (14 shorter events, 0.1 us)
Async XLA Ops:
  1.7 7.4 %all-to-all-start.1 = ((bf16[4,128,256]{2,1,0:T(8,128)(2,1)}), bf16[4,128,256]{2,1,0:T(8,128)(2,1)S(1)}, u32[]{:S(2)}, u32[]{:S(2)}) async-start(bf16[4,128,256]{2,1,0:T(8,128)(2,1)} %broadcast_in_dim.15), calls=%async_computation.1 | async-start | bytes 524288 | tf_op jit(solution)/shard_map/all_to_all | solution.py:209
  5.4 1.4 %copy-start = (bf16[1024,768]{1,0:T(8,128)(2,1)S(1)}, bf16[1024,768]{1,0:T(8,128)(2,1)}, u32[]{:S(2)}) copy-start(bf16[1024,768]{1,0:T(8,128)(2,1)} %noise_ref.1) | copy-start | bytes 4718596
  6.8 0.9 %copy-start.6 = (bf16[1,128,1024]{2,1,0:T(8,128)(2,1)S(1)}, bf16[1,128,1024]{2,1,0:T(8,128)(2,1)}, u32[]{:S(2)}) copy-start(bf16[1,128,1024]{2,1,0:T(8,128)(2,1)} %param.12) | copy-start | bytes 786436
  7.6 5.6 %copy-start.2 = (s32[4,4]{1,0:T(4,128)S(1)}, s32[4,4]{1,0:T(4,128)}, u32[]{:S(2)}) copy-start(s32[4,4]{1,0:T(4,128)} %ranks_ref.3) | copy-start | bytes 196
  11.1 3.3 %collective-permute-start.2 = (bf16[4,128,256]{2,1,0:T(8,128)(2,1)S(1)}, bf16[4,128,256]{2,1,0:T(8,128)(2,1)S(1)}, u32[]{:S(2)}, u32[]{:S(2)}) collective-permute-start(bf16[4,128,256]{2,1,0:T(8,128)(2,1)S(1)} %all-to-all-done.1.mine), channel_id=1, source_target_pairs={{0,4},{4,0},{8,12},{12,8},{16,20},{20,16},{24,28},{28,24},{1,5},{5... | collective-permute-start | bytes 786440 | tf_op jit(solution)/shard_map/ppermute | solution.py:214
  26.4 2.9 %collective-permute-start = (bf16[4,128,512]{2,1,0:T(8,128)(2,1)S(1)}, bf16[4,128,512]{2,1,0:T(8,128)(2,1)}, u32[]{:S(2)}, u32[]{:S(2)}) collective-permute-start(bf16[4,128,512]{2,1,0:T(8,128)(2,1)S(1)} %all_to_all.14), channel_id=1, source_target_pairs={{0,4},{4,0},{8,12},{12,8},{16,20},{20,16},{24,28},{28,24},{1,5},{5... | collective-permute-start | bytes 1572872 | tf_op jit(solution)/shard_map/cond/branch_1_fun/ppermute | solution.py:214
  29.3 5.3 %copy-start.5 = (bf16[4,128,512]{2,1,0:T(8,128)(2,1)S(1)}, bf16[4,128,512]{2,1,0:T(8,128)(2,1)}, u32[]{:S(2)}) copy-start(bf16[4,128,512]{2,1,0:T(8,128)(2,1)} %get-tuple-element.34.mine) | copy-start | bytes 1572868
  29.3 21.2 %all-to-all-start.2 = ((bf16[4,128,1280]{2,1,0:T(8,128)(2,1)}), bf16[4,128,1280]{2,1,0:T(8,128)(2,1)}, u32[]{:S(2)}, u32[]{:S(2)}) async-start(bf16[4,128,1280]{2,1,0:T(8,128)(2,1)} %broadcast_in_dim.17), calls=%async_computation.2 | async-start | bytes 2621440 | tf_op jit(solution)/shard_map/all_to_all | solution.py:209
  34.5 20.2 %collective-permute-start.3 = (bf16[256,768]{1,0:T(8,128)(2,1)S(1)}, bf16[256,768]{1,0:T(8,128)(2,1)S(1)}, u32[]{:S(2)}, u32[]{:S(2)}) collective-permute-start(bf16[256,768]{1,0:T(8,128)(2,1)S(1)} %project_1.1), channel_id=1, source_target_pairs={{0,2},{1,3},{2,0},{3,1},{4,6},{5,7},{6,4},{7,5},{8,10},{9,11},{10,... | collective-permute-start | bytes 1179656 | tf_op jit(solution)/shard_map/ppermute | solution.py:230
  37.5 17.3 %copy-start.1 = (bf16[1024,768]{1,0:T(8,128)(2,1)S(1)}, bf16[1024,768]{1,0:T(8,128)(2,1)}, u32[]{:S(2)}) copy-start(bf16[1024,768]{1,0:T(8,128)(2,1)} %noise_ref.1) | copy-start | bytes 4718596
  37.5 30.4 %collective-permute-start.5 = (bf16[256,768]{1,0:T(8,128)(2,1)}, bf16[256,768]{1,0:T(8,128)(2,1)S(1)}, u32[]{:S(2)}, u32[]{:S(2)}) collective-permute-start(bf16[256,768]{1,0:T(8,128)(2,1)} %get-tuple-element.41), channel_id=1, source_target_pairs={{0,3},{1,0},{2,1},{3,2},{4,7},{5,4},{6,5},{7,6},{8,11},{9,8},{10,9... | collective-permute-start | bytes 1179656 | tf_op jit(solution)/shard_map/ppermute | solution.py:230
  39.9 31.9 %collective-permute-start.4 = (bf16[256,768]{1,0:T(8,128)(2,1)S(1)}, bf16[256,768]{1,0:T(8,128)(2,1)S(1)}, u32[]{:S(2)}, u32[]{:S(2)}) collective-permute-start(bf16[256,768]{1,0:T(8,128)(2,1)S(1)} %get-tuple-element.37), channel_id=1, source_target_pairs={{0,1},{1,2},{2,3},{3,0},{4,5},{5,6},{6,7},{7,4},{8,9},{9,10},{10,1... | collective-permute-start | bytes 1179656 | tf_op jit(solution)/shard_map/ppermute | solution.py:230
  50.5 4.2 %collective-permute-start.1 = (bf16[4,128,1280]{2,1,0:T(8,128)(2,1)}, bf16[4,128,1280]{2,1,0:T(8,128)(2,1)}, u32[]{:S(2)}, u32[]{:S(2)}) collective-permute-start(bf16[4,128,1280]{2,1,0:T(8,128)(2,1)} %param.3), channel_id=1, source_target_pairs={{0,4},{4,0},{8,12},{12,8},{16,20},{20,16},{24,28},{28,24},{1,5},{5... | collective-permute-start | bytes 3932168 | tf_op jit(solution)/shard_map/cond/branch_1_fun/ppermute | solution.py:214
  54.7 17.1 %copy-start.3 = (f32[1024]{0:T(1024)S(1)}, f32[1024]{0:T(1024)}, u32[]{:S(2)}) copy-start(f32[1024]{0:T(1024)} %param.14) | copy-start | bytes 12292
  54.7 17.1 %copy-start.4 = (f32[1024]{0:T(1024)S(1)}, f32[1024]{0:T(1024)}, u32[]{:S(2)}) copy-start(f32[1024]{0:T(1024)} %param.15) | copy-start | bytes 12292

commit v13 on v11

--- a/solution.py
+++ b/solution.py
@@ -40,26 +40,56 @@
 
 
 def project_kernel(places, rows, noise_ref, *refs):
-    pieces, outs, whole = refs[: len(places)], refs[len(places) : -1], refs[-1]
-    stack_pieces(places, rows, pieces, whole)
+    pieces, outs = refs[: len(places)], refs[len(places) : -4]
+    whole, results, in_sems, out_sems = refs[-4:]
+    me = lax.axis_index("real")
+    arriving = []
+    for number, ((distance, row), piece) in enumerate(zip(places, pieces)):
+        height = piece.shape[0]
+        start = pl.multiple_of((me ^ distance) * rows + row, height)
+        copy = pltpu.make_async_copy(piece, whole.at[pl.ds(start, height), :], in_sems.at[number])
+        copy.start()
+        arriving.append(copy)
+    for copy in arriving:
+        copy.wait()
+    leaving = []
+    halves = out_sems.shape[0] // len(outs)
     for place, out_ref in enumerate(outs):
-        columns = out_ref.shape[0]
-        out_ref[...] = project_columns(
-            whole[:, place * columns : (place + 1) * columns], noise_ref
-        )
+        block = out_ref.shape[0] // halves
+        for half in range(halves):
+            number = place * halves + half
+            results[number] = project_columns(
+                whole[:, number * block : (number + 1) * block], noise_ref
+            )
+            span = pl.ds(half * block, block)
+            copy = pltpu.make_async_copy(
+                results.at[number], out_ref.at[span, :], out_sems.at[number]
+            )
+            copy.start()
+            leaving.append(copy)
+    for copy in leaving:
+        copy.wait()
 
 
 def project(n_shifts, noise, gathered):
     sites, reals = noise.shape
     places, pieces = zip(*gathered)
     rows, columns = pieces[0].shape
+    halves = 2 if n_shifts == 1 else 1
+    count = n_shifts * halves
+    anywhere = pl.BlockSpec(memory_space=pl.ANY)
     return pl.pallas_call(
         functools.partial(project_kernel, places, rows),
         out_shape=[jax.ShapeDtypeStruct((columns // n_shifts, reals), jnp.bfloat16)] * n_shifts,
-        in_specs=[VMEM] * (1 + len(pieces)),
-        out_specs=[VMEM] * n_shifts,
-        scratch_shapes=[pltpu.VMEM((sites, columns), jnp.bfloat16)],
-        compiler_params=vmem(noise.shape, (sites, 2 * columns)),
+        in_specs=[VMEM] + [anywhere] * len(pieces),
+        out_specs=[anywhere] * n_shifts,
+        scratch_shapes=[
+            pltpu.VMEM((sites, columns), jnp.bfloat16),
+            pltpu.VMEM((count, columns // count, reals), jnp.bfloat16),
+            pltpu.SemaphoreType.DMA((len(pieces),)),
+            pltpu.SemaphoreType.DMA((count,)),
+        ],
+        compiler_params=vmem(noise.shape, (sites, 2 * columns), (columns, reals)),
         cost_estimate=cost(2 * sites * columns * reals, noise, *pieces),
         name=f"project_{n_shifts}",
     )(noise, *pieces)
@@ -104,9 +134,14 @@
     return jnp.where(alive, coef.astype(jnp.float32), 0.0).astype(coef.dtype)
 
 
-def accumulate_kernel(shifts, places, rows, ranks_ref, noise_ref, *refs):
+def as_rows(ref, rows):
+    values = ref[:, rows]
+    return jnp.transpose(jnp.broadcast_to(values, (values.shape[1], values.shape[1])))
+
+
+def accumulate_kernel(shifts, places, rows, ranks_ref, noise_ref, skew_ref, tail_ref, *refs):
     pieces, coefs = refs[: len(places)], refs[len(places) : len(places) + len(shifts)]
-    u_ref, sum_ref, whole = refs[-3:]
+    u_ref, sum_ref, skew_rows, tail_rows, whole = refs[-5:]
     stack_pieces(places, rows, pieces, whole)
     per_source = whole.shape[1] - u_ref.shape[1]
     u_ref[...] = whole[:, per_source:]
@@ -120,9 +155,13 @@
             preferred_element_type=jnp.float32,
         )
     sum_ref[...] = total
-
-
-def accumulate(shifts, ranks, noise, gathered, coefs):
+    lanes = skew_rows.shape[1]
+    for start in range(0, skew_rows.shape[0], lanes):
+        part = slice(start, start + lanes)
+        skew_rows[part, :], tail_rows[part, :] = as_rows(skew_ref, part), as_rows(tail_ref, part)
+
+
+def accumulate(shifts, ranks, noise, skew, tail, gathered, coefs):
     places, pieces = zip(*gathered)
     sites, reals = noise.shape
     rows, columns = sites // lax.axis_size("real"), pieces[0].shape[1]
@@ -132,19 +171,16 @@
         out_shape=[
             jax.ShapeDtypeStruct((sites, columns - per_source), jnp.bfloat16),
             jax.ShapeDtypeStruct((sites, reals), jnp.float32),
+            jax.ShapeDtypeStruct((sites, min(sites, 128)), jnp.float32),
+            jax.ShapeDtypeStruct((sites, min(sites, 128)), jnp.float32),
         ],
-        in_specs=[SMEM] + [VMEM] * (1 + len(pieces) + len(coefs)),
-        out_specs=[VMEM] * 2,
+        in_specs=[SMEM] + [VMEM] * (3 + len(pieces) + len(coefs)),
+        out_specs=[VMEM] * 4,
         scratch_shapes=[pltpu.VMEM((sites, columns), jnp.bfloat16)],
         compiler_params=vmem((sites, 3 * reals), (sites, 2 * columns)),
         cost_estimate=cost(6 * sites * per_source * reals, noise, *pieces, *coefs),
         name="accumulate",
-    )(ranks, noise, *pieces, *coefs)
-
-
-def as_rows(ref, rows):
-    values = ref[:, rows]
-    return jnp.transpose(jnp.broadcast_to(values, (values.shape[1], values.shape[1])))
+    )(ranks, noise, skew, tail, *pieces, *coefs)
 
 
 def finish_kernel(shifts, ranks_ref, u_ref, sum_ref, skew_ref, tail_ref, *refs):
@@ -162,7 +198,7 @@
             gaussian += jnp.dot(
                 u_ref[rows, pl.ds(start, columns)], coef, preferred_element_type=jnp.float32
             )
-        skew, tail = as_rows(skew_ref, rows), as_rows(tail_ref, rows)
+        skew, tail = skew_ref[rows, :], tail_ref[rows, :]
         growth, turn, scale = LOG2E * skew, 0.5 * skew, 1.0 / skew
         spread = (0.5 * LOG2E) * tail
         lanes = skew.shape[1]
@@ -224,7 +260,7 @@
     return {place: array for place, array in with_other_core(pieces).items() if place not in pieces}
 
 
-def at_once(present, gather, pieces):
+def at_once(gather, pieces):
     places, arrays, new = list(pieces), list(pieces.values()), []
 
     def added(*arrays):
@@ -233,7 +269,7 @@
         return [more[place] for place in new]
 
     count = len(jax.eval_shape(added, *arrays))
-    results = lax.cond(present, added, lambda *same: [same[0]] * count, *arrays)
+    results = lax.cond(lax.axis_index("real") >= 0, added, lambda *same: [same[0]] * count, *arrays)
     return dict(zip(new, results))
 
 
@@ -263,23 +299,21 @@
     last = max(v_first)
     waiting = (v_first[last], stage(noise), v_rest, own_and_u)
     v_first[last], noise_here, v_rest, own_and_u = lax.optimization_barrier(waiting)
-    present = ranks[0, 0] > 0
-    noise_here, present = lax.optimization_barrier((noise_here, present))
     [far] = project(1, noise_here, with_other_core(v_first).items())
 
     u_swapped = swap(after(own_and_u, far), 1)
-    v_rest = after(v_rest, far, u_swapped)
-    v_pieces = {(0, 0): v_rest}
-    v_pieces.update(at_once(present, lambda own: with_other_core(from_chips(own[0, 0])), v_pieces))
-    u_pieces = from_chips(after(own_and_u, v_pieces))
+    v_pieces = {(0, 0): after(v_rest, far, u_swapped)}
+    v_pieces.update(at_once(lambda own: with_other_core(from_chips(own[0, 0])), v_pieces))
+    u_pieces = {**from_chips(after(own_and_u, v_pieces)), (1, 0): u_swapped}
     others = project(len(rest), noise_here, v_pieces.items())
     far = along_site(far, first)
     others = [others[0], *after(others[1:], far)]
-    u_pieces = {**u_pieces, (1, 0): u_swapped}
-    u_pieces.update(at_once(present, from_other_core, u_pieces))
+    u_pieces.update(at_once(from_other_core, u_pieces))
     others = [along_site(coef, shift) for coef, shift in zip(others, rest)]
-    u_whole, total = accumulate((first,), ranks, noise, u_pieces.items(), [far])
-    return finish(rest, ranks, u_whole, total, skew_g[None], tail_h[None], others)
+    u_whole, total, skew, tail = accumulate(
+        (first,), ranks, noise, skew_g[None], tail_h[None], u_pieces.items(), [far]
+    )
+    return finish(rest, ranks, u_whole, total, skew, tail, others)
 
 
 def solution(mesh):

time: 59 us -> 59.6 us (1.010)
  waiting for transfers between devices: 21.8 us -> 23.3 us
  between operations: 0.78 us -> 0.14 us
    ppermute x21, waiting for transfers between devices: 19.1 us -> 20.5 us  [swap(): lax.ppermute(array, 'real', [(k, k ^ distance) for k in range(count)])]
    pallas_call x2, Pallas kernels: 4.57 us -> 5.17 us  [project(): pl.pallas_call(functools.partial(project_kernel, places, rows), out_shape...]
  transfers between devices with their start and end apart: 24 -> 24, of which waited for: 11 -> 14; matrix products, arithmetic and copies ran while one was open for 2% -> 1% of each run, Pallas kernels for 12% -> 12%
where the time goes in v13:
time: 59.6 us; the launch traced here: 59.4 us
  waiting for transfers between devices  23.3 us (39%)
  starting transfers between devices  20.2 us (34%)
  Pallas kernels  12.6 us (21%)
  local copies, waits for them, and re-layouts  2.45 us (4%)
  other arithmetic  0.74 us (1%)
    ppermute x21, waiting for transfers between devices, swap(): lax.ppermute(array, 'real', [(k, k ^ distance) for k in range(count)])  20.5 us
    ppermute x21, starting transfers between devices, swap(): lax.ppermute(array, 'real', [(k, k ^ distance) for k in range(count)])  13.7 us
    ppermute x3, starting transfers between devices, along_site(): lax.ppermute(coef, 'site', [(k, (k + shift) % count) for k in range(count)])  6.47 us
    pallas_call x2, Pallas kernels, project(): pl.pallas_call(functools.partial(project_kernel, places, rows), out_shape...  5.17 us
    pallas_call x1, Pallas kernels, finish(): pl.pallas_call(functools.partial(finish_kernel, shifts), out_shape=jax.Sh...  3.33 us
    pallas_call x1, Pallas kernels, accumulate(): pl.pallas_call(functools.partial(accumulate_kernel, shifts, places, rows)...  3.29 us
    ppermute x3, waiting for transfers between devices, along_site(): lax.ppermute(coef, 'site', [(k, (k + shift) % count) for k in range(count)])  2.85 us
    unnamed x22, local copies, waits for them, and re-layouts  1.45 us
  transfers between devices with their start and end apart: 24, of which 14 were waited for; matrix products, arithmetic and copies ran while one was open for 1% of the time, Pallas kernels for 12%

profile of v13, /device:TPU:0, one launch (start us, length us, event | category | flops | bytes accessed | tf_op | source)
XLA Modules:
  0.0 59.4 jit_solution(4669748964868162764)
XLA Ops:
  0.0 1.0 %dynamic-slice_bitcast_fusion = (bf16[128,256]{1,0:T(8,128)(2,1)S(1)}, bf16[128,256]{1,0:T(8,128)(2,1)S(1)}, bf16[128,256]{1,0:T(8,128)(2,1)S(1)}, bf16[128,256]{1,0:T(8,128)(2,1)S(1)}) fusion(bf16[1,128,1024]{2,1,0:T(8,128)(2,1)} %param.11, s32[]{:T(128)S(6)} %select_n.15, s32[]{:T(128)S(6)} %select_n.13, s32[]{:T(128)S(6)} %select_n.12, s32[]{:T(128)S(6)} %select_n.14), kind=kLoop, calls=%fused_computation.2 | loop fusion | bytes 524304 | tf_op jit(solution)/shard_map/dynamic_slice | solution.py:293
  1.0 0.5 collective-permute-start.13
  1.5 2.6 %collective-permute-start.12 = (bf16[128,256]{1,0:T(8,128)(2,1)S(1)}, bf16[128,256]{1,0:T(8,128)(2,1)S(1)}, u32[]{:S(2)}, u32[]{:S(2)}) collective-permute-start(bf16[128,256]{1,0:T(8,128)(2,1)S(1)} %get-tuple-element.67.refs_0_), channel_id=1, source_target_pairs={{0,16},{4,20},{8,24},{12,28},{16,0},{20,4},{24,8},{28,12},{1,17},{... | collective-permute-start | bytes 196616 | tf_op jit(solution)/shard_map/ppermute | solution.py:241
  4.1 1.5 %collective-permute-start.11 = (bf16[128,256]{1,0:T(8,128)(2,1)S(1)}, bf16[128,256]{1,0:T(8,128)(2,1)S(1)}, u32[]{:S(2)}, u32[]{:S(2)}) collective-permute-start(bf16[128,256]{1,0:T(8,128)(2,1)S(1)} %get-tuple-element.67.refs_0_), channel_id=1, source_target_pairs={{0,8},{4,12},{8,0},{12,4},{16,24},{20,28},{24,16},{28,20},{1,9},{5... | collective-permute-start | bytes 196616 | tf_op jit(solution)/shard_map/ppermute | solution.py:241
  5.7 1.4 %copy-done = bf16[1024,768]{1,0:T(8,128)(2,1)S(1)} copy-done((bf16[1024,768]{1,0:T(8,128)(2,1)S(1)}, bf16[1024,768]{1,0:T(8,128)(2,1)}, u32[]{:S(2)}) %copy-start) | copy-done | bytes 1572888
  7.1 0.8 %stage.1.noise_ref = bf16[1024,768]{1,0:T(8,128)(2,1)S(1)} custom-call(bf16[1024,768]{1,0:T(8,128)(2,1)S(1)} %copy-done), custom_call_target="tpu_custom_call" | custom-call | bytes 3145728 | tf_op jit(solution)/shard_map/stage/pallas_call | solution.py:113
  7.9 0.7 %pad_maximum_fusion.1.refs_0_ = bf16[128,512]{1,0:T(8,128)(2,1)} fusion(bf16[128,256]{1,0:T(8,128)(2,1)S(1)} %get-tuple-element.68, bf16[128,256]{1,0:T(8,128)(2,1)S(1)} %get-tuple-element.66), kind=kLoop, calls=%fused_computation.1 | loop fusion | flops 262144 | bytes 262144 | tf_op jit(solution)/shard_map/concatenate | solution.py:296
  8.6 2.2 %collective-permute-done.10.refs_3_ = bf16[128,256]{1,0:T(8,128)(2,1)S(1)} collective-permute-done((bf16[128,256]{1,0:T(8,128)(2,1)S(1)}, bf16[128,256]{1,0:T(8,128)(2,1)S(1)}, u32[]{:S(2)}, u32[]{:S(2)}) %collective-permute-start.10) | collective-permute-done | bytes 65568 | tf_op jit(solution)/shard_map/ppermute | solution.py:241
  10.8 0.5 collective-permute-start.14
  11.4 0.7 %collective-permute-done.15.refs_6_ = bf16[128,256]{1,0:T(8,128)(2,1)S(1)} collective-permute-done((bf16[128,256]{1,0:T(8,128)(2,1)S(1)}, bf16[128,256]{1,0:T(8,128)(2,1)S(1)}, u32[]{:S(2)}, u32[]{:S(2)}) %collective-permute-start.15) | collective-permute-done | bytes 65568 | tf_op jit(solution)/shard_map/ppermute | solution.py:241
  12.5 2.0 %project_1.1 = bf16[256,768]{1,0:T(8,128)(2,1)} custom-call(bf16[1024,768]{1,0:T(8,128)(2,1)S(1)} %stage.1.noise_ref, bf16[128,256]{1,0:T(8,128)(2,1)S(1)} %get-tuple-element.67.refs_0_, bf16[128,256]{1,0:T(8,128)(2,1)S(1)} %collective-permute-done.11.refs_1_, bf16[128,256]{1,0:T(8,128)(2,1)S(1)} %collective-permute-done.12.refs_2_, ...), custom_call_target="tpu_custom_call" | custom-call | flops 402653184 | bytes 4194304 | tf_op jit(solution)/shard_map/project_1/pallas_call | solution.py:81
  14.8 2.6 %collective-permute-start.21 = (bf16[256,768]{1,0:T(8,128)(2,1)}, bf16[256,768]{1,0:T(8,128)(2,1)S(1)}, u32[]{:S(2)}, u32[]{:S(2)}) collective-permute-start(bf16[256,768]{1,0:T(8,128)(2,1)} %project_1.1), channel_id=1, source_target_pairs={{0,2},{1,3},{2,0},{3,1},{4,6},{5,7},{6,4},{7,5},{8,10},{9,11},{10,... | collective-permute-start | bytes 1179656 | tf_op jit(solution)/shard_map/ppermute | solution.py:278
  17.4 11.4 %conditional.2 = (bf16[128,512]{1,0:T(8,128)(2,1)}, bf16[128,512]{1,0:T(8,128)(2,1)}, bf16[128,512]{1,0:T(8,128)(2,1)}, bf16[128,512]{1,0:T(8,128)(2,1)}, bf16[1...) conditional(s32[]{:T(128)} %convert_element_type.4, ...), branch_computations={%region_0.0_spmd, %region_1.0_spmd} | conditional | bytes 3670352 | solution.py:272
  17.4 1.4 %collective-permute-start.2 = (bf16[128,512]{1,0:T(8,128)(2,1)}, bf16[128,512]{1,0:T(8,128)(2,1)}, u32[]{:S(2)}, u32[]{:S(2)}) collective-permute-start(bf16[128,512]{1,0:T(8,128)(2,1)} %param.1), channel_id=1, source_target_pairs={{0,24},{4,28},{8,16},{12,20},{16,8},{20,12},{24,0},{28,4},{1,25},{... | collective-permute-start | bytes 393224 | tf_op jit(solution)/shard_map/cond/branch_1_fun/ppermute | solution.py:241
  18.8 0.7 %collective-permute-start.1 = (bf16[128,512]{1,0:T(8,128)(2,1)}, bf16[128,512]{1,0:T(8,128)(2,1)}, u32[]{:S(2)}, u32[]{:S(2)}) collective-permute-start(bf16[128,512]{1,0:T(8,128)(2,1)} %param.1), channel_id=1, source_target_pairs={{0,16},{4,20},{8,24},{12,28},{16,0},{20,4},{24,8},{28,12},{1,17},{... | collective-permute-start | bytes 393224 | tf_op jit(solution)/shard_map/cond/branch_1_fun/ppermute | solution.py:241
  19.5 1.5 %collective-permute-start = (bf16[128,512]{1,0:T(8,128)(2,1)}, bf16[128,512]{1,0:T(8,128)(2,1)}, u32[]{:S(2)}, u32[]{:S(2)}) collective-permute-start(bf16[128,512]{1,0:T(8,128)(2,1)} %param.1), channel_id=1, source_target_pairs={{0,8},{4,12},{8,0},{12,4},{16,24},{20,28},{24,16},{28,20},{1,9},{5... | collective-permute-start | bytes 393224 | tf_op jit(solution)/shard_map/cond/branch_1_fun/ppermute | solution.py:241
  21.0 4.1 %collective-permute-done.2 = bf16[128,512]{1,0:T(8,128)(2,1)} collective-permute-done((bf16[128,512]{1,0:T(8,128)(2,1)}, bf16[128,512]{1,0:T(8,128)(2,1)}, u32[]{:S(2)}, u32[]{:S(2)}) %collective-permute-start.2) | collective-permute-done | bytes 131104 | tf_op jit(solution)/shard_map/cond/branch_1_fun/ppermute | solution.py:241
  25.1 1.9 %collective-permute-done.1 = bf16[128,512]{1,0:T(8,128)(2,1)} collective-permute-done((bf16[128,512]{1,0:T(8,128)(2,1)}, bf16[128,512]{1,0:T(8,128)(2,1)}, u32[]{:S(2)}, u32[]{:S(2)}) %collective-permute-start.1) | collective-permute-done | bytes 131104 | tf_op jit(solution)/shard_map/cond/branch_1_fun/ppermute | solution.py:241
  27.5 1.2 %collective-permute-done.5 = bf16[128,512]{1,0:T(8,128)(2,1)} collective-permute-done((bf16[128,512]{1,0:T(8,128)(2,1)}, bf16[128,512]{1,0:T(8,128)(2,1)}, u32[]{:S(2)}, u32[]{:S(2)}) %collective-permute-start.5) | collective-permute-done | bytes 131104 | tf_op jit(solution)/shard_map/cond/branch_1_fun/ppermute | solution.py:241
  28.9 1.4 %collective-permute-start.20 = (bf16[128,1280]{1,0:T(8,128)(2,1)}, bf16[128,1280]{1,0:T(8,128)(2,1)S(1)}, u32[]{:S(2)}, u32[]{:S(2)}) collective-permute-start(bf16[128,1280]{1,0:T(8,128)(2,1)} %copy-done.7), channel_id=1, source_target_pairs={{0,24},{4,28},{8,16},{12,20},{16,8},{20,12},{24,0},{28,4},{1,25},{... | collective-permute-start | bytes 983048 | tf_op jit(solution)/shard_map/ppermute | solution.py:241
  30.3 0.7 %collective-permute-start.19 = (bf16[128,1280]{1,0:T(8,128)(2,1)}, bf16[128,1280]{1,0:T(8,128)(2,1)}, u32[]{:S(2)}, u32[]{:S(2)}) collective-permute-start(bf16[128,1280]{1,0:T(8,128)(2,1)} %copy-done.7), channel_id=1, source_target_pairs={{0,16},{4,20},{8,24},{12,28},{16,0},{20,4},{24,8},{28,12},{1,17},{... | collective-permute-start | bytes 983048 | tf_op jit(solution)/shard_map/ppermute | solution.py:241
  31.0 1.5 %collective-permute-start.18 = (bf16[128,1280]{1,0:T(8,128)(2,1)}, bf16[128,1280]{1,0:T(8,128)(2,1)}, u32[]{:S(2)}, u32[]{:S(2)}) collective-permute-start(bf16[128,1280]{1,0:T(8,128)(2,1)} %copy-done.7), channel_id=1, source_target_pairs={{0,8},{4,12},{8,0},{12,4},{16,24},{20,28},{24,16},{28,20},{1,9},{5... | collective-permute-start | bytes 983048 | tf_op jit(solution)/shard_map/ppermute | solution.py:241
  32.4 3.1 %project_2.1 = (bf16[256,768]{1,0:T(8,128)(2,1)}, bf16[256,768]{1,0:T(8,128)(2,1)}) custom-call(bf16[1024,768]{1,0:T(8,128)(2,1)S(1)} %stage.1.noise_ref, bf16[128,512]{1,0:T(8,128)(2,1)} %pad_maximum_fusion.1.refs_0_, bf16[128,512]{1,0:T(8,128)(2,1)} %get-tuple-element.48.refs_1_, bf16[128,512]{1,0:T(8,128)(2,1)} %get-tuple-element.50.refs_2_, ...), custom_call_target="tpu_custom_call" | custom-call | flops 805306368 | bytes 5242880 | tf_op jit(solution)/shard_map/project_2/pallas_call | solution.py:81
  35.6 1.6 %collective-permute-start.22 = (bf16[256,768]{1,0:T(8,128)(2,1)}, bf16[256,768]{1,0:T(8,128)(2,1)S(1)}, u32[]{:S(2)}, u32[]{:S(2)}) collective-permute-start(bf16[256,768]{1,0:T(8,128)(2,1)} %get-tuple-element.62), channel_id=1, source_target_pairs={{0,1},{1,2},{2,3},{3,0},{4,5},{5,6},{6,7},{7,4},{8,9},{9,10},{10,1... | collective-permute-start | bytes 1179656 | tf_op jit(solution)/shard_map/ppermute | solution.py:278
  37.2 2.2 %collective-permute-start.23 = (bf16[256,768]{1,0:T(8,128)(2,1)}, bf16[256,768]{1,0:T(8,128)(2,1)S(1)}, u32[]{:S(2)}, u32[]{:S(2)}) collective-permute-start(bf16[256,768]{1,0:T(8,128)(2,1)} %get-tuple-element.64), channel_id=1, source_target_pairs={{0,3},{1,0},{2,1},{3,2},{4,7},{5,4},{6,5},{7,6},{8,11},{9,8},{10,9... | collective-permute-start | bytes 1179656 | tf_op jit(solution)/shard_map/ppermute | solution.py:278
  39.5 1.2 %collective-permute-done.20.refs_3_ = bf16[128,1280]{1,0:T(8,128)(2,1)S(1)} collective-permute-done((bf16[128,1280]{1,0:T(8,128)(2,1)}, bf16[128,1280]{1,0:T(8,128)(2,1)S(1)}, u32[]{:S(2)}, u32[]{:S(2)}) %collective-permute-start.20) | collective-permute-done | bytes 327712 | tf_op jit(solution)/shard_map/ppermute | solution.py:241
  40.6 6.5 %collective-permute-done.19.refs_2_ = bf16[128,1280]{1,0:T(8,128)(2,1)} collective-permute-done((bf16[128,1280]{1,0:T(8,128)(2,1)}, bf16[128,1280]{1,0:T(8,128)(2,1)}, u32[]{:S(2)}, u32[]{:S(2)}) %collective-permute-start.19) | collective-permute-done | bytes 327712 | tf_op jit(solution)/shard_map/ppermute | solution.py:241
  47.1 2.8 %conditional.3 = (bf16[128,1280]{1,0:T(8,128)(2,1)}, bf16[128,1280]{1,0:T(8,128)(2,1)}, bf16[128,1280]{1,0:T(8,128)(2,1)}) conditional(s32[]{:T(128)} %convert_element_type.4, bf16[128,1280]{1,0:T(8,128)(2,1)S(1)} %copy-done.8, (bf16[128,1280]{1,0:T(8,128)(2,1)}, bf16[128,1280]{1,0:T(8,128)(2,1)}, bf16[128,1280]{1,0:T(8,128)(2,1)S(1)}) %tuple.30), branch_computations={%region_2.0_spmd, %region_3.0_spmd} | conditional | bytes 3932304 | solution.py:272
  47.8 1.4 %collective-permute-done.7 = bf16[128,1280]{1,0:T(8,128)(2,1)} collective-permute-done((bf16[128,1280]{1,0:T(8,128)(2,1)}, bf16[128,1280]{1,0:T(8,128)(2,1)}, u32[]{:S(2)}, u32[]{:S(2)}) %collective-permute-start.7) | collective-permute-done | bytes 327712 | tf_op jit(solution)/shard_map/cond/branch_1_fun/ppermute | solution.py:241
  50.0 3.3 %accumulate.1 = (bf16[1024,1024]{1,0:T(8,128)(2,1)S(1)}, f32[1024,768]{1,0:T(8,128)S(1)}, f32[1024,128]{1,0:T(8,128)S(1)}, f32[1024,128]{1,0:T(8,128)S(1)}) custom-call(s32[4,4]{1,0:T(4,128)S(1)} %copy-done.4, bf16[1024,768]{1,0:T(8,128)(2,1)S(1)} %copy-done.1, f32[1,1024]{1,0:T(1,128)S(1)} %bitcast.11, f32[1,1024]{1,0:T(1,128)S(1)} %bitcast.12, ...), custom_call_target="tpu_custom_call" | custom-call | flops 1207959552 | bytes 9175040 | tf_op jit(solution)/shard_map/accumulate/pallas_call | solution.py:169
  53.3 2.8 %collective-permute-done.23.refs_1_ = bf16[256,768]{1,0:T(8,128)(2,1)S(1)} collective-permute-done((bf16[256,768]{1,0:T(8,128)(2,1)}, bf16[256,768]{1,0:T(8,128)(2,1)S(1)}, u32[]{:S(2)}, u32[]{:S(2)}) %collective-permute-start.23) | collective-permute-done | bytes 393248 | tf_op jit(solution)/shard_map/ppermute | solution.py:278
  56.1 3.3 %finish.1 = f32[1024,768]{1,0:T(8,128)} custom-call(s32[4,4]{1,0:T(4,128)S(1)} %copy-done.4, bf16[1024,1024]{1,0:T(8,128)(2,1)S(1)} %get-tuple-element.58.u_ref, f32[1024,768]{1,0:T(8,128)S(1)} %get-tuple-element.59.sum_ref, f32[1024,128]{1,0:T(8,128)S(1)} %get-tuple-element.60.skew_ref, f32[1024,128]{1,0:T(8,128)S(1)} %get-tuple-element.61.tail_ref, ...), custom_call_target="tpu_custom_call" | custom-call | flops 805306368 | bytes 12058624 | tf_op jit(solution)/shard_map/finish/pallas_call | solution.py:220
  (48 shorter events, 3.0 us)
Async XLA Ops:
  1.0 10.4 %collective-permute-start.13 = (bf16[128,256]{1,0:T(8,128)(2,1)S(1)}, bf16[128,256]{1,0:T(8,128)(2,1)S(1)}, u32[]{:S(2)}, u32[]{:S(2)}) collective-permute-start(bf16[128,256]{1,0:T(8,128)(2,1)S(1)} %get-tuple-element.67.refs_0_), channel_id=1, source_target_pairs={{0,4},{4,0},{8,12},{12,8},{16,20},{20,16},{24,28},{28,24},{1,5},{5... | collective-permute-start | bytes 196616 | tf_op jit(solution)/shard_map/ppermute | solution.py:241
  1.5 9.3 %collective-permute-start.12 = (bf16[128,256]{1,0:T(8,128)(2,1)S(1)}, bf16[128,256]{1,0:T(8,128)(2,1)S(1)}, u32[]{:S(2)}, u32[]{:S(2)}) collective-permute-start(bf16[128,256]{1,0:T(8,128)(2,1)S(1)} %get-tuple-element.67.refs_0_), channel_id=1, source_target_pairs={{0,16},{4,20},{8,24},{12,28},{16,0},{20,4},{24,8},{28,12},{1,17},{... | collective-permute-start | bytes 196616 | tf_op jit(solution)/shard_map/ppermute | solution.py:241
  4.1 6.7 %collective-permute-start.11 = (bf16[128,256]{1,0:T(8,128)(2,1)S(1)}, bf16[128,256]{1,0:T(8,128)(2,1)S(1)}, u32[]{:S(2)}, u32[]{:S(2)}) collective-permute-start(bf16[128,256]{1,0:T(8,128)(2,1)S(1)} %get-tuple-element.67.refs_0_), channel_id=1, source_target_pairs={{0,8},{4,12},{8,0},{12,4},{16,24},{20,28},{24,16},{28,20},{1,9},{5... | collective-permute-start | bytes 196616 | tf_op jit(solution)/shard_map/ppermute | solution.py:241
  5.6 5.2 %collective-permute-start.10 = (bf16[128,256]{1,0:T(8,128)(2,1)S(1)}, bf16[128,256]{1,0:T(8,128)(2,1)S(1)}, u32[]{:S(2)}, u32[]{:S(2)}) collective-permute-start(bf16[128,256]{1,0:T(8,128)(2,1)S(1)} %get-tuple-element.67.refs_0_), channel_id=1, source_target_pairs={{0,24},{4,28},{8,16},{12,20},{16,8},{20,12},{24,0},{28,4},{1,25},{... | collective-permute-start | bytes 196616 | tf_op jit(solution)/shard_map/ppermute | solution.py:241
  7.9 9.5 %copy-start.7 = (bf16[128,1280]{1,0:T(8,128)(2,1)}, bf16[128,1280]{1,0:T(8,128)(2,1)S(1)}, u32[]{:S(2)}) copy-start(bf16[128,1280]{1,0:T(8,128)(2,1)S(1)} %pad_maximum_fusion.refs_0_) | copy-start | bytes 983044
  10.8 1.3 %collective-permute-start.15 = (bf16[128,256]{1,0:T(8,128)(2,1)S(1)}, bf16[128,256]{1,0:T(8,128)(2,1)S(1)}, u32[]{:S(2)}, u32[]{:S(2)}) collective-permute-start(bf16[128,256]{1,0:T(8,128)(2,1)S(1)} %collective-permute-done.12.refs_2_), channel_id=1, source_target_pairs={{0,4},{4,0},{8,12},{12,8},{16,20},{20,16},{24,28},{28,24},{1,5},{5... | collective-permute-start | bytes 196616 | tf_op jit(solution)/shard_map/ppermute | solution.py:241
  10.8 1.4 %collective-permute-start.14 = (bf16[128,256]{1,0:T(8,128)(2,1)S(1)}, bf16[128,256]{1,0:T(8,128)(2,1)S(1)}, u32[]{:S(2)}, u32[]{:S(2)}) collective-permute-start(bf16[128,256]{1,0:T(8,128)(2,1)S(1)} %collective-permute-done.11.refs_1_), channel_id=1, source_target_pairs={{0,4},{4,0},{8,12},{12,8},{16,20},{20,16},{24,28},{28,24},{1,5},{5... | collective-permute-start | bytes 196616 | tf_op jit(solution)/shard_map/ppermute | solution.py:241
  11.3 1.3 %collective-permute-start.16 = (bf16[128,256]{1,0:T(8,128)(2,1)S(1)}, bf16[128,256]{1,0:T(8,128)(2,1)S(1)}, u32[]{:S(2)}, u32[]{:S(2)}) collective-permute-start(bf16[128,256]{1,0:T(8,128)(2,1)S(1)} %collective-permute-done.10.refs_3_), channel_id=1, source_target_pairs={{0,4},{4,0},{8,12},{12,8},{16,20},{20,16},{24,28},{28,24},{1,5},{5... | collective-permute-start | bytes 196616 | tf_op jit(solution)/shard_map/ppermute | solution.py:241
  14.6 2.8 %collective-permute-start.17 = (bf16[128,1280]{1,0:T(8,128)(2,1)S(1)}, bf16[128,1280]{1,0:T(8,128)(2,1)S(1)}, u32[]{:S(2)}, u32[]{:S(2)}) collective-permute-start(bf16[128,1280]{1,0:T(8,128)(2,1)S(1)} %pad_maximum_fusion.refs_0_), channel_id=1, source_target_pairs={{0,4},{4,0},{8,12},{12,8},{16,20},{20,16},{24,28},{28,24},{1,5},{5... | collective-permute-start | bytes 983048 | tf_op jit(solution)/shard_map/ppermute | solution.py:241
  14.8 22.4 %collective-permute-start.21 = (bf16[256,768]{1,0:T(8,128)(2,1)}, bf16[256,768]{1,0:T(8,128)(2,1)S(1)}, u32[]{:S(2)}, u32[]{:S(2)}) collective-permute-start(bf16[256,768]{1,0:T(8,128)(2,1)} %project_1.1), channel_id=1, source_target_pairs={{0,2},{1,3},{2,0},{3,1},{4,6},{5,7},{6,4},{7,5},{8,10},{9,11},{10,... | collective-permute-start | bytes 1179656 | tf_op jit(solution)/shard_map/ppermute | solution.py:278
  17.4 11.5 %copy-start.2 = (bf16[128,1280]{1,0:T(8,128)(2,1)}, bf16[128,1280]{1,0:T(8,128)(2,1)S(1)}, u32[]{:S(2)}) copy-start(bf16[128,1280]{1,0:T(8,128)(2,1)S(1)} %collective-permute-done.17.refs_4_) | copy-start | bytes 983044
  17.4 7.7 %collective-permute-start.2 = (bf16[128,512]{1,0:T(8,128)(2,1)}, bf16[128,512]{1,0:T(8,128)(2,1)}, u32[]{:S(2)}, u32[]{:S(2)}) collective-permute-start(bf16[128,512]{1,0:T(8,128)(2,1)} %param.1), channel_id=1, source_target_pairs={{0,24},{4,28},{8,16},{12,20},{16,8},{20,12},{24,0},{28,4},{1,25},{... | collective-permute-start | bytes 393224 | tf_op jit(solution)/shard_map/cond/branch_1_fun/ppermute | solution.py:241
  18.8 8.2 %collective-permute-start.1 = (bf16[128,512]{1,0:T(8,128)(2,1)}, bf16[128,512]{1,0:T(8,128)(2,1)}, u32[]{:S(2)}, u32[]{:S(2)}) collective-permute-start(bf16[128,512]{1,0:T(8,128)(2,1)} %param.1), channel_id=1, source_target_pairs={{0,16},{4,20},{8,24},{12,28},{16,0},{20,4},{24,8},{28,12},{1,17},{... | collective-permute-start | bytes 393224 | tf_op jit(solution)/shard_map/cond/branch_1_fun/ppermute | solution.py:241
  19.5 7.5 %collective-permute-start = (bf16[128,512]{1,0:T(8,128)(2,1)}, bf16[128,512]{1,0:T(8,128)(2,1)}, u32[]{:S(2)}, u32[]{:S(2)}) collective-permute-start(bf16[128,512]{1,0:T(8,128)(2,1)} %param.1), channel_id=1, source_target_pairs={{0,8},{4,12},{8,0},{12,4},{16,24},{20,28},{24,16},{28,20},{1,9},{5... | collective-permute-start | bytes 393224 | tf_op jit(solution)/shard_map/cond/branch_1_fun/ppermute | solution.py:241
  21.0 6.5 %collective-permute-start.3 = (bf16[128,512]{1,0:T(8,128)(2,1)}, bf16[128,512]{1,0:T(8,128)(2,1)}, u32[]{:S(2)}, u32[]{:S(2)}) collective-permute-start(bf16[128,512]{1,0:T(8,128)(2,1)} %param.1), channel_id=1, source_target_pairs={{0,4},{4,0},{8,12},{12,8},{16,20},{20,16},{24,28},{28,24},{1,5},{5... | collective-permute-start | bytes 393224 | tf_op jit(solution)/shard_map/cond/branch_1_fun/ppermute | solution.py:241
  25.1 2.4 %collective-permute-start.6 = (bf16[128,512]{1,0:T(8,128)(2,1)}, bf16[128,512]{1,0:T(8,128)(2,1)}, u32[]{:S(2)}, u32[]{:S(2)}) collective-permute-start(bf16[128,512]{1,0:T(8,128)(2,1)} %collective-permute-done.2), channel_id=1, source_target_pairs={{0,4},{4,0},{8,12},{12,8},{16,20},{20,16},{24,28},{28,24},{1,5},{5... | collective-permute-start | bytes 393224 | tf_op jit(solution)/shard_map/cond/branch_1_fun/ppermute | solution.py:241
  27.0 1.7 %collective-permute-start.5 = (bf16[128,512]{1,0:T(8,128)(2,1)}, bf16[128,512]{1,0:T(8,128)(2,1)}, u32[]{:S(2)}, u32[]{:S(2)}) collective-permute-start(bf16[128,512]{1,0:T(8,128)(2,1)} %collective-permute-done.1), channel_id=1, source_target_pairs={{0,4},{4,0},{8,12},{12,8},{16,20},{20,16},{24,28},{28,24},{1,5},{5... | collective-permute-start | bytes 393224 | tf_op jit(solution)/shard_map/cond/branch_1_fun/ppermute | solution.py:241
  27.0 1.9 %collective-permute-start.4 = (bf16[128,512]{1,0:T(8,128)(2,1)}, bf16[128,512]{1,0:T(8,128)(2,1)}, u32[]{:S(2)}, u32[]{:S(2)}) collective-permute-start(bf16[128,512]{1,0:T(8,128)(2,1)} %collective-permute-done), channel_id=1, source_target_pairs={{0,4},{4,0},{8,12},{12,8},{16,20},{20,16},{24,28},{28,24},{1,5},{5... | collective-permute-start | bytes 393224 | tf_op jit(solution)/shard_map/cond/branch_1_fun/ppermute | solution.py:241
  28.9 18.3 %copy-start.8 = (bf16[128,1280]{1,0:T(8,128)(2,1)S(1)}, bf16[128,1280]{1,0:T(8,128)(2,1)}, u32[]{:S(2)}) copy-start(bf16[128,1280]{1,0:T(8,128)(2,1)} %copy-done.7) | copy-start | bytes 983044
  28.9 21.1 %copy-start.1 = (bf16[1024,768]{1,0:T(8,128)(2,1)S(1)}, bf16[1024,768]{1,0:T(8,128)(2,1)}, u32[]{:S(2)}) copy-start(bf16[1024,768]{1,0:T(8,128)(2,1)} %noise_ref.1) | copy-start | bytes 4718596
  28.9 21.1 %copy-start.4 = (s32[4,4]{1,0:T(4,128)S(1)}, s32[4,4]{1,0:T(4,128)}, u32[]{:S(2)}) copy-start(s32[4,4]{1,0:T(4,128)} %ranks_ref.3) | copy-start | bytes 196
  28.9 21.1 %copy-start.5 = (f32[1024]{0:T(1024)S(1)}, f32[1024]{0:T(1024)}, u32[]{:S(2)}) copy-start(f32[1024]{0:T(1024)} %param.14) | copy-start | bytes 12292
  28.9 21.1 %copy-start.6 = (f32[1024]{0:T(1024)S(1)}, f32[1024]{0:T(1024)}, u32[]{:S(2)}) copy-start(f32[1024]{0:T(1024)} %param.15) | copy-start | bytes 12292
  28.9 11.7 %collective-permute-start.20 = (bf16[128,1280]{1,0:T(8,128)(2,1)}, bf16[128,1280]{1,0:T(8,128)(2,1)S(1)}, u32[]{:S(2)}, u32[]{:S(2)}) collective-permute-start(bf16[128,1280]{1,0:T(8,128)(2,1)} %copy-done.7), channel_id=1, source_target_pairs={{0,24},{4,28},{8,16},{12,20},{16,8},{20,12},{24,0},{28,4},{1,25},{... | collective-permute-start | bytes 983048 | tf_op jit(solution)/shard_map/ppermute | solution.py:241
  30.3 16.9 %collective-permute-start.19 = (bf16[128,1280]{1,0:T(8,128)(2,1)}, bf16[128,1280]{1,0:T(8,128)(2,1)}, u32[]{:S(2)}, u32[]{:S(2)}) collective-permute-start(bf16[128,1280]{1,0:T(8,128)(2,1)} %copy-done.7), channel_id=1, source_target_pairs={{0,16},{4,20},{8,24},{12,28},{16,0},{20,4},{24,8},{28,12},{1,17},{... | collective-permute-start | bytes 983048 | tf_op jit(solution)/shard_map/ppermute | solution.py:241
  31.0 16.2 %collective-permute-start.18 = (bf16[128,1280]{1,0:T(8,128)(2,1)}, bf16[128,1280]{1,0:T(8,128)(2,1)}, u32[]{:S(2)}, u32[]{:S(2)}) collective-permute-start(bf16[128,1280]{1,0:T(8,128)(2,1)} %copy-done.7), channel_id=1, source_target_pairs={{0,8},{4,12},{8,0},{12,4},{16,24},{20,28},{24,16},{28,20},{1,9},{5... | collective-permute-start | bytes 983048 | tf_op jit(solution)/shard_map/ppermute | solution.py:241
  35.6 14.4 %copy-start.3 = (bf16[128,1280]{1,0:T(8,128)(2,1)S(1)}, bf16[128,1280]{1,0:T(8,128)(2,1)}, u32[]{:S(2)}) copy-start(bf16[128,1280]{1,0:T(8,128)(2,1)} %copy-done.2) | copy-start | bytes 983044
  35.6 17.7 %collective-permute-start.22 = (bf16[256,768]{1,0:T(8,128)(2,1)}, bf16[256,768]{1,0:T(8,128)(2,1)S(1)}, u32[]{:S(2)}, u32[]{:S(2)}) collective-permute-start(bf16[256,768]{1,0:T(8,128)(2,1)} %get-tuple-element.62), channel_id=1, source_target_pairs={{0,1},{1,2},{2,3},{3,0},{4,5},{5,6},{6,7},{7,4},{8,9},{9,10},{10,1... | collective-permute-start | bytes 1179656 | tf_op jit(solution)/shard_map/ppermute | solution.py:278
  37.2 18.9 %collective-permute-start.23 = (bf16[256,768]{1,0:T(8,128)(2,1)}, bf16[256,768]{1,0:T(8,128)(2,1)S(1)}, u32[]{:S(2)}, u32[]{:S(2)}) collective-permute-start(bf16[256,768]{1,0:T(8,128)(2,1)} %get-tuple-element.64), channel_id=1, source_target_pairs={{0,3},{1,0},{2,1},{3,2},{4,7},{5,4},{6,5},{7,6},{8,11},{9,8},{10,9... | collective-permute-start | bytes 1179656 | tf_op jit(solution)/shard_map/ppermute | solution.py:278
  47.2 2.0 %collective-permute-start.7 = (bf16[128,1280]{1,0:T(8,128)(2,1)}, bf16[128,1280]{1,0:T(8,128)(2,1)}, u32[]{:S(2)}, u32[]{:S(2)}) collective-permute-start(bf16[128,1280]{1,0:T(8,128)(2,1)} %get-tuple-element.14), channel_id=1, source_target_pairs={{0,4},{4,0},{8,12},{12,8},{16,20},{20,16},{24,28},{28,24},{1,5},{5... | collective-permute-start | bytes 983048 | tf_op jit(solution)/shard_map/cond/branch_1_fun/ppermute | solution.py:241
  47.2 2.4 %collective-permute-start.8 = (bf16[128,1280]{1,0:T(8,128)(2,1)}, bf16[128,1280]{1,0:T(8,128)(2,1)}, u32[]{:S(2)}, u32[]{:S(2)}) collective-permute-start(bf16[128,1280]{1,0:T(8,128)(2,1)} %get-tuple-element.15), channel_id=1, source_target_pairs={{0,4},{4,0},{8,12},{12,8},{16,20},{20,16},{24,28},{28,24},{1,5},{5... | collective-permute-start | bytes 983048 | tf_op jit(solution)/shard_map/cond/branch_1_fun/ppermute | solution.py:241
  47.7 2.2 %collective-permute-start.9 = (bf16[128,1280]{1,0:T(8,128)(2,1)S(1)}, bf16[128,1280]{1,0:T(8,128)(2,1)}, u32[]{:S(2)}, u32[]{:S(2)}) collective-permute-start(bf16[128,1280]{1,0:T(8,128)(2,1)S(1)} %get-tuple-element.16), channel_id=1, source_target_pairs={{0,4},{4,0},{8,12},{12,8},{16,20},{20,16},{24,28},{28,24},{1,5},{5... | collective-permute-start | bytes 983048 | tf_op jit(solution)/shard_map/cond/branch_1_fun/ppermute | solution.py:241
  (3 other events, 15.8 us)

commit v14 on v11

--- a/solution.py
+++ b/solution.py
@@ -104,9 +104,14 @@
     return jnp.where(alive, coef.astype(jnp.float32), 0.0).astype(coef.dtype)
 
 
-def accumulate_kernel(shifts, places, rows, ranks_ref, noise_ref, *refs):
+def as_rows(ref, rows):
+    values = ref[:, rows]
+    return jnp.transpose(jnp.broadcast_to(values, (values.shape[1], values.shape[1])))
+
+
+def accumulate_kernel(shifts, places, rows, ranks_ref, noise_ref, skew_ref, tail_ref, *refs):
     pieces, coefs = refs[: len(places)], refs[len(places) : len(places) + len(shifts)]
-    u_ref, sum_ref, whole = refs[-3:]
+    u_ref, sum_ref, skew_rows, tail_rows, whole = refs[-5:]
     stack_pieces(places, rows, pieces, whole)
     per_source = whole.shape[1] - u_ref.shape[1]
     u_ref[...] = whole[:, per_source:]
@@ -120,9 +125,13 @@
             preferred_element_type=jnp.float32,
         )
     sum_ref[...] = total
-
-
-def accumulate(shifts, ranks, noise, gathered, coefs):
+    lanes = skew_rows.shape[1]
+    for start in range(0, skew_rows.shape[0], lanes):
+        part = slice(start, start + lanes)
+        skew_rows[part, :], tail_rows[part, :] = as_rows(skew_ref, part), as_rows(tail_ref, part)
+
+
+def accumulate(shifts, ranks, noise, skew, tail, gathered, coefs):
     places, pieces = zip(*gathered)
     sites, reals = noise.shape
     rows, columns = sites // lax.axis_size("real"), pieces[0].shape[1]
@@ -132,19 +141,16 @@
         out_shape=[
             jax.ShapeDtypeStruct((sites, columns - per_source), jnp.bfloat16),
             jax.ShapeDtypeStruct((sites, reals), jnp.float32),
+            jax.ShapeDtypeStruct((sites, min(sites, 128)), jnp.float32),
+            jax.ShapeDtypeStruct((sites, min(sites, 128)), jnp.float32),
         ],
-        in_specs=[SMEM] + [VMEM] * (1 + len(pieces) + len(coefs)),
-        out_specs=[VMEM] * 2,
+        in_specs=[SMEM] + [VMEM] * (3 + len(pieces) + len(coefs)),
+        out_specs=[VMEM] * 4,
         scratch_shapes=[pltpu.VMEM((sites, columns), jnp.bfloat16)],
         compiler_params=vmem((sites, 3 * reals), (sites, 2 * columns)),
         cost_estimate=cost(6 * sites * per_source * reals, noise, *pieces, *coefs),
         name="accumulate",
-    )(ranks, noise, *pieces, *coefs)
-
-
-def as_rows(ref, rows):
-    values = ref[:, rows]
-    return jnp.transpose(jnp.broadcast_to(values, (values.shape[1], values.shape[1])))
+    )(ranks, noise, skew, tail, *pieces, *coefs)
 
 
 def finish_kernel(shifts, ranks_ref, u_ref, sum_ref, skew_ref, tail_ref, *refs):
@@ -162,7 +168,7 @@
             gaussian += jnp.dot(
                 u_ref[rows, pl.ds(start, columns)], coef, preferred_element_type=jnp.float32
             )
-        skew, tail = as_rows(skew_ref, rows), as_rows(tail_ref, rows)
+        skew, tail = skew_ref[rows, :], tail_ref[rows, :]
         growth, turn, scale = LOG2E * skew, 0.5 * skew, 1.0 / skew
         spread = (0.5 * LOG2E) * tail
         lanes = skew.shape[1]
@@ -224,7 +230,7 @@
     return {place: array for place, array in with_other_core(pieces).items() if place not in pieces}
 
 
-def at_once(present, gather, pieces):
+def at_once(gather, pieces):
     places, arrays, new = list(pieces), list(pieces.values()), []
 
     def added(*arrays):
@@ -233,7 +239,7 @@
         return [more[place] for place in new]
 
     count = len(jax.eval_shape(added, *arrays))
-    results = lax.cond(present, added, lambda *same: [same[0]] * count, *arrays)
+    results = lax.cond(lax.axis_index("real") >= 0, added, lambda *same: [same[0]] * count, *arrays)
     return dict(zip(new, results))
 
 
@@ -260,26 +266,24 @@
     v_rest = jnp.concatenate([columns_for(shift) for shift in rest], axis=1)
     own_and_u = jnp.concatenate([columns_for(0), u_factors[0]], axis=1)
     v_first = from_chips(v_first)
-    last = max(v_first)
+    last = (2, 0)
     waiting = (v_first[last], stage(noise), v_rest, own_and_u)
     v_first[last], noise_here, v_rest, own_and_u = lax.optimization_barrier(waiting)
-    present = ranks[0, 0] > 0
-    noise_here, present = lax.optimization_barrier((noise_here, present))
     [far] = project(1, noise_here, with_other_core(v_first).items())
 
     u_swapped = swap(after(own_and_u, far), 1)
-    v_rest = after(v_rest, far, u_swapped)
-    v_pieces = {(0, 0): v_rest}
-    v_pieces.update(at_once(present, lambda own: with_other_core(from_chips(own[0, 0])), v_pieces))
-    u_pieces = from_chips(after(own_and_u, v_pieces))
+    v_pieces = {(0, 0): after(v_rest, far, u_swapped)}
+    v_pieces.update(at_once(lambda own: with_other_core(from_chips(own[0, 0])), v_pieces))
+    u_pieces = {**from_chips(after(own_and_u, v_pieces)), (1, 0): u_swapped}
     others = project(len(rest), noise_here, v_pieces.items())
     far = along_site(far, first)
     others = [others[0], *after(others[1:], far)]
-    u_pieces = {**u_pieces, (1, 0): u_swapped}
-    u_pieces.update(at_once(present, from_other_core, u_pieces))
+    u_pieces.update(at_once(from_other_core, u_pieces))
     others = [along_site(coef, shift) for coef, shift in zip(others, rest)]
-    u_whole, total = accumulate((first,), ranks, noise, u_pieces.items(), [far])
-    return finish(rest, ranks, u_whole, total, skew_g[None], tail_h[None], others)
+    u_whole, total, skew, tail = accumulate(
+        (first,), ranks, noise, skew_g[None], tail_h[None], u_pieces.items(), [far]
+    )
+    return finish(rest, ranks, u_whole, total, skew, tail, others)
 
 
 def solution(mesh):

time: 59 us -> 57.9 us (0.981)
  between operations: 0.78 us -> 0.12 us
  waiting for transfers between devices: 21.8 us -> 22.4 us
  transfers between devices with their start and end apart: 24 -> 24, of which waited for: 11 -> 15; matrix products, arithmetic and copies ran while one was open for 2% -> 1% of each run, Pallas kernels for 12% -> 12%
where the time goes in v14:
time: 57.9 us; the launch traced here: 57.7 us
  waiting for transfers between devices  22.4 us (39%)
  starting transfers between devices  20 us (35%)
  Pallas kernels  11.9 us (21%)
  local copies, waits for them, and re-layouts  2.45 us (4%)
  other arithmetic  0.74 us (1%)
    ppermute x21, waiting for transfers between devices, swap(): lax.ppermute(array, 'real', [(k, k ^ distance) for k in range(count)])  19.6 us
    ppermute x21, starting transfers between devices, swap(): lax.ppermute(array, 'real', [(k, k ^ distance) for k in range(count)])  13.6 us
    ppermute x3, starting transfers between devices, along_site(): lax.ppermute(coef, 'site', [(k, (k + shift) % count) for k in range(count)])  6.41 us
    pallas_call x2, Pallas kernels, project(): pl.pallas_call(functools.partial(project_kernel, places, rows), out_shape...  4.54 us
    pallas_call x1, Pallas kernels, finish(): pl.pallas_call(functools.partial(finish_kernel, shifts), out_shape=jax.Sh...  3.33 us
    pallas_call x1, Pallas kernels, accumulate(): pl.pallas_call(functools.partial(accumulate_kernel, shifts, places, rows)...  3.29 us
    ppermute x3, waiting for transfers between devices, along_site(): lax.ppermute(coef, 'site', [(k, (k + shift) % count) for k in range(count)])  2.78 us
    unnamed x22, local copies, waits for them, and re-layouts  1.45 us
  transfers between devices with their start and end apart: 24, of which 15 were waited for; matrix products, arithmetic and copies ran while one was open for 1% of the time, Pallas kernels for 12%

profile of v14, /device:TPU:0, one launch (start us, length us, event | category | flops | bytes accessed | tf_op | source)
XLA Modules:
  0.0 57.7 jit_solution(3318511050331226078)
XLA Ops:
  0.0 1.0 %dynamic-slice_bitcast_fusion = (bf16[128,256]{1,0:T(8,128)(2,1)S(1)}, bf16[128,256]{1,0:T(8,128)(2,1)S(1)}, bf16[128,256]{1,0:T(8,128)(2,1)S(1)}, bf16[128,256]{1,0:T(8,128)(2,1)S(1)}) fusion(bf16[1,128,1024]{2,1,0:T(8,128)(2,1)} %param.11, s32[]{:T(128)S(6)} %select_n.15, s32[]{:T(128)S(6)} %select_n.13, s32[]{:T(128)S(6)} %select_n.12, s32[]{:T(128)S(6)} %select_n.14), kind=kLoop, calls=%fused_computation.2 | loop fusion | bytes 524304 | tf_op jit(solution)/shard_map/dynamic_slice | solution.py:263
  1.0 0.5 collective-permute-start.13
  1.5 3.5 %collective-permute-start.12 = (bf16[128,256]{1,0:T(8,128)(2,1)S(1)}, bf16[128,256]{1,0:T(8,128)(2,1)S(1)}, u32[]{:S(2)}, u32[]{:S(2)}) collective-permute-start(bf16[128,256]{1,0:T(8,128)(2,1)S(1)} %get-tuple-element.67.refs_0_), channel_id=1, source_target_pairs={{0,24},{4,28},{8,16},{12,20},{16,8},{20,12},{24,0},{28,4},{1,25},{... | collective-permute-start | bytes 196616 | tf_op jit(solution)/shard_map/ppermute | solution.py:211
  5.0 0.5 collective-permute-start.11
  5.7 1.4 %copy-done = bf16[1024,768]{1,0:T(8,128)(2,1)S(1)} copy-done((bf16[1024,768]{1,0:T(8,128)(2,1)S(1)}, bf16[1024,768]{1,0:T(8,128)(2,1)}, u32[]{:S(2)}) %copy-start) | copy-done | bytes 1572888
  7.1 0.8 %stage.1.noise_ref = bf16[1024,768]{1,0:T(8,128)(2,1)S(1)} custom-call(bf16[1024,768]{1,0:T(8,128)(2,1)S(1)} %copy-done), custom_call_target="tpu_custom_call" | custom-call | bytes 3145728 | tf_op jit(solution)/shard_map/stage/pallas_call | solution.py:83
  7.9 0.7 %pad_maximum_fusion.1.refs_0_ = bf16[128,512]{1,0:T(8,128)(2,1)} fusion(bf16[128,256]{1,0:T(8,128)(2,1)S(1)} %get-tuple-element.68, bf16[128,256]{1,0:T(8,128)(2,1)S(1)} %get-tuple-element.66), kind=kLoop, calls=%fused_computation.1 | loop fusion | flops 262144 | bytes 262144 | tf_op jit(solution)/shard_map/concatenate | solution.py:266
  8.6 1.2 %collective-permute-done.10.refs_1_ = bf16[128,256]{1,0:T(8,128)(2,1)S(1)} collective-permute-done((bf16[128,256]{1,0:T(8,128)(2,1)S(1)}, bf16[128,256]{1,0:T(8,128)(2,1)S(1)}, u32[]{:S(2)}, u32[]{:S(2)}) %collective-permute-start.10) | collective-permute-done | bytes 65568 | tf_op jit(solution)/shard_map/ppermute | solution.py:211
  9.8 0.5 collective-permute-start.15
  10.4 0.7 %collective-permute-done.16.refs_7_ = bf16[128,256]{1,0:T(8,128)(2,1)S(1)} collective-permute-done((bf16[128,256]{1,0:T(8,128)(2,1)S(1)}, bf16[128,256]{1,0:T(8,128)(2,1)S(1)}, u32[]{:S(2)}, u32[]{:S(2)}) %collective-permute-start.16) | collective-permute-done | bytes 65568 | tf_op jit(solution)/shard_map/ppermute | solution.py:211
  11.6 1.4 %project_1.1 = bf16[256,768]{1,0:T(8,128)(2,1)} custom-call(bf16[1024,768]{1,0:T(8,128)(2,1)S(1)} %stage.1.noise_ref, bf16[128,256]{1,0:T(8,128)(2,1)S(1)} %get-tuple-element.67.refs_0_, bf16[128,256]{1,0:T(8,128)(2,1)S(1)} %collective-permute-done.10.refs_1_, bf16[128,256]{1,0:T(8,128)(2,1)S(1)} %collective-permute-done.11.refs_2_, ...), custom_call_target="tpu_custom_call" | custom-call | flops 402653184 | bytes 4194304 | tf_op jit(solution)/shard_map/project_1/pallas_call | solution.py:56
  13.2 2.6 %collective-permute-start.21 = (bf16[256,768]{1,0:T(8,128)(2,1)}, bf16[256,768]{1,0:T(8,128)(2,1)S(1)}, u32[]{:S(2)}, u32[]{:S(2)}) collective-permute-start(bf16[256,768]{1,0:T(8,128)(2,1)} %project_1.1), channel_id=1, source_target_pairs={{0,2},{1,3},{2,0},{3,1},{4,6},{5,7},{6,4},{7,5},{8,10},{9,11},{10,... | collective-permute-start | bytes 1179656 | tf_op jit(solution)/shard_map/ppermute | solution.py:248
  15.8 11.4 %conditional.2 = (bf16[128,512]{1,0:T(8,128)(2,1)}, bf16[128,512]{1,0:T(8,128)(2,1)}, bf16[128,512]{1,0:T(8,128)(2,1)}, bf16[128,512]{1,0:T(8,128)(2,1)}, bf16[1...) conditional(s32[]{:T(128)} %convert_element_type.4, ...), branch_computations={%region_0.0_spmd, %region_1.0_spmd} | conditional | bytes 3670352 | solution.py:242
  15.8 1.7 %collective-permute-start.2 = (bf16[128,512]{1,0:T(8,128)(2,1)}, bf16[128,512]{1,0:T(8,128)(2,1)}, u32[]{:S(2)}, u32[]{:S(2)}) collective-permute-start(bf16[128,512]{1,0:T(8,128)(2,1)} %param.1), channel_id=1, source_target_pairs={{0,24},{4,28},{8,16},{12,20},{16,8},{20,12},{24,0},{28,4},{1,25},{... | collective-permute-start | bytes 393224 | tf_op jit(solution)/shard_map/cond/branch_1_fun/ppermute | solution.py:211
  17.5 0.9 %collective-permute-start.1 = (bf16[128,512]{1,0:T(8,128)(2,1)}, bf16[128,512]{1,0:T(8,128)(2,1)}, u32[]{:S(2)}, u32[]{:S(2)}) collective-permute-start(bf16[128,512]{1,0:T(8,128)(2,1)} %param.1), channel_id=1, source_target_pairs={{0,16},{4,20},{8,24},{12,28},{16,0},{20,4},{24,8},{28,12},{1,17},{... | collective-permute-start | bytes 393224 | tf_op jit(solution)/shard_map/cond/branch_1_fun/ppermute | solution.py:211
  18.4 1.0 %collective-permute-start = (bf16[128,512]{1,0:T(8,128)(2,1)}, bf16[128,512]{1,0:T(8,128)(2,1)}, u32[]{:S(2)}, u32[]{:S(2)}) collective-permute-start(bf16[128,512]{1,0:T(8,128)(2,1)} %param.1), channel_id=1, source_target_pairs={{0,8},{4,12},{8,0},{12,4},{16,24},{20,28},{24,16},{28,20},{1,9},{5... | collective-permute-start | bytes 393224 | tf_op jit(solution)/shard_map/cond/branch_1_fun/ppermute | solution.py:211
  19.3 4.1 %collective-permute-done.2 = bf16[128,512]{1,0:T(8,128)(2,1)} collective-permute-done((bf16[128,512]{1,0:T(8,128)(2,1)}, bf16[128,512]{1,0:T(8,128)(2,1)}, u32[]{:S(2)}, u32[]{:S(2)}) %collective-permute-start.2) | collective-permute-done | bytes 131104 | tf_op jit(solution)/shard_map/cond/branch_1_fun/ppermute | solution.py:211
  23.4 1.9 %collective-permute-done.1 = bf16[128,512]{1,0:T(8,128)(2,1)} collective-permute-done((bf16[128,512]{1,0:T(8,128)(2,1)}, bf16[128,512]{1,0:T(8,128)(2,1)}, u32[]{:S(2)}, u32[]{:S(2)}) %collective-permute-start.1) | collective-permute-done | bytes 131104 | tf_op jit(solution)/shard_map/cond/branch_1_fun/ppermute | solution.py:211
  25.8 1.2 %collective-permute-done.5 = bf16[128,512]{1,0:T(8,128)(2,1)} collective-permute-done((bf16[128,512]{1,0:T(8,128)(2,1)}, bf16[128,512]{1,0:T(8,128)(2,1)}, u32[]{:S(2)}, u32[]{:S(2)}) %collective-permute-start.5) | collective-permute-done | bytes 131104 | tf_op jit(solution)/shard_map/cond/branch_1_fun/ppermute | solution.py:211
  27.2 1.7 %collective-permute-start.20 = (bf16[128,1280]{1,0:T(8,128)(2,1)}, bf16[128,1280]{1,0:T(8,128)(2,1)S(1)}, u32[]{:S(2)}, u32[]{:S(2)}) collective-permute-start(bf16[128,1280]{1,0:T(8,128)(2,1)} %copy-done.7), channel_id=1, source_target_pairs={{0,24},{4,28},{8,16},{12,20},{16,8},{20,12},{24,0},{28,4},{1,25},{... | collective-permute-start | bytes 983048 | tf_op jit(solution)/shard_map/ppermute | solution.py:211
  29.0 0.9 %collective-permute-start.19 = (bf16[128,1280]{1,0:T(8,128)(2,1)}, bf16[128,1280]{1,0:T(8,128)(2,1)}, u32[]{:S(2)}, u32[]{:S(2)}) collective-permute-start(bf16[128,1280]{1,0:T(8,128)(2,1)} %copy-done.7), channel_id=1, source_target_pairs={{0,16},{4,20},{8,24},{12,28},{16,0},{20,4},{24,8},{28,12},{1,17},{... | collective-permute-start | bytes 983048 | tf_op jit(solution)/shard_map/ppermute | solution.py:211
  29.8 1.0 %collective-permute-start.18 = (bf16[128,1280]{1,0:T(8,128)(2,1)}, bf16[128,1280]{1,0:T(8,128)(2,1)}, u32[]{:S(2)}, u32[]{:S(2)}) collective-permute-start(bf16[128,1280]{1,0:T(8,128)(2,1)} %copy-done.7), channel_id=1, source_target_pairs={{0,8},{4,12},{8,0},{12,4},{16,24},{20,28},{24,16},{28,20},{1,9},{5... | collective-permute-start | bytes 983048 | tf_op jit(solution)/shard_map/ppermute | solution.py:211
  30.8 3.1 %project_2.1 = (bf16[256,768]{1,0:T(8,128)(2,1)}, bf16[256,768]{1,0:T(8,128)(2,1)}) custom-call(bf16[1024,768]{1,0:T(8,128)(2,1)S(1)} %stage.1.noise_ref, bf16[128,512]{1,0:T(8,128)(2,1)} %pad_maximum_fusion.1.refs_0_, bf16[128,512]{1,0:T(8,128)(2,1)} %get-tuple-element.48.refs_1_, bf16[128,512]{1,0:T(8,128)(2,1)} %get-tuple-element.50.refs_2_, ...), custom_call_target="tpu_custom_call" | custom-call | flops 805306368 | bytes 5242880 | tf_op jit(solution)/shard_map/project_2/pallas_call | solution.py:56
  33.9 1.6 %collective-permute-start.22 = (bf16[256,768]{1,0:T(8,128)(2,1)}, bf16[256,768]{1,0:T(8,128)(2,1)S(1)}, u32[]{:S(2)}, u32[]{:S(2)}) collective-permute-start(bf16[256,768]{1,0:T(8,128)(2,1)} %get-tuple-element.62), channel_id=1, source_target_pairs={{0,1},{1,2},{2,3},{3,0},{4,5},{5,6},{6,7},{7,4},{8,9},{9,10},{10,1... | collective-permute-start | bytes 1179656 | tf_op jit(solution)/shard_map/ppermute | solution.py:248
  35.5 2.2 %collective-permute-start.23 = (bf16[256,768]{1,0:T(8,128)(2,1)}, bf16[256,768]{1,0:T(8,128)(2,1)S(1)}, u32[]{:S(2)}, u32[]{:S(2)}) collective-permute-start(bf16[256,768]{1,0:T(8,128)(2,1)} %get-tuple-element.64), channel_id=1, source_target_pairs={{0,3},{1,0},{2,1},{3,2},{4,7},{5,4},{6,5},{7,6},{8,11},{9,8},{10,9... | collective-permute-start | bytes 1179656 | tf_op jit(solution)/shard_map/ppermute | solution.py:248
  37.8 1.2 %collective-permute-done.20.refs_3_ = bf16[128,1280]{1,0:T(8,128)(2,1)S(1)} collective-permute-done((bf16[128,1280]{1,0:T(8,128)(2,1)}, bf16[128,1280]{1,0:T(8,128)(2,1)S(1)}, u32[]{:S(2)}, u32[]{:S(2)}) %collective-permute-start.20) | collective-permute-done | bytes 327712 | tf_op jit(solution)/shard_map/ppermute | solution.py:211
  39.0 6.5 %collective-permute-done.19.refs_2_ = bf16[128,1280]{1,0:T(8,128)(2,1)} collective-permute-done((bf16[128,1280]{1,0:T(8,128)(2,1)}, bf16[128,1280]{1,0:T(8,128)(2,1)}, u32[]{:S(2)}, u32[]{:S(2)}) %collective-permute-start.19) | collective-permute-done | bytes 327712 | tf_op jit(solution)/shard_map/ppermute | solution.py:211
  45.5 2.8 %conditional.3 = (bf16[128,1280]{1,0:T(8,128)(2,1)}, bf16[128,1280]{1,0:T(8,128)(2,1)}, bf16[128,1280]{1,0:T(8,128)(2,1)}) conditional(s32[]{:T(128)} %convert_element_type.4, bf16[128,1280]{1,0:T(8,128)(2,1)S(1)} %copy-done.8, (bf16[128,1280]{1,0:T(8,128)(2,1)}, bf16[128,1280]{1,0:T(8,128)(2,1)}, bf16[128,1280]{1,0:T(8,128)(2,1)S(1)}) %tuple.30), branch_computations={%region_2.0_spmd, %region_3.0_spmd} | conditional | bytes 3932304 | solution.py:242
  46.2 1.4 %collective-permute-done.7 = bf16[128,1280]{1,0:T(8,128)(2,1)} collective-permute-done((bf16[128,1280]{1,0:T(8,128)(2,1)}, bf16[128,1280]{1,0:T(8,128)(2,1)}, u32[]{:S(2)}, u32[]{:S(2)}) %collective-permute-start.7) | collective-permute-done | bytes 327712 | tf_op jit(solution)/shard_map/cond/branch_1_fun/ppermute | solution.py:211
  48.3 3.3 %accumulate.1 = (bf16[1024,1024]{1,0:T(8,128)(2,1)S(1)}, f32[1024,768]{1,0:T(8,128)S(1)}, f32[1024,128]{1,0:T(8,128)S(1)}, f32[1024,128]{1,0:T(8,128)S(1)}) custom-call(s32[4,4]{1,0:T(4,128)S(1)} %copy-done.4, bf16[1024,768]{1,0:T(8,128)(2,1)S(1)} %copy-done.1, f32[1,1024]{1,0:T(1,128)S(1)} %bitcast.11, f32[1,1024]{1,0:T(1,128)S(1)} %bitcast.12, ...), custom_call_target="tpu_custom_call" | custom-call | flops 1207959552 | bytes 9175040 | tf_op jit(solution)/shard_map/accumulate/pallas_call | solution.py:139
  51.6 2.8 %collective-permute-done.23.refs_1_ = bf16[256,768]{1,0:T(8,128)(2,1)S(1)} collective-permute-done((bf16[256,768]{1,0:T(8,128)(2,1)}, bf16[256,768]{1,0:T(8,128)(2,1)S(1)}, u32[]{:S(2)}, u32[]{:S(2)}) %collective-permute-start.23) | collective-permute-done | bytes 393248 | tf_op jit(solution)/shard_map/ppermute | solution.py:248
  54.4 3.3 %finish.1 = f32[1024,768]{1,0:T(8,128)} custom-call(s32[4,4]{1,0:T(4,128)S(1)} %copy-done.4, bf16[1024,1024]{1,0:T(8,128)(2,1)S(1)} %get-tuple-element.58.u_ref, f32[1024,768]{1,0:T(8,128)S(1)} %get-tuple-element.59.sum_ref, f32[1024,128]{1,0:T(8,128)S(1)} %get-tuple-element.60.skew_ref, f32[1024,128]{1,0:T(8,128)S(1)} %get-tuple-element.61.tail_ref, ...), custom_call_target="tpu_custom_call" | custom-call | flops 805306368 | bytes 12058624 | tf_op jit(solution)/shard_map/finish/pallas_call | solution.py:190
  (48 shorter events, 3.1 us)
Async XLA Ops:
  0.0 7.9 %copy-start.10 = (bf16[1,128,1024]{2,1,0:T(8,128)(2,1)S(1)}, bf16[1,128,1024]{2,1,0:T(8,128)(2,1)}, u32[]{:S(2)}) copy-start(bf16[1,128,1024]{2,1,0:T(8,128)(2,1)} %param.12) | copy-start | bytes 786436
  1.0 9.4 %collective-permute-start.13 = (bf16[128,256]{1,0:T(8,128)(2,1)S(1)}, bf16[128,256]{1,0:T(8,128)(2,1)S(1)}, u32[]{:S(2)}, u32[]{:S(2)}) collective-permute-start(bf16[128,256]{1,0:T(8,128)(2,1)S(1)} %get-tuple-element.67.refs_0_), channel_id=1, source_target_pairs={{0,4},{4,0},{8,12},{12,8},{16,20},{20,16},{24,28},{28,24},{1,5},{5... | collective-permute-start | bytes 196616 | tf_op jit(solution)/shard_map/ppermute | solution.py:211
  1.5 8.3 %collective-permute-start.12 = (bf16[128,256]{1,0:T(8,128)(2,1)S(1)}, bf16[128,256]{1,0:T(8,128)(2,1)S(1)}, u32[]{:S(2)}, u32[]{:S(2)}) collective-permute-start(bf16[128,256]{1,0:T(8,128)(2,1)S(1)} %get-tuple-element.67.refs_0_), channel_id=1, source_target_pairs={{0,24},{4,28},{8,16},{12,20},{16,8},{20,12},{24,0},{28,4},{1,25},{... | collective-permute-start | bytes 196616 | tf_op jit(solution)/shard_map/ppermute | solution.py:211
  5.0 4.8 %collective-permute-start.11 = (bf16[128,256]{1,0:T(8,128)(2,1)S(1)}, bf16[128,256]{1,0:T(8,128)(2,1)S(1)}, u32[]{:S(2)}, u32[]{:S(2)}) collective-permute-start(bf16[128,256]{1,0:T(8,128)(2,1)S(1)} %get-tuple-element.67.refs_0_), channel_id=1, source_target_pairs={{0,16},{4,20},{8,24},{12,28},{16,0},{20,4},{24,8},{28,12},{1,17},{... | collective-permute-start | bytes 196616 | tf_op jit(solution)/shard_map/ppermute | solution.py:211
  5.5 4.3 %collective-permute-start.10 = (bf16[128,256]{1,0:T(8,128)(2,1)S(1)}, bf16[128,256]{1,0:T(8,128)(2,1)S(1)}, u32[]{:S(2)}, u32[]{:S(2)}) collective-permute-start(bf16[128,256]{1,0:T(8,128)(2,1)S(1)} %get-tuple-element.67.refs_0_), channel_id=1, source_target_pairs={{0,8},{4,12},{8,0},{12,4},{16,24},{20,28},{24,16},{28,20},{1,9},{5... | collective-permute-start | bytes 196616 | tf_op jit(solution)/shard_map/ppermute | solution.py:211
  9.8 1.3 %collective-permute-start.16 = (bf16[128,256]{1,0:T(8,128)(2,1)S(1)}, bf16[128,256]{1,0:T(8,128)(2,1)S(1)}, u32[]{:S(2)}, u32[]{:S(2)}) collective-permute-start(bf16[128,256]{1,0:T(8,128)(2,1)S(1)} %collective-permute-done.12.refs_3_), channel_id=1, source_target_pairs={{0,4},{4,0},{8,12},{12,8},{16,20},{20,16},{24,28},{28,24},{1,5},{5... | collective-permute-start | bytes 196616 | tf_op jit(solution)/shard_map/ppermute | solution.py:211
  9.8 1.4 %collective-permute-start.15 = (bf16[128,256]{1,0:T(8,128)(2,1)S(1)}, bf16[128,256]{1,0:T(8,128)(2,1)S(1)}, u32[]{:S(2)}, u32[]{:S(2)}) collective-permute-start(bf16[128,256]{1,0:T(8,128)(2,1)S(1)} %collective-permute-done.11.refs_2_), channel_id=1, source_target_pairs={{0,4},{4,0},{8,12},{12,8},{16,20},{20,16},{24,28},{28,24},{1,5},{5... | collective-permute-start | bytes 196616 | tf_op jit(solution)/shard_map/ppermute | solution.py:211
  10.3 1.3 %collective-permute-start.14 = (bf16[128,256]{1,0:T(8,128)(2,1)S(1)}, bf16[128,256]{1,0:T(8,128)(2,1)S(1)}, u32[]{:S(2)}, u32[]{:S(2)}) collective-permute-start(bf16[128,256]{1,0:T(8,128)(2,1)S(1)} %collective-permute-done.10.refs_1_), channel_id=1, source_target_pairs={{0,4},{4,0},{8,12},{12,8},{16,20},{20,16},{24,28},{28,24},{1,5},{5... | collective-permute-start | bytes 196616 | tf_op jit(solution)/shard_map/ppermute | solution.py:211
  13.0 2.8 %collective-permute-start.17 = (bf16[128,1280]{1,0:T(8,128)(2,1)S(1)}, bf16[128,1280]{1,0:T(8,128)(2,1)S(1)}, u32[]{:S(2)}, u32[]{:S(2)}) collective-permute-start(bf16[128,1280]{1,0:T(8,128)(2,1)S(1)} %pad_maximum_fusion.refs_0_), channel_id=1, source_target_pairs={{0,4},{4,0},{8,12},{12,8},{16,20},{20,16},{24,28},{28,24},{1,5},{5... | collective-permute-start | bytes 983048 | tf_op jit(solution)/shard_map/ppermute | solution.py:211
  13.2 22.4 %collective-permute-start.21 = (bf16[256,768]{1,0:T(8,128)(2,1)}, bf16[256,768]{1,0:T(8,128)(2,1)S(1)}, u32[]{:S(2)}, u32[]{:S(2)}) collective-permute-start(bf16[256,768]{1,0:T(8,128)(2,1)} %project_1.1), channel_id=1, source_target_pairs={{0,2},{1,3},{2,0},{3,1},{4,6},{5,7},{6,4},{7,5},{8,10},{9,11},{10,... | collective-permute-start | bytes 1179656 | tf_op jit(solution)/shard_map/ppermute | solution.py:248
  15.8 11.5 %copy-start.2 = (bf16[128,1280]{1,0:T(8,128)(2,1)}, bf16[128,1280]{1,0:T(8,128)(2,1)S(1)}, u32[]{:S(2)}) copy-start(bf16[128,1280]{1,0:T(8,128)(2,1)S(1)} %collective-permute-done.17.refs_4_) | copy-start | bytes 983044
  15.8 7.6 %collective-permute-start.2 = (bf16[128,512]{1,0:T(8,128)(2,1)}, bf16[128,512]{1,0:T(8,128)(2,1)}, u32[]{:S(2)}, u32[]{:S(2)}) collective-permute-start(bf16[128,512]{1,0:T(8,128)(2,1)} %param.1), channel_id=1, source_target_pairs={{0,24},{4,28},{8,16},{12,20},{16,8},{20,12},{24,0},{28,4},{1,25},{... | collective-permute-start | bytes 393224 | tf_op jit(solution)/shard_map/cond/branch_1_fun/ppermute | solution.py:211
  17.5 7.8 %collective-permute-start.1 = (bf16[128,512]{1,0:T(8,128)(2,1)}, bf16[128,512]{1,0:T(8,128)(2,1)}, u32[]{:S(2)}, u32[]{:S(2)}) collective-permute-start(bf16[128,512]{1,0:T(8,128)(2,1)} %param.1), channel_id=1, source_target_pairs={{0,16},{4,20},{8,24},{12,28},{16,0},{20,4},{24,8},{28,12},{1,17},{... | collective-permute-start | bytes 393224 | tf_op jit(solution)/shard_map/cond/branch_1_fun/ppermute | solution.py:211
  18.4 7.1 %collective-permute-start = (bf16[128,512]{1,0:T(8,128)(2,1)}, bf16[128,512]{1,0:T(8,128)(2,1)}, u32[]{:S(2)}, u32[]{:S(2)}) collective-permute-start(bf16[128,512]{1,0:T(8,128)(2,1)} %param.1), channel_id=1, source_target_pairs={{0,8},{4,12},{8,0},{12,4},{16,24},{20,28},{24,16},{28,20},{1,9},{5... | collective-permute-start | bytes 393224 | tf_op jit(solution)/shard_map/cond/branch_1_fun/ppermute | solution.py:211
  19.3 6.5 %collective-permute-start.3 = (bf16[128,512]{1,0:T(8,128)(2,1)}, bf16[128,512]{1,0:T(8,128)(2,1)}, u32[]{:S(2)}, u32[]{:S(2)}) collective-permute-start(bf16[128,512]{1,0:T(8,128)(2,1)} %param.1), channel_id=1, source_target_pairs={{0,4},{4,0},{8,12},{12,8},{16,20},{20,16},{24,28},{28,24},{1,5},{5... | collective-permute-start | bytes 393224 | tf_op jit(solution)/shard_map/cond/branch_1_fun/ppermute | solution.py:211
  23.4 2.5 %collective-permute-start.6 = (bf16[128,512]{1,0:T(8,128)(2,1)}, bf16[128,512]{1,0:T(8,128)(2,1)}, u32[]{:S(2)}, u32[]{:S(2)}) collective-permute-start(bf16[128,512]{1,0:T(8,128)(2,1)} %collective-permute-done.2), channel_id=1, source_target_pairs={{0,4},{4,0},{8,12},{12,8},{16,20},{20,16},{24,28},{28,24},{1,5},{5... | collective-permute-start | bytes 393224 | tf_op jit(solution)/shard_map/cond/branch_1_fun/ppermute | solution.py:211
  25.3 1.7 %collective-permute-start.5 = (bf16[128,512]{1,0:T(8,128)(2,1)}, bf16[128,512]{1,0:T(8,128)(2,1)}, u32[]{:S(2)}, u32[]{:S(2)}) collective-permute-start(bf16[128,512]{1,0:T(8,128)(2,1)} %collective-permute-done.1), channel_id=1, source_target_pairs={{0,4},{4,0},{8,12},{12,8},{16,20},{20,16},{24,28},{28,24},{1,5},{5... | collective-permute-start | bytes 393224 | tf_op jit(solution)/shard_map/cond/branch_1_fun/ppermute | solution.py:211
  25.4 1.8 %collective-permute-start.4 = (bf16[128,512]{1,0:T(8,128)(2,1)}, bf16[128,512]{1,0:T(8,128)(2,1)}, u32[]{:S(2)}, u32[]{:S(2)}) collective-permute-start(bf16[128,512]{1,0:T(8,128)(2,1)} %collective-permute-done), channel_id=1, source_target_pairs={{0,4},{4,0},{8,12},{12,8},{16,20},{20,16},{24,28},{28,24},{1,5},{5... | collective-permute-start | bytes 393224 | tf_op jit(solution)/shard_map/cond/branch_1_fun/ppermute | solution.py:211
  27.2 18.3 %copy-start.8 = (bf16[128,1280]{1,0:T(8,128)(2,1)S(1)}, bf16[128,1280]{1,0:T(8,128)(2,1)}, u32[]{:S(2)}) copy-start(bf16[128,1280]{1,0:T(8,128)(2,1)} %copy-done.7) | copy-start | bytes 983044
  27.2 21.1 %copy-start.1 = (bf16[1024,768]{1,0:T(8,128)(2,1)S(1)}, bf16[1024,768]{1,0:T(8,128)(2,1)}, u32[]{:S(2)}) copy-start(bf16[1024,768]{1,0:T(8,128)(2,1)} %noise_ref.1) | copy-start | bytes 4718596
  27.2 21.1 %copy-start.4 = (s32[4,4]{1,0:T(4,128)S(1)}, s32[4,4]{1,0:T(4,128)}, u32[]{:S(2)}) copy-start(s32[4,4]{1,0:T(4,128)} %ranks_ref.3) | copy-start | bytes 196
  27.2 21.1 %copy-start.5 = (f32[1024]{0:T(1024)S(1)}, f32[1024]{0:T(1024)}, u32[]{:S(2)}) copy-start(f32[1024]{0:T(1024)} %param.14) | copy-start | bytes 12292
  27.2 21.1 %copy-start.6 = (f32[1024]{0:T(1024)S(1)}, f32[1024]{0:T(1024)}, u32[]{:S(2)}) copy-start(f32[1024]{0:T(1024)} %param.15) | copy-start | bytes 12292
  27.2 11.7 %collective-permute-start.20 = (bf16[128,1280]{1,0:T(8,128)(2,1)}, bf16[128,1280]{1,0:T(8,128)(2,1)S(1)}, u32[]{:S(2)}, u32[]{:S(2)}) collective-permute-start(bf16[128,1280]{1,0:T(8,128)(2,1)} %copy-done.7), channel_id=1, source_target_pairs={{0,24},{4,28},{8,16},{12,20},{16,8},{20,12},{24,0},{28,4},{1,25},{... | collective-permute-start | bytes 983048 | tf_op jit(solution)/shard_map/ppermute | solution.py:211
  29.0 16.5 %collective-permute-start.19 = (bf16[128,1280]{1,0:T(8,128)(2,1)}, bf16[128,1280]{1,0:T(8,128)(2,1)}, u32[]{:S(2)}, u32[]{:S(2)}) collective-permute-start(bf16[128,1280]{1,0:T(8,128)(2,1)} %copy-done.7), channel_id=1, source_target_pairs={{0,16},{4,20},{8,24},{12,28},{16,0},{20,4},{24,8},{28,12},{1,17},{... | collective-permute-start | bytes 983048 | tf_op jit(solution)/shard_map/ppermute | solution.py:211
  29.8 15.6 %collective-permute-start.18 = (bf16[128,1280]{1,0:T(8,128)(2,1)}, bf16[128,1280]{1,0:T(8,128)(2,1)}, u32[]{:S(2)}, u32[]{:S(2)}) collective-permute-start(bf16[128,1280]{1,0:T(8,128)(2,1)} %copy-done.7), channel_id=1, source_target_pairs={{0,8},{4,12},{8,0},{12,4},{16,24},{20,28},{24,16},{28,20},{1,9},{5... | collective-permute-start | bytes 983048 | tf_op jit(solution)/shard_map/ppermute | solution.py:211
  33.9 14.4 %copy-start.3 = (bf16[128,1280]{1,0:T(8,128)(2,1)S(1)}, bf16[128,1280]{1,0:T(8,128)(2,1)}, u32[]{:S(2)}) copy-start(bf16[128,1280]{1,0:T(8,128)(2,1)} %copy-done.2) | copy-start | bytes 983044
  33.9 17.7 %collective-permute-start.22 = (bf16[256,768]{1,0:T(8,128)(2,1)}, bf16[256,768]{1,0:T(8,128)(2,1)S(1)}, u32[]{:S(2)}, u32[]{:S(2)}) collective-permute-start(bf16[256,768]{1,0:T(8,128)(2,1)} %get-tuple-element.62), channel_id=1, source_target_pairs={{0,1},{1,2},{2,3},{3,0},{4,5},{5,6},{6,7},{7,4},{8,9},{9,10},{10,1... | collective-permute-start | bytes 1179656 | tf_op jit(solution)/shard_map/ppermute | solution.py:248
  35.5 18.9 %collective-permute-start.23 = (bf16[256,768]{1,0:T(8,128)(2,1)}, bf16[256,768]{1,0:T(8,128)(2,1)S(1)}, u32[]{:S(2)}, u32[]{:S(2)}) collective-permute-start(bf16[256,768]{1,0:T(8,128)(2,1)} %get-tuple-element.64), channel_id=1, source_target_pairs={{0,3},{1,0},{2,1},{3,2},{4,7},{5,4},{6,5},{7,6},{8,11},{9,8},{10,9... | collective-permute-start | bytes 1179656 | tf_op jit(solution)/shard_map/ppermute | solution.py:248
  45.5 2.0 %collective-permute-start.7 = (bf16[128,1280]{1,0:T(8,128)(2,1)}, bf16[128,1280]{1,0:T(8,128)(2,1)}, u32[]{:S(2)}, u32[]{:S(2)}) collective-permute-start(bf16[128,1280]{1,0:T(8,128)(2,1)} %get-tuple-element.14), channel_id=1, source_target_pairs={{0,4},{4,0},{8,12},{12,8},{16,20},{20,16},{24,28},{28,24},{1,5},{5... | collective-permute-start | bytes 983048 | tf_op jit(solution)/shard_map/cond/branch_1_fun/ppermute | solution.py:211
  45.6 2.4 %collective-permute-start.8 = (bf16[128,1280]{1,0:T(8,128)(2,1)}, bf16[128,1280]{1,0:T(8,128)(2,1)}, u32[]{:S(2)}, u32[]{:S(2)}) collective-permute-start(bf16[128,1280]{1,0:T(8,128)(2,1)} %get-tuple-element.15), channel_id=1, source_target_pairs={{0,4},{4,0},{8,12},{12,8},{16,20},{20,16},{24,28},{28,24},{1,5},{5... | collective-permute-start | bytes 983048 | tf_op jit(solution)/shard_map/cond/branch_1_fun/ppermute | solution.py:211
  46.1 2.2 %collective-permute-start.9 = (bf16[128,1280]{1,0:T(8,128)(2,1)S(1)}, bf16[128,1280]{1,0:T(8,128)(2,1)}, u32[]{:S(2)}, u32[]{:S(2)}) collective-permute-start(bf16[128,1280]{1,0:T(8,128)(2,1)S(1)} %get-tuple-element.16), channel_id=1, source_target_pairs={{0,4},{4,0},{8,12},{12,8},{16,20},{20,16},{24,28},{28,24},{1,5},{5... | collective-permute-start | bytes 983048 | tf_op jit(solution)/shard_map/cond/branch_1_fun/ppermute | solution.py:211
  (3 other events, 15.7 us)

commit v15 on v14

--- a/solution.py
+++ b/solution.py
@@ -40,28 +40,27 @@
 
 
 def project_kernel(places, rows, noise_ref, *refs):
-    pieces, outs, whole = refs[: len(places)], refs[len(places) : -1], refs[-1]
+    pieces, out_ref, whole = refs[: len(places)], refs[-2], refs[-1]
     stack_pieces(places, rows, pieces, whole)
-    for place, out_ref in enumerate(outs):
-        columns = out_ref.shape[0]
-        out_ref[...] = project_columns(
-            whole[:, place * columns : (place + 1) * columns], noise_ref
-        )
-
-
-def project(n_shifts, noise, gathered):
+    out_ref[...] = project_columns(whole[...], noise_ref)
+
+
+def project(part, parts, noise, gathered):
     sites, reals = noise.shape
     places, pieces = zip(*gathered)
     rows, columns = pieces[0].shape
+    columns //= parts
+    piece = VMEM if parts == 1 else pl.BlockSpec((rows, columns), lambda _: (0, part))
     return pl.pallas_call(
         functools.partial(project_kernel, places, rows),
-        out_shape=[jax.ShapeDtypeStruct((columns // n_shifts, reals), jnp.bfloat16)] * n_shifts,
-        in_specs=[VMEM] * (1 + len(pieces)),
-        out_specs=[VMEM] * n_shifts,
+        out_shape=jax.ShapeDtypeStruct((columns, reals), jnp.bfloat16),
+        grid=(1,),
+        in_specs=[VMEM] + [piece] * len(pieces),
+        out_specs=VMEM,
         scratch_shapes=[pltpu.VMEM((sites, columns), jnp.bfloat16)],
         compiler_params=vmem(noise.shape, (sites, 2 * columns)),
         cost_estimate=cost(2 * sites * columns * reals, noise, *pieces),
-        name=f"project_{n_shifts}",
+        name=f"project_{parts}",
     )(noise, *pieces)
 
 
@@ -269,15 +268,18 @@
     last = (2, 0)
     waiting = (v_first[last], stage(noise), v_rest, own_and_u)
     v_first[last], noise_here, v_rest, own_and_u = lax.optimization_barrier(waiting)
-    [far] = project(1, noise_here, with_other_core(v_first).items())
+    far = project(0, 1, noise_here, with_other_core(v_first).items())
 
     u_swapped = swap(after(own_and_u, far), 1)
     v_pieces = {(0, 0): after(v_rest, far, u_swapped)}
     v_pieces.update(at_once(lambda own: with_other_core(from_chips(own[0, 0])), v_pieces))
     u_pieces = {**from_chips(after(own_and_u, v_pieces)), (1, 0): u_swapped}
-    others = project(len(rest), noise_here, v_pieces.items())
+    others = [project(0, len(rest), noise_here, v_pieces.items())]
     far = along_site(far, first)
-    others = [others[0], *after(others[1:], far)]
+    noise_here = after(noise_here, far, others[0])
+    for part in range(1, len(rest)):
+        others.append(project(part, len(rest), noise_here, v_pieces.items()))
+    u_pieces = after(u_pieces, others[-1])
     u_pieces.update(at_once(from_other_core, u_pieces))
     others = [along_site(coef, shift) for coef, shift in zip(others, rest)]
     u_whole, total, skew, tail = accumulate(

time: 57.9 us -> 59.3 us (1.024)
  Pallas kernels: 11.9 us -> 13.9 us
    pallas_call x2 -> x3, Pallas kernels: 4.54 us -> 6.33 us  [project(): pl.pallas_call(functools.partial(project_kernel, places, rows), out_shape...]
    concatenate x1, other arithmetic: 0.02 us -> 0.75 us  [per_device(): own_and_u = jnp.concatenate([columns_for(0), u_factors[0]], axis=1)]
    concatenate x1, other arithmetic: 0.71 us -> 0.01 us  [per_device(): v_rest = jnp.concatenate([columns_for(shift) for shift in rest], axis=1)]
    unnamed x22 -> x20, local copies, waits for them, and re-layouts: 1.45 us -> 1.44 us
  transfers between devices with their start and end apart: 24 -> 24, of which waited for: 15 -> 15; matrix products, arithmetic and copies ran while one was open for 1% -> 1% of each run, Pallas kernels for 12% -> 15%
where the time goes in v15:
time: 59.3 us; the launch traced here: 59 us
  waiting for transfers between devices  22.1 us (37%)
  starting transfers between devices  19.7 us (33%)
  Pallas kernels  13.9 us (23%)
  local copies, waits for them, and re-layouts  2.44 us (4%)
  other arithmetic  0.76 us (1%)
    ppermute x21, waiting for transfers between devices, swap(): lax.ppermute(array, 'real', [(k, k ^ distance) for k in range(count)])  19.4 us
    ppermute x21, starting transfers between devices, swap(): lax.ppermute(array, 'real', [(k, k ^ distance) for k in range(count)])  13.3 us
    ppermute x3, starting transfers between devices, along_site(): lax.ppermute(coef, 'site', [(k, (k + shift) % count) for k in range(count)])  6.47 us
    pallas_call x3, Pallas kernels, project(): pl.pallas_call(functools.partial(project_kernel, places, rows), out_shape...  6.33 us
    pallas_call x1, Pallas kernels, accumulate(): pl.pallas_call(functools.partial(accumulate_kernel, shifts, places, rows)...  3.42 us
    pallas_call x1, Pallas kernels, finish(): pl.pallas_call(functools.partial(finish_kernel, shifts), out_shape=jax.Sh...  3.33 us
    ppermute x3, waiting for transfers between devices, along_site(): lax.ppermute(coef, 'site', [(k, (k + shift) % count) for k in range(count)])  2.62 us
    unnamed x20, local copies, waits for them, and re-layouts  1.44 us
  transfers between devices with their start and end apart: 24, of which 15 were waited for; matrix products, arithmetic and copies ran while one was open for 1% of the time, Pallas kernels for 15%

profile of v15, /device:TPU:0, one launch (start us, length us, event | category | flops | bytes accessed | tf_op | source)
XLA Modules:
  0.0 59.0 jit_solution(12645805598747823351)
XLA Ops:
  0.0 1.0 %dynamic-slice_bitcast_fusion = (bf16[128,256]{1,0:T(8,128)(2,1)S(1)}, bf16[128,256]{1,0:T(8,128)(2,1)S(1)}, bf16[128,256]{1,0:T(8,128)(2,1)S(1)}, bf16[128,256]{1,0:T(8,128)(2,1)S(1)}) fusion(bf16[1,128,1024]{2,1,0:T(8,128)(2,1)} %param.11, s32[]{:T(128)S(6)} %select_n.15, s32[]{:T(128)S(6)} %select_n.13, s32[]{:T(128)S(6)} %select_n.12, s32[]{:T(128)S(6)} %select_n.14), kind=kLoop, calls=%fused_computation.2 | loop fusion | bytes 524304 | tf_op jit(solution)/shard_map/dynamic_slice | solution.py:262
  1.0 0.5 collective-permute-start.13
  1.5 3.5 %collective-permute-start.12 = (bf16[128,256]{1,0:T(8,128)(2,1)S(1)}, bf16[128,256]{1,0:T(8,128)(2,1)S(1)}, u32[]{:S(2)}, u32[]{:S(2)}) collective-permute-start(bf16[128,256]{1,0:T(8,128)(2,1)S(1)} %get-tuple-element.73.refs_0_), channel_id=1, source_target_pairs={{0,24},{4,28},{8,16},{12,20},{16,8},{20,12},{24,0},{28,4},{1,25},{... | collective-permute-start | bytes 196616 | tf_op jit(solution)/shard_map/ppermute | solution.py:210
  5.0 0.5 collective-permute-start.11
  5.7 1.4 %copy-done = bf16[1024,768]{1,0:T(8,128)(2,1)S(1)} copy-done((bf16[1024,768]{1,0:T(8,128)(2,1)S(1)}, bf16[1024,768]{1,0:T(8,128)(2,1)}, u32[]{:S(2)}) %copy-start) | copy-done | bytes 1572888
  7.1 0.8 %stage.1.noise_ref = bf16[1024,768]{1,0:T(8,128)(2,1)S(1)} custom-call(bf16[1024,768]{1,0:T(8,128)(2,1)S(1)} %copy-done), custom_call_target="tpu_custom_call" | custom-call | bytes 3145728 | tf_op jit(solution)/shard_map/stage/pallas_call | solution.py:82
  7.9 0.8 %pad_maximum_fusion.refs_0_ = bf16[128,1280]{1,0:T(8,128)(2,1)} fusion(bf16[128,1024]{1,0:T(8,128)(2,1)S(1)} %bitcast.13, bf16[128,256]{1,0:T(8,128)(2,1)S(1)} %get-tuple-element.71), kind=kLoop, calls=%fused_computation | loop fusion | flops 655360 | bytes 655360 | tf_op jit(solution)/shard_map/concatenate | solution.py:266
  8.7 1.1 %collective-permute-done.10.refs_1_ = bf16[128,256]{1,0:T(8,128)(2,1)S(1)} collective-permute-done((bf16[128,256]{1,0:T(8,128)(2,1)S(1)}, bf16[128,256]{1,0:T(8,128)(2,1)S(1)}, u32[]{:S(2)}, u32[]{:S(2)}) %collective-permute-start.10) | collective-permute-done | bytes 65568 | tf_op jit(solution)/shard_map/ppermute | solution.py:210
  10.4 0.7 %collective-permute-done.16.refs_7_ = bf16[128,256]{1,0:T(8,128)(2,1)S(1)} collective-permute-done((bf16[128,256]{1,0:T(8,128)(2,1)S(1)}, bf16[128,256]{1,0:T(8,128)(2,1)S(1)}, u32[]{:S(2)}, u32[]{:S(2)}) %collective-permute-start.16) | collective-permute-done | bytes 65568 | tf_op jit(solution)/shard_map/ppermute | solution.py:210
  11.6 1.4 %project_1.1 = bf16[256,768]{1,0:T(8,128)(2,1)} custom-call(bf16[1024,768]{1,0:T(8,128)(2,1)S(1)} %stage.1.noise_ref, bf16[128,256]{1,0:T(8,128)(2,1)S(1)} %get-tuple-element.73.refs_0_, bf16[128,256]{1,0:T(8,128)(2,1)S(1)} %collective-permute-done.10.refs_1_, bf16[128,256]{1,0:T(8,128)(2,1)S(1)} %collective-permute-done.11.refs_2_, ...), custom_call_target="tpu_custom_call" | custom-call | flops 402653184 | bytes 4194304 | tf_op jit(solution)/shard_map/project_1/pallas_call | solution.py:54
  13.0 2.6 %collective-permute-start.21 = (bf16[256,768]{1,0:T(8,128)(2,1)}, bf16[256,768]{1,0:T(8,128)(2,1)}, u32[]{:S(2)}, u32[]{:S(2)}) collective-permute-start(bf16[256,768]{1,0:T(8,128)(2,1)} %project_1.1), channel_id=1, source_target_pairs={{0,2},{1,3},{2,0},{3,1},{4,6},{5,7},{6,4},{7,5},{8,10},{9,11},{10,... | collective-permute-start | bytes 1179656 | tf_op jit(solution)/shard_map/ppermute | solution.py:247
  15.6 1.8 %collective-permute-done.17.refs_1_ = bf16[128,1280]{1,0:T(8,128)(2,1)S(1)} collective-permute-done((bf16[128,1280]{1,0:T(8,128)(2,1)}, bf16[128,1280]{1,0:T(8,128)(2,1)S(1)}, u32[]{:S(2)}, u32[]{:S(2)}) %collective-permute-start.17) | collective-permute-done | bytes 327712 | tf_op jit(solution)/shard_map/ppermute | solution.py:210
  17.4 11.2 %conditional.2 = (bf16[128,512]{1,0:T(8,128)(2,1)}, bf16[128,512]{1,0:T(8,128)(2,1)}, bf16[128,512]{1,0:T(8,128)(2,1)}, bf16[128,512]{1,0:T(8,128)(2,1)}, bf16[1...) conditional(s32[]{:T(128)} %convert_element_type.4, ...), branch_computations={%region_0.0_spmd, %region_1.0_spmd} | conditional | bytes 3670352 | solution.py:241
  17.4 1.8 %collective-permute-start.2 = (bf16[128,512]{1,0:T(8,128)(2,1)S(1)}, bf16[128,512]{1,0:T(8,128)(2,1)}, u32[]{:S(2)}, u32[]{:S(2)}) collective-permute-start(bf16[128,512]{1,0:T(8,128)(2,1)S(1)} %param.1), channel_id=1, source_target_pairs={{0,24},{4,28},{8,16},{12,20},{16,8},{20,12},{24,0},{28,4},{1,25},{... | collective-permute-start | bytes 393224 | tf_op jit(solution)/shard_map/cond/branch_1_fun/ppermute | solution.py:210
  19.2 0.8 %collective-permute-start.1 = (bf16[128,512]{1,0:T(8,128)(2,1)S(1)}, bf16[128,512]{1,0:T(8,128)(2,1)}, u32[]{:S(2)}, u32[]{:S(2)}) collective-permute-start(bf16[128,512]{1,0:T(8,128)(2,1)S(1)} %param.1), channel_id=1, source_target_pairs={{0,16},{4,20},{8,24},{12,28},{16,0},{20,4},{24,8},{28,12},{1,17},{... | collective-permute-start | bytes 393224 | tf_op jit(solution)/shard_map/cond/branch_1_fun/ppermute | solution.py:210
  20.0 1.0 %collective-permute-start = (bf16[128,512]{1,0:T(8,128)(2,1)S(1)}, bf16[128,512]{1,0:T(8,128)(2,1)}, u32[]{:S(2)}, u32[]{:S(2)}) collective-permute-start(bf16[128,512]{1,0:T(8,128)(2,1)S(1)} %param.1), channel_id=1, source_target_pairs={{0,8},{4,12},{8,0},{12,4},{16,24},{20,28},{24,16},{28,20},{1,9},{5... | collective-permute-start | bytes 393224 | tf_op jit(solution)/shard_map/cond/branch_1_fun/ppermute | solution.py:210
  20.9 3.9 %collective-permute-done.2 = bf16[128,512]{1,0:T(8,128)(2,1)} collective-permute-done((bf16[128,512]{1,0:T(8,128)(2,1)S(1)}, bf16[128,512]{1,0:T(8,128)(2,1)}, u32[]{:S(2)}, u32[]{:S(2)}) %collective-permute-start.2) | collective-permute-done | bytes 131104 | tf_op jit(solution)/shard_map/cond/branch_1_fun/ppermute | solution.py:210
  24.8 2.0 %collective-permute-done.1 = bf16[128,512]{1,0:T(8,128)(2,1)} collective-permute-done((bf16[128,512]{1,0:T(8,128)(2,1)S(1)}, bf16[128,512]{1,0:T(8,128)(2,1)}, u32[]{:S(2)}, u32[]{:S(2)}) %collective-permute-start.1) | collective-permute-done | bytes 131104 | tf_op jit(solution)/shard_map/cond/branch_1_fun/ppermute | solution.py:210
  27.3 1.2 %collective-permute-done.5 = bf16[128,512]{1,0:T(8,128)(2,1)} collective-permute-done((bf16[128,512]{1,0:T(8,128)(2,1)}, bf16[128,512]{1,0:T(8,128)(2,1)}, u32[]{:S(2)}, u32[]{:S(2)}) %collective-permute-start.5) | collective-permute-done | bytes 131104 | tf_op jit(solution)/shard_map/cond/branch_1_fun/ppermute | solution.py:210
  28.7 1.7 %collective-permute-start.20 = (bf16[128,1280]{1,0:T(8,128)(2,1)}, bf16[128,1280]{1,0:T(8,128)(2,1)S(1)}, u32[]{:S(2)}, u32[]{:S(2)}) collective-permute-start(bf16[128,1280]{1,0:T(8,128)(2,1)} %pad_maximum_fusion.refs_0_), channel_id=1, source_target_pairs={{0,24},{4,28},{8,16},{12,20},{16,8},{20,12},{24,0},{28,4},{1,25},{... | collective-permute-start | bytes 983048 | tf_op jit(solution)/shard_map/ppermute | solution.py:210
  30.4 0.8 %collective-permute-start.19 = (bf16[128,1280]{1,0:T(8,128)(2,1)}, bf16[128,1280]{1,0:T(8,128)(2,1)}, u32[]{:S(2)}, u32[]{:S(2)}) collective-permute-start(bf16[128,1280]{1,0:T(8,128)(2,1)} %pad_maximum_fusion.refs_0_), channel_id=1, source_target_pairs={{0,16},{4,20},{8,24},{12,28},{16,0},{20,4},{24,8},{28,12},{1,17},{... | collective-permute-start | bytes 983048 | tf_op jit(solution)/shard_map/ppermute | solution.py:210
  31.2 1.0 %collective-permute-start.18 = (bf16[128,1280]{1,0:T(8,128)(2,1)}, bf16[128,1280]{1,0:T(8,128)(2,1)}, u32[]{:S(2)}, u32[]{:S(2)}) collective-permute-start(bf16[128,1280]{1,0:T(8,128)(2,1)} %pad_maximum_fusion.refs_0_), channel_id=1, source_target_pairs={{0,8},{4,12},{8,0},{12,4},{16,24},{20,28},{24,16},{28,20},{1,9},{5... | collective-permute-start | bytes 983048 | tf_op jit(solution)/shard_map/ppermute | solution.py:210
  32.2 2.4 %project_2.2 = bf16[256,768]{1,0:T(8,128)(2,1)} custom-call(bf16[1024,768]{1,0:T(8,128)(2,1)S(1)} %stage.1.noise_ref, bf16[128,512]{1,0:T(8,128)(2,1)S(1)} %pad_maximum_fusion.1.refs_0_, bf16[128,512]{1,0:T(8,128)(2,1)} %get-tuple-element.51.refs_1_, bf16[128,512]{1,0:T(8,128)(2,1)} %get-tuple-element.53.refs_2_, ...), custom_call_target="tpu_custom_call" | custom-call | flops 402653184 | bytes 5242880 | tf_op jit(solution)/shard_map/project_2/pallas_call | solution.py:54
  34.6 1.6 %collective-permute-start.22 = (bf16[256,768]{1,0:T(8,128)(2,1)}, bf16[256,768]{1,0:T(8,128)(2,1)S(1)}, u32[]{:S(2)}, u32[]{:S(2)}) collective-permute-start(bf16[256,768]{1,0:T(8,128)(2,1)} %project_2.2), channel_id=1, source_target_pairs={{0,1},{1,2},{2,3},{3,0},{4,5},{5,6},{6,7},{7,4},{8,9},{9,10},{10,1... | collective-permute-start | bytes 1179656 | tf_op jit(solution)/shard_map/ppermute | solution.py:247
  36.3 2.5 %project_2.3 = bf16[256,768]{1,0:T(8,128)(2,1)} custom-call(bf16[1024,768]{1,0:T(8,128)(2,1)S(1)} %stage.1.noise_ref, bf16[128,512]{1,0:T(8,128)(2,1)} %copy-done.7, bf16[128,512]{1,0:T(8,128)(2,1)} %get-tuple-element.51.refs_1_, bf16[128,512]{1,0:T(8,128)(2,1)} %get-tuple-element.53.refs_2_, bf16[128,512]{1,0:T(8,128)(2,1)} %get-tuple-element.55.refs_3_, ...), custom_call_target="tpu_custom_call" | custom-call | flops 402653184 | bytes 5242880 | tf_op jit(solution)/shard_map/project_2/pallas_call | solution.py:54
  38.7 2.2 %collective-permute-start.23 = (bf16[256,768]{1,0:T(8,128)(2,1)}, bf16[256,768]{1,0:T(8,128)(2,1)S(1)}, u32[]{:S(2)}, u32[]{:S(2)}) collective-permute-start(bf16[256,768]{1,0:T(8,128)(2,1)} %project_2.3), channel_id=1, source_target_pairs={{0,3},{1,0},{2,1},{3,2},{4,7},{5,4},{6,5},{7,6},{8,11},{9,8},{10,9... | collective-permute-start | bytes 1179656 | tf_op jit(solution)/shard_map/ppermute | solution.py:247
  41.0 5.9 %collective-permute-done.19.refs_3_ = bf16[128,1280]{1,0:T(8,128)(2,1)} collective-permute-done((bf16[128,1280]{1,0:T(8,128)(2,1)}, bf16[128,1280]{1,0:T(8,128)(2,1)}, u32[]{:S(2)}, u32[]{:S(2)}) %collective-permute-start.19) | collective-permute-done | bytes 327712 | tf_op jit(solution)/shard_map/ppermute | solution.py:210
  46.9 2.7 %conditional.3 = (bf16[128,1280]{1,0:T(8,128)(2,1)}, bf16[128,1280]{1,0:T(8,128)(2,1)}, bf16[128,1280]{1,0:T(8,128)(2,1)}) conditional(s32[]{:T(128)} %convert_element_type.4, bf16[128,1280]{1,0:T(8,128)(2,1)} %pad_maximum_fusion.refs_0_, (bf16[128,1280]{1,0:T(8,128)(2,1)}, bf16[128,1280]{1,0:T(8,128)(2,1)}, bf16[128,1280]{1,0:T(8,128)(2,1)S(1)}) %tuple.33), branch_computations={%region_2.0_spmd, %region_3.0_spmd} | conditional | bytes 3932304 | solution.py:241
  47.4 1.4 %collective-permute-done.7 = bf16[128,1280]{1,0:T(8,128)(2,1)} collective-permute-done((bf16[128,1280]{1,0:T(8,128)(2,1)}, bf16[128,1280]{1,0:T(8,128)(2,1)}, u32[]{:S(2)}, u32[]{:S(2)}) %collective-permute-start.7) | collective-permute-done | bytes 327712 | tf_op jit(solution)/shard_map/cond/branch_1_fun/ppermute | solution.py:210
  49.6 3.4 %accumulate.1 = (bf16[1024,1024]{1,0:T(8,128)(2,1)S(1)}, f32[1024,768]{1,0:T(8,128)S(1)}, f32[1024,128]{1,0:T(8,128)S(1)}, f32[1024,128]{1,0:T(8,128)S(1)}) custom-call(s32[4,4]{1,0:T(4,128)S(1)} %copy-done.4, bf16[1024,768]{1,0:T(8,128)(2,1)S(1)} %copy-done.1, f32[1,1024]{1,0:T(1,128)S(1)} %bitcast.11, f32[1,1024]{1,0:T(1,128)S(1)} %bitcast.12, ...), custom_call_target="tpu_custom_call" | custom-call | flops 1207959552 | bytes 9175040 | tf_op jit(solution)/shard_map/accumulate/pallas_call | solution.py:138
  53.0 2.6 %collective-permute-done.23.refs_1_ = bf16[256,768]{1,0:T(8,128)(2,1)S(1)} collective-permute-done((bf16[256,768]{1,0:T(8,128)(2,1)}, bf16[256,768]{1,0:T(8,128)(2,1)S(1)}, u32[]{:S(2)}, u32[]{:S(2)}) %collective-permute-start.23) | collective-permute-done | bytes 393248 | tf_op jit(solution)/shard_map/ppermute | solution.py:247
  55.6 3.3 %finish.1 = f32[1024,768]{1,0:T(8,128)} custom-call(s32[4,4]{1,0:T(4,128)S(1)} %copy-done.4, bf16[1024,1024]{1,0:T(8,128)(2,1)S(1)} %get-tuple-element.67.u_ref, f32[1024,768]{1,0:T(8,128)S(1)} %get-tuple-element.68.sum_ref, f32[1024,128]{1,0:T(8,128)S(1)} %get-tuple-element.69.skew_ref, f32[1024,128]{1,0:T(8,128)S(1)} %get-tuple-element.70.tail_ref, ...), custom_call_target="tpu_custom_call" | custom-call | flops 805306368 | bytes 12058624 | tf_op jit(solution)/shard_map/finish/pallas_call | solution.py:189
  (47 shorter events, 3.3 us)
Async XLA Ops:
  0.0 7.9 %copy-start.9 = (bf16[1,128,1024]{2,1,0:T(8,128)(2,1)S(1)}, bf16[1,128,1024]{2,1,0:T(8,128)(2,1)}, u32[]{:S(2)}) copy-start(bf16[1,128,1024]{2,1,0:T(8,128)(2,1)} %param.12) | copy-start | bytes 786436
  1.0 9.4 %collective-permute-start.13 = (bf16[128,256]{1,0:T(8,128)(2,1)S(1)}, bf16[128,256]{1,0:T(8,128)(2,1)S(1)}, u32[]{:S(2)}, u32[]{:S(2)}) collective-permute-start(bf16[128,256]{1,0:T(8,128)(2,1)S(1)} %get-tuple-element.73.refs_0_), channel_id=1, source_target_pairs={{0,4},{4,0},{8,12},{12,8},{16,20},{20,16},{24,28},{28,24},{1,5},{5... | collective-permute-start | bytes 196616 | tf_op jit(solution)/shard_map/ppermute | solution.py:210
  1.5 8.3 %collective-permute-start.12 = (bf16[128,256]{1,0:T(8,128)(2,1)S(1)}, bf16[128,256]{1,0:T(8,128)(2,1)S(1)}, u32[]{:S(2)}, u32[]{:S(2)}) collective-permute-start(bf16[128,256]{1,0:T(8,128)(2,1)S(1)} %get-tuple-element.73.refs_0_), channel_id=1, source_target_pairs={{0,24},{4,28},{8,16},{12,20},{16,8},{20,12},{24,0},{28,4},{1,25},{... | collective-permute-start | bytes 196616 | tf_op jit(solution)/shard_map/ppermute | solution.py:210
  5.0 4.8 %collective-permute-start.11 = (bf16[128,256]{1,0:T(8,128)(2,1)S(1)}, bf16[128,256]{1,0:T(8,128)(2,1)S(1)}, u32[]{:S(2)}, u32[]{:S(2)}) collective-permute-start(bf16[128,256]{1,0:T(8,128)(2,1)S(1)} %get-tuple-element.73.refs_0_), channel_id=1, source_target_pairs={{0,16},{4,20},{8,24},{12,28},{16,0},{20,4},{24,8},{28,12},{1,17},{... | collective-permute-start | bytes 196616 | tf_op jit(solution)/shard_map/ppermute | solution.py:210
  5.5 4.3 %collective-permute-start.10 = (bf16[128,256]{1,0:T(8,128)(2,1)S(1)}, bf16[128,256]{1,0:T(8,128)(2,1)S(1)}, u32[]{:S(2)}, u32[]{:S(2)}) collective-permute-start(bf16[128,256]{1,0:T(8,128)(2,1)S(1)} %get-tuple-element.73.refs_0_), channel_id=1, source_target_pairs={{0,8},{4,12},{8,0},{12,4},{16,24},{20,28},{24,16},{28,20},{1,9},{5... | collective-permute-start | bytes 196616 | tf_op jit(solution)/shard_map/ppermute | solution.py:210
  8.7 23.5 %copy-start.7 = (bf16[128,512]{1,0:T(8,128)(2,1)}, bf16[128,512]{1,0:T(8,128)(2,1)S(1)}, u32[]{:S(2)}) copy-start(bf16[128,512]{1,0:T(8,128)(2,1)S(1)} %pad_maximum_fusion.1.refs_0_) | copy-start | bytes 393220
  9.8 1.3 %collective-permute-start.16 = (bf16[128,256]{1,0:T(8,128)(2,1)S(1)}, bf16[128,256]{1,0:T(8,128)(2,1)S(1)}, u32[]{:S(2)}, u32[]{:S(2)}) collective-permute-start(bf16[128,256]{1,0:T(8,128)(2,1)S(1)} %collective-permute-done.12.refs_3_), channel_id=1, source_target_pairs={{0,4},{4,0},{8,12},{12,8},{16,20},{20,16},{24,28},{28,24},{1,5},{5... | collective-permute-start | bytes 196616 | tf_op jit(solution)/shard_map/ppermute | solution.py:210
  9.8 1.4 %collective-permute-start.15 = (bf16[128,256]{1,0:T(8,128)(2,1)S(1)}, bf16[128,256]{1,0:T(8,128)(2,1)S(1)}, u32[]{:S(2)}, u32[]{:S(2)}) collective-permute-start(bf16[128,256]{1,0:T(8,128)(2,1)S(1)} %collective-permute-done.11.refs_2_), channel_id=1, source_target_pairs={{0,4},{4,0},{8,12},{12,8},{16,20},{20,16},{24,28},{28,24},{1,5},{5... | collective-permute-start | bytes 196616 | tf_op jit(solution)/shard_map/ppermute | solution.py:210
  10.3 1.3 %collective-permute-start.14 = (bf16[128,256]{1,0:T(8,128)(2,1)S(1)}, bf16[128,256]{1,0:T(8,128)(2,1)S(1)}, u32[]{:S(2)}, u32[]{:S(2)}) collective-permute-start(bf16[128,256]{1,0:T(8,128)(2,1)S(1)} %collective-permute-done.10.refs_1_), channel_id=1, source_target_pairs={{0,4},{4,0},{8,12},{12,8},{16,20},{20,16},{24,28},{28,24},{1,5},{5... | collective-permute-start | bytes 196616 | tf_op jit(solution)/shard_map/ppermute | solution.py:210
  13.0 23.3 %collective-permute-start.21 = (bf16[256,768]{1,0:T(8,128)(2,1)}, bf16[256,768]{1,0:T(8,128)(2,1)}, u32[]{:S(2)}, u32[]{:S(2)}) collective-permute-start(bf16[256,768]{1,0:T(8,128)(2,1)} %project_1.1), channel_id=1, source_target_pairs={{0,2},{1,3},{2,0},{3,1},{4,6},{5,7},{6,4},{7,5},{8,10},{9,11},{10,... | collective-permute-start | bytes 1179656 | tf_op jit(solution)/shard_map/ppermute | solution.py:247
  15.6 1.8 %collective-permute-start.17 = (bf16[128,1280]{1,0:T(8,128)(2,1)}, bf16[128,1280]{1,0:T(8,128)(2,1)S(1)}, u32[]{:S(2)}, u32[]{:S(2)}) collective-permute-start(bf16[128,1280]{1,0:T(8,128)(2,1)} %pad_maximum_fusion.refs_0_), channel_id=1, source_target_pairs={{0,4},{4,0},{8,12},{12,8},{16,20},{20,16},{24,28},{28,24},{1,5},{5... | collective-permute-start | bytes 983048 | tf_op jit(solution)/shard_map/ppermute | solution.py:210
  17.4 14.7 %copy-start.2 = (bf16[128,1280]{1,0:T(8,128)(2,1)}, bf16[128,1280]{1,0:T(8,128)(2,1)S(1)}, u32[]{:S(2)}) copy-start(bf16[128,1280]{1,0:T(8,128)(2,1)S(1)} %collective-permute-done.17.refs_1_) | copy-start | bytes 983044
  17.4 7.3 %collective-permute-start.2 = (bf16[128,512]{1,0:T(8,128)(2,1)S(1)}, bf16[128,512]{1,0:T(8,128)(2,1)}, u32[]{:S(2)}, u32[]{:S(2)}) collective-permute-start(bf16[128,512]{1,0:T(8,128)(2,1)S(1)} %param.1), channel_id=1, source_target_pairs={{0,24},{4,28},{8,16},{12,20},{16,8},{20,12},{24,0},{28,4},{1,25},{... | collective-permute-start | bytes 393224 | tf_op jit(solution)/shard_map/cond/branch_1_fun/ppermute | solution.py:210
  19.2 7.6 %collective-permute-start.1 = (bf16[128,512]{1,0:T(8,128)(2,1)S(1)}, bf16[128,512]{1,0:T(8,128)(2,1)}, u32[]{:S(2)}, u32[]{:S(2)}) collective-permute-start(bf16[128,512]{1,0:T(8,128)(2,1)S(1)} %param.1), channel_id=1, source_target_pairs={{0,16},{4,20},{8,24},{12,28},{16,0},{20,4},{24,8},{28,12},{1,17},{... | collective-permute-start | bytes 393224 | tf_op jit(solution)/shard_map/cond/branch_1_fun/ppermute | solution.py:210
  20.0 6.9 %collective-permute-start = (bf16[128,512]{1,0:T(8,128)(2,1)S(1)}, bf16[128,512]{1,0:T(8,128)(2,1)}, u32[]{:S(2)}, u32[]{:S(2)}) collective-permute-start(bf16[128,512]{1,0:T(8,128)(2,1)S(1)} %param.1), channel_id=1, source_target_pairs={{0,8},{4,12},{8,0},{12,4},{16,24},{20,28},{24,16},{28,20},{1,9},{5... | collective-permute-start | bytes 393224 | tf_op jit(solution)/shard_map/cond/branch_1_fun/ppermute | solution.py:210
  20.9 6.4 %collective-permute-start.3 = (bf16[128,512]{1,0:T(8,128)(2,1)S(1)}, bf16[128,512]{1,0:T(8,128)(2,1)}, u32[]{:S(2)}, u32[]{:S(2)}) collective-permute-start(bf16[128,512]{1,0:T(8,128)(2,1)S(1)} %param.1), channel_id=1, source_target_pairs={{0,4},{4,0},{8,12},{12,8},{16,20},{20,16},{24,28},{28,24},{1,5},{5... | collective-permute-start | bytes 393224 | tf_op jit(solution)/shard_map/cond/branch_1_fun/ppermute | solution.py:210
  24.8 2.5 %collective-permute-start.6 = (bf16[128,512]{1,0:T(8,128)(2,1)}, bf16[128,512]{1,0:T(8,128)(2,1)}, u32[]{:S(2)}, u32[]{:S(2)}) collective-permute-start(bf16[128,512]{1,0:T(8,128)(2,1)} %collective-permute-done.2), channel_id=1, source_target_pairs={{0,4},{4,0},{8,12},{12,8},{16,20},{20,16},{24,28},{28,24},{1,5},{5... | collective-permute-start | bytes 393224 | tf_op jit(solution)/shard_map/cond/branch_1_fun/ppermute | solution.py:210
  26.8 1.7 %collective-permute-start.5 = (bf16[128,512]{1,0:T(8,128)(2,1)}, bf16[128,512]{1,0:T(8,128)(2,1)}, u32[]{:S(2)}, u32[]{:S(2)}) collective-permute-start(bf16[128,512]{1,0:T(8,128)(2,1)} %collective-permute-done.1), channel_id=1, source_target_pairs={{0,4},{4,0},{8,12},{12,8},{16,20},{20,16},{24,28},{28,24},{1,5},{5... | collective-permute-start | bytes 393224 | tf_op jit(solution)/shard_map/cond/branch_1_fun/ppermute | solution.py:210
  26.9 1.8 %collective-permute-start.4 = (bf16[128,512]{1,0:T(8,128)(2,1)}, bf16[128,512]{1,0:T(8,128)(2,1)}, u32[]{:S(2)}, u32[]{:S(2)}) collective-permute-start(bf16[128,512]{1,0:T(8,128)(2,1)} %collective-permute-done), channel_id=1, source_target_pairs={{0,4},{4,0},{8,12},{12,8},{16,20},{20,16},{24,28},{28,24},{1,5},{5... | collective-permute-start | bytes 393224 | tf_op jit(solution)/shard_map/cond/branch_1_fun/ppermute | solution.py:210
  28.7 12.3 %collective-permute-start.20 = (bf16[128,1280]{1,0:T(8,128)(2,1)}, bf16[128,1280]{1,0:T(8,128)(2,1)S(1)}, u32[]{:S(2)}, u32[]{:S(2)}) collective-permute-start(bf16[128,1280]{1,0:T(8,128)(2,1)} %pad_maximum_fusion.refs_0_), channel_id=1, source_target_pairs={{0,24},{4,28},{8,16},{12,20},{16,8},{20,12},{24,0},{28,4},{1,25},{... | collective-permute-start | bytes 983048 | tf_op jit(solution)/shard_map/ppermute | solution.py:210
  30.4 16.4 %collective-permute-start.19 = (bf16[128,1280]{1,0:T(8,128)(2,1)}, bf16[128,1280]{1,0:T(8,128)(2,1)}, u32[]{:S(2)}, u32[]{:S(2)}) collective-permute-start(bf16[128,1280]{1,0:T(8,128)(2,1)} %pad_maximum_fusion.refs_0_), channel_id=1, source_target_pairs={{0,16},{4,20},{8,24},{12,28},{16,0},{20,4},{24,8},{28,12},{1,17},{... | collective-permute-start | bytes 983048 | tf_op jit(solution)/shard_map/ppermute | solution.py:210
  31.2 15.6 %collective-permute-start.18 = (bf16[128,1280]{1,0:T(8,128)(2,1)}, bf16[128,1280]{1,0:T(8,128)(2,1)}, u32[]{:S(2)}, u32[]{:S(2)}) collective-permute-start(bf16[128,1280]{1,0:T(8,128)(2,1)} %pad_maximum_fusion.refs_0_), channel_id=1, source_target_pairs={{0,8},{4,12},{8,0},{12,4},{16,24},{20,28},{24,16},{28,20},{1,9},{5... | collective-permute-start | bytes 983048 | tf_op jit(solution)/shard_map/ppermute | solution.py:210
  34.6 14.9 %copy-start.1 = (bf16[1024,768]{1,0:T(8,128)(2,1)S(1)}, bf16[1024,768]{1,0:T(8,128)(2,1)}, u32[]{:S(2)}) copy-start(bf16[1024,768]{1,0:T(8,128)(2,1)} %noise_ref.1) | copy-start | bytes 4718596
  34.6 14.9 %copy-start.4 = (s32[4,4]{1,0:T(4,128)S(1)}, s32[4,4]{1,0:T(4,128)}, u32[]{:S(2)}) copy-start(s32[4,4]{1,0:T(4,128)} %ranks_ref.3) | copy-start | bytes 196
  34.6 14.9 %copy-start.5 = (f32[1024]{0:T(1024)S(1)}, f32[1024]{0:T(1024)}, u32[]{:S(2)}) copy-start(f32[1024]{0:T(1024)} %param.14) | copy-start | bytes 12292
  34.6 14.9 %copy-start.6 = (f32[1024]{0:T(1024)S(1)}, f32[1024]{0:T(1024)}, u32[]{:S(2)}) copy-start(f32[1024]{0:T(1024)} %param.15) | copy-start | bytes 12292
  34.6 18.4 %collective-permute-start.22 = (bf16[256,768]{1,0:T(8,128)(2,1)}, bf16[256,768]{1,0:T(8,128)(2,1)S(1)}, u32[]{:S(2)}, u32[]{:S(2)}) collective-permute-start(bf16[256,768]{1,0:T(8,128)(2,1)} %project_2.2), channel_id=1, source_target_pairs={{0,1},{1,2},{2,3},{3,0},{4,5},{5,6},{6,7},{7,4},{8,9},{9,10},{10,1... | collective-permute-start | bytes 1179656 | tf_op jit(solution)/shard_map/ppermute | solution.py:247
  38.7 10.8 %copy-start.3 = (bf16[128,1280]{1,0:T(8,128)(2,1)S(1)}, bf16[128,1280]{1,0:T(8,128)(2,1)}, u32[]{:S(2)}) copy-start(bf16[128,1280]{1,0:T(8,128)(2,1)} %copy-done.2) | copy-start | bytes 983044
  38.7 16.9 %collective-permute-start.23 = (bf16[256,768]{1,0:T(8,128)(2,1)}, bf16[256,768]{1,0:T(8,128)(2,1)S(1)}, u32[]{:S(2)}, u32[]{:S(2)}) collective-permute-start(bf16[256,768]{1,0:T(8,128)(2,1)} %project_2.3), channel_id=1, source_target_pairs={{0,3},{1,0},{2,1},{3,2},{4,7},{5,4},{6,5},{7,6},{8,11},{9,8},{10,9... | collective-permute-start | bytes 1179656 | tf_op jit(solution)/shard_map/ppermute | solution.py:247
  46.9 2.0 %collective-permute-start.7 = (bf16[128,1280]{1,0:T(8,128)(2,1)}, bf16[128,1280]{1,0:T(8,128)(2,1)}, u32[]{:S(2)}, u32[]{:S(2)}) collective-permute-start(bf16[128,1280]{1,0:T(8,128)(2,1)} %get-tuple-element.14), channel_id=1, source_target_pairs={{0,4},{4,0},{8,12},{12,8},{16,20},{20,16},{24,28},{28,24},{1,5},{5... | collective-permute-start | bytes 983048 | tf_op jit(solution)/shard_map/cond/branch_1_fun/ppermute | solution.py:210
  46.9 2.4 %collective-permute-start.8 = (bf16[128,1280]{1,0:T(8,128)(2,1)}, bf16[128,1280]{1,0:T(8,128)(2,1)}, u32[]{:S(2)}, u32[]{:S(2)}) collective-permute-start(bf16[128,1280]{1,0:T(8,128)(2,1)} %get-tuple-element.15), channel_id=1, source_target_pairs={{0,4},{4,0},{8,12},{12,8},{16,20},{20,16},{24,28},{28,24},{1,5},{5... | collective-permute-start | bytes 983048 | tf_op jit(solution)/shard_map/cond/branch_1_fun/ppermute | solution.py:210
  47.4 2.2 %collective-permute-start.9 = (bf16[128,1280]{1,0:T(8,128)(2,1)S(1)}, bf16[128,1280]{1,0:T(8,128)(2,1)}, u32[]{:S(2)}, u32[]{:S(2)}) collective-permute-start(bf16[128,1280]{1,0:T(8,128)(2,1)S(1)} %get-tuple-element.16), channel_id=1, source_target_pairs={{0,4},{4,0},{8,12},{12,8},{16,20},{20,16},{24,28},{28,24},{1,5},{5... | collective-permute-start | bytes 983048 | tf_op jit(solution)/shard_map/cond/branch_1_fun/ppermute | solution.py:210
  (2 other events, 7.3 us)

commit v16 on v14

--- a/solution.py
+++ b/solution.py
@@ -271,11 +271,12 @@
     v_first[last], noise_here, v_rest, own_and_u = lax.optimization_barrier(waiting)
     [far] = project(1, noise_here, with_other_core(v_first).items())
 
-    u_swapped = swap(after(own_and_u, far), 1)
-    v_pieces = {(0, 0): after(v_rest, far, u_swapped)}
+    v_pieces = {(0, 0): after(v_rest, far)}
     v_pieces.update(at_once(lambda own: with_other_core(from_chips(own[0, 0])), v_pieces))
-    u_pieces = {**from_chips(after(own_and_u, v_pieces)), (1, 0): u_swapped}
+    own_and_u = after(own_and_u, v_pieces)
+    u_pieces = {**from_chips(own_and_u), (1, 0): swap(own_and_u, 1)}
     others = project(len(rest), noise_here, v_pieces.items())
+    others, u_pieces[1, 0] = lax.optimization_barrier((others, u_pieces[1, 0]))
     far = along_site(far, first)
     others = [others[0], *after(others[1:], far)]
     u_pieces.update(at_once(from_other_core, u_pieces))

time: 57.9 us -> 58.4 us (level)
  waiting for transfers between devices: 22.4 us -> 21.5 us
  local copies, waits for them, and re-layouts: 2.45 us -> 3.16 us
  other arithmetic: 0.74 us -> 1.4 us
    ppermute x21, waiting for transfers between devices: 19.6 us -> 18 us  [swap(): lax.ppermute(array, 'real', [(k, k ^ distance) for k in range(count)])]
    concatenate x1, other arithmetic: 0.02 us -> 0.75 us  [per_device(): own_and_u = jnp.concatenate([columns_for(0), u_factors[0]], axis=1)]
    unnamed x22 -> x20, local copies, waits for them, and re-layouts: 1.45 us -> 2.17 us
    ppermute x3, waiting for transfers between devices: 2.78 us -> 3.47 us  [along_site(): lax.ppermute(coef, 'site', [(k, (k + shift) % count) for k in range(count)])]
  transfers between devices with their start and end apart: 24 -> 24, of which waited for: 15 -> 16; matrix products, arithmetic and copies ran while one was open for 1% -> 2% of each run, Pallas kernels for 12% -> 12%
where the time goes in v16:
time: 58.4 us; the launch traced here: 58.2 us
  waiting for transfers between devices  21.5 us (37%)
  starting transfers between devices  20.1 us (34%)
  Pallas kernels  11.9 us (20%)
  local copies, waits for them, and re-layouts  3.16 us (5%)
  other arithmetic  1.4 us (2%)
    ppermute x21, waiting for transfers between devices, swap(): lax.ppermute(array, 'real', [(k, k ^ distance) for k in range(count)])  18 us
    ppermute x21, starting transfers between devices, swap(): lax.ppermute(array, 'real', [(k, k ^ distance) for k in range(count)])  13.7 us
    ppermute x3, starting transfers between devices, along_site(): lax.ppermute(coef, 'site', [(k, (k + shift) % count) for k in range(count)])  6.42 us
    pallas_call x2, Pallas kernels, project(): pl.pallas_call(functools.partial(project_kernel, places, rows), out_shape...  4.53 us
    ppermute x3, waiting for transfers between devices, along_site(): lax.ppermute(coef, 'site', [(k, (k + shift) % count) for k in range(count)])  3.47 us
    pallas_call x1, Pallas kernels, finish(): pl.pallas_call(functools.partial(finish_kernel, shifts), out_shape=jax.Sh...  3.33 us
    pallas_call x1, Pallas kernels, accumulate(): pl.pallas_call(functools.partial(accumulate_kernel, shifts, places, rows)...  3.29 us
    unnamed x20, local copies, waits for them, and re-layouts  2.17 us
  transfers between devices with their start and end apart: 24, of which 16 were waited for; matrix products, arithmetic and copies ran while one was open for 2% of the time, Pallas kernels for 12%

profile of v16, /device:TPU:0, one launch (start us, length us, event | category | flops | bytes accessed | tf_op | source)
XLA Modules:
  0.0 58.2 jit_solution(14453078315325034849)
XLA Ops:
  0.0 1.0 %dynamic-slice_bitcast_fusion = (bf16[128,256]{1,0:T(8,128)(2,1)S(1)}, bf16[128,256]{1,0:T(8,128)(2,1)S(1)}, bf16[128,256]{1,0:T(8,128)(2,1)S(1)}, bf16[128,256]{1,0:T(8,128)(2,1)S(1)}) fusion(bf16[1,128,1024]{2,1,0:T(8,128)(2,1)} %param.11, s32[]{:T(128)S(6)} %select_n.15, s32[]{:T(128)S(6)} %select_n.13, s32[]{:T(128)S(6)} %select_n.12, s32[]{:T(128)S(6)} %select_n.14), kind=kLoop, calls=%fused_computation.2 | loop fusion | bytes 524304 | tf_op jit(solution)/shard_map/dynamic_slice | solution.py:263
  1.0 0.5 collective-permute-start.13
  1.5 3.5 %collective-permute-start.12 = (bf16[128,256]{1,0:T(8,128)(2,1)S(1)}, bf16[128,256]{1,0:T(8,128)(2,1)S(1)}, u32[]{:S(2)}, u32[]{:S(2)}) collective-permute-start(bf16[128,256]{1,0:T(8,128)(2,1)S(1)} %get-tuple-element.71.refs_0_), channel_id=1, source_target_pairs={{0,24},{4,28},{8,16},{12,20},{16,8},{20,12},{24,0},{28,4},{1,25},{... | collective-permute-start | bytes 196616 | tf_op jit(solution)/shard_map/ppermute | solution.py:211
  5.0 0.5 collective-permute-start.11
  5.7 1.4 %copy-done = bf16[1024,768]{1,0:T(8,128)(2,1)S(1)} copy-done((bf16[1024,768]{1,0:T(8,128)(2,1)S(1)}, bf16[1024,768]{1,0:T(8,128)(2,1)}, u32[]{:S(2)}) %copy-start) | copy-done | bytes 1572888
  7.1 0.8 %stage.1.noise_ref = bf16[1024,768]{1,0:T(8,128)(2,1)S(1)} custom-call(bf16[1024,768]{1,0:T(8,128)(2,1)S(1)} %copy-done), custom_call_target="tpu_custom_call" | custom-call | bytes 3145728 | tf_op jit(solution)/shard_map/stage/pallas_call | solution.py:83
  7.9 0.8 %pad_maximum_fusion.refs_0_ = bf16[128,1280]{1,0:T(8,128)(2,1)} fusion(bf16[128,1024]{1,0:T(8,128)(2,1)S(1)} %bitcast.13, bf16[128,256]{1,0:T(8,128)(2,1)S(1)} %get-tuple-element.69), kind=kLoop, calls=%fused_computation | loop fusion | flops 655360 | bytes 655360 | tf_op jit(solution)/shard_map/concatenate | solution.py:267
  8.6 0.7 %pad_maximum_fusion.1.refs_0_ = bf16[128,512]{1,0:T(8,128)(2,1)} fusion(bf16[128,256]{1,0:T(8,128)(2,1)S(1)} %get-tuple-element.72, bf16[128,256]{1,0:T(8,128)(2,1)S(1)} %get-tuple-element.70), kind=kLoop, calls=%fused_computation.1 | loop fusion | flops 262144 | bytes 262144 | tf_op jit(solution)/shard_map/concatenate | solution.py:266
  9.3 0.5 collective-permute-done.10.refs_1_
  10.4 0.7 %collective-permute-done.16.refs_7_ = bf16[128,256]{1,0:T(8,128)(2,1)S(1)} collective-permute-done((bf16[128,256]{1,0:T(8,128)(2,1)S(1)}, bf16[128,256]{1,0:T(8,128)(2,1)S(1)}, u32[]{:S(2)}, u32[]{:S(2)}) %collective-permute-start.16) | collective-permute-done | bytes 65568 | tf_op jit(solution)/shard_map/ppermute | solution.py:211
  11.6 1.4 %project_1.1 = bf16[256,768]{1,0:T(8,128)(2,1)} custom-call(bf16[1024,768]{1,0:T(8,128)(2,1)S(1)} %stage.1.noise_ref, bf16[128,256]{1,0:T(8,128)(2,1)S(1)} %get-tuple-element.71.refs_0_, bf16[128,256]{1,0:T(8,128)(2,1)S(1)} %collective-permute-done.10.refs_1_, bf16[128,256]{1,0:T(8,128)(2,1)S(1)} %collective-permute-done.11.refs_2_, ...), custom_call_target="tpu_custom_call" | custom-call | flops 402653184 | bytes 4194304 | tf_op jit(solution)/shard_map/project_1/pallas_call | solution.py:56
  13.0 2.6 %collective-permute-start.21 = (bf16[256,768]{1,0:T(8,128)(2,1)}, bf16[256,768]{1,0:T(8,128)(2,1)S(1)}, u32[]{:S(2)}, u32[]{:S(2)}) collective-permute-start(bf16[256,768]{1,0:T(8,128)(2,1)} %project_1.1), channel_id=1, source_target_pairs={{0,2},{1,3},{2,0},{3,1},{4,6},{5,7},{6,4},{7,5},{8,10},{9,11},{10,... | collective-permute-start | bytes 1179656 | tf_op jit(solution)/shard_map/ppermute | solution.py:248
  15.6 11.2 %conditional.2 = (bf16[128,512]{1,0:T(8,128)(2,1)}, bf16[128,512]{1,0:T(8,128)(2,1)}, bf16[128,512]{1,0:T(8,128)(2,1)}, bf16[128,512]{1,0:T(8,128)(2,1)}, bf16[1...) conditional(s32[]{:T(128)} %convert_element_type.4, ...), branch_computations={%region_0.0_spmd, %region_1.0_spmd} | conditional | bytes 3670352 | solution.py:242
  15.6 2.3 %collective-permute-start.2 = (bf16[128,512]{1,0:T(8,128)(2,1)}, bf16[128,512]{1,0:T(8,128)(2,1)}, u32[]{:S(2)}, u32[]{:S(2)}) collective-permute-start(bf16[128,512]{1,0:T(8,128)(2,1)} %param.1), channel_id=1, source_target_pairs={{0,24},{4,28},{8,16},{12,20},{16,8},{20,12},{24,0},{28,4},{1,25},{... | collective-permute-start | bytes 393224 | tf_op jit(solution)/shard_map/cond/branch_1_fun/ppermute | solution.py:211
  18.4 0.7 %collective-permute-start = (bf16[128,512]{1,0:T(8,128)(2,1)}, bf16[128,512]{1,0:T(8,128)(2,1)}, u32[]{:S(2)}, u32[]{:S(2)}) collective-permute-start(bf16[128,512]{1,0:T(8,128)(2,1)} %param.1), channel_id=1, source_target_pairs={{0,8},{4,12},{8,0},{12,4},{16,24},{20,28},{24,16},{28,20},{1,9},{5... | collective-permute-start | bytes 393224 | tf_op jit(solution)/shard_map/cond/branch_1_fun/ppermute | solution.py:211
  19.1 3.4 %collective-permute-done.2 = bf16[128,512]{1,0:T(8,128)(2,1)} collective-permute-done((bf16[128,512]{1,0:T(8,128)(2,1)}, bf16[128,512]{1,0:T(8,128)(2,1)}, u32[]{:S(2)}, u32[]{:S(2)}) %collective-permute-start.2) | collective-permute-done | bytes 131104 | tf_op jit(solution)/shard_map/cond/branch_1_fun/ppermute | solution.py:211
  22.5 2.4 %collective-permute-done.1 = bf16[128,512]{1,0:T(8,128)(2,1)} collective-permute-done((bf16[128,512]{1,0:T(8,128)(2,1)}, bf16[128,512]{1,0:T(8,128)(2,1)}, u32[]{:S(2)}, u32[]{:S(2)}) %collective-permute-start.1) | collective-permute-done | bytes 131104 | tf_op jit(solution)/shard_map/cond/branch_1_fun/ppermute | solution.py:211
  25.4 1.2 %collective-permute-done.5 = bf16[128,512]{1,0:T(8,128)(2,1)} collective-permute-done((bf16[128,512]{1,0:T(8,128)(2,1)}, bf16[128,512]{1,0:T(8,128)(2,1)}, u32[]{:S(2)}, u32[]{:S(2)}) %collective-permute-start.5) | collective-permute-done | bytes 131104 | tf_op jit(solution)/shard_map/cond/branch_1_fun/ppermute | solution.py:211
  27.2 1.7 %collective-permute-start.19 = (bf16[128,1280]{1,0:T(8,128)(2,1)}, bf16[128,1280]{1,0:T(8,128)(2,1)S(1)}, u32[]{:S(2)}, u32[]{:S(2)}) collective-permute-start(bf16[128,1280]{1,0:T(8,128)(2,1)} %pad_maximum_fusion.refs_0_), channel_id=1, source_target_pairs={{0,24},{4,28},{8,16},{12,20},{16,8},{20,12},{24,0},{28,4},{1,25},{... | collective-permute-start | bytes 983048 | tf_op jit(solution)/shard_map/ppermute | solution.py:211
  28.9 1.1 %collective-permute-start.18 = (bf16[128,1280]{1,0:T(8,128)(2,1)}, bf16[128,1280]{1,0:T(8,128)(2,1)}, u32[]{:S(2)}, u32[]{:S(2)}) collective-permute-start(bf16[128,1280]{1,0:T(8,128)(2,1)} %pad_maximum_fusion.refs_0_), channel_id=1, source_target_pairs={{0,16},{4,20},{8,24},{12,28},{16,0},{20,4},{24,8},{28,12},{1,17},{... | collective-permute-start | bytes 983048 | tf_op jit(solution)/shard_map/ppermute | solution.py:211
  30.0 0.7 %collective-permute-start.17 = (bf16[128,1280]{1,0:T(8,128)(2,1)}, bf16[128,1280]{1,0:T(8,128)(2,1)}, u32[]{:S(2)}, u32[]{:S(2)}) collective-permute-start(bf16[128,1280]{1,0:T(8,128)(2,1)} %pad_maximum_fusion.refs_0_), channel_id=1, source_target_pairs={{0,8},{4,12},{8,0},{12,4},{16,24},{20,28},{24,16},{28,20},{1,9},{5... | collective-permute-start | bytes 983048 | tf_op jit(solution)/shard_map/ppermute | solution.py:211
  30.7 3.1 %project_2.1 = (bf16[256,768]{1,0:T(8,128)(2,1)}, bf16[256,768]{1,0:T(8,128)(2,1)}) custom-call(bf16[1024,768]{1,0:T(8,128)(2,1)S(1)} %stage.1.noise_ref, bf16[128,512]{1,0:T(8,128)(2,1)} %pad_maximum_fusion.1.refs_0_, bf16[128,512]{1,0:T(8,128)(2,1)} %get-tuple-element.49.refs_1_, bf16[128,512]{1,0:T(8,128)(2,1)} %get-tuple-element.51.refs_2_, ...), custom_call_target="tpu_custom_call" | custom-call | flops 805306368 | bytes 5242880 | tf_op jit(solution)/shard_map/project_2/pallas_call | solution.py:56
  33.8 0.7 %copy-done.2 = bf16[128,1280]{1,0:T(8,128)(2,1)} copy-done((bf16[128,1280]{1,0:T(8,128)(2,1)}, bf16[128,1280]{1,0:T(8,128)(2,1)S(1)}, u32[]{:S(2)}) %copy-start.2) | copy-done | bytes 327704
  34.5 1.6 %collective-permute-start.22 = (bf16[256,768]{1,0:T(8,128)(2,1)}, bf16[256,768]{1,0:T(8,128)(2,1)S(1)}, u32[]{:S(2)}, u32[]{:S(2)}) collective-permute-start(bf16[256,768]{1,0:T(8,128)(2,1)} %get-tuple-element.66), channel_id=1, source_target_pairs={{0,1},{1,2},{2,3},{3,0},{4,5},{5,6},{6,7},{7,4},{8,9},{9,10},{10,1... | collective-permute-start | bytes 1179656 | tf_op jit(solution)/shard_map/ppermute | solution.py:248
  36.1 2.2 %collective-permute-start.23 = (bf16[256,768]{1,0:T(8,128)(2,1)}, bf16[256,768]{1,0:T(8,128)(2,1)S(1)}, u32[]{:S(2)}, u32[]{:S(2)}) collective-permute-start(bf16[256,768]{1,0:T(8,128)(2,1)} %get-tuple-element.68), channel_id=1, source_target_pairs={{0,3},{1,0},{2,1},{3,2},{4,7},{5,4},{6,5},{7,6},{8,11},{9,8},{10,9... | collective-permute-start | bytes 1179656 | tf_op jit(solution)/shard_map/ppermute | solution.py:248
  38.4 0.5 collective-permute-done.19.refs_3_
  38.9 6.3 %collective-permute-done.18.refs_2_ = bf16[128,1280]{1,0:T(8,128)(2,1)} collective-permute-done((bf16[128,1280]{1,0:T(8,128)(2,1)}, bf16[128,1280]{1,0:T(8,128)(2,1)}, u32[]{:S(2)}, u32[]{:S(2)}) %collective-permute-start.18) | collective-permute-done | bytes 327712 | tf_op jit(solution)/shard_map/ppermute | solution.py:211
  45.3 2.7 %conditional.3 = (bf16[128,1280]{1,0:T(8,128)(2,1)}, bf16[128,1280]{1,0:T(8,128)(2,1)}, bf16[128,1280]{1,0:T(8,128)(2,1)}) conditional(s32[]{:T(128)} %convert_element_type.4, bf16[128,1280]{1,0:T(8,128)(2,1)S(1)} %copy-done.7, (bf16[128,1280]{1,0:T(8,128)(2,1)}, bf16[128,1280]{1,0:T(8,128)(2,1)}, bf16[128,1280]{1,0:T(8,128)(2,1)S(1)}) %tuple.30), branch_computations={%region_2.0_spmd, %region_3.0_spmd} | conditional | bytes 3932304 | solution.py:242
  45.9 1.4 %collective-permute-done.7 = bf16[128,1280]{1,0:T(8,128)(2,1)} collective-permute-done((bf16[128,1280]{1,0:T(8,128)(2,1)}, bf16[128,1280]{1,0:T(8,128)(2,1)}, u32[]{:S(2)}, u32[]{:S(2)}) %collective-permute-start.7) | collective-permute-done | bytes 327712 | tf_op jit(solution)/shard_map/cond/branch_1_fun/ppermute | solution.py:211
  48.1 3.3 %accumulate.1 = (bf16[1024,1024]{1,0:T(8,128)(2,1)S(1)}, f32[1024,768]{1,0:T(8,128)S(1)}, f32[1024,128]{1,0:T(8,128)S(1)}, f32[1024,128]{1,0:T(8,128)S(1)}) custom-call(s32[4,4]{1,0:T(4,128)S(1)} %copy-done.4, bf16[1024,768]{1,0:T(8,128)(2,1)S(1)} %copy-done.1, f32[1,1024]{1,0:T(1,128)S(1)} %bitcast.11, f32[1,1024]{1,0:T(1,128)S(1)} %bitcast.12, ...), custom_call_target="tpu_custom_call" | custom-call | flops 1207959552 | bytes 9175040 | tf_op jit(solution)/shard_map/accumulate/pallas_call | solution.py:139
  51.4 3.5 %collective-permute-done.23.refs_1_ = bf16[256,768]{1,0:T(8,128)(2,1)S(1)} collective-permute-done((bf16[256,768]{1,0:T(8,128)(2,1)}, bf16[256,768]{1,0:T(8,128)(2,1)S(1)}, u32[]{:S(2)}, u32[]{:S(2)}) %collective-permute-start.23) | collective-permute-done | bytes 393248 | tf_op jit(solution)/shard_map/ppermute | solution.py:248
  54.8 3.3 %finish.1 = f32[1024,768]{1,0:T(8,128)} custom-call(s32[4,4]{1,0:T(4,128)S(1)} %copy-done.4, bf16[1024,1024]{1,0:T(8,128)(2,1)S(1)} %get-tuple-element.62.u_ref, f32[1024,768]{1,0:T(8,128)S(1)} %get-tuple-element.63.sum_ref, f32[1024,128]{1,0:T(8,128)S(1)} %get-tuple-element.64.skew_ref, f32[1024,128]{1,0:T(8,128)S(1)} %get-tuple-element.65.tail_ref, ...), custom_call_target="tpu_custom_call" | custom-call | flops 805306368 | bytes 12058624 | tf_op jit(solution)/shard_map/finish/pallas_call | solution.py:190
  (46 shorter events, 4.3 us)
Async XLA Ops:
  0.0 7.9 %copy-start.9 = (bf16[1,128,1024]{2,1,0:T(8,128)(2,1)S(1)}, bf16[1,128,1024]{2,1,0:T(8,128)(2,1)}, u32[]{:S(2)}) copy-start(bf16[1,128,1024]{2,1,0:T(8,128)(2,1)} %param.12) | copy-start | bytes 786436
  1.0 9.4 %collective-permute-start.13 = (bf16[128,256]{1,0:T(8,128)(2,1)S(1)}, bf16[128,256]{1,0:T(8,128)(2,1)S(1)}, u32[]{:S(2)}, u32[]{:S(2)}) collective-permute-start(bf16[128,256]{1,0:T(8,128)(2,1)S(1)} %get-tuple-element.71.refs_0_), channel_id=1, source_target_pairs={{0,4},{4,0},{8,12},{12,8},{16,20},{20,16},{24,28},{28,24},{1,5},{5... | collective-permute-start | bytes 196616 | tf_op jit(solution)/shard_map/ppermute | solution.py:211
  1.5 8.3 %collective-permute-start.12 = (bf16[128,256]{1,0:T(8,128)(2,1)S(1)}, bf16[128,256]{1,0:T(8,128)(2,1)S(1)}, u32[]{:S(2)}, u32[]{:S(2)}) collective-permute-start(bf16[128,256]{1,0:T(8,128)(2,1)S(1)} %get-tuple-element.71.refs_0_), channel_id=1, source_target_pairs={{0,24},{4,28},{8,16},{12,20},{16,8},{20,12},{24,0},{28,4},{1,25},{... | collective-permute-start | bytes 196616 | tf_op jit(solution)/shard_map/ppermute | solution.py:211
  5.0 4.8 %collective-permute-start.11 = (bf16[128,256]{1,0:T(8,128)(2,1)S(1)}, bf16[128,256]{1,0:T(8,128)(2,1)S(1)}, u32[]{:S(2)}, u32[]{:S(2)}) collective-permute-start(bf16[128,256]{1,0:T(8,128)(2,1)S(1)} %get-tuple-element.71.refs_0_), channel_id=1, source_target_pairs={{0,16},{4,20},{8,24},{12,28},{16,0},{20,4},{24,8},{28,12},{1,17},{... | collective-permute-start | bytes 196616 | tf_op jit(solution)/shard_map/ppermute | solution.py:211
  5.5 4.3 %collective-permute-start.10 = (bf16[128,256]{1,0:T(8,128)(2,1)S(1)}, bf16[128,256]{1,0:T(8,128)(2,1)S(1)}, u32[]{:S(2)}, u32[]{:S(2)}) collective-permute-start(bf16[128,256]{1,0:T(8,128)(2,1)S(1)} %get-tuple-element.71.refs_0_), channel_id=1, source_target_pairs={{0,8},{4,12},{8,0},{12,4},{16,24},{20,28},{24,16},{28,20},{1,9},{5... | collective-permute-start | bytes 196616 | tf_op jit(solution)/shard_map/ppermute | solution.py:211
  9.8 1.3 %collective-permute-start.16 = (bf16[128,256]{1,0:T(8,128)(2,1)S(1)}, bf16[128,256]{1,0:T(8,128)(2,1)S(1)}, u32[]{:S(2)}, u32[]{:S(2)}) collective-permute-start(bf16[128,256]{1,0:T(8,128)(2,1)S(1)} %collective-permute-done.12.refs_3_), channel_id=1, source_target_pairs={{0,4},{4,0},{8,12},{12,8},{16,20},{20,16},{24,28},{28,24},{1,5},{5... | collective-permute-start | bytes 196616 | tf_op jit(solution)/shard_map/ppermute | solution.py:211
  9.8 1.4 %collective-permute-start.15 = (bf16[128,256]{1,0:T(8,128)(2,1)S(1)}, bf16[128,256]{1,0:T(8,128)(2,1)S(1)}, u32[]{:S(2)}, u32[]{:S(2)}) collective-permute-start(bf16[128,256]{1,0:T(8,128)(2,1)S(1)} %collective-permute-done.11.refs_2_), channel_id=1, source_target_pairs={{0,4},{4,0},{8,12},{12,8},{16,20},{20,16},{24,28},{28,24},{1,5},{5... | collective-permute-start | bytes 196616 | tf_op jit(solution)/shard_map/ppermute | solution.py:211
  10.3 1.3 %collective-permute-start.14 = (bf16[128,256]{1,0:T(8,128)(2,1)S(1)}, bf16[128,256]{1,0:T(8,128)(2,1)S(1)}, u32[]{:S(2)}, u32[]{:S(2)}) collective-permute-start(bf16[128,256]{1,0:T(8,128)(2,1)S(1)} %collective-permute-done.10.refs_1_), channel_id=1, source_target_pairs={{0,4},{4,0},{8,12},{12,8},{16,20},{20,16},{24,28},{28,24},{1,5},{5... | collective-permute-start | bytes 196616 | tf_op jit(solution)/shard_map/ppermute | solution.py:211
  13.0 23.1 %collective-permute-start.21 = (bf16[256,768]{1,0:T(8,128)(2,1)}, bf16[256,768]{1,0:T(8,128)(2,1)S(1)}, u32[]{:S(2)}, u32[]{:S(2)}) collective-permute-start(bf16[256,768]{1,0:T(8,128)(2,1)} %project_1.1), channel_id=1, source_target_pairs={{0,2},{1,3},{2,0},{3,1},{4,6},{5,7},{6,4},{7,5},{8,10},{9,11},{10,... | collective-permute-start | bytes 1179656 | tf_op jit(solution)/shard_map/ppermute | solution.py:248
  15.6 6.9 %collective-permute-start.2 = (bf16[128,512]{1,0:T(8,128)(2,1)}, bf16[128,512]{1,0:T(8,128)(2,1)}, u32[]{:S(2)}, u32[]{:S(2)}) collective-permute-start(bf16[128,512]{1,0:T(8,128)(2,1)} %param.1), channel_id=1, source_target_pairs={{0,24},{4,28},{8,16},{12,20},{16,8},{20,12},{24,0},{28,4},{1,25},{... | collective-permute-start | bytes 393224 | tf_op jit(solution)/shard_map/cond/branch_1_fun/ppermute | solution.py:211
  17.9 7.0 %collective-permute-start.1 = (bf16[128,512]{1,0:T(8,128)(2,1)}, bf16[128,512]{1,0:T(8,128)(2,1)}, u32[]{:S(2)}, u32[]{:S(2)}) collective-permute-start(bf16[128,512]{1,0:T(8,128)(2,1)} %param.1), channel_id=1, source_target_pairs={{0,16},{4,20},{8,24},{12,28},{16,0},{20,4},{24,8},{28,12},{1,17},{... | collective-permute-start | bytes 393224 | tf_op jit(solution)/shard_map/cond/branch_1_fun/ppermute | solution.py:211
  18.4 6.5 %collective-permute-start = (bf16[128,512]{1,0:T(8,128)(2,1)}, bf16[128,512]{1,0:T(8,128)(2,1)}, u32[]{:S(2)}, u32[]{:S(2)}) collective-permute-start(bf16[128,512]{1,0:T(8,128)(2,1)} %param.1), channel_id=1, source_target_pairs={{0,8},{4,12},{8,0},{12,4},{16,24},{20,28},{24,16},{28,20},{1,9},{5... | collective-permute-start | bytes 393224 | tf_op jit(solution)/shard_map/cond/branch_1_fun/ppermute | solution.py:211
  19.1 6.3 %collective-permute-start.3 = (bf16[128,512]{1,0:T(8,128)(2,1)}, bf16[128,512]{1,0:T(8,128)(2,1)}, u32[]{:S(2)}, u32[]{:S(2)}) collective-permute-start(bf16[128,512]{1,0:T(8,128)(2,1)} %param.1), channel_id=1, source_target_pairs={{0,4},{4,0},{8,12},{12,8},{16,20},{20,16},{24,28},{28,24},{1,5},{5... | collective-permute-start | bytes 393224 | tf_op jit(solution)/shard_map/cond/branch_1_fun/ppermute | solution.py:211
  22.5 2.9 %collective-permute-start.6 = (bf16[128,512]{1,0:T(8,128)(2,1)}, bf16[128,512]{1,0:T(8,128)(2,1)}, u32[]{:S(2)}, u32[]{:S(2)}) collective-permute-start(bf16[128,512]{1,0:T(8,128)(2,1)} %collective-permute-done.2), channel_id=1, source_target_pairs={{0,4},{4,0},{8,12},{12,8},{16,20},{20,16},{24,28},{28,24},{1,5},{5... | collective-permute-start | bytes 393224 | tf_op jit(solution)/shard_map/cond/branch_1_fun/ppermute | solution.py:211
  24.9 1.7 %collective-permute-start.5 = (bf16[128,512]{1,0:T(8,128)(2,1)}, bf16[128,512]{1,0:T(8,128)(2,1)}, u32[]{:S(2)}, u32[]{:S(2)}) collective-permute-start(bf16[128,512]{1,0:T(8,128)(2,1)} %collective-permute-done.1), channel_id=1, source_target_pairs={{0,4},{4,0},{8,12},{12,8},{16,20},{20,16},{24,28},{28,24},{1,5},{5... | collective-permute-start | bytes 393224 | tf_op jit(solution)/shard_map/cond/branch_1_fun/ppermute | solution.py:211
  25.0 1.8 %collective-permute-start.4 = (bf16[128,512]{1,0:T(8,128)(2,1)}, bf16[128,512]{1,0:T(8,128)(2,1)}, u32[]{:S(2)}, u32[]{:S(2)}) collective-permute-start(bf16[128,512]{1,0:T(8,128)(2,1)} %collective-permute-done), channel_id=1, source_target_pairs={{0,4},{4,0},{8,12},{12,8},{16,20},{20,16},{24,28},{28,24},{1,5},{5... | collective-permute-start | bytes 393224 | tf_op jit(solution)/shard_map/cond/branch_1_fun/ppermute | solution.py:211
  26.8 18.6 %copy-start.7 = (bf16[128,1280]{1,0:T(8,128)(2,1)S(1)}, bf16[128,1280]{1,0:T(8,128)(2,1)}, u32[]{:S(2)}) copy-start(bf16[128,1280]{1,0:T(8,128)(2,1)} %pad_maximum_fusion.refs_0_) | copy-start | bytes 983044
  26.8 21.3 %copy-start.1 = (bf16[1024,768]{1,0:T(8,128)(2,1)S(1)}, bf16[1024,768]{1,0:T(8,128)(2,1)}, u32[]{:S(2)}) copy-start(bf16[1024,768]{1,0:T(8,128)(2,1)} %noise_ref.1) | copy-start | bytes 4718596
  26.8 21.3 %copy-start.4 = (s32[4,4]{1,0:T(4,128)S(1)}, s32[4,4]{1,0:T(4,128)}, u32[]{:S(2)}) copy-start(s32[4,4]{1,0:T(4,128)} %ranks_ref.3) | copy-start | bytes 196
  26.8 21.3 %copy-start.5 = (f32[1024]{0:T(1024)S(1)}, f32[1024]{0:T(1024)}, u32[]{:S(2)}) copy-start(f32[1024]{0:T(1024)} %param.14) | copy-start | bytes 12292
  26.8 21.3 %copy-start.6 = (f32[1024]{0:T(1024)S(1)}, f32[1024]{0:T(1024)}, u32[]{:S(2)}) copy-start(f32[1024]{0:T(1024)} %param.15) | copy-start | bytes 12292
  26.8 7.0 %collective-permute-start.20 = (bf16[128,1280]{1,0:T(8,128)(2,1)}, bf16[128,1280]{1,0:T(8,128)(2,1)S(1)}, u32[]{:S(2)}, u32[]{:S(2)}) collective-permute-start(bf16[128,1280]{1,0:T(8,128)(2,1)} %pad_maximum_fusion.refs_0_), channel_id=1, source_target_pairs={{0,4},{4,0},{8,12},{12,8},{16,20},{20,16},{24,28},{28,24},{1,5},{5... | collective-permute-start | bytes 983048 | tf_op jit(solution)/shard_map/ppermute | solution.py:211
  27.2 11.7 %collective-permute-start.19 = (bf16[128,1280]{1,0:T(8,128)(2,1)}, bf16[128,1280]{1,0:T(8,128)(2,1)S(1)}, u32[]{:S(2)}, u32[]{:S(2)}) collective-permute-start(bf16[128,1280]{1,0:T(8,128)(2,1)} %pad_maximum_fusion.refs_0_), channel_id=1, source_target_pairs={{0,24},{4,28},{8,16},{12,20},{16,8},{20,12},{24,0},{28,4},{1,25},{... | collective-permute-start | bytes 983048 | tf_op jit(solution)/shard_map/ppermute | solution.py:211
  28.9 16.3 %collective-permute-start.18 = (bf16[128,1280]{1,0:T(8,128)(2,1)}, bf16[128,1280]{1,0:T(8,128)(2,1)}, u32[]{:S(2)}, u32[]{:S(2)}) collective-permute-start(bf16[128,1280]{1,0:T(8,128)(2,1)} %pad_maximum_fusion.refs_0_), channel_id=1, source_target_pairs={{0,16},{4,20},{8,24},{12,28},{16,0},{20,4},{24,8},{28,12},{1,17},{... | collective-permute-start | bytes 983048 | tf_op jit(solution)/shard_map/ppermute | solution.py:211
  30.0 15.3 %collective-permute-start.17 = (bf16[128,1280]{1,0:T(8,128)(2,1)}, bf16[128,1280]{1,0:T(8,128)(2,1)}, u32[]{:S(2)}, u32[]{:S(2)}) collective-permute-start(bf16[128,1280]{1,0:T(8,128)(2,1)} %pad_maximum_fusion.refs_0_), channel_id=1, source_target_pairs={{0,8},{4,12},{8,0},{12,4},{16,24},{20,28},{24,16},{28,20},{1,9},{5... | collective-permute-start | bytes 983048 | tf_op jit(solution)/shard_map/ppermute | solution.py:211
  34.5 13.5 %copy-start.3 = (bf16[128,1280]{1,0:T(8,128)(2,1)S(1)}, bf16[128,1280]{1,0:T(8,128)(2,1)}, u32[]{:S(2)}) copy-start(bf16[128,1280]{1,0:T(8,128)(2,1)} %copy-done.2) | copy-start | bytes 983044
  34.5 16.8 %collective-permute-start.22 = (bf16[256,768]{1,0:T(8,128)(2,1)}, bf16[256,768]{1,0:T(8,128)(2,1)S(1)}, u32[]{:S(2)}, u32[]{:S(2)}) collective-permute-start(bf16[256,768]{1,0:T(8,128)(2,1)} %get-tuple-element.66), channel_id=1, source_target_pairs={{0,1},{1,2},{2,3},{3,0},{4,5},{5,6},{6,7},{7,4},{8,9},{9,10},{10,1... | collective-permute-start | bytes 1179656 | tf_op jit(solution)/shard_map/ppermute | solution.py:248
  36.1 18.7 %collective-permute-start.23 = (bf16[256,768]{1,0:T(8,128)(2,1)}, bf16[256,768]{1,0:T(8,128)(2,1)S(1)}, u32[]{:S(2)}, u32[]{:S(2)}) collective-permute-start(bf16[256,768]{1,0:T(8,128)(2,1)} %get-tuple-element.68), channel_id=1, source_target_pairs={{0,3},{1,0},{2,1},{3,2},{4,7},{5,4},{6,5},{7,6},{8,11},{9,8},{10,9... | collective-permute-start | bytes 1179656 | tf_op jit(solution)/shard_map/ppermute | solution.py:248
  38.9 6.4 %copy-start.8 = (bf16[128,1280]{1,0:T(8,128)(2,1)}, bf16[128,1280]{1,0:T(8,128)(2,1)S(1)}, u32[]{:S(2)}) copy-start(bf16[128,1280]{1,0:T(8,128)(2,1)S(1)} %collective-permute-done.19.refs_3_) | copy-start | bytes 983044
  45.3 2.0 %collective-permute-start.7 = (bf16[128,1280]{1,0:T(8,128)(2,1)}, bf16[128,1280]{1,0:T(8,128)(2,1)}, u32[]{:S(2)}, u32[]{:S(2)}) collective-permute-start(bf16[128,1280]{1,0:T(8,128)(2,1)} %get-tuple-element.14), channel_id=1, source_target_pairs={{0,4},{4,0},{8,12},{12,8},{16,20},{20,16},{24,28},{28,24},{1,5},{5... | collective-permute-start | bytes 983048 | tf_op jit(solution)/shard_map/cond/branch_1_fun/ppermute | solution.py:211
  45.4 2.4 %collective-permute-start.8 = (bf16[128,1280]{1,0:T(8,128)(2,1)}, bf16[128,1280]{1,0:T(8,128)(2,1)}, u32[]{:S(2)}, u32[]{:S(2)}) collective-permute-start(bf16[128,1280]{1,0:T(8,128)(2,1)} %get-tuple-element.15), channel_id=1, source_target_pairs={{0,4},{4,0},{8,12},{12,8},{16,20},{20,16},{24,28},{28,24},{1,5},{5... | collective-permute-start | bytes 983048 | tf_op jit(solution)/shard_map/cond/branch_1_fun/ppermute | solution.py:211
  45.8 2.2 %collective-permute-start.9 = (bf16[128,1280]{1,0:T(8,128)(2,1)S(1)}, bf16[128,1280]{1,0:T(8,128)(2,1)}, u32[]{:S(2)}, u32[]{:S(2)}) collective-permute-start(bf16[128,1280]{1,0:T(8,128)(2,1)S(1)} %get-tuple-element.16), channel_id=1, source_target_pairs={{0,4},{4,0},{8,12},{12,8},{16,20},{20,16},{24,28},{28,24},{1,5},{5... | collective-permute-start | bytes 983048 | tf_op jit(solution)/shard_map/cond/branch_1_fun/ppermute | solution.py:211
  (2 other events, 2.1 us)

commit v17 on v14

--- a/solution.py
+++ b/solution.py
@@ -186,7 +186,7 @@
 def finish(shifts, ranks, u_whole, total, skew, tail, coefs):
     rows, columns = u_whole.shape
     per_source, reals = coefs[0].shape
-    block = min(rows, 128)
+    block = min(rows, 256)
     return pl.pallas_call(
         functools.partial(finish_kernel, shifts),
         out_shape=jax.ShapeDtypeStruct((rows, reals), jnp.float32),

time: 57.9 us -> 58 us (level)
  no operation moved by 1% of the time
where the time goes in v17:
time: 58 us; the launch traced here: 57.7 us
  waiting for transfers between devices  22.4 us (39%)
  starting transfers between devices  20 us (34%)
  Pallas kernels  12 us (21%)
  local copies, waits for them, and re-layouts  2.45 us (4%)
  other arithmetic  0.74 us (1%)
    ppermute x21, waiting for transfers between devices, swap(): lax.ppermute(array, 'real', [(k, k ^ distance) for k in range(count)])  19.6 us
    ppermute x21, starting transfers between devices, swap(): lax.ppermute(array, 'real', [(k, k ^ distance) for k in range(count)])  13.6 us
    ppermute x3, starting transfers between devices, along_site(): lax.ppermute(coef, 'site', [(k, (k + shift) % count) for k in range(count)])  6.41 us
    pallas_call x2, Pallas kernels, project(): pl.pallas_call(functools.partial(project_kernel, places, rows), out_shape...  4.54 us
    pallas_call x1, Pallas kernels, finish(): pl.pallas_call(functools.partial(finish_kernel, shifts), out_shape=jax.Sh...  3.36 us
    pallas_call x1, Pallas kernels, accumulate(): pl.pallas_call(functools.partial(accumulate_kernel, shifts, places, rows)...  3.29 us
    ppermute x3, waiting for transfers between devices, along_site(): lax.ppermute(coef, 'site', [(k, (k + shift) % count) for k in range(count)])  2.78 us
    unnamed x22, local copies, waits for them, and re-layouts  1.45 us
  transfers between devices with their start and end apart: 24, of which 15 were waited for; matrix products, arithmetic and copies ran while one was open for 1% of the time, Pallas kernels for 12%

profile of v17, /device:TPU:0, one launch (start us, length us, event | category | flops | bytes accessed | tf_op | source)
XLA Modules:
  0.0 57.7 jit_solution(13304476625890997075)
XLA Ops:
  0.0 1.0 %dynamic-slice_bitcast_fusion = (bf16[128,256]{1,0:T(8,128)(2,1)S(1)}, bf16[128,256]{1,0:T(8,128)(2,1)S(1)}, bf16[128,256]{1,0:T(8,128)(2,1)S(1)}, bf16[128,256]{1,0:T(8,128)(2,1)S(1)}) fusion(bf16[1,128,1024]{2,1,0:T(8,128)(2,1)} %param.11, s32[]{:T(128)S(6)} %select_n.15, s32[]{:T(128)S(6)} %select_n.13, s32[]{:T(128)S(6)} %select_n.12, s32[]{:T(128)S(6)} %select_n.14), kind=kLoop, calls=%fused_computation.2 | loop fusion | bytes 524304 | tf_op jit(solution)/shard_map/dynamic_slice | solution.py:263
  1.0 0.5 collective-permute-start.13
  1.5 3.5 %collective-permute-start.12 = (bf16[128,256]{1,0:T(8,128)(2,1)S(1)}, bf16[128,256]{1,0:T(8,128)(2,1)S(1)}, u32[]{:S(2)}, u32[]{:S(2)}) collective-permute-start(bf16[128,256]{1,0:T(8,128)(2,1)S(1)} %get-tuple-element.67.refs_0_), channel_id=1, source_target_pairs={{0,24},{4,28},{8,16},{12,20},{16,8},{20,12},{24,0},{28,4},{1,25},{... | collective-permute-start | bytes 196616 | tf_op jit(solution)/shard_map/ppermute | solution.py:211
  5.0 0.5 collective-permute-start.11
  5.7 1.4 %copy-done = bf16[1024,768]{1,0:T(8,128)(2,1)S(1)} copy-done((bf16[1024,768]{1,0:T(8,128)(2,1)S(1)}, bf16[1024,768]{1,0:T(8,128)(2,1)}, u32[]{:S(2)}) %copy-start) | copy-done | bytes 1572888
  7.1 0.8 %stage.1.noise_ref = bf16[1024,768]{1,0:T(8,128)(2,1)S(1)} custom-call(bf16[1024,768]{1,0:T(8,128)(2,1)S(1)} %copy-done), custom_call_target="tpu_custom_call" | custom-call | bytes 3145728 | tf_op jit(solution)/shard_map/stage/pallas_call | solution.py:83
  7.9 0.7 %pad_maximum_fusion.1.refs_0_ = bf16[128,512]{1,0:T(8,128)(2,1)} fusion(bf16[128,256]{1,0:T(8,128)(2,1)S(1)} %get-tuple-element.68, bf16[128,256]{1,0:T(8,128)(2,1)S(1)} %get-tuple-element.66), kind=kLoop, calls=%fused_computation.1 | loop fusion | flops 262144 | bytes 262144 | tf_op jit(solution)/shard_map/concatenate | solution.py:266
  8.6 1.2 %collective-permute-done.10.refs_1_ = bf16[128,256]{1,0:T(8,128)(2,1)S(1)} collective-permute-done((bf16[128,256]{1,0:T(8,128)(2,1)S(1)}, bf16[128,256]{1,0:T(8,128)(2,1)S(1)}, u32[]{:S(2)}, u32[]{:S(2)}) %collective-permute-start.10) | collective-permute-done | bytes 65568 | tf_op jit(solution)/shard_map/ppermute | solution.py:211
  9.8 0.5 collective-permute-start.15
  10.4 0.7 %collective-permute-done.16.refs_7_ = bf16[128,256]{1,0:T(8,128)(2,1)S(1)} collective-permute-done((bf16[128,256]{1,0:T(8,128)(2,1)S(1)}, bf16[128,256]{1,0:T(8,128)(2,1)S(1)}, u32[]{:S(2)}, u32[]{:S(2)}) %collective-permute-start.16) | collective-permute-done | bytes 65568 | tf_op jit(solution)/shard_map/ppermute | solution.py:211
  11.6 1.4 %project_1.1 = bf16[256,768]{1,0:T(8,128)(2,1)} custom-call(bf16[1024,768]{1,0:T(8,128)(2,1)S(1)} %stage.1.noise_ref, bf16[128,256]{1,0:T(8,128)(2,1)S(1)} %get-tuple-element.67.refs_0_, bf16[128,256]{1,0:T(8,128)(2,1)S(1)} %collective-permute-done.10.refs_1_, bf16[128,256]{1,0:T(8,128)(2,1)S(1)} %collective-permute-done.11.refs_2_, ...), custom_call_target="tpu_custom_call" | custom-call | flops 402653184 | bytes 4194304 | tf_op jit(solution)/shard_map/project_1/pallas_call | solution.py:56
  13.2 2.6 %collective-permute-start.21 = (bf16[256,768]{1,0:T(8,128)(2,1)}, bf16[256,768]{1,0:T(8,128)(2,1)S(1)}, u32[]{:S(2)}, u32[]{:S(2)}) collective-permute-start(bf16[256,768]{1,0:T(8,128)(2,1)} %project_1.1), channel_id=1, source_target_pairs={{0,2},{1,3},{2,0},{3,1},{4,6},{5,7},{6,4},{7,5},{8,10},{9,11},{10,... | collective-permute-start | bytes 1179656 | tf_op jit(solution)/shard_map/ppermute | solution.py:248
  15.8 11.4 %conditional.2 = (bf16[128,512]{1,0:T(8,128)(2,1)}, bf16[128,512]{1,0:T(8,128)(2,1)}, bf16[128,512]{1,0:T(8,128)(2,1)}, bf16[128,512]{1,0:T(8,128)(2,1)}, bf16[1...) conditional(s32[]{:T(128)} %convert_element_type.4, ...), branch_computations={%region_0.0_spmd, %region_1.0_spmd} | conditional | bytes 3670352 | solution.py:242
  15.8 1.7 %collective-permute-start.2 = (bf16[128,512]{1,0:T(8,128)(2,1)}, bf16[128,512]{1,0:T(8,128)(2,1)}, u32[]{:S(2)}, u32[]{:S(2)}) collective-permute-start(bf16[128,512]{1,0:T(8,128)(2,1)} %param.1), channel_id=1, source_target_pairs={{0,24},{4,28},{8,16},{12,20},{16,8},{20,12},{24,0},{28,4},{1,25},{... | collective-permute-start | bytes 393224 | tf_op jit(solution)/shard_map/cond/branch_1_fun/ppermute | solution.py:211
  17.5 0.9 %collective-permute-start.1 = (bf16[128,512]{1,0:T(8,128)(2,1)}, bf16[128,512]{1,0:T(8,128)(2,1)}, u32[]{:S(2)}, u32[]{:S(2)}) collective-permute-start(bf16[128,512]{1,0:T(8,128)(2,1)} %param.1), channel_id=1, source_target_pairs={{0,16},{4,20},{8,24},{12,28},{16,0},{20,4},{24,8},{28,12},{1,17},{... | collective-permute-start | bytes 393224 | tf_op jit(solution)/shard_map/cond/branch_1_fun/ppermute | solution.py:211
  18.4 1.0 %collective-permute-start = (bf16[128,512]{1,0:T(8,128)(2,1)}, bf16[128,512]{1,0:T(8,128)(2,1)}, u32[]{:S(2)}, u32[]{:S(2)}) collective-permute-start(bf16[128,512]{1,0:T(8,128)(2,1)} %param.1), channel_id=1, source_target_pairs={{0,8},{4,12},{8,0},{12,4},{16,24},{20,28},{24,16},{28,20},{1,9},{5... | collective-permute-start | bytes 393224 | tf_op jit(solution)/shard_map/cond/branch_1_fun/ppermute | solution.py:211
  19.3 4.1 %collective-permute-done.2 = bf16[128,512]{1,0:T(8,128)(2,1)} collective-permute-done((bf16[128,512]{1,0:T(8,128)(2,1)}, bf16[128,512]{1,0:T(8,128)(2,1)}, u32[]{:S(2)}, u32[]{:S(2)}) %collective-permute-start.2) | collective-permute-done | bytes 131104 | tf_op jit(solution)/shard_map/cond/branch_1_fun/ppermute | solution.py:211
  23.4 1.9 %collective-permute-done.1 = bf16[128,512]{1,0:T(8,128)(2,1)} collective-permute-done((bf16[128,512]{1,0:T(8,128)(2,1)}, bf16[128,512]{1,0:T(8,128)(2,1)}, u32[]{:S(2)}, u32[]{:S(2)}) %collective-permute-start.1) | collective-permute-done | bytes 131104 | tf_op jit(solution)/shard_map/cond/branch_1_fun/ppermute | solution.py:211
  25.8 1.2 %collective-permute-done.5 = bf16[128,512]{1,0:T(8,128)(2,1)} collective-permute-done((bf16[128,512]{1,0:T(8,128)(2,1)}, bf16[128,512]{1,0:T(8,128)(2,1)}, u32[]{:S(2)}, u32[]{:S(2)}) %collective-permute-start.5) | collective-permute-done | bytes 131104 | tf_op jit(solution)/shard_map/cond/branch_1_fun/ppermute | solution.py:211
  27.2 1.7 %collective-permute-start.20 = (bf16[128,1280]{1,0:T(8,128)(2,1)}, bf16[128,1280]{1,0:T(8,128)(2,1)S(1)}, u32[]{:S(2)}, u32[]{:S(2)}) collective-permute-start(bf16[128,1280]{1,0:T(8,128)(2,1)} %copy-done.7), channel_id=1, source_target_pairs={{0,24},{4,28},{8,16},{12,20},{16,8},{20,12},{24,0},{28,4},{1,25},{... | collective-permute-start | bytes 983048 | tf_op jit(solution)/shard_map/ppermute | solution.py:211
  29.0 0.9 %collective-permute-start.19 = (bf16[128,1280]{1,0:T(8,128)(2,1)}, bf16[128,1280]{1,0:T(8,128)(2,1)}, u32[]{:S(2)}, u32[]{:S(2)}) collective-permute-start(bf16[128,1280]{1,0:T(8,128)(2,1)} %copy-done.7), channel_id=1, source_target_pairs={{0,16},{4,20},{8,24},{12,28},{16,0},{20,4},{24,8},{28,12},{1,17},{... | collective-permute-start | bytes 983048 | tf_op jit(solution)/shard_map/ppermute | solution.py:211
  29.8 1.0 %collective-permute-start.18 = (bf16[128,1280]{1,0:T(8,128)(2,1)}, bf16[128,1280]{1,0:T(8,128)(2,1)}, u32[]{:S(2)}, u32[]{:S(2)}) collective-permute-start(bf16[128,1280]{1,0:T(8,128)(2,1)} %copy-done.7), channel_id=1, source_target_pairs={{0,8},{4,12},{8,0},{12,4},{16,24},{20,28},{24,16},{28,20},{1,9},{5... | collective-permute-start | bytes 983048 | tf_op jit(solution)/shard_map/ppermute | solution.py:211
  30.8 3.1 %project_2.1 = (bf16[256,768]{1,0:T(8,128)(2,1)}, bf16[256,768]{1,0:T(8,128)(2,1)}) custom-call(bf16[1024,768]{1,0:T(8,128)(2,1)S(1)} %stage.1.noise_ref, bf16[128,512]{1,0:T(8,128)(2,1)} %pad_maximum_fusion.1.refs_0_, bf16[128,512]{1,0:T(8,128)(2,1)} %get-tuple-element.48.refs_1_, bf16[128,512]{1,0:T(8,128)(2,1)} %get-tuple-element.50.refs_2_, ...), custom_call_target="tpu_custom_call" | custom-call | flops 805306368 | bytes 5242880 | tf_op jit(solution)/shard_map/project_2/pallas_call | solution.py:56
  33.9 1.6 %collective-permute-start.22 = (bf16[256,768]{1,0:T(8,128)(2,1)}, bf16[256,768]{1,0:T(8,128)(2,1)S(1)}, u32[]{:S(2)}, u32[]{:S(2)}) collective-permute-start(bf16[256,768]{1,0:T(8,128)(2,1)} %get-tuple-element.62), channel_id=1, source_target_pairs={{0,1},{1,2},{2,3},{3,0},{4,5},{5,6},{6,7},{7,4},{8,9},{9,10},{10,1... | collective-permute-start | bytes 1179656 | tf_op jit(solution)/shard_map/ppermute | solution.py:248
  35.5 2.2 %collective-permute-start.23 = (bf16[256,768]{1,0:T(8,128)(2,1)}, bf16[256,768]{1,0:T(8,128)(2,1)S(1)}, u32[]{:S(2)}, u32[]{:S(2)}) collective-permute-start(bf16[256,768]{1,0:T(8,128)(2,1)} %get-tuple-element.64), channel_id=1, source_target_pairs={{0,3},{1,0},{2,1},{3,2},{4,7},{5,4},{6,5},{7,6},{8,11},{9,8},{10,9... | collective-permute-start | bytes 1179656 | tf_op jit(solution)/shard_map/ppermute | solution.py:248
  37.8 1.2 %collective-permute-done.20.refs_3_ = bf16[128,1280]{1,0:T(8,128)(2,1)S(1)} collective-permute-done((bf16[128,1280]{1,0:T(8,128)(2,1)}, bf16[128,1280]{1,0:T(8,128)(2,1)S(1)}, u32[]{:S(2)}, u32[]{:S(2)}) %collective-permute-start.20) | collective-permute-done | bytes 327712 | tf_op jit(solution)/shard_map/ppermute | solution.py:211
  39.0 6.5 %collective-permute-done.19.refs_2_ = bf16[128,1280]{1,0:T(8,128)(2,1)} collective-permute-done((bf16[128,1280]{1,0:T(8,128)(2,1)}, bf16[128,1280]{1,0:T(8,128)(2,1)}, u32[]{:S(2)}, u32[]{:S(2)}) %collective-permute-start.19) | collective-permute-done | bytes 327712 | tf_op jit(solution)/shard_map/ppermute | solution.py:211
  45.5 2.8 %conditional.3 = (bf16[128,1280]{1,0:T(8,128)(2,1)}, bf16[128,1280]{1,0:T(8,128)(2,1)}, bf16[128,1280]{1,0:T(8,128)(2,1)}) conditional(s32[]{:T(128)} %convert_element_type.4, bf16[128,1280]{1,0:T(8,128)(2,1)S(1)} %copy-done.8, (bf16[128,1280]{1,0:T(8,128)(2,1)}, bf16[128,1280]{1,0:T(8,128)(2,1)}, bf16[128,1280]{1,0:T(8,128)(2,1)S(1)}) %tuple.30), branch_computations={%region_2.0_spmd, %region_3.0_spmd} | conditional | bytes 3932304 | solution.py:242
  46.2 1.4 %collective-permute-done.7 = bf16[128,1280]{1,0:T(8,128)(2,1)} collective-permute-done((bf16[128,1280]{1,0:T(8,128)(2,1)}, bf16[128,1280]{1,0:T(8,128)(2,1)}, u32[]{:S(2)}, u32[]{:S(2)}) %collective-permute-start.7) | collective-permute-done | bytes 327712 | tf_op jit(solution)/shard_map/cond/branch_1_fun/ppermute | solution.py:211
  48.3 3.3 %accumulate.1 = (bf16[1024,1024]{1,0:T(8,128)(2,1)S(1)}, f32[1024,768]{1,0:T(8,128)S(1)}, f32[1024,128]{1,0:T(8,128)S(1)}, f32[1024,128]{1,0:T(8,128)S(1)}) custom-call(s32[4,4]{1,0:T(4,128)S(1)} %copy-done.4, bf16[1024,768]{1,0:T(8,128)(2,1)S(1)} %copy-done.1, f32[1,1024]{1,0:T(1,128)S(1)} %bitcast.11, f32[1,1024]{1,0:T(1,128)S(1)} %bitcast.12, ...), custom_call_target="tpu_custom_call" | custom-call | flops 1207959552 | bytes 9175040 | tf_op jit(solution)/shard_map/accumulate/pallas_call | solution.py:139
  51.6 2.8 %collective-permute-done.23.refs_1_ = bf16[256,768]{1,0:T(8,128)(2,1)S(1)} collective-permute-done((bf16[256,768]{1,0:T(8,128)(2,1)}, bf16[256,768]{1,0:T(8,128)(2,1)S(1)}, u32[]{:S(2)}, u32[]{:S(2)}) %collective-permute-start.23) | collective-permute-done | bytes 393248 | tf_op jit(solution)/shard_map/ppermute | solution.py:248
  54.4 3.4 %finish.1 = f32[1024,768]{1,0:T(8,128)} custom-call(s32[4,4]{1,0:T(4,128)S(1)} %copy-done.4, bf16[1024,1024]{1,0:T(8,128)(2,1)S(1)} %get-tuple-element.58.u_ref, f32[1024,768]{1,0:T(8,128)S(1)} %get-tuple-element.59.sum_ref, f32[1024,128]{1,0:T(8,128)S(1)} %get-tuple-element.60.skew_ref, f32[1024,128]{1,0:T(8,128)S(1)} %get-tuple-element.61.tail_ref, ...), custom_call_target="tpu_custom_call" | custom-call | flops 805306368 | bytes 12058624 | tf_op jit(solution)/shard_map/finish/pallas_call | solution.py:190
  (48 shorter events, 3.1 us)
Async XLA Ops:
  0.0 7.9 %copy-start.10 = (bf16[1,128,1024]{2,1,0:T(8,128)(2,1)S(1)}, bf16[1,128,1024]{2,1,0:T(8,128)(2,1)}, u32[]{:S(2)}) copy-start(bf16[1,128,1024]{2,1,0:T(8,128)(2,1)} %param.12) | copy-start | bytes 786436
  1.0 9.4 %collective-permute-start.13 = (bf16[128,256]{1,0:T(8,128)(2,1)S(1)}, bf16[128,256]{1,0:T(8,128)(2,1)S(1)}, u32[]{:S(2)}, u32[]{:S(2)}) collective-permute-start(bf16[128,256]{1,0:T(8,128)(2,1)S(1)} %get-tuple-element.67.refs_0_), channel_id=1, source_target_pairs={{0,4},{4,0},{8,12},{12,8},{16,20},{20,16},{24,28},{28,24},{1,5},{5... | collective-permute-start | bytes 196616 | tf_op jit(solution)/shard_map/ppermute | solution.py:211
  1.5 8.3 %collective-permute-start.12 = (bf16[128,256]{1,0:T(8,128)(2,1)S(1)}, bf16[128,256]{1,0:T(8,128)(2,1)S(1)}, u32[]{:S(2)}, u32[]{:S(2)}) collective-permute-start(bf16[128,256]{1,0:T(8,128)(2,1)S(1)} %get-tuple-element.67.refs_0_), channel_id=1, source_target_pairs={{0,24},{4,28},{8,16},{12,20},{16,8},{20,12},{24,0},{28,4},{1,25},{... | collective-permute-start | bytes 196616 | tf_op jit(solution)/shard_map/ppermute | solution.py:211
  5.0 4.8 %collective-permute-start.11 = (bf16[128,256]{1,0:T(8,128)(2,1)S(1)}, bf16[128,256]{1,0:T(8,128)(2,1)S(1)}, u32[]{:S(2)}, u32[]{:S(2)}) collective-permute-start(bf16[128,256]{1,0:T(8,128)(2,1)S(1)} %get-tuple-element.67.refs_0_), channel_id=1, source_target_pairs={{0,16},{4,20},{8,24},{12,28},{16,0},{20,4},{24,8},{28,12},{1,17},{... | collective-permute-start | bytes 196616 | tf_op jit(solution)/shard_map/ppermute | solution.py:211
  5.5 4.3 %collective-permute-start.10 = (bf16[128,256]{1,0:T(8,128)(2,1)S(1)}, bf16[128,256]{1,0:T(8,128)(2,1)S(1)}, u32[]{:S(2)}, u32[]{:S(2)}) collective-permute-start(bf16[128,256]{1,0:T(8,128)(2,1)S(1)} %get-tuple-element.67.refs_0_), channel_id=1, source_target_pairs={{0,8},{4,12},{8,0},{12,4},{16,24},{20,28},{24,16},{28,20},{1,9},{5... | collective-permute-start | bytes 196616 | tf_op jit(solution)/shard_map/ppermute | solution.py:211
  9.8 1.3 %collective-permute-start.16 = (bf16[128,256]{1,0:T(8,128)(2,1)S(1)}, bf16[128,256]{1,0:T(8,128)(2,1)S(1)}, u32[]{:S(2)}, u32[]{:S(2)}) collective-permute-start(bf16[128,256]{1,0:T(8,128)(2,1)S(1)} %collective-permute-done.12.refs_3_), channel_id=1, source_target_pairs={{0,4},{4,0},{8,12},{12,8},{16,20},{20,16},{24,28},{28,24},{1,5},{5... | collective-permute-start | bytes 196616 | tf_op jit(solution)/shard_map/ppermute | solution.py:211
  9.8 1.4 %collective-permute-start.15 = (bf16[128,256]{1,0:T(8,128)(2,1)S(1)}, bf16[128,256]{1,0:T(8,128)(2,1)S(1)}, u32[]{:S(2)}, u32[]{:S(2)}) collective-permute-start(bf16[128,256]{1,0:T(8,128)(2,1)S(1)} %collective-permute-done.11.refs_2_), channel_id=1, source_target_pairs={{0,4},{4,0},{8,12},{12,8},{16,20},{20,16},{24,28},{28,24},{1,5},{5... | collective-permute-start | bytes 196616 | tf_op jit(solution)/shard_map/ppermute | solution.py:211
  10.3 1.3 %collective-permute-start.14 = (bf16[128,256]{1,0:T(8,128)(2,1)S(1)}, bf16[128,256]{1,0:T(8,128)(2,1)S(1)}, u32[]{:S(2)}, u32[]{:S(2)}) collective-permute-start(bf16[128,256]{1,0:T(8,128)(2,1)S(1)} %collective-permute-done.10.refs_1_), channel_id=1, source_target_pairs={{0,4},{4,0},{8,12},{12,8},{16,20},{20,16},{24,28},{28,24},{1,5},{5... | collective-permute-start | bytes 196616 | tf_op jit(solution)/shard_map/ppermute | solution.py:211
  13.0 2.8 %collective-permute-start.17 = (bf16[128,1280]{1,0:T(8,128)(2,1)S(1)}, bf16[128,1280]{1,0:T(8,128)(2,1)S(1)}, u32[]{:S(2)}, u32[]{:S(2)}) collective-permute-start(bf16[128,1280]{1,0:T(8,128)(2,1)S(1)} %pad_maximum_fusion.refs_0_), channel_id=1, source_target_pairs={{0,4},{4,0},{8,12},{12,8},{16,20},{20,16},{24,28},{28,24},{1,5},{5... | collective-permute-start | bytes 983048 | tf_op jit(solution)/shard_map/ppermute | solution.py:211
  13.2 22.4 %collective-permute-start.21 = (bf16[256,768]{1,0:T(8,128)(2,1)}, bf16[256,768]{1,0:T(8,128)(2,1)S(1)}, u32[]{:S(2)}, u32[]{:S(2)}) collective-permute-start(bf16[256,768]{1,0:T(8,128)(2,1)} %project_1.1), channel_id=1, source_target_pairs={{0,2},{1,3},{2,0},{3,1},{4,6},{5,7},{6,4},{7,5},{8,10},{9,11},{10,... | collective-permute-start | bytes 1179656 | tf_op jit(solution)/shard_map/ppermute | solution.py:248
  15.8 11.5 %copy-start.2 = (bf16[128,1280]{1,0:T(8,128)(2,1)}, bf16[128,1280]{1,0:T(8,128)(2,1)S(1)}, u32[]{:S(2)}) copy-start(bf16[128,1280]{1,0:T(8,128)(2,1)S(1)} %collective-permute-done.17.refs_4_) | copy-start | bytes 983044
  15.8 7.6 %collective-permute-start.2 = (bf16[128,512]{1,0:T(8,128)(2,1)}, bf16[128,512]{1,0:T(8,128)(2,1)}, u32[]{:S(2)}, u32[]{:S(2)}) collective-permute-start(bf16[128,512]{1,0:T(8,128)(2,1)} %param.1), channel_id=1, source_target_pairs={{0,24},{4,28},{8,16},{12,20},{16,8},{20,12},{24,0},{28,4},{1,25},{... | collective-permute-start | bytes 393224 | tf_op jit(solution)/shard_map/cond/branch_1_fun/ppermute | solution.py:211
  17.5 7.8 %collective-permute-start.1 = (bf16[128,512]{1,0:T(8,128)(2,1)}, bf16[128,512]{1,0:T(8,128)(2,1)}, u32[]{:S(2)}, u32[]{:S(2)}) collective-permute-start(bf16[128,512]{1,0:T(8,128)(2,1)} %param.1), channel_id=1, source_target_pairs={{0,16},{4,20},{8,24},{12,28},{16,0},{20,4},{24,8},{28,12},{1,17},{... | collective-permute-start | bytes 393224 | tf_op jit(solution)/shard_map/cond/branch_1_fun/ppermute | solution.py:211
  18.4 7.1 %collective-permute-start = (bf16[128,512]{1,0:T(8,128)(2,1)}, bf16[128,512]{1,0:T(8,128)(2,1)}, u32[]{:S(2)}, u32[]{:S(2)}) collective-permute-start(bf16[128,512]{1,0:T(8,128)(2,1)} %param.1), channel_id=1, source_target_pairs={{0,8},{4,12},{8,0},{12,4},{16,24},{20,28},{24,16},{28,20},{1,9},{5... | collective-permute-start | bytes 393224 | tf_op jit(solution)/shard_map/cond/branch_1_fun/ppermute | solution.py:211
  19.3 6.5 %collective-permute-start.3 = (bf16[128,512]{1,0:T(8,128)(2,1)}, bf16[128,512]{1,0:T(8,128)(2,1)}, u32[]{:S(2)}, u32[]{:S(2)}) collective-permute-start(bf16[128,512]{1,0:T(8,128)(2,1)} %param.1), channel_id=1, source_target_pairs={{0,4},{4,0},{8,12},{12,8},{16,20},{20,16},{24,28},{28,24},{1,5},{5... | collective-permute-start | bytes 393224 | tf_op jit(solution)/shard_map/cond/branch_1_fun/ppermute | solution.py:211
  23.4 2.5 %collective-permute-start.6 = (bf16[128,512]{1,0:T(8,128)(2,1)}, bf16[128,512]{1,0:T(8,128)(2,1)}, u32[]{:S(2)}, u32[]{:S(2)}) collective-permute-start(bf16[128,512]{1,0:T(8,128)(2,1)} %collective-permute-done.2), channel_id=1, source_target_pairs={{0,4},{4,0},{8,12},{12,8},{16,20},{20,16},{24,28},{28,24},{1,5},{5... | collective-permute-start | bytes 393224 | tf_op jit(solution)/shard_map/cond/branch_1_fun/ppermute | solution.py:211
  25.3 1.7 %collective-permute-start.5 = (bf16[128,512]{1,0:T(8,128)(2,1)}, bf16[128,512]{1,0:T(8,128)(2,1)}, u32[]{:S(2)}, u32[]{:S(2)}) collective-permute-start(bf16[128,512]{1,0:T(8,128)(2,1)} %collective-permute-done.1), channel_id=1, source_target_pairs={{0,4},{4,0},{8,12},{12,8},{16,20},{20,16},{24,28},{28,24},{1,5},{5... | collective-permute-start | bytes 393224 | tf_op jit(solution)/shard_map/cond/branch_1_fun/ppermute | solution.py:211
  25.4 1.8 %collective-permute-start.4 = (bf16[128,512]{1,0:T(8,128)(2,1)}, bf16[128,512]{1,0:T(8,128)(2,1)}, u32[]{:S(2)}, u32[]{:S(2)}) collective-permute-start(bf16[128,512]{1,0:T(8,128)(2,1)} %collective-permute-done), channel_id=1, source_target_pairs={{0,4},{4,0},{8,12},{12,8},{16,20},{20,16},{24,28},{28,24},{1,5},{5... | collective-permute-start | bytes 393224 | tf_op jit(solution)/shard_map/cond/branch_1_fun/ppermute | solution.py:211
  27.2 18.3 %copy-start.8 = (bf16[128,1280]{1,0:T(8,128)(2,1)S(1)}, bf16[128,1280]{1,0:T(8,128)(2,1)}, u32[]{:S(2)}) copy-start(bf16[128,1280]{1,0:T(8,128)(2,1)} %copy-done.7) | copy-start | bytes 983044
  27.2 21.1 %copy-start.1 = (bf16[1024,768]{1,0:T(8,128)(2,1)S(1)}, bf16[1024,768]{1,0:T(8,128)(2,1)}, u32[]{:S(2)}) copy-start(bf16[1024,768]{1,0:T(8,128)(2,1)} %noise_ref.1) | copy-start | bytes 4718596
  27.2 21.1 %copy-start.4 = (s32[4,4]{1,0:T(4,128)S(1)}, s32[4,4]{1,0:T(4,128)}, u32[]{:S(2)}) copy-start(s32[4,4]{1,0:T(4,128)} %ranks_ref.3) | copy-start | bytes 196
  27.2 21.1 %copy-start.5 = (f32[1024]{0:T(1024)S(1)}, f32[1024]{0:T(1024)}, u32[]{:S(2)}) copy-start(f32[1024]{0:T(1024)} %param.14) | copy-start | bytes 12292
  27.2 21.1 %copy-start.6 = (f32[1024]{0:T(1024)S(1)}, f32[1024]{0:T(1024)}, u32[]{:S(2)}) copy-start(f32[1024]{0:T(1024)} %param.15) | copy-start | bytes 12292
  27.2 11.7 %collective-permute-start.20 = (bf16[128,1280]{1,0:T(8,128)(2,1)}, bf16[128,1280]{1,0:T(8,128)(2,1)S(1)}, u32[]{:S(2)}, u32[]{:S(2)}) collective-permute-start(bf16[128,1280]{1,0:T(8,128)(2,1)} %copy-done.7), channel_id=1, source_target_pairs={{0,24},{4,28},{8,16},{12,20},{16,8},{20,12},{24,0},{28,4},{1,25},{... | collective-permute-start | bytes 983048 | tf_op jit(solution)/shard_map/ppermute | solution.py:211
  29.0 16.5 %collective-permute-start.19 = (bf16[128,1280]{1,0:T(8,128)(2,1)}, bf16[128,1280]{1,0:T(8,128)(2,1)}, u32[]{:S(2)}, u32[]{:S(2)}) collective-permute-start(bf16[128,1280]{1,0:T(8,128)(2,1)} %copy-done.7), channel_id=1, source_target_pairs={{0,16},{4,20},{8,24},{12,28},{16,0},{20,4},{24,8},{28,12},{1,17},{... | collective-permute-start | bytes 983048 | tf_op jit(solution)/shard_map/ppermute | solution.py:211
  29.8 15.6 %collective-permute-start.18 = (bf16[128,1280]{1,0:T(8,128)(2,1)}, bf16[128,1280]{1,0:T(8,128)(2,1)}, u32[]{:S(2)}, u32[]{:S(2)}) collective-permute-start(bf16[128,1280]{1,0:T(8,128)(2,1)} %copy-done.7), channel_id=1, source_target_pairs={{0,8},{4,12},{8,0},{12,4},{16,24},{20,28},{24,16},{28,20},{1,9},{5... | collective-permute-start | bytes 983048 | tf_op jit(solution)/shard_map/ppermute | solution.py:211
  33.9 14.4 %copy-start.3 = (bf16[128,1280]{1,0:T(8,128)(2,1)S(1)}, bf16[128,1280]{1,0:T(8,128)(2,1)}, u32[]{:S(2)}) copy-start(bf16[128,1280]{1,0:T(8,128)(2,1)} %copy-done.2) | copy-start | bytes 983044
  33.9 17.7 %collective-permute-start.22 = (bf16[256,768]{1,0:T(8,128)(2,1)}, bf16[256,768]{1,0:T(8,128)(2,1)S(1)}, u32[]{:S(2)}, u32[]{:S(2)}) collective-permute-start(bf16[256,768]{1,0:T(8,128)(2,1)} %get-tuple-element.62), channel_id=1, source_target_pairs={{0,1},{1,2},{2,3},{3,0},{4,5},{5,6},{6,7},{7,4},{8,9},{9,10},{10,1... | collective-permute-start | bytes 1179656 | tf_op jit(solution)/shard_map/ppermute | solution.py:248
  35.5 18.9 %collective-permute-start.23 = (bf16[256,768]{1,0:T(8,128)(2,1)}, bf16[256,768]{1,0:T(8,128)(2,1)S(1)}, u32[]{:S(2)}, u32[]{:S(2)}) collective-permute-start(bf16[256,768]{1,0:T(8,128)(2,1)} %get-tuple-element.64), channel_id=1, source_target_pairs={{0,3},{1,0},{2,1},{3,2},{4,7},{5,4},{6,5},{7,6},{8,11},{9,8},{10,9... | collective-permute-start | bytes 1179656 | tf_op jit(solution)/shard_map/ppermute | solution.py:248
  45.5 2.0 %collective-permute-start.7 = (bf16[128,1280]{1,0:T(8,128)(2,1)}, bf16[128,1280]{1,0:T(8,128)(2,1)}, u32[]{:S(2)}, u32[]{:S(2)}) collective-permute-start(bf16[128,1280]{1,0:T(8,128)(2,1)} %get-tuple-element.14), channel_id=1, source_target_pairs={{0,4},{4,0},{8,12},{12,8},{16,20},{20,16},{24,28},{28,24},{1,5},{5... | collective-permute-start | bytes 983048 | tf_op jit(solution)/shard_map/cond/branch_1_fun/ppermute | solution.py:211
  45.6 2.4 %collective-permute-start.8 = (bf16[128,1280]{1,0:T(8,128)(2,1)}, bf16[128,1280]{1,0:T(8,128)(2,1)}, u32[]{:S(2)}, u32[]{:S(2)}) collective-permute-start(bf16[128,1280]{1,0:T(8,128)(2,1)} %get-tuple-element.15), channel_id=1, source_target_pairs={{0,4},{4,0},{8,12},{12,8},{16,20},{20,16},{24,28},{28,24},{1,5},{5... | collective-permute-start | bytes 983048 | tf_op jit(solution)/shard_map/cond/branch_1_fun/ppermute | solution.py:211
  46.1 2.2 %collective-permute-start.9 = (bf16[128,1280]{1,0:T(8,128)(2,1)S(1)}, bf16[128,1280]{1,0:T(8,128)(2,1)}, u32[]{:S(2)}, u32[]{:S(2)}) collective-permute-start(bf16[128,1280]{1,0:T(8,128)(2,1)S(1)} %get-tuple-element.16), channel_id=1, source_target_pairs={{0,4},{4,0},{8,12},{12,8},{16,20},{20,16},{24,28},{28,24},{1,5},{5... | collective-permute-start | bytes 983048 | tf_op jit(solution)/shard_map/cond/branch_1_fun/ppermute | solution.py:211
  (3 other events, 15.7 us)
